TPU v7x, 32 devices: a whole 2x2x4 slice. The times are simulated.
32 devices in a mesh: ctx: 8 (over z, y), head: 4 (over x, core).
Axes of the slice: x: 2, y: 2, z: 4, core: 2. Of those that a mesh axis runs over, the one named last changes fastest.
Arguments:
- q_lin: bfloat16 [1024, 8192], P('ctx', 'head'), may hold values from -6 to 6
- k_lin: bfloat16 [1024, 8192], P('ctx', 'head'), may hold values from -6 to 6
- v_lin: bfloat16 [1024, 8192], P('ctx', 'head'), may hold values from -70 to 70
- log_decay: float32 [64, 1024], P('head', 'ctx'), may hold values from -1 to 0
- gate: bfloat16 [1024, 8192], P('ctx', 'head'), may hold values from -6 to 6
- norm_gain: float32 [8192], P('head'), may hold values from 0.1 to 1.9
- queries: bfloat16 [1024, 8192], P('ctx', 'head'), may hold values from -8 to 8
- keys: bfloat16 [1024, 1024], P('ctx', 'head'), may hold values from -4 to 4
- values: bfloat16 [1024, 1024], P('ctx', 'head'), may hold values from -6 to 6
- order: int32 [8], P('ctx'), may hold values from 0 to 7, each once
Outputs:
- mixed: bfloat16 [1024, 8192], P('ctx', 'head')
- attended: bfloat16 [1024, 8192], P('ctx', 'head')
Inputs may be any that keep to these rules, and one draw needn't show every extreme that they name: order is a permutation of the 8 sequence shards.
All inputs are finite; a program needn't handle non-finite values.
Results may differ from a plain program's by a relative error of at most 0.0045.
Values may be sent and summed in bfloat16 or wider, within the bound.
No kernel may reach another device: no remote copies, remote signals or barrier semaphores. Data moves between devices by JAX's collectives and lax.ppermute only.
A program may use at most 128 MiB of HBM per device.

v0:
```python
import math

import jax
import jax.numpy as jnp
from jax import lax
from jax.sharding import PartitionSpec as P

H = 64
HD = 128
BLOCK = 128


EPS = 1e-06
HIGH = lax.Precision.HIGHEST


def entering(array, axis, combine, identity):
    size, index = (lax.axis_size(axis), lax.axis_index(axis))
    everything = jax.tree.map(lambda part: lax.all_gather(part, axis), array)
    start = jax.tree.map(
        lambda part, zero: jnp.broadcast_to(jnp.asarray(zero, part.dtype), part.shape),
        array,
        identity,
    )

    def hop(k, before):
        reached = k < index
        new = combine(before, jax.tree.map(lambda part: part[k], everything))
        return jax.tree.map(lambda a, b: jnp.where(reached, a, b), new, before)

    return lax.fori_loop(0, size, hop, start)


def lightning_blocks(qa, ka, va, decay_log, state0):
    total = qa.shape[0]
    heads = qa.shape[1]
    count = total // BLOCK
    qb_all = qa.reshape(count, BLOCK, heads, HD)
    kb_all = ka.reshape(count, BLOCK, heads, HD)
    vb_all = va.reshape(count, BLOCK, heads, HD)
    gb_all = decay_log.reshape(heads, count, BLOCK).transpose(1, 0, 2)

    def step(state, pieces):
        qb, kb, vb, gb = pieces
        cum = jnp.cumsum(gb, axis=1)
        scores = jnp.einsum("thd,shd->hts", qb, kb, preferred_element_type=jnp.float32)
        lower = lax.iota(jnp.int32, BLOCK)[:, None] >= lax.iota(jnp.int32, BLOCK)[None, :]
        diff = cum[:, :, None] - cum[:, None, :]
        decay = jnp.where(lower[None], jnp.exp(jnp.where(lower[None], diff, 0.0)), 0.0)
        weights = (scores * decay).astype(jnp.bfloat16)
        intra = jnp.einsum("hts,shd->thd", weights, vb, preferred_element_type=jnp.float32)
        qdec = qb.astype(jnp.float32) * jnp.exp(cum).T[:, :, None]
        inter = jnp.einsum("thd,hde->the", qdec, state, precision=HIGH)
        kdec = kb.astype(jnp.float32) * jnp.exp(cum[:, -1:] - cum).T[:, :, None]
        update = jnp.einsum("thd,the->hde", kdec, vb.astype(jnp.float32), precision=HIGH)
        state_new = jnp.exp(cum[:, -1])[:, None, None] * state + update
        return (state_new, intra + inter)

    state, outs = lax.scan(step, state0, (qb_all, kb_all, vb_all, gb_all))
    return (outs.reshape(total, heads, HD), state)


def combine_states(earlier, later):
    return (earlier[0] * later[0], later[0][:, None, None] * earlier[1] + later[1])


def body(q_lin, k_lin, v_lin, log_decay, gate, norm_gain, queries, keys, values, order):
    tokens = q_lin.shape[0]
    heads = log_decay.shape[0]
    width = q_lin.shape[1]
    qa = jax.nn.silu(q_lin.astype(jnp.float32)).astype(jnp.bfloat16).reshape(tokens, heads, HD)
    ka = jax.nn.silu(k_lin.astype(jnp.float32)).astype(jnp.bfloat16).reshape(tokens, heads, HD)
    va = jax.nn.silu(v_lin.astype(jnp.float32)).astype(jnp.bfloat16).reshape(tokens, heads, HD)
    empty = jnp.zeros((heads, HD, HD), jnp.float32)
    decay_total = jnp.exp(jnp.sum(log_decay, axis=1))
    unit = jnp.ones_like(decay_total)
    local_out, local_state = lightning_blocks(qa, ka, va, log_decay, empty)
    prefix = entering((decay_total, local_state), "ctx", combine_states, (unit, empty))
    carried = prefix[1]
    cum_full = jnp.cumsum(log_decay, axis=1)
    qdec = qa.astype(jnp.float32) * jnp.exp(cum_full).T[:, :, None]
    lin = local_out + jnp.einsum("thd,hde->the", qdec, carried, precision=HIGH)
    squares = jnp.sum(lin * lin, axis=(1, 2))
    total = lax.psum(squares, "head")
    inv = lax.rsqrt(total / (H * HD) + EPS)
    gated = jax.nn.sigmoid(gate.astype(jnp.float32).reshape(tokens, heads, HD))
    mixed = (
        (lin * inv[:, None, None] * norm_gain.reshape(heads, HD) * gated)
        .astype(jnp.bfloat16)
        .reshape(tokens, width)
    )
    kv_heads = keys.shape[1] // HD
    group = heads // kv_heads
    qgroup = queries.reshape(tokens, kv_heads, group, HD)
    first_pos = order[0] * tokens
    qpos = first_pos + lax.iota(jnp.int32, tokens)
    last_pos = first_pos + tokens - 1
    scale = 1.0 / math.sqrt(HD)

    def update(carry, kblock, vblock, kstart):
        top, den, acc = carry
        count = kblock.shape[0]
        kparts = kblock.reshape(count, kv_heads, HD)
        vparts = vblock.reshape(count, kv_heads, HD)
        scores = (
            jnp.einsum("tkgd,skd->kgts", qgroup, kparts, preferred_element_type=jnp.float32) * scale
        )
        kpos = kstart + lax.iota(jnp.int32, count)
        mask = kpos[None, :] <= qpos[:, None]
        masked = jnp.where(mask, scores, -1e30)
        top_new = jnp.maximum(top, jnp.max(masked, axis=-1))
        alpha = jnp.exp(top - top_new)
        probs = jnp.where(mask, jnp.exp(masked - top_new[..., None]), 0.0)
        den_new = den * alpha + jnp.sum(probs, axis=-1)
        acc_new = acc * alpha[..., None] + jnp.einsum(
            "kgts,skd->kgtd", probs.astype(jnp.bfloat16), vparts, preferred_element_type=jnp.float32
        )
        return (top_new, den_new, acc_new)

    def visit(carry, kblock, vblock, kstart):
        return lax.cond(
            kstart > last_pos,
            lambda held: held,
            lambda held: update(held, kblock, vblock, kstart),
            carry,
        )

    init = (
        jnp.full((kv_heads, group, tokens), -1e30, jnp.float32),
        jnp.zeros((kv_heads, group, tokens), jnp.float32),
        jnp.zeros((kv_heads, group, tokens, HD), jnp.float32),
    )
    kpiece = lax.all_gather(keys, "ctx", axis=0, tiled=True)
    vpiece = lax.all_gather(values, "ctx", axis=0, tiled=True)
    rows = kpiece.shape[0]
    stride = 512
    count = rows // stride

    def loop_body(index, held):
        offset = index * stride
        kslice = lax.dynamic_slice_in_dim(kpiece, offset, stride, 0)
        vslice = lax.dynamic_slice_in_dim(vpiece, offset, stride, 0)
        return visit(held, kslice, vslice, offset)

    top, den, acc = lax.fori_loop(0, count, loop_body, init)
    attended = (
        (acc / den[..., None]).transpose(2, 0, 1, 3).reshape(tokens, width).astype(jnp.bfloat16)
    )
    return (mixed, attended)


def solution(mesh):
    return jax.shard_map(
        body,
        mesh=mesh,
        in_specs=(
            P("ctx", "head"),
            P("ctx", "head"),
            P("ctx", "head"),
            P("head", "ctx"),
            P("ctx", "head"),
            P("head"),
            P("ctx", "head"),
            P("ctx", "head"),
            P("ctx", "head"),
            P("ctx"),
        ),
        out_specs=(P("ctx", "head"), P("ctx", "head")),
        check_vma=False,
    )
```

profile of v0, /device:TPU:0, one launch (start us, length us, event | category | flops | bytes accessed | tf_op | source)
XLA Modules:
  0.0 190.0 jit_solution(13610800309384847638)
XLA Ops:
  10.2 1.9 %fusion.36 = (bf16[16,16,8,128]{3,2,1,0:T(8,128)(2,1)S(1)}, bf16[16,16,8,128]{3,2,1,0:T(8,128)(2,1)S(1)}) fusion(bf16[128,2048]{1,0:T(8,128)(2,1)} %param.16, bf16[128,2048]{1,0:T(8,128)(2,1)} %param.18), kind=kLoop, calls=%fused_computation.58 | loop fusion | flops 3145728 | bytes 2097152
  12.2 1.6 convolution_add_fusion.1
  15.3 23.6 %all-reduce = f32[128]{0:T(128)S(1)} all-reduce(f32[128]{0:T(128)S(1)} %exponential_dynamic-update-slice_fusion), channel_id=2, replica_groups=mesh['ctx'=8,'head'=4] {'ctx'}, use_global_device_ids=true, to_apply=%add | all-reduce | flops 128 | bytes 1024
  43.2 30.5 %all_gather.19 = bf16[1024,256]{0,1:T(8,128)(2,1)S(1)} all-gather(bf16[128,256]{0,1:T(8,128)(2,1)S(1)} %copy.50), channel_id=1, replica_groups=mesh['ctx'=8,'head'=4] {'ctx'}, dimensions={0}, use_global_device_ids=true | all-gather | bytes 589824 | tf_op jit(solution)/shard_map/all_gather | solution.py:133
  73.7 31.1 %all_gather.20 = bf16[1024,256]{0,1:T(8,128)(2,1)S(1)} all-gather(bf16[128,256]{0,1:T(8,128)(2,1)S(1)} %copy.52), channel_id=1, replica_groups=mesh['ctx'=8,'head'=4] {'ctx'}, dimensions={0}, use_global_device_ids=true | all-gather | bytes 589824 | tf_op jit(solution)/shard_map/all_gather | solution.py:134
  105.9 4.8 %while.37 = (s32[]{:T(128)}, f32[2,8,128]{2,1,0:T(8,128)S(1)}, f32[2,8,128]{2,1,0:T(8,128)S(1)}, f32[2,8,128,128]{3,2,1,0:T(8,128)}, s32[]{:T(128)}, /*index=5*/...) while((s32[]{:T(128)}, f32[2,8,128]{2,1,0:T(8,128)S(1)}, ...), condition=%wide.region_11.12_spmd.clone, body=%wide.region_6.11_spmd.clone.sunk | while | flops 551096960 | bytes 25565540 | solution.py:145
  105.9 4.8 %conditional.3 = (f32[2,8,128]{2,1,0:T(8,128)S(1)}, f32[2,8,128]{2,1,0:T(8,128)S(1)}, f32[2,8,128,128]{3,2,1,0:T(8,128)}) conditional(s32[]{:T(128)} %convert_element_type.145, (s32[]{:T(128)}, s32[]{:T(128)}, bf16[1024,256]{0,1:T(8,128)(2,1)S(1)}, bf16[128,2,8,128]{3,0,2,1:T(8,128)(2,1)S(1)}, f32[2,8,128]{2,1,0:T(8,128)S(1)}, ...), branch_computations={%region_7.9_spmd, %region_10.10_spmd} | conditional | flops 551096960 | bytes 25548414 | solution.py:121
  108.0 1.7 fusion.8
  110.7 1.6 fusion.51
  113.6 1.9 %fusion.16 = f32[16,128,128]{2,1,0:T(8,128)S(1)} fusion(bf16[128,16,128]{0,2,1:T(8,128)(2,1)} %bitcast.89, f32[16,128]{1,0:T(8,128)S(1)} %reduce_window_sum.13, pred[128,128]{1,0:T(8,128)(4,1)S(1)} %iota_compare_fusion, bf16[16,16,8,128]{3,2,1,0:T(8,128)(2,1)} %copy-done.4, bf16[16,16,8,128]{3,2,1,0:T(8,128)(2,1)S(1)} %get-tuple-element.495), kind=kOutput, calls=%fused_computation.33 | convolution fusion | flops 135528448 | bytes 2646016 | tf_op jit(solution)/shard_map/while/body/eval_jaxpr/hts,shd->thd/dot_general | solution.py:51
  115.5 3.3 %convolution_add_fusion.2 = f32[16,128,128]{2,1,0:T(8,128)} fusion(f32[16,128,128]{2,1,0:T(8,128)S(1)} %fusion.16, f32[128,16]{0,1:T(8,128)S(1)} %get-tuple-element.492, bf16[16,16,8,128]{3,2,1,0:T(8,128)(2,1)S(1)} %get-tuple-element.495), kind=kOutput, calls=%fused_computation.24 | convolution fusion | flops 403439616 | bytes 2629632 | tf_op jit(solution)/shard_map/while/body/eval_jaxpr/thd,hde->the/dot_general | solution.py:53
  118.9 39.1 %all-gather.4.cloned.1.call-done = f32[128,128,128]{2,1,0:T(8,128)} async-done(((f32[16,128,128]{2,1,0:T(8,128)}), f32[128,128,128]{2,1,0:T(8,128)}) %all-gather.4.cloned.1.call-update) | async-done | bytes 8388624 | tf_op jit(solution)/shard_map/all_gather | solution.py:19
  158.0 11.9 %while.38 = (s32[]{:T(128)}, f32[16,128,128]{2,1,0:T(8,128)S(1)}, s32[]{:T(128)}, f32[8,16]{1,0:T(8,128)S(1)}, f32[8,16,128,128]{3,2,1,0:T(8,128)}, /*index=5*/s32[]{:T(128)}, s32[]{:T(128)}) while((s32[]{:T(128)}, f32[16,128,128]{2,1,0:T(8,128)S(1)}, s32[]{:T(128)}, f32[8,16]{1,0:T(8,128)S(1)}, f32[8,16,128,128]{3,2,1,0:T(8,128)}, ...), condition=%wide.region_3.4_spmd.clone, body=%wide.region_2.3_spmd.clone.sunk | while | flops 1048580 | bytes 3146025 | solution.py:31
  158.0 1.5 fusion.67
  159.5 1.5 fusion.67
  161.0 1.5 fusion.67
  162.5 1.5 fusion.67
  163.9 1.5 fusion.67
  165.4 1.5 fusion.67
  166.9 1.5 fusion.67
  168.4 1.5 fusion.67
  169.9 4.4 %multiply_reduce_fusion = (f32[128]{0:T(128)S(1)}, f32[16,128,128]{2,1,0:T(8,128)}) fusion(f32[16,128,128]{2,1,0:T(8,128)} %convolution_add_fusion.2, f32[16,128,128]{2,1,0:T(8,128)S(1)} %get-tuple-element.385, f32[128,16]{0,1:T(8,128)S(1)} %get-tuple-element.492, bf16[16,16,8,128]{3,2,1,0:T(8,128)(2,1)S(1)} %get-tuple-element.495), kind=kOutput, calls=%fused_computation.50 | convolution fusion | flops 403963776 | bytes 3678720 | tf_op jit(solution)/shard_map/thd,hde->the/dot_general | solution.py:82
  174.3 6.2 %psum.7 = f32[128]{0:T(128)S(1)} all-reduce(f32[128]{0:T(128)S(1)} %get-tuple-element.493), channel_id=1, replica_groups=mesh['ctx'=8,'head'=4] {'head'}, use_global_device_ids=true, to_apply=%region_5.6 | all-reduce | flops 128 | bytes 1024 | tf_op jit(solution)/shard_map/psum | solution.py:84
  180.5 1.6 fusion.29
  (72 shorter events, 13.8 us)
Async XLA Ops:
  7.2 6.8 %copy-start.10 = (u32[32]{0:T(128)S(1)}, u32[32]{0:T(128)}, u32[]{:S(2)}) copy-start(u32[32]{0:T(128)} %constant.136) | copy-start | bytes 388
  7.2 6.7 %copy-start.8 = (f32[16,128]{1,0:T(8,128)S(1)}, f32[16,128]{1,0:T(8,128)}, u32[]{:S(2)}) copy-start(f32[16,128]{1,0:T(8,128)} %param.19) | copy-start | bytes 24580
  7.2 31.8 %copy-start.5 = (bf16[128,2048]{1,0:T(8,128)(2,1)S(1)}, bf16[128,2048]{1,0:T(8,128)(2,1)}, u32[]{:S(2)}) copy-start(bf16[128,2048]{1,0:T(8,128)(2,1)} %param.20) | copy-start | bytes 1572868
  7.2 150.8 %all-gather.4.cloned.1.call-start = ((), (), s32[]{:S(2)}) async-start(), calls=%async_computation | async-start | bytes 9437184 | tf_op jit(solution)/shard_map/all_gather | solution.py:19
  10.2 3.7 %copy-start.3 = (bf16[128,2048]{0,1:T(8,128)(2,1)}, bf16[128,2048]{0,1:T(8,128)(2,1)S(1)}, u32[]{:S(2)}) copy-start(bf16[128,2048]{0,1:T(8,128)(2,1)S(1)} %copy.65) | copy-start | bytes 1572868
  12.1 1.7 copy-start.4
  12.1 30.8 %copy-start.6 = (bf16[128,256]{1,0:T(8,128)(2,1)S(1)}, bf16[128,256]{1,0:T(8,128)(2,1)}, u32[]{:S(2)}) copy-start(bf16[128,256]{1,0:T(8,128)(2,1)} %param.23) | copy-start | bytes 196612
  12.1 31.0 %copy-start.7 = (bf16[128,256]{1,0:T(8,128)(2,1)S(1)}, bf16[128,256]{1,0:T(8,128)(2,1)}, u32[]{:S(2)}) copy-start(bf16[128,256]{1,0:T(8,128)(2,1)} %param.24) | copy-start | bytes 196612
  106.1 1.9 %copy-start.1 = (f32[2,8,128,128]{3,2,1,0:T(8,128)S(1)}, f32[2,8,128,128]{3,2,1,0:T(8,128)}, u32[]{:S(2)}) copy-start(f32[2,8,128,128]{3,2,1,0:T(8,128)} %get-tuple-element.365) | copy-start | bytes 3145732 | tf_op jit(solution)/shard_map/while/body/eval_jaxpr/cond
  109.7 1.0 copy-start.2
  158.0 22.6 %copy-start.9 = (f32[2048]{0:T(1024)S(1)}, f32[2048]{0:T(1024)}, u32[]{:S(2)}) copy-start(f32[2048]{0:T(1024)} %param.21) | copy-start | bytes 24580
  169.9 10.6 %copy-start = (f32[128,2048]{0,1:T(8,128)S(1)}, f32[128,2048]{0,1:T(8,128)}, u32[]{:S(2)}) copy-start(f32[128,2048]{0,1:T(8,128)} %copy.49) | copy-start | bytes 3145732
Sparse Core Ops, SparseCore 0:
  13.9 143.9 all-gather.3
where the time goes:
time: 191 us; the launch traced here: 190 us
  blocking collectives  91.4 us (48%)
  waiting for transfers between devices  39.1 us (20%)
  other arithmetic  20.8 us (11%)
  between operations  15.6 us (8%)
  matrix products  13.8 us (7%)
  local copies, waits for them, and re-layouts  8.92 us (5%)
    all_gather x1, waiting for transfers between devices, entering(): everything = jax.tree.map(lambda part: lax.all_gather(part, axis), array)  39.1 us
    all_gather x1, blocking collectives, body(): vpiece = lax.all_gather(values, 'ctx', axis=0, tiled=True)  31.1 us
    all_gather x1, blocking collectives, body(): kpiece = lax.all_gather(keys, 'ctx', axis=0, tiled=True)  30.5 us
    unnamed x1, blocking collectives  23.6 us
    select_n x8, other arithmetic, hop(): return jax.tree.map(lambda a, b: jnp.where(reached, a, b), new, before)  11.7 us
    psum x1, blocking collectives, body(): total = lax.psum(squares, 'head')  6.2 us
    unnamed x27, local copies, waits for them, and re-layouts  4.49 us
    dot_general x1, matrix products, body(): lin = local_out + jnp.einsum('thd,hde->the', qdec, carried, precision=HIGH)  4.39 us
  transfers between devices with their start and end apart: 1, of which 1 were waited for; matrix products, arithmetic and copies ran while one was open for 9% of the time, Pallas kernels for 0%

commit v1 on v0

v1 whole, which is shorter than its diff:
```python
import functools
import math

import jax
import jax.numpy as jnp
from jax import lax
from jax.experimental import pallas as pl
from jax.experimental.pallas import tpu as pltpu
from jax.sharding import PartitionSpec as P

HD = 128
EPS = 1e-06
HIGH = lax.Precision.HIGHEST
F32 = jnp.float32
BF16 = jnp.bfloat16
NT = (((1,), (1,)), ((), ()))
TN = (((0,), (0,)), ((), ()))
MIB = 1 << 20


def silu16(x):
    x = x.astype(F32)
    return (x / (1.0 + jnp.exp(-x))).astype(BF16)


def lower_ones(size):
    rows = lax.broadcasted_iota(jnp.int32, (size, size), 0)
    cols = lax.broadcasted_iota(jnp.int32, (size, size), 1)
    return rows >= cols


def head_cols(h):
    return slice(h * HD, (h + 1) * HD)


def my_rank(group):
    return lax.rem(lax.axis_index("ctx"), group)


def dyn(index, size):
    return pl.ds(pl.multiple_of(index * size, size), size)


def state_kernel(group, heads, ld_ref, k_ref, v_ref, *rest):
    outs, (states, totals) = rest[:group], rest[group:]
    tokens = k_ref.shape[0]
    per = heads // group
    rank = my_rank(group)
    ld = ld_ref[...]
    tri = lower_ones(tokens).astype(F32)
    cum = lax.dot_general(tri, ld, NT, precision=HIGH, preferred_element_type=F32)
    weight = jnp.exp(cum[tokens - 1 : tokens, :] - cum)
    total = jnp.broadcast_to(jnp.exp(jnp.sum(ld, axis=1, keepdims=True)), (heads, HD))
    high = total.astype(BF16).astype(F32)
    low = total - high
    totals[...] = jnp.zeros_like(totals)
    for k in range(group):
        totals[k * 16 : k * 16 + per, :] = high[k * per : (k + 1) * per]
        totals[k * 16 + 8 : k * 16 + 8 + per, :] = low[k * per : (k + 1) * per]
    for h in range(heads):
        ka = silu16(k_ref[:, head_cols(h)])
        va = silu16(v_ref[:, head_cols(h)])
        kdec = ka.astype(F32) * weight[:, h : h + 1]
        khigh = kdec.astype(BF16)
        klow = (kdec - khigh.astype(F32)).astype(BF16)
        state = lax.dot_general(khigh, va, TN, preferred_element_type=F32)
        state += lax.dot_general(klow, va, TN, preferred_element_type=F32)
        states[h * HD : (h + 1) * HD, :] = state.astype(BF16)
    for s in range(group):
        dest = rank ^ s
        outs[s][: per * HD, :] = states[dyn(dest, per * HD), :]
        outs[s][per * HD :, :] = totals[dyn(dest, 16), :].astype(BF16)


def decay_row(slots, k, base, j):
    tail = slots[k, base : base + 16, :].astype(F32)
    return tail[j : j + 1] + tail[8 + j : 9 + j]


def fill_slots(group, rank, pays, slots):
    for s in range(group):
        slots[rank ^ s] = pays[s][...]


def total_kernel(group, per, *refs):
    pays, out, slots = refs[:group], refs[group], refs[group + 1]
    fill_slots(group, my_rank(group), pays, slots)
    base = per * HD
    tails = []
    for j in range(per):
        state = slots[0, j * HD : (j + 1) * HD, :].astype(F32)
        whole = decay_row(slots, 0, base, j)
        for k in range(1, group):
            decay = decay_row(slots, k, base, j)
            state = decay * state + slots[k, j * HD : (j + 1) * HD, :].astype(F32)
            whole = whole * decay
        out[j * HD : (j + 1) * HD, :] = state.astype(BF16)
        tails.append(whole)
    pad = [jnp.zeros((8 - per, HD), F32)] if per < 8 else []
    total = jnp.concatenate(tails + pad, axis=0)
    high = total.astype(BF16).astype(F32)
    out[base:, :] = jnp.concatenate([high, total - high], axis=0).astype(BF16)


def prefix_kernel(group, per, carried, *refs):
    pays, refs = refs[:group], refs[group:]
    carry = None
    if carried:
        carry, refs = refs[0], refs[1:]
    outs, slots, prefixes = refs[:group], refs[group], refs[group + 1]
    rank = my_rank(group)
    fill_slots(group, rank, pays, slots)
    base = per * HD
    for j in range(per):
        rows = slice(j * HD, (j + 1) * HD)
        state = carry[rows, :].astype(F32) if carried else jnp.zeros((HD, HD), F32)
        prefixes[0, rows, :] = state.astype(BF16)
        for k in range(group - 1):
            state = decay_row(slots, k, base, j) * state + slots[k, rows, :].astype(F32)
            prefixes[k + 1, rows, :] = state.astype(BF16)
    for s in range(group):
        outs[s][...] = prefixes[rank ^ s]


def intra_kernel(heads, ld_ref, q_ref, k_ref, v_ref, out_ref):
    tokens = q_ref.shape[0]
    ld = ld_ref[...]
    lower = lower_ones(tokens)
    tri = lower.astype(F32)
    cum = lax.dot_general(tri, ld, NT, precision=HIGH, preferred_element_type=F32)
    cum_t = lax.dot_general(ld, tri, NT, precision=HIGH, preferred_element_type=F32)
    bias = jnp.where(lower, 0.0, -1e30)
    for h in range(heads):
        qa = silu16(q_ref[:, head_cols(h)])
        ka = silu16(k_ref[:, head_cols(h)])
        va = silu16(v_ref[:, head_cols(h)])
        scores = lax.dot_general(qa, ka, NT, preferred_element_type=F32)
        decay = jnp.exp((cum[:, h : h + 1] - cum_t[h : h + 1, :]) + bias)
        weights = (scores * decay).astype(BF16)
        out_ref[:, head_cols(h)] = jnp.dot(weights, va, preferred_element_type=F32)


def inter_kernel(group, heads, ld_ref, q_ref, intra_ref, *rest):
    parts, (lin_ref, squares_ref, states) = rest[:group], rest[group:]
    tokens = q_ref.shape[0]
    per = heads // group
    rank = my_rank(group)
    for s in range(group):
        states[dyn(rank ^ s, per * HD), :] = parts[s][...]
    tri = lower_ones(tokens).astype(F32)
    cum = lax.dot_general(tri, ld_ref[...], NT, precision=HIGH, preferred_element_type=F32)
    decay = jnp.exp(cum)
    acc = jnp.zeros((tokens, HD), F32)
    for h in range(heads):
        qa = silu16(q_ref[:, head_cols(h)])
        inter = jnp.dot(qa, states[h * HD : (h + 1) * HD, :], preferred_element_type=F32)
        lin = intra_ref[:, head_cols(h)] + inter * decay[:, h : h + 1]
        lin_ref[:, head_cols(h)] = lin
        acc += lin * lin
    ones = jnp.ones((8, HD), F32)
    squares_ref[...] = lax.dot_general(ones, acc, NT, precision=HIGH, preferred_element_type=F32)


def mixed_kernel(heads, columns, lin_ref, gate_ref, gain_ref, *rest):
    squares, out_ref = rest[:-1], rest[-1]
    total = squares[0][...]
    for part in squares[1:]:
        total = total + part[...]
    inv = jnp.transpose(lax.rsqrt(total / columns + EPS))[:, 0:1]
    for h in range(heads):
        cols = head_cols(h)
        gate = 1.0 / (1.0 + jnp.exp(-gate_ref[:, cols].astype(F32)))
        out_ref[:, cols] = (lin_ref[:, cols] * inv * gain_ref[:, cols] * gate).astype(BF16)


def softmax_kernel(count, group, block, heads, order_ref, q_ref, *rest):
    chunks, (out_ref, kv, bias_ref) = rest[:count], rest[count:]
    tokens = q_ref.shape[0]
    width = chunks[0].shape[1] // 2
    kv_heads = width // HD
    share = heads // kv_heads
    me = lax.axis_index("ctx")
    rank, mine = lax.rem(me, group), lax.div(me, group)
    groups = count // group
    for i in range(count):
        s, d = divmod(i, groups)
        place = lax.rem(mine + groups - d, groups) * group + (rank ^ s)
        kv[dyn(place, tokens), :] = chunks[i][...]
    first = order_ref[0] * tokens
    scale = math.log2(math.e) / math.sqrt(HD)
    blocks = count * tokens // block
    pack = 2 if share % 2 == 0 else 1

    def allowed(start):
        qpos = first + lax.broadcasted_iota(jnp.int32, (tokens, block), 0)
        kpos = start + lax.broadcasted_iota(jnp.int32, (tokens, block), 1)
        return jnp.where(kpos <= qpos, 0.0, -1e30)

    def query(h):
        return jnp.concatenate([q_ref[:, head_cols(h + i)] for i in range(pack)], axis=0)

    def store(h, value):
        for i in range(pack):
            out_ref[:, head_cols(h + i)] = value[i * tokens : (i + 1) * tokens]

    def scores(h, start):
        g = h // share
        keys = kv[pl.ds(start, block), head_cols(g)]
        raw = lax.dot_general(query(h), keys, NT, preferred_element_type=F32)
        return raw.reshape(pack, tokens, block) + bias_ref[...][None]

    def weigh(h, start, probs):
        values = kv[pl.ds(start, block), width + (h // share) * HD : width + (h // share + 1) * HD]
        flat = probs.astype(BF16).reshape(pack * tokens, block)
        return jnp.dot(flat, values, preferred_element_type=F32)

    if blocks == 1:
        bias_ref[...] = allowed(0)
        for h in range(0, heads, pack):
            raw = scores(h, 0)
            top = jnp.max(raw, axis=-1, keepdims=True)
            probs = jnp.exp2((raw - top) * scale)
            den = jnp.sum(probs, axis=-1, keepdims=True).reshape(pack * tokens, 1)
            store(h, (weigh(h, 0, probs) / den).astype(BF16))
        return

    reach = lax.div(first + tokens - 1, block) + 1
    for h in range(0, heads, pack):

        def step(i, carry):
            top, den, acc = carry
            start = pl.multiple_of(i * block, block)
            bias_ref[...] = allowed(start)
            raw = scores(h, start)
            new = jnp.maximum(top, jnp.max(raw, axis=-1, keepdims=True))
            alpha = jnp.exp2((top - new) * scale)
            probs = jnp.exp2((raw - new) * scale)
            den = den * alpha + jnp.sum(probs, axis=-1, keepdims=True)
            acc = acc * alpha.reshape(pack * tokens, 1) + weigh(h, start, probs)
            return new, den, acc

        top, den, acc = lax.fori_loop(
            0,
            reach,
            step,
            (
                jnp.full((pack, tokens, 1), -1e30, F32),
                jnp.zeros((pack, tokens, 1), F32),
                jnp.zeros((pack * tokens, HD), F32),
            ),
        )
        store(h, (acc / den.reshape(pack * tokens, 1)).astype(BF16))


def call(kernel, name, outs, args, scratch=(), flops=0, exps=0, limit=16, smem=()):
    size = sum(math.prod(x.shape) * x.dtype.itemsize for x in list(args) + list(outs))
    spaces = [pltpu.SMEM if i in smem else pltpu.VMEM for i in range(len(args))]
    return pl.pallas_call(
        kernel,
        name=name,
        out_shape=list(outs),
        in_specs=[pl.BlockSpec(memory_space=space) for space in spaces],
        out_specs=[pl.BlockSpec(memory_space=pltpu.VMEM) for _ in outs],
        scratch_shapes=list(scratch),
        cost_estimate=pl.CostEstimate(flops=flops, bytes_accessed=size, transcendentals=exps),
        compiler_params=pltpu.CompilerParams(vmem_limit_bytes=limit * MIB),
    )(*args)


def body(q_lin, k_lin, v_lin, log_decay, gate, norm_gain, queries, keys, values, order):
    tokens, width = q_lin.shape
    heads = log_decay.shape[0]
    n, nh = lax.axis_size("ctx"), lax.axis_size("head")
    group = 4 if n % 4 == 0 else 2 if n % 2 == 0 else 1
    groups = n // group
    per = heads // group
    rows = per * HD + 16
    cube = tokens * width * HD
    shape = jax.ShapeDtypeStruct

    def swap(x, s):
        return lax.ppermute(x, "ctx", [(c, c ^ s) for c in range(n)])

    def ahead(x, d, wrap):
        pairs = [(c, (c + d * group) % n) for c in range(n) if wrap or c + d * group < n]
        return lax.ppermute(x, "ctx", pairs)

    pays = call(
        functools.partial(state_kernel, group, heads),
        "block_states",
        [shape((rows, HD), BF16)] * group,
        (log_decay, k_lin, v_lin),
        [pltpu.VMEM((heads * HD, HD), BF16), pltpu.VMEM((group * 16, HD), F32)],
        flops=4 * cube,
        exps=2 * tokens * width,
    )
    pays = [pays[0]] + [swap(pays[s], s) for s in range(1, group)]

    kv = jnp.concatenate([keys, values], axis=1)
    own = [kv] + [ahead(kv, d, True) for d in range(1, groups)]
    chunks = own + [swap(x, s) for s in range(1, group) for x in own]

    (intra,) = call(
        functools.partial(intra_kernel, heads),
        "intra_block",
        [shape((tokens, width), F32)],
        (log_decay, q_lin, k_lin, v_lin),
        flops=4 * cube,
        exps=4 * tokens * width,
    )

    slots = pltpu.VMEM((group, rows, HD), BF16)
    carry = ()
    if groups > 1:
        (total,) = call(
            functools.partial(total_kernel, group, per),
            "group_state",
            [shape((rows, HD), BF16)],
            pays,
            [slots],
            flops=2 * per * HD * HD * group,
        )
        before = ahead(total, 1, False)
        shift = 1
        while shift < groups - 1:
            earlier = ahead(before, shift, False).astype(F32)
            later = before.astype(F32)
            decay = later[per * HD :][:per] + later[per * HD + 8 :][:per]
            prior = earlier[per * HD :][:per] + earlier[per * HD + 8 :][:per]
            state = later[: per * HD] + jnp.repeat(decay, HD, axis=0) * earlier[: per * HD]
            both = decay * prior
            high = both.astype(BF16).astype(F32)
            pad = jnp.zeros((8 - per, HD), F32)
            before = jnp.concatenate([state, high, pad, both - high, pad], axis=0).astype(BF16)
            shift *= 2
        carry = (before,)
    prefixes = call(
        functools.partial(prefix_kernel, group, per, bool(carry)),
        "prefix_states",
        [shape((per * HD, HD), BF16)] * group,
        (*pays, *carry),
        [slots, pltpu.VMEM((group, per * HD, HD), BF16)],
        flops=2 * per * HD * HD * group,
    )
    prefixes = [prefixes[0]] + [swap(prefixes[s], s) for s in range(1, group)]

    lin, squares = call(
        functools.partial(inter_kernel, group, heads),
        "inter_block",
        [shape((tokens, width), F32), shape((8, tokens), F32)],
        (log_decay, q_lin, intra, *prefixes),
        [pltpu.VMEM((heads * HD, HD), BF16)],
        flops=2 * cube,
        exps=tokens * width,
    )
    parts = [squares] + [
        lax.ppermute(squares, "head", [(i, (i + d) % nh) for i in range(nh)]) for d in range(1, nh)
    ]
    (mixed,) = call(
        functools.partial(mixed_kernel, heads, float(width * nh)),
        "gated_norm",
        [shape((tokens, width), BF16)],
        (lin, gate, norm_gain.reshape(1, width), *parts),
        flops=4 * tokens * width,
        exps=tokens * width,
    )

    span = n * tokens
    block = min(span, 1024)
    (attended,) = call(
        functools.partial(softmax_kernel, n, group, block, heads),
        "softmax_attention",
        [shape((tokens, width), BF16)],
        (order, queries, *chunks),
        [pltpu.VMEM((span, kv.shape[1]), BF16), pltpu.VMEM((tokens, block), F32)],
        flops=4 * tokens * width * span,
        exps=tokens * span * heads,
        limit=16 + 5 * span * kv.shape[1] // MIB,
        smem=(0,),
    )
    return (mixed, attended)


def solution(mesh):
    return jax.shard_map(
        body,
        mesh=mesh,
        in_specs=(
            P("ctx", "head"),
            P("ctx", "head"),
            P("ctx", "head"),
            P("head", "ctx"),
            P("ctx", "head"),
            P("head"),
            P("ctx", "head"),
            P("ctx", "head"),
            P("ctx", "head"),
            P("ctx"),
        ),
        out_specs=(P("ctx", "head"), P("ctx", "head")),
        check_vma=False,
    )
```

time: 191 us -> 55.2 us (0.29)
  blocking collectives: 91.4 us -> 0 us
  waiting for transfers between devices: 39.1 us -> 8.98 us
  starting transfers between devices: 0.04 us -> 29.8 us
  other arithmetic: 20.8 us -> 0 us
  between operations: 15.6 us -> 1.46 us
  matrix products: 13.8 us -> 0 us
  Pallas kernels: 0 us -> 11.8 us
  local copies, waits for them, and re-layouts: 8.92 us -> 2.83 us
    all_gather x2 -> x0, blocking collectives: 61.6 us -> none  [the longest x1 31.1 us: body(): vpiece = lax.all_gather(values, 'ctx', axis=0, tiled=True)]
    all_gather x1 -> x0, waiting for transfers between devices: 39.1 us -> none  [entering(): everything = jax.tree.map(lambda part: lax.all_gather(part, axis), array)]
    ppermute x0 -> x17, starting transfers between devices: none -> 29.8 us  [the longest x12 22 us: swap(): return lax.ppermute(x, 'ctx', [(c, c ^ s) for c in range(n)])]
    unnamed x1 -> x0, blocking collectives: 23.6 us -> none
    dot_general x6 -> x0, matrix products: 13.8 us -> none  [the longest x1 4.39 us: body(): lin = local_out + jnp.einsum('thd,hde->the', qdec, carried, precision=HIGH)]
    pallas_call x0 -> x7, Pallas kernels: none -> 11.8 us  [call(): pl.pallas_call(kernel, name=name, out_shape=list(outs), in_specs=[pl.Bloc...]
    select_n x8 -> x0, other arithmetic: 11.7 us -> none  [hop(): return jax.tree.map(lambda a, b: jnp.where(reached, a, b), new, before)]
    ppermute x0 -> x17, waiting for transfers between devices: none -> 8.98 us  [the longest x12 7.27 us: swap(): return lax.ppermute(x, 'ctx', [(c, c ^ s) for c in range(n)])]
  transfers between devices with their start and end apart: 1 -> 17, of which waited for: 1 -> 7; matrix products, arithmetic and copies ran while one was open for 9% -> 0% of each run, Pallas kernels for 0% -> 16%
where the time goes in v1:
time: 55.2 us; the launch traced here: 54.9 us
  starting transfers between devices  29.8 us (54%)
  Pallas kernels  11.8 us (21%)
  waiting for transfers between devices  8.98 us (16%)
  local copies, waits for them, and re-layouts  2.83 us (5%)
  between operations  1.46 us (3%)
    ppermute x12, starting transfers between devices, swap(): return lax.ppermute(x, 'ctx', [(c, c ^ s) for c in range(n)])  22 us
    pallas_call x7, Pallas kernels, call(): pl.pallas_call(kernel, name=name, out_shape=list(outs), in_specs=[pl.Bloc...  11.8 us
    ppermute x12, waiting for transfers between devices, swap(): return lax.ppermute(x, 'ctx', [(c, c ^ s) for c in range(n)])  7.27 us
    ppermute x2, starting transfers between devices, ahead(): return lax.ppermute(x, 'ctx', pairs)  4.85 us
    ppermute x3, starting transfers between devices, body(): lax.ppermute(squares, 'head', [(i, (i + d) % nh) for i in range(nh)])  2.97 us
    unnamed x25, local copies, waits for them, and re-layouts  2.82 us
    ppermute x2, waiting for transfers between devices, ahead(): return lax.ppermute(x, 'ctx', pairs)  1.71 us
  transfers between devices with their start and end apart: 17, of which 7 were waited for; matrix products, arithmetic and copies ran while one was open for 0% of the time, Pallas kernels for 16%

profile of v1, /device:TPU:0, one launch (start us, length us, event | category | flops | bytes accessed | tf_op | source)
XLA Modules:
  0.0 54.9 jit_solution(1560582411645044445)
XLA Ops:
  0.6 1.0 %copy-done = bf16[128,2048]{1,0:T(8,128)(2,1)S(1)} copy-done((bf16[128,2048]{1,0:T(8,128)(2,1)S(1)}, bf16[128,2048]{1,0:T(8,128)(2,1)}, u32[]{:S(2)}) %copy-start) | copy-done | bytes 524312
  1.7 1.0 %copy-done.2 = bf16[128,2048]{1,0:T(8,128)(2,1)S(1)} copy-done((bf16[128,2048]{1,0:T(8,128)(2,1)S(1)}, bf16[128,2048]{1,0:T(8,128)(2,1)}, u32[]{:S(2)}) %copy-start.2) | copy-done | bytes 524312
  3.4 1.5 %block_states.1 = (bf16[528,128]{1,0:T(8,128)(2,1)S(1)}, bf16[528,128]{1,0:T(8,128)(2,1)S(1)}, bf16[528,128]{1,0:T(8,128)(2,1)S(1)}, bf16[528,128]{1,0:T(8,128)(2,1)S(1)}) custom-call(f32[16,128]{1,0:T(8,128)S(1)} %copy-done.6, bf16[128,2048]{1,0:T(8,128)(2,1)S(1)} %copy-done, bf16[128,2048]{1,0:T(8,128)(2,1)S(1)} %copy-done.2), custom_call_target="tpu_custom_call" | custom-call | flops 134217728 | bytes 1597440 | tf_op jit(solution)/shard_map/block_states/pallas_call | solution.py:258
  4.9 3.0 %collective-permute-start = (bf16[528,128]{1,0:T(8,128)(2,1)S(1)}, bf16[528,128]{1,0:T(8,128)(2,1)S(1)}, u32[]{:S(2)}, u32[]{:S(2)}) collective-permute-start(bf16[528,128]{1,0:T(8,128)(2,1)S(1)} %get-tuple-element.13), channel_id=1, source_target_pairs={{0,4},{4,0},{8,12},{12,8},{16,20},{20,16},{24,28},{28,24},{1,5},{5... | collective-permute-start | bytes 405512 | tf_op jit(solution)/shard_map/ppermute | solution.py:282
  7.9 1.6 %collective-permute-start.1 = (bf16[528,128]{1,0:T(8,128)(2,1)S(1)}, bf16[528,128]{1,0:T(8,128)(2,1)S(1)}, u32[]{:S(2)}, u32[]{:S(2)}) collective-permute-start(bf16[528,128]{1,0:T(8,128)(2,1)S(1)} %get-tuple-element.14), channel_id=1, source_target_pairs={{0,8},{4,12},{8,0},{12,4},{16,24},{20,28},{24,16},{28,20},{1,9},{5... | collective-permute-start | bytes 405512 | tf_op jit(solution)/shard_map/ppermute | solution.py:282
  9.5 2.0 %collective-permute-done.refs_1_ = bf16[528,128]{1,0:T(8,128)(2,1)S(1)} collective-permute-done((bf16[528,128]{1,0:T(8,128)(2,1)S(1)}, bf16[528,128]{1,0:T(8,128)(2,1)S(1)}, u32[]{:S(2)}, u32[]{:S(2)}) %collective-permute-start) | collective-permute-done | bytes 135200 | tf_op jit(solution)/shard_map/ppermute | solution.py:282
  11.5 2.9 %collective-permute-done.1.refs_2_ = bf16[528,128]{1,0:T(8,128)(2,1)S(1)} collective-permute-done((bf16[528,128]{1,0:T(8,128)(2,1)S(1)}, bf16[528,128]{1,0:T(8,128)(2,1)S(1)}, u32[]{:S(2)}, u32[]{:S(2)}) %collective-permute-start.1) | collective-permute-done | bytes 135200 | tf_op jit(solution)/shard_map/ppermute | solution.py:282
  14.4 1.2 %collective-permute-done.2.refs_3_ = bf16[528,128]{1,0:T(8,128)(2,1)S(1)} collective-permute-done((bf16[528,128]{1,0:T(8,128)(2,1)S(1)}, bf16[528,128]{1,0:T(8,128)(2,1)S(1)}, u32[]{:S(2)}, u32[]{:S(2)}) %collective-permute-start.2) | collective-permute-done | bytes 135200 | tf_op jit(solution)/shard_map/ppermute | solution.py:282
  15.8 4.8 %collective-permute-start.3 = (bf16[528,128]{1,0:T(8,128)(2,1)S(1)}, bf16[528,128]{1,0:T(8,128)(2,1)S(1)}, u32[]{:S(2)}, u32[]{:S(2)}) collective-permute-start(bf16[528,128]{1,0:T(8,128)(2,1)S(1)} %group_state.1), channel_id=1, source_target_pairs={{0,16},{4,20},{8,24},{12,28},{1,17},{5,21},{9,25},{13,29},{2,18},{... | collective-permute-start | bytes 405512 | tf_op jit(solution)/shard_map/ppermute | solution.py:286
  20.8 1.6 %collective-permute-start.11 = (bf16[128,512]{1,0:T(8,128)(2,1)S(1)}, bf16[128,512]{1,0:T(8,128)(2,1)S(1)}, u32[]{:S(2)}, u32[]{:S(2)}) collective-permute-start(bf16[128,512]{1,0:T(8,128)(2,1)S(1)} %constant_dynamic-update-slice_fusion.rest_0_), channel_id=1, source_target_pairs={{0,4},{4,0},{8,12},{12,8},{16,20},{20,16},{24,28},{28,24},{1,5},{5... | collective-permute-start | bytes 393224 | tf_op jit(solution)/shard_map/ppermute | solution.py:282
  22.4 1.7 %collective-permute-done.3.refs_4_ = bf16[528,128]{1,0:T(8,128)(2,1)S(1)} collective-permute-done((bf16[528,128]{1,0:T(8,128)(2,1)S(1)}, bf16[528,128]{1,0:T(8,128)(2,1)S(1)}, u32[]{:S(2)}, u32[]{:S(2)}) %collective-permute-start.3) | collective-permute-done | bytes 135200 | tf_op jit(solution)/shard_map/ppermute | solution.py:286
  24.3 0.9 %collective-permute-start.4 = (bf16[512,128]{1,0:T(8,128)(2,1)S(1)}, bf16[512,128]{1,0:T(8,128)(2,1)S(1)}, u32[]{:S(2)}, u32[]{:S(2)}) collective-permute-start(bf16[512,128]{1,0:T(8,128)(2,1)S(1)} %get-tuple-element.17), channel_id=1, source_target_pairs={{0,4},{4,0},{8,12},{12,8},{16,20},{20,16},{24,28},{28,24},{1,5},{5... | collective-permute-start | bytes 393224 | tf_op jit(solution)/shard_map/ppermute | solution.py:282
  25.2 5.8 %collective-permute-start.5 = (bf16[512,128]{1,0:T(8,128)(2,1)S(1)}, bf16[512,128]{1,0:T(8,128)(2,1)S(1)}, u32[]{:S(2)}, u32[]{:S(2)}) collective-permute-start(bf16[512,128]{1,0:T(8,128)(2,1)S(1)} %get-tuple-element.18), channel_id=1, source_target_pairs={{0,8},{4,12},{8,0},{12,4},{16,24},{20,28},{24,16},{28,20},{1,9},{5... | collective-permute-start | bytes 393224 | tf_op jit(solution)/shard_map/ppermute | solution.py:282
  31.7 2.0 %collective-permute-start.13 = (bf16[128,512]{1,0:T(8,128)(2,1)S(1)}, bf16[128,512]{1,0:T(8,128)(2,1)S(1)}, u32[]{:S(2)}, u32[]{:S(2)}) collective-permute-start(bf16[128,512]{1,0:T(8,128)(2,1)S(1)} %constant_dynamic-update-slice_fusion.rest_0_), channel_id=1, source_target_pairs={{0,8},{4,12},{8,0},{12,4},{16,24},{20,28},{24,16},{28,20},{1,9},{5... | collective-permute-start | bytes 393224 | tf_op jit(solution)/shard_map/ppermute | solution.py:282
  34.0 1.2 %collective-permute-start.12 = (bf16[128,512]{1,0:T(8,128)(2,1)S(1)}, bf16[128,512]{1,0:T(8,128)(2,1)S(1)}, u32[]{:S(2)}, u32[]{:S(2)}) collective-permute-start(bf16[128,512]{1,0:T(8,128)(2,1)S(1)} %collective-permute-done.10.rest_1_), channel_id=1, source_target_pairs={{0,4},{4,0},{8,12},{12,8},{16,20},{20,16},{24,28},{28,24},{1,5},{5... | collective-permute-start | bytes 393224 | tf_op jit(solution)/shard_map/ppermute | solution.py:282
  35.4 2.1 %collective-permute-start.14 = (bf16[128,512]{1,0:T(8,128)(2,1)S(1)}, bf16[128,512]{1,0:T(8,128)(2,1)S(1)}, u32[]{:S(2)}, u32[]{:S(2)}) collective-permute-start(bf16[128,512]{1,0:T(8,128)(2,1)S(1)} %collective-permute-done.10.rest_1_), channel_id=1, source_target_pairs={{0,8},{4,12},{8,0},{12,4},{16,24},{20,28},{24,16},{28,20},{1,9},{5... | collective-permute-start | bytes 393224 | tf_op jit(solution)/shard_map/ppermute | solution.py:282
  37.4 0.9 %collective-permute-done.6.rest_3_ = bf16[512,128]{1,0:T(8,128)(2,1)S(1)} collective-permute-done((bf16[512,128]{1,0:T(8,128)(2,1)S(1)}, bf16[512,128]{1,0:T(8,128)(2,1)S(1)}, u32[]{:S(2)}, u32[]{:S(2)}) %collective-permute-start.6) | collective-permute-done | bytes 131104 | tf_op jit(solution)/shard_map/ppermute | solution.py:282
  38.4 2.8 %collective-permute-start.16 = (bf16[128,512]{1,0:T(8,128)(2,1)S(1)}, bf16[128,512]{1,0:T(8,128)(2,1)S(1)}, u32[]{:S(2)}, u32[]{:S(2)}) collective-permute-start(bf16[128,512]{1,0:T(8,128)(2,1)S(1)} %collective-permute-done.10.rest_1_), channel_id=1, source_target_pairs={{0,12},{4,8},{8,4},{12,0},{16,28},{20,24},{24,20},{28,16},{1,13},{... | collective-permute-start | bytes 393224 | tf_op jit(solution)/shard_map/ppermute | solution.py:282
  41.8 2.8 %intra_block.1.intra_ref = f32[128,2048]{1,0:T(8,128)S(1)} custom-call(f32[16,128]{1,0:T(8,128)S(1)} %copy-done.7, bf16[128,2048]{1,0:T(8,128)(2,1)S(1)} %copy-done.4, bf16[128,2048]{1,0:T(8,128)(2,1)S(1)} %copy-done.1, bf16[128,2048]{1,0:T(8,128)(2,1)S(1)} %copy-done.3), custom_call_target="tpu_custom_call" | custom-call | flops 134217728 | bytes 2629632 | tf_op jit(solution)/shard_map/intra_block/pallas_call | solution.py:258
  44.7 1.0 %inter_block.1 = (f32[128,2048]{1,0:T(8,128)S(1)}, f32[8,128]{1,0:T(8,128)S(1)}) custom-call(f32[16,128]{1,0:T(8,128)S(1)} %copy-done.7, bf16[128,2048]{1,0:T(8,128)(2,1)S(1)} %copy-done.4, f32[128,2048]{1,0:T(8,128)S(1)} %intra_block.1.intra_ref, bf16[512,128]{1,0:T(8,128)(2,1)S(1)} %get-tuple-element.16.rest_0_, ...), custom_call_target="tpu_custom_call" | custom-call | flops 67108864 | bytes 3158016 | tf_op jit(solution)/shard_map/inter_block/pallas_call | solution.py:258
  45.7 1.6 %collective-permute-start.8 = (f32[8,128]{1,0:T(8,128)S(1)}, f32[8,128]{1,0:T(8,128)S(1)}, u32[]{:S(2)}, u32[]{:S(2)}) collective-permute-start(f32[8,128]{1,0:T(8,128)S(1)} %get-tuple-element.21.rest_0_), channel_id=1, source_target_pairs={{0,2},{1,3},{2,0},{3,1},{4,6},{5,7},{6,4},{7,5},{8,10},{9,11},{10,... | collective-permute-start | bytes 12296 | tf_op jit(solution)/shard_map/ppermute | solution.py:357
  47.2 1.4 %collective-permute-start.9 = (f32[8,128]{1,0:T(8,128)S(1)}, f32[8,128]{1,0:T(8,128)S(1)}, u32[]{:S(2)}, u32[]{:S(2)}) collective-permute-start(f32[8,128]{1,0:T(8,128)S(1)} %get-tuple-element.21.rest_0_), channel_id=1, source_target_pairs={{0,3},{1,0},{2,1},{3,2},{4,7},{5,4},{6,5},{7,6},{8,11},{9,8},{10,9... | collective-permute-start | bytes 12296 | tf_op jit(solution)/shard_map/ppermute | solution.py:357
  48.7 5.0 %softmax_attention.1 = bf16[128,2048]{1,0:T(8,128)(2,1)} custom-call(s32[1]{0:T(128)S(6)} %copy.13.order_ref, bf16[128,2048]{1,0:T(8,128)(2,1)S(1)} %copy-done.9, bf16[128,512]{1,0:T(8,128)(2,1)S(1)} %constant_dynamic-update-slice_fusion.rest_0_, bf16[128,512]{1,0:T(8,128)(2,1)S(1)} %collective-permute-done.10.rest_1_, ...), custom_call_target="tpu_custom_call" | custom-call | flops 1073741824 | bytes 2097156 | tf_op jit(solution)/shard_map/softmax_attention/pallas_call | solution.py:258
  53.7 1.2 %gated_norm.1 = bf16[128,2048]{1,0:T(8,128)(2,1)} custom-call(f32[128,2048]{1,0:T(8,128)S(1)} %get-tuple-element.20.lin_ref, bf16[128,2048]{1,0:T(8,128)(2,1)S(1)} %copy-done.5, f32[1,2048]{1,0:T(1,128)S(1)} %bitcast.1, f32[8,128]{1,0:T(8,128)S(1)} %get-tuple-element.21.rest_0_, f32[8,128]{1,0:T(8,128)S(1)} %collective-permute-done.7.rest_1_, ...), custom_call_target="tpu_custom_call" | custom-call | flops 1048576 | bytes 2121728 | tf_op jit(solution)/shard_map/gated_norm/pallas_call | solution.py:258
  (43 shorter events, 2.4 us)
Async XLA Ops:
  3.4 17.2 %copy-start.10 = (bf16[128,256]{1,0:T(8,128)(2,1)S(1)}, bf16[128,256]{1,0:T(8,128)(2,1)}, u32[]{:S(2)}) copy-start(bf16[128,256]{1,0:T(8,128)(2,1)} %param.17) | copy-start | bytes 196612
  3.4 17.2 %copy-start.11 = (bf16[128,256]{1,0:T(8,128)(2,1)S(1)}, bf16[128,256]{1,0:T(8,128)(2,1)}, u32[]{:S(2)}) copy-start(bf16[128,256]{1,0:T(8,128)(2,1)} %param.18) | copy-start | bytes 196612
  4.9 6.6 %collective-permute-start = (bf16[528,128]{1,0:T(8,128)(2,1)S(1)}, bf16[528,128]{1,0:T(8,128)(2,1)S(1)}, u32[]{:S(2)}, u32[]{:S(2)}) collective-permute-start(bf16[528,128]{1,0:T(8,128)(2,1)S(1)} %get-tuple-element.13), channel_id=1, source_target_pairs={{0,4},{4,0},{8,12},{12,8},{16,20},{20,16},{24,28},{28,24},{1,5},{5... | collective-permute-start | bytes 405512 | tf_op jit(solution)/shard_map/ppermute | solution.py:282
  7.9 6.5 %collective-permute-start.1 = (bf16[528,128]{1,0:T(8,128)(2,1)S(1)}, bf16[528,128]{1,0:T(8,128)(2,1)S(1)}, u32[]{:S(2)}, u32[]{:S(2)}) collective-permute-start(bf16[528,128]{1,0:T(8,128)(2,1)S(1)} %get-tuple-element.14), channel_id=1, source_target_pairs={{0,8},{4,12},{8,0},{12,4},{16,24},{20,28},{24,16},{28,20},{1,9},{5... | collective-permute-start | bytes 405512 | tf_op jit(solution)/shard_map/ppermute | solution.py:282
  9.5 6.1 %collective-permute-start.2 = (bf16[528,128]{1,0:T(8,128)(2,1)S(1)}, bf16[528,128]{1,0:T(8,128)(2,1)S(1)}, u32[]{:S(2)}, u32[]{:S(2)}) collective-permute-start(bf16[528,128]{1,0:T(8,128)(2,1)S(1)} %get-tuple-element.15), channel_id=1, source_target_pairs={{0,12},{4,8},{8,4},{12,0},{16,28},{20,24},{24,20},{28,16},{1,13},{... | collective-permute-start | bytes 405512 | tf_op jit(solution)/shard_map/ppermute | solution.py:282
  15.7 26.1 %copy-start.3 = (bf16[128,2048]{1,0:T(8,128)(2,1)S(1)}, bf16[128,2048]{1,0:T(8,128)(2,1)}, u32[]{:S(2)}) copy-start(bf16[128,2048]{1,0:T(8,128)(2,1)} %v_ref.3) | copy-start | bytes 1572868
  15.7 26.1 %copy-start.4 = (bf16[128,2048]{1,0:T(8,128)(2,1)S(1)}, bf16[128,2048]{1,0:T(8,128)(2,1)}, u32[]{:S(2)}) copy-start(bf16[128,2048]{1,0:T(8,128)(2,1)} %q_ref.4) | copy-start | bytes 1572868
  15.8 26.0 %copy-start.1 = (bf16[128,2048]{1,0:T(8,128)(2,1)S(1)}, bf16[128,2048]{1,0:T(8,128)(2,1)}, u32[]{:S(2)}) copy-start(bf16[128,2048]{1,0:T(8,128)(2,1)} %k_ref.3) | copy-start | bytes 1572868
  15.8 8.2 %collective-permute-start.3 = (bf16[528,128]{1,0:T(8,128)(2,1)S(1)}, bf16[528,128]{1,0:T(8,128)(2,1)S(1)}, u32[]{:S(2)}, u32[]{:S(2)}) collective-permute-start(bf16[528,128]{1,0:T(8,128)(2,1)S(1)} %group_state.1), channel_id=1, source_target_pairs={{0,16},{4,20},{8,24},{12,28},{1,17},{5,21},{9,25},{13,29},{2,18},{... | collective-permute-start | bytes 405512 | tf_op jit(solution)/shard_map/ppermute | solution.py:286
  20.7 11.0 %collective-permute-start.10 = (bf16[128,512]{1,0:T(8,128)(2,1)S(1)}, bf16[128,512]{1,0:T(8,128)(2,1)S(1)}, u32[]{:S(2)}, u32[]{:S(2)}) collective-permute-start(bf16[128,512]{1,0:T(8,128)(2,1)S(1)} %constant_dynamic-update-slice_fusion.rest_0_), channel_id=1, source_target_pairs={{0,16},{4,20},{8,24},{12,28},{16,0},{20,4},{24,8},{28,12},{1,17},{... | collective-permute-start | bytes 393224 | tf_op jit(solution)/shard_map/ppermute | solution.py:286
  20.8 12.9 %collective-permute-start.11 = (bf16[128,512]{1,0:T(8,128)(2,1)S(1)}, bf16[128,512]{1,0:T(8,128)(2,1)S(1)}, u32[]{:S(2)}, u32[]{:S(2)}) collective-permute-start(bf16[128,512]{1,0:T(8,128)(2,1)S(1)} %constant_dynamic-update-slice_fusion.rest_0_), channel_id=1, source_target_pairs={{0,4},{4,0},{8,12},{12,8},{16,20},{20,16},{24,28},{28,24},{1,5},{5... | collective-permute-start | bytes 393224 | tf_op jit(solution)/shard_map/ppermute | solution.py:282
  24.1 17.8 %copy-start.7 = (f32[16,128]{1,0:T(8,128)S(1)}, f32[16,128]{1,0:T(8,128)}, u32[]{:S(2)}) copy-start(f32[16,128]{1,0:T(8,128)} %ld_ref.5) | copy-start | bytes 24580
  24.3 9.8 %collective-permute-start.4 = (bf16[512,128]{1,0:T(8,128)(2,1)S(1)}, bf16[512,128]{1,0:T(8,128)(2,1)S(1)}, u32[]{:S(2)}, u32[]{:S(2)}) collective-permute-start(bf16[512,128]{1,0:T(8,128)(2,1)S(1)} %get-tuple-element.17), channel_id=1, source_target_pairs={{0,4},{4,0},{8,12},{12,8},{16,20},{20,16},{24,28},{28,24},{1,5},{5... | collective-permute-start | bytes 393224 | tf_op jit(solution)/shard_map/ppermute | solution.py:282
  25.2 10.2 %collective-permute-start.5 = (bf16[512,128]{1,0:T(8,128)(2,1)S(1)}, bf16[512,128]{1,0:T(8,128)(2,1)S(1)}, u32[]{:S(2)}, u32[]{:S(2)}) collective-permute-start(bf16[512,128]{1,0:T(8,128)(2,1)S(1)} %get-tuple-element.18), channel_id=1, source_target_pairs={{0,8},{4,12},{8,0},{12,4},{16,24},{20,28},{24,16},{28,20},{1,9},{5... | collective-permute-start | bytes 393224 | tf_op jit(solution)/shard_map/ppermute | solution.py:282
  31.0 7.3 %collective-permute-start.6 = (bf16[512,128]{1,0:T(8,128)(2,1)S(1)}, bf16[512,128]{1,0:T(8,128)(2,1)S(1)}, u32[]{:S(2)}, u32[]{:S(2)}) collective-permute-start(bf16[512,128]{1,0:T(8,128)(2,1)S(1)} %get-tuple-element.19), channel_id=1, source_target_pairs={{0,12},{4,8},{8,4},{12,0},{16,28},{20,24},{24,20},{28,16},{1,13},{... | collective-permute-start | bytes 393224 | tf_op jit(solution)/shard_map/ppermute | solution.py:282
  31.7 13.9 %collective-permute-start.13 = (bf16[128,512]{1,0:T(8,128)(2,1)S(1)}, bf16[128,512]{1,0:T(8,128)(2,1)S(1)}, u32[]{:S(2)}, u32[]{:S(2)}) collective-permute-start(bf16[128,512]{1,0:T(8,128)(2,1)S(1)} %constant_dynamic-update-slice_fusion.rest_0_), channel_id=1, source_target_pairs={{0,8},{4,12},{8,0},{12,4},{16,24},{20,28},{24,16},{28,20},{1,9},{5... | collective-permute-start | bytes 393224 | tf_op jit(solution)/shard_map/ppermute | solution.py:282
  33.7 11.9 %collective-permute-start.15 = (bf16[128,512]{1,0:T(8,128)(2,1)S(1)}, bf16[128,512]{1,0:T(8,128)(2,1)S(1)}, u32[]{:S(2)}, u32[]{:S(2)}) collective-permute-start(bf16[128,512]{1,0:T(8,128)(2,1)S(1)} %constant_dynamic-update-slice_fusion.rest_0_), channel_id=1, source_target_pairs={{0,12},{4,8},{8,4},{12,0},{16,28},{20,24},{24,20},{28,16},{1,13},{... | collective-permute-start | bytes 393224 | tf_op jit(solution)/shard_map/ppermute | solution.py:282
  34.0 13.2 %collective-permute-start.12 = (bf16[128,512]{1,0:T(8,128)(2,1)S(1)}, bf16[128,512]{1,0:T(8,128)(2,1)S(1)}, u32[]{:S(2)}, u32[]{:S(2)}) collective-permute-start(bf16[128,512]{1,0:T(8,128)(2,1)S(1)} %collective-permute-done.10.rest_1_), channel_id=1, source_target_pairs={{0,4},{4,0},{8,12},{12,8},{16,20},{20,16},{24,28},{28,24},{1,5},{5... | collective-permute-start | bytes 393224 | tf_op jit(solution)/shard_map/ppermute | solution.py:282
  35.4 13.2 %collective-permute-start.14 = (bf16[128,512]{1,0:T(8,128)(2,1)S(1)}, bf16[128,512]{1,0:T(8,128)(2,1)S(1)}, u32[]{:S(2)}, u32[]{:S(2)}) collective-permute-start(bf16[128,512]{1,0:T(8,128)(2,1)S(1)} %collective-permute-done.10.rest_1_), channel_id=1, source_target_pairs={{0,8},{4,12},{8,0},{12,4},{16,24},{20,28},{24,16},{28,20},{1,9},{5... | collective-permute-start | bytes 393224 | tf_op jit(solution)/shard_map/ppermute | solution.py:282
  38.4 10.3 %collective-permute-start.16 = (bf16[128,512]{1,0:T(8,128)(2,1)S(1)}, bf16[128,512]{1,0:T(8,128)(2,1)S(1)}, u32[]{:S(2)}, u32[]{:S(2)}) collective-permute-start(bf16[128,512]{1,0:T(8,128)(2,1)S(1)} %collective-permute-done.10.rest_1_), channel_id=1, source_target_pairs={{0,12},{4,8},{8,4},{12,0},{16,28},{20,24},{24,20},{28,16},{1,13},{... | collective-permute-start | bytes 393224 | tf_op jit(solution)/shard_map/ppermute | solution.py:282
  45.6 8.0 %copy-start.5 = (bf16[128,2048]{1,0:T(8,128)(2,1)S(1)}, bf16[128,2048]{1,0:T(8,128)(2,1)}, u32[]{:S(2)}) copy-start(bf16[128,2048]{1,0:T(8,128)(2,1)} %gate_ref.1) | copy-start | bytes 1572868
  45.6 8.0 %collective-permute-start.7 = (f32[8,128]{1,0:T(8,128)S(1)}, f32[8,128]{1,0:T(8,128)S(1)}, u32[]{:S(2)}, u32[]{:S(2)}) collective-permute-start(f32[8,128]{1,0:T(8,128)S(1)} %get-tuple-element.21.rest_0_), channel_id=1, source_target_pairs={{0,1},{1,2},{2,3},{3,0},{4,5},{5,6},{6,7},{7,4},{8,9},{9,10},{10,1... | collective-permute-start | bytes 12296 | tf_op jit(solution)/shard_map/ppermute | solution.py:357
  45.7 8.0 %collective-permute-start.8 = (f32[8,128]{1,0:T(8,128)S(1)}, f32[8,128]{1,0:T(8,128)S(1)}, u32[]{:S(2)}, u32[]{:S(2)}) collective-permute-start(f32[8,128]{1,0:T(8,128)S(1)} %get-tuple-element.21.rest_0_), channel_id=1, source_target_pairs={{0,2},{1,3},{2,0},{3,1},{4,6},{5,7},{6,4},{7,5},{8,10},{9,11},{10,... | collective-permute-start | bytes 12296 | tf_op jit(solution)/shard_map/ppermute | solution.py:357
  47.2 6.4 %collective-permute-start.9 = (f32[8,128]{1,0:T(8,128)S(1)}, f32[8,128]{1,0:T(8,128)S(1)}, u32[]{:S(2)}, u32[]{:S(2)}) collective-permute-start(f32[8,128]{1,0:T(8,128)S(1)} %get-tuple-element.21.rest_0_), channel_id=1, source_target_pairs={{0,3},{1,0},{2,1},{3,2},{4,7},{5,4},{6,5},{7,6},{8,11},{9,8},{10,9... | collective-permute-start | bytes 12296 | tf_op jit(solution)/shard_map/ppermute | solution.py:357
  (5 other events, 11.8 us)

commit v2 on v1

--- a/solution.py
+++ b/solution.py
@@ -33,19 +33,13 @@
     return slice(h * HD, (h + 1) * HD)
 
 
-def my_rank(group):
-    return lax.rem(lax.axis_index("ctx"), group)
-
-
 def dyn(index, size):
     return pl.ds(pl.multiple_of(index * size, size), size)
 
 
-def state_kernel(group, heads, ld_ref, k_ref, v_ref, *rest):
-    outs, (states, totals) = rest[:group], rest[group:]
+def state_kernel(group, heads, ld_ref, k_ref, v_ref, out_ref):
     tokens = k_ref.shape[0]
     per = heads // group
-    rank = my_rank(group)
     ld = ld_ref[...]
     tri = lower_ones(tokens).astype(F32)
     cum = lax.dot_general(tri, ld, NT, precision=HIGH, preferred_element_type=F32)
@@ -53,10 +47,7 @@
     total = jnp.broadcast_to(jnp.exp(jnp.sum(ld, axis=1, keepdims=True)), (heads, HD))
     high = total.astype(BF16).astype(F32)
     low = total - high
-    totals[...] = jnp.zeros_like(totals)
-    for k in range(group):
-        totals[k * 16 : k * 16 + per, :] = high[k * per : (k + 1) * per]
-        totals[k * 16 + 8 : k * 16 + 8 + per, :] = low[k * per : (k + 1) * per]
+    pad = [jnp.zeros((8 - per, HD), F32)] if per < 8 else []
     for h in range(heads):
         ka = silu16(k_ref[:, head_cols(h)])
         va = silu16(v_ref[:, head_cols(h)])
@@ -65,11 +56,12 @@
         klow = (kdec - khigh.astype(F32)).astype(BF16)
         state = lax.dot_general(khigh, va, TN, preferred_element_type=F32)
         state += lax.dot_general(klow, va, TN, preferred_element_type=F32)
-        states[h * HD : (h + 1) * HD, :] = state.astype(BF16)
-    for s in range(group):
-        dest = rank ^ s
-        outs[s][: per * HD, :] = states[dyn(dest, per * HD), :]
-        outs[s][per * HD :, :] = totals[dyn(dest, 16), :].astype(BF16)
+        k, j = divmod(h, per)
+        out_ref[k, j * HD : (j + 1) * HD, :] = state.astype(BF16)
+    for k in range(group):
+        mine = slice(k * per, (k + 1) * per)
+        tail = jnp.concatenate([high[mine], *pad, low[mine], *pad], axis=0)
+        out_ref[k, per * HD :, :] = tail.astype(BF16)
 
 
 def decay_row(slots, k, base, j):
@@ -77,14 +69,7 @@
     return tail[j : j + 1] + tail[8 + j : 9 + j]
 
 
-def fill_slots(group, rank, pays, slots):
-    for s in range(group):
-        slots[rank ^ s] = pays[s][...]
-
-
-def total_kernel(group, per, *refs):
-    pays, out, slots = refs[:group], refs[group], refs[group + 1]
-    fill_slots(group, my_rank(group), pays, slots)
+def total_kernel(group, per, slots, out):
     base = per * HD
     tails = []
     for j in range(per):
@@ -102,24 +87,16 @@
     out[base:, :] = jnp.concatenate([high, total - high], axis=0).astype(BF16)
 
 
-def prefix_kernel(group, per, carried, *refs):
-    pays, refs = refs[:group], refs[group:]
-    carry = None
-    if carried:
-        carry, refs = refs[0], refs[1:]
-    outs, slots, prefixes = refs[:group], refs[group], refs[group + 1]
-    rank = my_rank(group)
-    fill_slots(group, rank, pays, slots)
+def prefix_kernel(group, per, carried, slots, *refs):
+    out = refs[-1]
     base = per * HD
     for j in range(per):
         rows = slice(j * HD, (j + 1) * HD)
-        state = carry[rows, :].astype(F32) if carried else jnp.zeros((HD, HD), F32)
-        prefixes[0, rows, :] = state.astype(BF16)
+        state = refs[0][rows, :].astype(F32) if carried else jnp.zeros((HD, HD), F32)
+        out[0, rows, :] = state.astype(BF16)
         for k in range(group - 1):
             state = decay_row(slots, k, base, j) * state + slots[k, rows, :].astype(F32)
-            prefixes[k + 1, rows, :] = state.astype(BF16)
-    for s in range(group):
-        outs[s][...] = prefixes[rank ^ s]
+            out[k + 1, rows, :] = state.astype(BF16)
 
 
 def intra_kernel(heads, ld_ref, q_ref, k_ref, v_ref, out_ref):
@@ -140,20 +117,18 @@
         out_ref[:, head_cols(h)] = jnp.dot(weights, va, preferred_element_type=F32)
 
 
-def inter_kernel(group, heads, ld_ref, q_ref, intra_ref, *rest):
-    parts, (lin_ref, squares_ref, states) = rest[:group], rest[group:]
+def inter_kernel(group, heads, ld_ref, q_ref, intra_ref, states, lin_ref, squares_ref):
     tokens = q_ref.shape[0]
     per = heads // group
-    rank = my_rank(group)
-    for s in range(group):
-        states[dyn(rank ^ s, per * HD), :] = parts[s][...]
     tri = lower_ones(tokens).astype(F32)
     cum = lax.dot_general(tri, ld_ref[...], NT, precision=HIGH, preferred_element_type=F32)
     decay = jnp.exp(cum)
     acc = jnp.zeros((tokens, HD), F32)
     for h in range(heads):
         qa = silu16(q_ref[:, head_cols(h)])
-        inter = jnp.dot(qa, states[h * HD : (h + 1) * HD, :], preferred_element_type=F32)
+        k, j = divmod(h, per)
+        state = states[k, j * HD : (j + 1) * HD, :]
+        inter = jnp.dot(qa, state, preferred_element_type=F32)
         lin = intra_ref[:, head_cols(h)] + inter * decay[:, h : h + 1]
         lin_ref[:, head_cols(h)] = lin
         acc += lin * lin
@@ -174,7 +149,7 @@
 
 
 def softmax_kernel(count, group, block, heads, order_ref, q_ref, *rest):
-    chunks, (out_ref, kv, bias_ref) = rest[:count], rest[count:]
+    chunks, (out_ref, kv, bias_ref) = rest[:group], rest[group:]
     tokens = q_ref.shape[0]
     width = chunks[0].shape[1] // 2
     kv_heads = width // HD
@@ -185,7 +160,7 @@
     for i in range(count):
         s, d = divmod(i, groups)
         place = lax.rem(mine + groups - d, groups) * group + (rank ^ s)
-        kv[dyn(place, tokens), :] = chunks[i][...]
+        kv[dyn(place, tokens), :] = chunks[s][d * tokens : (d + 1) * tokens, :]
     first = order_ref[0] * tokens
     scale = math.log2(math.e) / math.sqrt(HD)
     blocks = count * tokens // block
@@ -278,27 +253,30 @@
     cube = tokens * width * HD
     shape = jax.ShapeDtypeStruct
 
-    def swap(x, s):
-        return lax.ppermute(x, "ctx", [(c, c ^ s) for c in range(n)])
+    ranks = [[a * group + r for r in range(group)] for a in range(groups)]
+
+    def exchange(x):
+        return lax.all_to_all(x, "ctx", 0, 0, axis_index_groups=ranks)
 
     def ahead(x, d, wrap):
         pairs = [(c, (c + d * group) % n) for c in range(n) if wrap or c + d * group < n]
         return lax.ppermute(x, "ctx", pairs)
 
-    pays = call(
+    kv = jnp.concatenate([keys, values], axis=1)
+    own = jnp.concatenate([kv] + [ahead(kv, d, True) for d in range(1, groups)], axis=0)
+
+    (pays,) = call(
         functools.partial(state_kernel, group, heads),
         "block_states",
-        [shape((rows, HD), BF16)] * group,
+        [shape((group, rows, HD), BF16)],
         (log_decay, k_lin, v_lin),
-        [pltpu.VMEM((heads * HD, HD), BF16), pltpu.VMEM((group * 16, HD), F32)],
         flops=4 * cube,
         exps=2 * tokens * width,
     )
-    pays = [pays[0]] + [swap(pays[s], s) for s in range(1, group)]
-
-    kv = jnp.concatenate([keys, values], axis=1)
-    own = [kv] + [ahead(kv, d, True) for d in range(1, groups)]
-    chunks = own + [swap(x, s) for s in range(1, group) for x in own]
+    pays = exchange(pays)
+    chunks = [own] + [
+        lax.ppermute(own, "ctx", [(c, c ^ s) for c in range(n)]) for s in range(1, group)
+    ]
 
     (intra,) = call(
         functools.partial(intra_kernel, heads),
@@ -309,15 +287,13 @@
         exps=4 * tokens * width,
     )
 
-    slots = pltpu.VMEM((group, rows, HD), BF16)
     carry = ()
     if groups > 1:
         (total,) = call(
             functools.partial(total_kernel, group, per),
             "group_state",
             [shape((rows, HD), BF16)],
-            pays,
-            [slots],
+            (pays,),
             flops=2 * per * HD * HD * group,
         )
         before = ahead(total, 1, False)
@@ -334,22 +310,20 @@
             before = jnp.concatenate([state, high, pad, both - high, pad], axis=0).astype(BF16)
             shift *= 2
         carry = (before,)
-    prefixes = call(
+    (prefixes,) = call(
         functools.partial(prefix_kernel, group, per, bool(carry)),
         "prefix_states",
-        [shape((per * HD, HD), BF16)] * group,
-        (*pays, *carry),
-        [slots, pltpu.VMEM((group, per * HD, HD), BF16)],
+        [shape((group, per * HD, HD), BF16)],
+        (pays, *carry),
         flops=2 * per * HD * HD * group,
     )
-    prefixes = [prefixes[0]] + [swap(prefixes[s], s) for s in range(1, group)]
+    prefixes = exchange(prefixes)
 
     lin, squares = call(
         functools.partial(inter_kernel, group, heads),
         "inter_block",
         [shape((tokens, width), F32), shape((8, tokens), F32)],
-        (log_decay, q_lin, intra, *prefixes),
-        [pltpu.VMEM((heads * HD, HD), BF16)],
+        (log_decay, q_lin, intra, prefixes),
         flops=2 * cube,
         exps=tokens * width,
     )

time: 55.2 us -> 64.5 us (1.17)
  blocking collectives: 0 us -> 14.1 us
  starting transfers between devices: 29.8 us -> 24.3 us
  Pallas kernels: 11.8 us -> 13.3 us
  waiting for transfers between devices: 8.98 us -> 8.21 us
    all_to_all x0 -> x1, blocking collectives: none -> 14.1 us  [exchange(): return lax.all_to_all(x, 'ctx', 0, 0, axis_index_groups=ranks)]
    ppermute x12 -> x3, starting transfers between devices: 22 us -> 9.34 us  [body(): lax.ppermute(own, 'ctx', [(c, c ^ s) for c in range(n)])]
    ppermute x12 -> x3, waiting for transfers between devices: 7.27 us -> 2.19 us  [body(): lax.ppermute(own, 'ctx', [(c, c ^ s) for c in range(n)])]
    ppermute x2, waiting for transfers between devices: 1.71 us -> 6.01 us  [ahead(): return lax.ppermute(x, 'ctx', pairs)]
    all_to_all x0 -> x1, starting transfers between devices: none -> 4 us  [exchange(): return lax.all_to_all(x, 'ctx', 0, 0, axis_index_groups=ranks)]
    ppermute x2, starting transfers between devices: 4.85 us -> 7.95 us  [ahead(): return lax.ppermute(x, 'ctx', pairs)]
    pallas_call x7, Pallas kernels: 11.8 us -> 13.3 us  [call(): pl.pallas_call(kernel, name=name, out_shape=list(outs), in_specs=[pl.Bloc...]
  transfers between devices with their start and end apart: 17 -> 9, of which waited for: 7 -> 3; matrix products, arithmetic and copies ran while one was open for 0% -> 0% of each run, Pallas kernels for 16% -> 15%
where the time goes in v2:
time: 64.5 us; the launch traced here: 64.1 us
  starting transfers between devices  24.3 us (38%)
  blocking collectives  14.1 us (22%)
  Pallas kernels  13.3 us (21%)
  waiting for transfers between devices  8.21 us (13%)
  local copies, waits for them, and re-layouts  2.82 us (4%)
  between operations  1.42 us (2%)
    all_to_all x1, blocking collectives, exchange(): return lax.all_to_all(x, 'ctx', 0, 0, axis_index_groups=ranks)  14.1 us
    pallas_call x7, Pallas kernels, call(): pl.pallas_call(kernel, name=name, out_shape=list(outs), in_specs=[pl.Bloc...  13.3 us
    ppermute x3, starting transfers between devices, body(): lax.ppermute(own, 'ctx', [(c, c ^ s) for c in range(n)])  9.34 us
    ppermute x2, starting transfers between devices, ahead(): return lax.ppermute(x, 'ctx', pairs)  7.95 us
    ppermute x2, waiting for transfers between devices, ahead(): return lax.ppermute(x, 'ctx', pairs)  6.01 us
    all_to_all x1, starting transfers between devices, exchange(): return lax.all_to_all(x, 'ctx', 0, 0, axis_index_groups=ranks)  4 us
    ppermute x3, starting transfers between devices, body(): lax.ppermute(squares, 'head', [(i, (i + d) % nh) for i in range(nh)])  2.98 us
    unnamed x25, local copies, waits for them, and re-layouts  2.82 us
  transfers between devices with their start and end apart: 9, of which 3 were waited for; matrix products, arithmetic and copies ran while one was open for 0% of the time, Pallas kernels for 15%

profile of v2, /device:TPU:0, one launch (start us, length us, event | category | flops | bytes accessed | tf_op | source)
XLA Modules:
  0.0 64.1 jit_solution(13935661967739824494)
XLA Ops:
  0.6 1.0 %copy-done = bf16[128,2048]{1,0:T(8,128)(2,1)S(1)} copy-done((bf16[128,2048]{1,0:T(8,128)(2,1)S(1)}, bf16[128,2048]{1,0:T(8,128)(2,1)}, u32[]{:S(2)}) %copy-start) | copy-done | bytes 524312
  1.7 1.0 %copy-done.2 = bf16[128,2048]{1,0:T(8,128)(2,1)S(1)} copy-done((bf16[128,2048]{1,0:T(8,128)(2,1)S(1)}, bf16[128,2048]{1,0:T(8,128)(2,1)}, u32[]{:S(2)}) %copy-start.2) | copy-done | bytes 524312
  2.7 0.7 %copy-done.6 = f32[16,128]{1,0:T(8,128)S(1)} copy-done((f32[16,128]{1,0:T(8,128)S(1)}, f32[16,128]{1,0:T(8,128)}, u32[]{:S(2)}) %copy-start.6) | copy-done | bytes 8216
  3.4 1.4 %block_states.1 = bf16[4,528,128]{2,1,0:T(8,128)(2,1)S(1)} custom-call(f32[16,128]{1,0:T(8,128)S(1)} %copy-done.6, bf16[128,2048]{1,0:T(8,128)(2,1)S(1)} %copy-done, bf16[128,2048]{1,0:T(8,128)(2,1)S(1)} %copy-done.2), custom_call_target="tpu_custom_call" | custom-call | flops 134217728 | bytes 1597440 | tf_op jit(solution)/shard_map/block_states/pallas_call | solution.py:233
  4.9 14.1 %all_to_all.10.slots = bf16[4,528,128]{2,1,0:T(8,128)(2,1)S(1)} all-to-all(bf16[4,528,128]{2,1,0:T(8,128)(2,1)S(1)} %block_states.1), channel_id=1, replica_groups={{0,4,8,12},{16,20,24,28},{1,5,9,13},{17,21,25,29},{2,6,10,14},{18,22,26..., dimensions={0} | all-to-all | bytes 1081344 | tf_op jit(solution)/shard_map/all_to_all | solution.py:259
  18.9 0.1 group_state.1
  19.0 4.5 %collective-permute-start = (bf16[528,128]{1,0:T(8,128)(2,1)S(1)}, bf16[528,128]{1,0:T(8,128)(2,1)S(1)}, u32[]{:S(2)}, u32[]{:S(2)}) collective-permute-start(bf16[528,128]{1,0:T(8,128)(2,1)S(1)} %group_state.1), channel_id=1, source_target_pairs={{0,16},{4,20},{8,24},{12,28},{1,17},{5,21},{9,25},{13,29},{2,18},{... | collective-permute-start | bytes 405512 | tf_op jit(solution)/shard_map/ppermute | solution.py:263
  23.5 2.5 %collective-permute-done.refs_0_ = bf16[528,128]{1,0:T(8,128)(2,1)S(1)} collective-permute-done((bf16[528,128]{1,0:T(8,128)(2,1)S(1)}, bf16[528,128]{1,0:T(8,128)(2,1)S(1)}, u32[]{:S(2)}, u32[]{:S(2)}) %collective-permute-start) | collective-permute-done | bytes 135200 | tf_op jit(solution)/shard_map/ppermute | solution.py:263
  26.1 0.9 %prefix_states.1 = bf16[4,512,128]{2,1,0:T(8,128)(2,1)} custom-call(bf16[4,528,128]{2,1,0:T(8,128)(2,1)S(1)} %all_to_all.10.slots, bf16[528,128]{1,0:T(8,128)(2,1)S(1)} %collective-permute-done.refs_0_), custom_call_target="tpu_custom_call" | custom-call | flops 524288 | bytes 1200128 | tf_op jit(solution)/shard_map/prefix_states/pallas_call | solution.py:233
  27.0 4.0 %all-to-all-start.1 = ((bf16[4,512,128]{2,1,0:T(8,128)(2,1)}), bf16[4,512,128]{2,1,0:T(8,128)(2,1)S(1)}, u32[]{:S(2)}, u32[]{:S(2)}) async-start(bf16[4,512,128]{2,1,0:T(8,128)(2,1)} %prefix_states.1), calls=%async_computation.1 | async-start | bytes 1048576 | tf_op jit(solution)/shard_map/all_to_all | solution.py:259
  31.0 0.0 copy-start.7
  31.1 3.4 %collective-permute-start.4 = (bf16[128,512]{1,0:T(8,128)(2,1)S(1)}, bf16[128,512]{1,0:T(8,128)(2,1)S(1)}, u32[]{:S(2)}, u32[]{:S(2)}) collective-permute-start(bf16[128,512]{1,0:T(8,128)(2,1)S(1)} %constant_dynamic-update-slice_fusion), channel_id=1, source_target_pairs={{0,16},{4,20},{8,24},{12,28},{16,0},{20,4},{24,8},{28,12},{1,17},{... | collective-permute-start | bytes 393224 | tf_op jit(solution)/shard_map/ppermute | solution.py:263
  34.5 3.5 %collective-permute-done.4 = bf16[128,512]{1,0:T(8,128)(2,1)S(1)} collective-permute-done((bf16[128,512]{1,0:T(8,128)(2,1)S(1)}, bf16[128,512]{1,0:T(8,128)(2,1)S(1)}, u32[]{:S(2)}, u32[]{:S(2)}) %collective-permute-start.4) | collective-permute-done | bytes 131104 | tf_op jit(solution)/shard_map/ppermute | solution.py:263
  38.0 2.1 %collective-permute-start.5 = (bf16[256,512]{1,0:T(8,128)(2,1)S(1)}, bf16[256,512]{1,0:T(8,128)(2,1)S(1)}, u32[]{:S(2)}, u32[]{:S(2)}) collective-permute-start(bf16[256,512]{1,0:T(8,128)(2,1)S(1)} %pad_maximum_fusion.rest_0_), channel_id=1, source_target_pairs={{0,4},{4,0},{8,12},{12,8},{16,20},{20,16},{24,28},{28,24},{1,5},{5... | collective-permute-start | bytes 786440 | tf_op jit(solution)/shard_map/ppermute | solution.py:278
  40.1 6.0 %collective-permute-start.6 = (bf16[256,512]{1,0:T(8,128)(2,1)S(1)}, bf16[256,512]{1,0:T(8,128)(2,1)S(1)}, u32[]{:S(2)}, u32[]{:S(2)}) collective-permute-start(bf16[256,512]{1,0:T(8,128)(2,1)S(1)} %pad_maximum_fusion.rest_0_), channel_id=1, source_target_pairs={{0,8},{4,12},{8,0},{12,4},{16,24},{20,28},{24,16},{28,20},{1,9},{5... | collective-permute-start | bytes 786440 | tf_op jit(solution)/shard_map/ppermute | solution.py:278
  46.0 1.3 %collective-permute-start.7 = (bf16[256,512]{1,0:T(8,128)(2,1)S(1)}, bf16[256,512]{1,0:T(8,128)(2,1)}, u32[]{:S(2)}, u32[]{:S(2)}) collective-permute-start(bf16[256,512]{1,0:T(8,128)(2,1)S(1)} %pad_maximum_fusion.rest_0_), channel_id=1, source_target_pairs={{0,12},{4,8},{8,4},{12,0},{16,28},{20,24},{24,20},{28,16},{1,13},{... | collective-permute-start | bytes 786440 | tf_op jit(solution)/shard_map/ppermute | solution.py:278
  48.0 2.8 %intra_block.1.intra_ref = f32[128,2048]{1,0:T(8,128)S(1)} custom-call(f32[16,128]{1,0:T(8,128)S(1)} %copy-done.7, bf16[128,2048]{1,0:T(8,128)(2,1)S(1)} %copy-done.4, bf16[128,2048]{1,0:T(8,128)(2,1)S(1)} %copy-done.1, bf16[128,2048]{1,0:T(8,128)(2,1)S(1)} %copy-done.3), custom_call_target="tpu_custom_call" | custom-call | flops 134217728 | bytes 2629632 | tf_op jit(solution)/shard_map/intra_block/pallas_call | solution.py:233
  50.8 0.0 copy-start.9
  50.8 0.9 %inter_block.1 = (f32[128,2048]{1,0:T(8,128)S(1)}, f32[8,128]{1,0:T(8,128)S(1)}) custom-call(f32[16,128]{1,0:T(8,128)S(1)} %copy-done.7, bf16[128,2048]{1,0:T(8,128)(2,1)S(1)} %copy-done.4, f32[128,2048]{1,0:T(8,128)S(1)} %intra_block.1.intra_ref, bf16[4,512,128]{2,1,0:T(8,128)(2,1)S(1)} %all-to-all-done.1.states), custom_call_target="tpu_custom_call" | custom-call | flops 67108864 | bytes 3158016 | tf_op jit(solution)/shard_map/inter_block/pallas_call | solution.py:233
  51.7 1.5 %collective-permute-start.2 = (f32[8,128]{1,0:T(8,128)S(1)}, f32[8,128]{1,0:T(8,128)S(1)}, u32[]{:S(2)}, u32[]{:S(2)}) collective-permute-start(f32[8,128]{1,0:T(8,128)S(1)} %get-tuple-element.5.rest_0_), channel_id=1, source_target_pairs={{0,2},{1,3},{2,0},{3,1},{4,6},{5,7},{6,4},{7,5},{8,10},{9,11},{10,... | collective-permute-start | bytes 12296 | tf_op jit(solution)/shard_map/ppermute | solution.py:331
  53.3 1.4 %collective-permute-start.3 = (f32[8,128]{1,0:T(8,128)S(1)}, f32[8,128]{1,0:T(8,128)S(1)}, u32[]{:S(2)}, u32[]{:S(2)}) collective-permute-start(f32[8,128]{1,0:T(8,128)S(1)} %get-tuple-element.5.rest_0_), channel_id=1, source_target_pairs={{0,3},{1,0},{2,1},{3,2},{4,7},{5,4},{6,5},{7,6},{8,11},{9,8},{10,9... | collective-permute-start | bytes 12296 | tf_op jit(solution)/shard_map/ppermute | solution.py:331
  54.7 2.2 %collective-permute-done.7.rest_3_ = bf16[256,512]{1,0:T(8,128)(2,1)} collective-permute-done((bf16[256,512]{1,0:T(8,128)(2,1)S(1)}, bf16[256,512]{1,0:T(8,128)(2,1)}, u32[]{:S(2)}, u32[]{:S(2)}) %collective-permute-start.7) | collective-permute-done | bytes 262176 | tf_op jit(solution)/shard_map/ppermute | solution.py:278
  56.9 5.9 %softmax_attention.1 = bf16[128,2048]{1,0:T(8,128)(2,1)} custom-call(s32[1]{0:T(128)S(6)} %copy.13.order_ref, bf16[128,2048]{1,0:T(8,128)(2,1)S(1)} %copy-done.9, bf16[256,512]{1,0:T(8,128)(2,1)S(1)} %pad_maximum_fusion.rest_0_, bf16[256,512]{1,0:T(8,128)(2,1)S(1)} %collective-permute-done.5.rest_1_, bf16[256,512]{1,0:T(8,128)(2,1)S(1)} %collective-permute-done.6.rest_2_, ...), custom_call_target="tpu_custom_call" | custom-call | flops 1073741824 | bytes 2097156 | tf_op jit(solution)/shard_map/softmax_attention/pallas_call | solution.py:233
  62.9 1.2 %gated_norm.1 = bf16[128,2048]{1,0:T(8,128)(2,1)} custom-call(f32[128,2048]{1,0:T(8,128)S(1)} %get-tuple-element.4.lin_ref, bf16[128,2048]{1,0:T(8,128)(2,1)S(1)} %copy-done.5, f32[1,2048]{1,0:T(1,128)S(1)} %bitcast.1, f32[8,128]{1,0:T(8,128)S(1)} %get-tuple-element.5.rest_0_, f32[8,128]{1,0:T(8,128)S(1)} %collective-permute-done.1.rest_1_, ...), custom_call_target="tpu_custom_call" | custom-call | flops 1048576 | bytes 2121728 | tf_op jit(solution)/shard_map/gated_norm/pallas_call | solution.py:233
  (29 shorter events, 0.1 us)
Async XLA Ops:
  0.6 1.0 %copy-start = (bf16[128,2048]{1,0:T(8,128)(2,1)S(1)}, bf16[128,2048]{1,0:T(8,128)(2,1)}, u32[]{:S(2)}) copy-start(bf16[128,2048]{1,0:T(8,128)(2,1)} %k_ref.3) | copy-start | bytes 1572868
  1.7 1.0 %copy-start.2 = (bf16[128,2048]{1,0:T(8,128)(2,1)S(1)}, bf16[128,2048]{1,0:T(8,128)(2,1)}, u32[]{:S(2)}) copy-start(bf16[128,2048]{1,0:T(8,128)(2,1)} %v_ref.3) | copy-start | bytes 1572868
  2.7 0.7 %copy-start.6 = (f32[16,128]{1,0:T(8,128)S(1)}, f32[16,128]{1,0:T(8,128)}, u32[]{:S(2)}) copy-start(f32[16,128]{1,0:T(8,128)} %ld_ref.5) | copy-start | bytes 24580
  19.0 7.1 %collective-permute-start = (bf16[528,128]{1,0:T(8,128)(2,1)S(1)}, bf16[528,128]{1,0:T(8,128)(2,1)S(1)}, u32[]{:S(2)}, u32[]{:S(2)}) collective-permute-start(bf16[528,128]{1,0:T(8,128)(2,1)S(1)} %group_state.1), channel_id=1, source_target_pairs={{0,16},{4,20},{8,24},{12,28},{1,17},{5,21},{9,25},{13,29},{2,18},{... | collective-permute-start | bytes 405512 | tf_op jit(solution)/shard_map/ppermute | solution.py:263
  26.1 4.9 %copy-start.10 = (bf16[128,256]{1,0:T(8,128)(2,1)S(1)}, bf16[128,256]{1,0:T(8,128)(2,1)}, u32[]{:S(2)}) copy-start(bf16[128,256]{1,0:T(8,128)(2,1)} %param.17) | copy-start | bytes 196612
  27.0 4.0 %copy-start.11 = (bf16[128,256]{1,0:T(8,128)(2,1)S(1)}, bf16[128,256]{1,0:T(8,128)(2,1)}, u32[]{:S(2)}) copy-start(bf16[128,256]{1,0:T(8,128)(2,1)} %param.18) | copy-start | bytes 196612
  27.0 21.0 %copy-start.3 = (bf16[128,2048]{1,0:T(8,128)(2,1)S(1)}, bf16[128,2048]{1,0:T(8,128)(2,1)}, u32[]{:S(2)}) copy-start(bf16[128,2048]{1,0:T(8,128)(2,1)} %v_ref.3) | copy-start | bytes 1572868
  27.0 21.0 %copy-start.4 = (bf16[128,2048]{1,0:T(8,128)(2,1)S(1)}, bf16[128,2048]{1,0:T(8,128)(2,1)}, u32[]{:S(2)}) copy-start(bf16[128,2048]{1,0:T(8,128)(2,1)} %q_ref.4) | copy-start | bytes 1572868
  27.0 23.8 %all-to-all-start.1 = ((bf16[4,512,128]{2,1,0:T(8,128)(2,1)}), bf16[4,512,128]{2,1,0:T(8,128)(2,1)S(1)}, u32[]{:S(2)}, u32[]{:S(2)}) async-start(bf16[4,512,128]{2,1,0:T(8,128)(2,1)} %prefix_states.1), calls=%async_computation.1 | async-start | bytes 1048576 | tf_op jit(solution)/shard_map/all_to_all | solution.py:259
  31.0 17.0 %copy-start.1 = (bf16[128,2048]{1,0:T(8,128)(2,1)S(1)}, bf16[128,2048]{1,0:T(8,128)(2,1)}, u32[]{:S(2)}) copy-start(bf16[128,2048]{1,0:T(8,128)(2,1)} %k_ref.3) | copy-start | bytes 1572868
  31.0 17.0 %copy-start.7 = (f32[16,128]{1,0:T(8,128)S(1)}, f32[16,128]{1,0:T(8,128)}, u32[]{:S(2)}) copy-start(f32[16,128]{1,0:T(8,128)} %ld_ref.5) | copy-start | bytes 24580
  31.1 6.9 %collective-permute-start.4 = (bf16[128,512]{1,0:T(8,128)(2,1)S(1)}, bf16[128,512]{1,0:T(8,128)(2,1)S(1)}, u32[]{:S(2)}, u32[]{:S(2)}) collective-permute-start(bf16[128,512]{1,0:T(8,128)(2,1)S(1)} %constant_dynamic-update-slice_fusion), channel_id=1, source_target_pairs={{0,16},{4,20},{8,24},{12,28},{16,0},{20,4},{24,8},{28,12},{1,17},{... | collective-permute-start | bytes 393224 | tf_op jit(solution)/shard_map/ppermute | solution.py:263
  38.0 15.3 %collective-permute-start.5 = (bf16[256,512]{1,0:T(8,128)(2,1)S(1)}, bf16[256,512]{1,0:T(8,128)(2,1)S(1)}, u32[]{:S(2)}, u32[]{:S(2)}) collective-permute-start(bf16[256,512]{1,0:T(8,128)(2,1)S(1)} %pad_maximum_fusion.rest_0_), channel_id=1, source_target_pairs={{0,4},{4,0},{8,12},{12,8},{16,20},{20,16},{24,28},{28,24},{1,5},{5... | collective-permute-start | bytes 786440 | tf_op jit(solution)/shard_map/ppermute | solution.py:278
  40.1 14.7 %collective-permute-start.6 = (bf16[256,512]{1,0:T(8,128)(2,1)S(1)}, bf16[256,512]{1,0:T(8,128)(2,1)S(1)}, u32[]{:S(2)}, u32[]{:S(2)}) collective-permute-start(bf16[256,512]{1,0:T(8,128)(2,1)S(1)} %pad_maximum_fusion.rest_0_), channel_id=1, source_target_pairs={{0,8},{4,12},{8,0},{12,4},{16,24},{20,28},{24,16},{28,20},{1,9},{5... | collective-permute-start | bytes 786440 | tf_op jit(solution)/shard_map/ppermute | solution.py:278
  46.0 10.9 %collective-permute-start.7 = (bf16[256,512]{1,0:T(8,128)(2,1)S(1)}, bf16[256,512]{1,0:T(8,128)(2,1)}, u32[]{:S(2)}, u32[]{:S(2)}) collective-permute-start(bf16[256,512]{1,0:T(8,128)(2,1)S(1)} %pad_maximum_fusion.rest_0_), channel_id=1, source_target_pairs={{0,12},{4,8},{8,4},{12,0},{16,28},{20,24},{24,20},{28,16},{1,13},{... | collective-permute-start | bytes 786440 | tf_op jit(solution)/shard_map/ppermute | solution.py:278
  50.8 6.1 %copy-start.9 = (bf16[128,2048]{1,0:T(8,128)(2,1)S(1)}, bf16[128,2048]{1,0:T(8,128)(2,1)}, u32[]{:S(2)}) copy-start(bf16[128,2048]{1,0:T(8,128)(2,1)} %q_ref.5) | copy-start | bytes 1572868
  51.7 11.1 %copy-start.5 = (bf16[128,2048]{1,0:T(8,128)(2,1)S(1)}, bf16[128,2048]{1,0:T(8,128)(2,1)}, u32[]{:S(2)}) copy-start(bf16[128,2048]{1,0:T(8,128)(2,1)} %gate_ref.1) | copy-start | bytes 1572868
  51.7 11.1 %collective-permute-start.1 = (f32[8,128]{1,0:T(8,128)S(1)}, f32[8,128]{1,0:T(8,128)S(1)}, u32[]{:S(2)}, u32[]{:S(2)}) collective-permute-start(f32[8,128]{1,0:T(8,128)S(1)} %get-tuple-element.5.rest_0_), channel_id=1, source_target_pairs={{0,1},{1,2},{2,3},{3,0},{4,5},{5,6},{6,7},{7,4},{8,9},{9,10},{10,1... | collective-permute-start | bytes 12296 | tf_op jit(solution)/shard_map/ppermute | solution.py:331
  51.7 11.1 %collective-permute-start.2 = (f32[8,128]{1,0:T(8,128)S(1)}, f32[8,128]{1,0:T(8,128)S(1)}, u32[]{:S(2)}, u32[]{:S(2)}) collective-permute-start(f32[8,128]{1,0:T(8,128)S(1)} %get-tuple-element.5.rest_0_), channel_id=1, source_target_pairs={{0,2},{1,3},{2,0},{3,1},{4,6},{5,7},{6,4},{7,5},{8,10},{9,11},{10,... | collective-permute-start | bytes 12296 | tf_op jit(solution)/shard_map/ppermute | solution.py:331
  53.3 9.6 %collective-permute-start.3 = (f32[8,128]{1,0:T(8,128)S(1)}, f32[8,128]{1,0:T(8,128)S(1)}, u32[]{:S(2)}, u32[]{:S(2)}) collective-permute-start(f32[8,128]{1,0:T(8,128)S(1)} %get-tuple-element.5.rest_0_), channel_id=1, source_target_pairs={{0,3},{1,0},{2,1},{3,2},{4,7},{5,4},{6,5},{7,6},{8,11},{9,8},{10,9... | collective-permute-start | bytes 12296 | tf_op jit(solution)/shard_map/ppermute | solution.py:331
  56.9 6.0 %copy-start.8 = (f32[2048]{0:T(1024)S(1)}, f32[2048]{0:T(1024)}, u32[]{:S(2)}) copy-start(f32[2048]{0:T(1024)} %param.15) | copy-start | bytes 24580

commit v3 on v1

v3 whole, which is shorter than its diff:
```python
import functools
import math

import jax
import jax.numpy as jnp
from jax import lax
from jax.experimental import pallas as pl
from jax.experimental.pallas import tpu as pltpu
from jax.sharding import PartitionSpec as P

HD = 128
EPS = 1e-06
HIGH = lax.Precision.HIGHEST
F32 = jnp.float32
BF16 = jnp.bfloat16
NT = (((1,), (1,)), ((), ()))
TN = (((0,), (0,)), ((), ()))
MIB = 1 << 20
VMEM = pl.BlockSpec(memory_space=pltpu.VMEM)
HBM = pl.BlockSpec(memory_space=pltpu.HBM)


def silu16(x):
    x = x.astype(F32)
    return (x / (1.0 + jnp.exp(-x))).astype(BF16)


def lower_ones(size):
    rows = lax.broadcasted_iota(jnp.int32, (size, size), 0)
    cols = lax.broadcasted_iota(jnp.int32, (size, size), 1)
    return rows >= cols


def head_cols(h):
    return slice(h * HD, (h + 1) * HD)


def my_rank(group):
    return lax.rem(lax.axis_index("ctx"), group)


def dyn(index, size):
    return pl.ds(pl.multiple_of(index * size, size), size)


def triangle_kernel(ones_ref, bias_ref):
    lower = lower_ones(ones_ref.shape[0])
    ones_ref[...] = lower.astype(F32)
    bias_ref[...] = jnp.where(lower, 0.0, -1e30)


def state_kernel(group, heads, tri_ref, ld_ref, k_ref, v_ref, *rest):
    outs, (ka_ref, va_ref, states, totals) = rest[:group], rest[group:]
    tokens = k_ref.shape[0]
    per = heads // group
    rank = my_rank(group)
    ld = ld_ref[...]
    cum = lax.dot_general(tri_ref[...], ld, NT, precision=HIGH, preferred_element_type=F32)
    weight = jnp.exp(cum[tokens - 1 : tokens, :] - cum)
    total = jnp.broadcast_to(jnp.exp(jnp.sum(ld, axis=1, keepdims=True)), (heads, HD))
    high = total.astype(BF16).astype(F32)
    low = total - high
    totals[...] = jnp.zeros_like(totals)
    for k in range(group):
        totals[k * 16 : k * 16 + per, :] = high[k * per : (k + 1) * per]
        totals[k * 16 + 8 : k * 16 + 8 + per, :] = low[k * per : (k + 1) * per]
    for h in range(heads):
        ka = silu16(k_ref[:, head_cols(h)])
        va = silu16(v_ref[:, head_cols(h)])
        ka_ref[:, head_cols(h)] = ka
        va_ref[:, head_cols(h)] = va
        kdec = ka.astype(F32) * weight[:, h : h + 1]
        khigh = kdec.astype(BF16)
        klow = (kdec - khigh.astype(F32)).astype(BF16)
        state = lax.dot_general(khigh, va, TN, preferred_element_type=F32)
        state += lax.dot_general(klow, va, TN, preferred_element_type=F32)
        states[h * HD : (h + 1) * HD, :] = state.astype(BF16)
    for s in range(group):
        dest = rank ^ s
        outs[s][: per * HD, :] = states[dyn(dest, per * HD), :]
        outs[s][per * HD :, :] = totals[dyn(dest, 16), :].astype(BF16)


def decay_row(slots, k, base, j):
    tail = slots[k, base : base + 16, :].astype(F32)
    return tail[j : j + 1] + tail[8 + j : 9 + j]


def fill_slots(group, rank, pays, slots):
    for s in range(group):
        slots[rank ^ s] = pays[s][...]


def total_kernel(group, per, *refs):
    pays, out, slots = refs[:group], refs[group], refs[group + 1]
    fill_slots(group, my_rank(group), pays, slots)
    base = per * HD
    tails = []
    for j in range(per):
        state = slots[0, j * HD : (j + 1) * HD, :].astype(F32)
        whole = decay_row(slots, 0, base, j)
        for k in range(1, group):
            decay = decay_row(slots, k, base, j)
            state = decay * state + slots[k, j * HD : (j + 1) * HD, :].astype(F32)
            whole = whole * decay
        out[j * HD : (j + 1) * HD, :] = state.astype(BF16)
        tails.append(whole)
    pad = [jnp.zeros((8 - per, HD), F32)] if per < 8 else []
    total = jnp.concatenate(tails + pad, axis=0)
    high = total.astype(BF16).astype(F32)
    out[base:, :] = jnp.concatenate([high, total - high], axis=0).astype(BF16)


def prefix_kernel(group, per, carried, *refs):
    pays, refs = refs[:group], refs[group:]
    carry = None
    if carried:
        carry, refs = refs[0], refs[1:]
    outs, slots, prefixes = refs[:group], refs[group], refs[group + 1]
    rank = my_rank(group)
    later = lax.axis_index("ctx") >= group
    fill_slots(group, rank, pays, slots)
    base = per * HD
    for j in range(per):
        rows = slice(j * HD, (j + 1) * HD)
        state = jnp.zeros((HD, HD), F32)
        if carried:
            state = jnp.where(later, carry[rows, :].astype(F32), state)
        prefixes[0, rows, :] = state.astype(BF16)
        for k in range(group - 1):
            state = decay_row(slots, k, base, j) * state + slots[k, rows, :].astype(F32)
            prefixes[k + 1, rows, :] = state.astype(BF16)
    for s in range(group):
        outs[s][...] = prefixes[rank ^ s]


def intra_kernel(heads, tri_ref, bias_ref, ld_ref, q_ref, ka_ref, va_ref, gate_ref, gain_ref, *outs):
    intra_ref, qa_ref, gain_out, decay_out = outs
    ld = ld_ref[...]
    tri = tri_ref[...]
    bias = bias_ref[...]
    cum = lax.dot_general(tri, ld, NT, precision=HIGH, preferred_element_type=F32)
    cum_t = lax.dot_general(ld, tri, NT, precision=HIGH, preferred_element_type=F32)
    decay_out[...] = jnp.exp(cum)
    for h in range(heads):
        cols = head_cols(h)
        qa = silu16(q_ref[:, cols])
        qa_ref[:, cols] = qa
        scores = lax.dot_general(qa, ka_ref[:, cols], NT, preferred_element_type=F32)
        decay = jnp.exp((cum[:, h : h + 1] - cum_t[h : h + 1, :]) + bias)
        weights = (scores * decay).astype(BF16)
        intra_ref[:, cols] = jnp.dot(weights, va_ref[:, cols], preferred_element_type=F32)
        gate = 1.0 / (1.0 + jnp.exp(-gate_ref[:, cols].astype(F32)))
        gain_out[:, cols] = gate * gain_ref[:, cols]


def inter_kernel(group, heads, decay_ref, qa_ref, intra_ref, *rest):
    parts, (lin_ref, squares_ref, states) = rest[:group], rest[group:]
    tokens = qa_ref.shape[0]
    per = heads // group
    rank = my_rank(group)
    for s in range(group):
        states[dyn(rank ^ s, per * HD), :] = parts[s][...]
    decay = decay_ref[...]
    acc = jnp.zeros((tokens, HD), F32)
    for h in range(heads):
        cols = head_cols(h)
        state = states[h * HD : (h + 1) * HD, :]
        inter = jnp.dot(qa_ref[:, cols], state, preferred_element_type=F32)
        lin = intra_ref[:, cols] + inter * decay[:, h : h + 1]
        lin_ref[:, cols] = lin
        acc += lin * lin
    ones = jnp.ones((8, HD), F32)
    squares_ref[...] = lax.dot_general(ones, acc, NT, precision=HIGH, preferred_element_type=F32)


def mixed_kernel(heads, columns, lin_ref, gain_ref, *rest):
    squares, out_ref = rest[:-1], rest[-1]
    total = squares[0][...]
    for part in squares[1:]:
        total = total + part[...]
    inv = jnp.transpose(lax.rsqrt(total / columns + EPS))[:, 0:1]
    for h in range(heads):
        cols = head_cols(h)
        out_ref[:, cols] = (lin_ref[:, cols] * inv * gain_ref[:, cols]).astype(BF16)


def softmax_kernel(count, group, block, g, kv_heads, order_ref, q_ref, *rest):
    chunks, (out_ref, kv, bias_ref) = rest[:group], rest[-3:]
    tokens = q_ref.shape[0]
    heads = q_ref.shape[1] // HD
    me = lax.axis_index("ctx")
    rank, mine = lax.rem(me, group), lax.div(me, group)
    groups = count // group
    for i in range(count):
        s, d = divmod(i, groups)
        place = lax.rem(mine + groups - d, groups) * group + (rank ^ s)
        rows = slice(d * tokens, (d + 1) * tokens)
        kv[dyn(place, tokens), :HD] = chunks[s][rows, head_cols(g)]
        kv[dyn(place, tokens), HD:] = chunks[s][rows, head_cols(kv_heads + g)]
    first = order_ref[0] * tokens
    scale = math.log2(math.e) / math.sqrt(HD)
    blocks = count * tokens // block
    pack = 2 if heads % 2 == 0 else 1

    def allowed(start):
        qpos = first + lax.broadcasted_iota(jnp.int32, (tokens, block), 0)
        kpos = start + lax.broadcasted_iota(jnp.int32, (tokens, block), 1)
        return jnp.where(kpos <= qpos, 0.0, -1e30)

    def query(h):
        return jnp.concatenate([q_ref[:, head_cols(h + i)] for i in range(pack)], axis=0)

    def store(h, value):
        for i in range(pack):
            out_ref[:, head_cols(h + i)] = value[i * tokens : (i + 1) * tokens]

    def scores(h, start):
        keys = kv[pl.ds(start, block), :HD]
        raw = lax.dot_general(query(h), keys, NT, preferred_element_type=F32)
        return raw.reshape(pack, tokens, block) + bias_ref[...][None]

    def weigh(start, probs):
        values = kv[pl.ds(start, block), HD:]
        flat = probs.astype(BF16).reshape(pack * tokens, block)
        return jnp.dot(flat, values, preferred_element_type=F32)

    if blocks == 1:
        bias_ref[...] = allowed(0)
        for h in range(0, heads, pack):
            raw = scores(h, 0)
            top = jnp.max(raw, axis=-1, keepdims=True)
            probs = jnp.exp2((raw - top) * scale)
            den = jnp.sum(probs, axis=-1, keepdims=True).reshape(pack * tokens, 1)
            store(h, (weigh(0, probs) / den).astype(BF16))
        return

    reach = lax.div(first + tokens - 1, block) + 1
    for h in range(0, heads, pack):

        def step(i, carry):
            top, den, acc = carry
            start = pl.multiple_of(i * block, block)
            bias_ref[...] = allowed(start)
            raw = scores(h, start)
            new = jnp.maximum(top, jnp.max(raw, axis=-1, keepdims=True))
            alpha = jnp.exp2((top - new) * scale)
            probs = jnp.exp2((raw - new) * scale)
            den = den * alpha + jnp.sum(probs, axis=-1, keepdims=True)
            acc = acc * alpha.reshape(pack * tokens, 1) + weigh(start, probs)
            return new, den, acc

        top, den, acc = lax.fori_loop(
            0,
            reach,
            step,
            (
                jnp.full((pack, tokens, 1), -1e30, F32),
                jnp.zeros((pack, tokens, 1), F32),
                jnp.zeros((pack * tokens, HD), F32),
            ),
        )
        store(h, (acc / den.reshape(pack * tokens, 1)).astype(BF16))


def call(
    kernel, name, outs, args, scratch=(), flops=0, exps=0, limit=16, specs=None, after=(), **more
):
    size = sum(math.prod(x.shape) * x.dtype.itemsize for x in list(args) + list(outs))
    more.setdefault("out_specs", [VMEM for _ in outs])
    specs = list(specs or [VMEM for _ in args]) + [HBM for _ in after]
    count = len(args)

    def run(*refs):
        kernel(*refs[:count], *refs[count + len(after) :])

    return pl.pallas_call(
        run,
        name=name,
        out_shape=list(outs),
        in_specs=specs,
        scratch_shapes=list(scratch),
        cost_estimate=pl.CostEstimate(flops=flops, bytes_accessed=size, transcendentals=exps),
        compiler_params=pltpu.CompilerParams(vmem_limit_bytes=limit * MIB),
        **more,
    )(*args, *after)


def body(q_lin, k_lin, v_lin, log_decay, gate, norm_gain, queries, keys, values, order):
    tokens, width = q_lin.shape
    heads = log_decay.shape[0]
    kv_width = keys.shape[1]
    kv_heads = kv_width // HD
    n, nh = lax.axis_size("ctx"), lax.axis_size("head")
    group = 4 if n % 4 == 0 else 2 if n % 2 == 0 else 1
    groups = n // group
    per = heads // group
    rows = per * HD + 16
    cube = tokens * width * HD
    shape = jax.ShapeDtypeStruct

    def swap(x, s):
        return lax.ppermute(x, "ctx", [(c, c ^ s) for c in range(n)])

    def swap_all(xs):
        return [xs[0]] + [swap(xs[s], s) for s in range(1, group)]

    def ahead(x, d):
        return lax.ppermute(x, "ctx", [(c, (c + d * group) % n) for c in range(n)])

    tri, bias = call(
        triangle_kernel, "triangle", [shape((tokens, tokens), F32)] * 2, (), flops=1 << 31
    )
    kv = jnp.concatenate([keys, values], axis=1)
    far = [ahead(kv, d) for d in range(1, groups)]
    own = jnp.concatenate([kv] + far, axis=0)

    *pays, ka, va = call(
        functools.partial(state_kernel, group, heads),
        "block_states",
        [shape((rows, HD), BF16)] * group + [shape((tokens, width), BF16)] * 2,
        (tri, log_decay, k_lin, v_lin),
        [pltpu.VMEM((heads * HD, HD), BF16), pltpu.VMEM((group * 16, HD), F32)],
        flops=4 * cube,
        exps=2 * tokens * width,
    )
    pays = swap_all(pays)
    chunks = [own] + [swap(own, s) for s in range(1, group)]

    intra, qa, gain, decay = call(
        functools.partial(intra_kernel, heads),
        "intra_block",
        [
            shape((tokens, width), F32),
            shape((tokens, width), BF16),
            shape((tokens, width), F32),
            shape((tokens, heads), F32),
        ],
        (tri, bias, log_decay, q_lin, ka, va, gate, norm_gain.reshape(1, width)),
        flops=4 * cube,
        exps=4 * tokens * width,
    )

    slots = pltpu.VMEM((group, rows, HD), BF16)
    carry = ()
    if groups > 1:
        (total,) = call(
            functools.partial(total_kernel, group, per),
            "group_state",
            [shape((rows, HD), BF16)],
            pays,
            [slots],
            flops=2 * per * HD * HD * group,
            after=far,
        )
        before = ahead(total, 1)
        shift = 1
        while shift < groups - 1:
            mine = lax.div(lax.axis_index("ctx"), group)
            later = jnp.where(mine >= 1, before, 0).astype(F32)
            earlier = ahead(later.astype(BF16), shift)
            earlier = jnp.where(mine >= shift + 1, earlier, 0).astype(F32)
            step = later[per * HD :][:per] + later[per * HD + 8 :][:per]
            prior = earlier[per * HD :][:per] + earlier[per * HD + 8 :][:per]
            state = later[: per * HD] + jnp.repeat(step, HD, axis=0) * earlier[: per * HD]
            both = jnp.where(mine >= shift + 1, step * prior, step)
            high = both.astype(BF16).astype(F32)
            pad = jnp.zeros((8 - per, HD), F32)
            before = jnp.concatenate([state, high, pad, both - high, pad], axis=0).astype(BF16)
            shift *= 2
        carry = (before,)
    prefixes = call(
        functools.partial(prefix_kernel, group, per, bool(carry)),
        "prefix_states",
        [shape((per * HD, HD), BF16)] * group,
        (*pays, *carry),
        [slots, pltpu.VMEM((group, per * HD, HD), BF16)],
        flops=2 * per * HD * HD * group,
        after=(intra,),
    )
    prefixes = swap_all(prefixes)

    span = n * tokens
    block = min(span, 1024)
    share = width // kv_heads

    def attend(g, *done):
        columns = pl.BlockSpec((tokens, share), functools.partial(lambda g, i: (0, g), g))
        held = [pl.BlockSpec(x.shape, lambda i: (0, 0)) for x in chunks]
        return call(
            functools.partial(softmax_kernel, n, group, block, g, kv_heads),
            "softmax_attention",
            [shape((tokens, width), BF16)],
            (order, queries, *chunks, *done),
            [pltpu.VMEM((span, 2 * HD), BF16), pltpu.VMEM((tokens, block), F32)],
            flops=4 * tokens * share * span,
            exps=tokens * span * share // HD,
            limit=16 + 6 * span * 2 * kv_width // MIB,
            specs=[pl.BlockSpec(memory_space=pltpu.SMEM), columns, *held, *[HBM for _ in done]],
            out_specs=[columns],
            grid=(1,),
            input_output_aliases={2 + group: 0} if done else {},
        )

    attended = attend(0)
    lin, squares = call(
        functools.partial(inter_kernel, group, heads),
        "inter_block",
        [shape((tokens, width), F32), shape((8, tokens), F32)],
        (decay, qa, intra, *prefixes),
        [pltpu.VMEM((heads * HD, HD), BF16)],
        flops=2 * cube,
        after=attended,
    )
    if nh & (nh - 1) == 0:
        parts, shift = [squares], 1
        while shift < nh:
            held = parts[0] if len(parts) == 1 else parts[0] + parts[1]
            parts = [held, lax.ppermute(held, "head", [(i, i ^ shift) for i in range(nh)])]
            shift *= 2
    else:
        turns = [[(i, (i + d) % nh) for i in range(nh)] for d in range(1, nh)]
        parts = [squares] + [lax.ppermute(squares, "head", turn) for turn in turns]
    (mixed,) = call(
        functools.partial(mixed_kernel, heads, float(width * nh)),
        "gated_norm",
        [shape((tokens, width), BF16)],
        (lin, gain, *parts),
        flops=4 * tokens * width,
    )

    for g in range(1, kv_heads):
        attended = attend(g, *attended)
    return (mixed, attended[0])


def solution(mesh):
    return jax.shard_map(
        body,
        mesh=mesh,
        in_specs=(
            P("ctx", "head"),
            P("ctx", "head"),
            P("ctx", "head"),
            P("head", "ctx"),
            P("ctx", "head"),
            P("head"),
            P("ctx", "head"),
            P("ctx", "head"),
            P("ctx", "head"),
            P("ctx"),
        ),
        out_specs=(P("ctx", "head"), P("ctx", "head")),
        check_vma=False,
    )
```

time: 55.2 us -> 48 us (0.87)
  starting transfers between devices: 29.8 us -> 17 us
  waiting for transfers between devices: 8.98 us -> 15.2 us
  local copies, waits for them, and re-layouts: 2.83 us -> 1.96 us
    ppermute x12 -> x9, starting transfers between devices: 22 us -> 10.9 us  [swap(): return lax.ppermute(x, 'ctx', [(c, c ^ s) for c in range(n)])]
    ppermute x5 -> x4, waiting for transfers between devices: 1.72 us -> 9.7 us  [the longest x2 8.5 us: ahead(): return lax.ppermute(x, 'ctx', [(c, (c + d * group) % n) for c in range(n)])]
    ppermute x12 -> x9, waiting for transfers between devices: 7.27 us -> 5.54 us  [swap(): return lax.ppermute(x, 'ctx', [(c, c ^ s) for c in range(n)])]
    ppermute x5 -> x4, starting transfers between devices: 7.82 us -> 6.15 us  [the longest x2 4.66 us: ahead(): return lax.ppermute(x, 'ctx', [(c, (c + d * group) % n) for c in range(n)])]
    unnamed x25 -> x19, local copies, waits for them, and re-layouts: 2.82 us -> 1.96 us
    pallas_call x7 -> x9, Pallas kernels: 11.8 us -> 12.1 us  [call(): pl.pallas_call(run, name=name, out_shape=list(outs), in_specs=specs, scra...]
  transfers between devices with their start and end apart: 17 -> 13, of which waited for: 7 -> 5; matrix products, arithmetic and copies ran while one was open for 0% -> 0% of each run, Pallas kernels for 16% -> 22%
where the time goes in v3:
time: 48 us; the launch traced here: 47.8 us
  starting transfers between devices  17 us (35%)
  waiting for transfers between devices  15.2 us (32%)
  Pallas kernels  12.1 us (25%)
  local copies, waits for them, and re-layouts  1.96 us (4%)
  between operations  1.41 us (3%)
    pallas_call x9, Pallas kernels, call(): pl.pallas_call(run, name=name, out_shape=list(outs), in_specs=specs, scra...  12.1 us
    ppermute x9, starting transfers between devices, swap(): return lax.ppermute(x, 'ctx', [(c, c ^ s) for c in range(n)])  10.9 us
    ppermute x2, waiting for transfers between devices, ahead(): return lax.ppermute(x, 'ctx', [(c, (c + d * group) % n) for c in range(n)])  8.5 us
    ppermute x9, waiting for transfers between devices, swap(): return lax.ppermute(x, 'ctx', [(c, c ^ s) for c in range(n)])  5.54 us
    ppermute x2, starting transfers between devices, ahead(): return lax.ppermute(x, 'ctx', [(c, (c + d * group) % n) for c in range(n)])  4.66 us
    unnamed x19, local copies, waits for them, and re-layouts  1.96 us
    ppermute x2, starting transfers between devices, body(): lax.ppermute(held, 'head', [(i, i ^ shift) for i in range(nh)])  1.5 us
    ppermute x2, waiting for transfers between devices, body(): lax.ppermute(held, 'head', [(i, i ^ shift) for i in range(nh)])  1.2 us
  transfers between devices with their start and end apart: 13, of which 5 were waited for; matrix products, arithmetic and copies ran while one was open for 0% of the time, Pallas kernels for 22%

profile of v3, /device:TPU:0, one launch (start us, length us, event | category | flops | bytes accessed | tf_op | source)
XLA Modules:
  0.0 47.8 jit_solution(4359425579173305887)
XLA Ops:
  0.6 0.9 %constant_dynamic-update-slice_fusion.1 = bf16[128,512]{1,0:T(8,128)(2,1)S(1)} fusion(bf16[128,256]{1,0:T(8,128)(2,1)} %param.17), kind=kLoop, calls=%fused_computation.2 | loop fusion | bytes 131072
  1.6 4.1 %collective-permute-start.3 = (bf16[128,512]{1,0:T(8,128)(2,1)S(1)}, bf16[128,512]{1,0:T(8,128)(2,1)S(1)}, u32[]{:S(2)}, u32[]{:S(2)}) collective-permute-start(bf16[128,512]{1,0:T(8,128)(2,1)S(1)} %constant_dynamic-update-slice_fusion), channel_id=1, source_target_pairs={{0,16},{4,20},{8,24},{12,28},{16,0},{20,4},{24,8},{28,12},{1,17},{... | collective-permute-start | bytes 393224 | tf_op jit(solution)/shard_map/ppermute | solution.py:309
  5.7 1.5 %block_states.1 = (bf16[528,128]{1,0:T(8,128)(2,1)S(1)}, bf16[528,128]{1,0:T(8,128)(2,1)S(1)}, bf16[528,128]{1,0:T(8,128)(2,1)S(1)}, bf16[528,128]{1,0:T(8,128)(...) custom-call(f32[128,128]{1,0:T(8,128)S(1)} %get-tuple-element.20.refs_0_, ...), custom_call_target="tpu_custom_call" | custom-call | flops 134217728 | bytes 2711552 | tf_op jit(solution)/shard_map/block_states/pallas_call | solution.py:277
  7.2 1.6 %collective-permute-start = (bf16[528,128]{1,0:T(8,128)(2,1)S(1)}, bf16[528,128]{1,0:T(8,128)(2,1)S(1)}, u32[]{:S(2)}, u32[]{:S(2)}) collective-permute-start(bf16[528,128]{1,0:T(8,128)(2,1)S(1)} %get-tuple-element.28), channel_id=1, source_target_pairs={{0,4},{4,0},{8,12},{12,8},{16,20},{20,16},{24,28},{28,24},{1,5},{5... | collective-permute-start | bytes 405512 | tf_op jit(solution)/shard_map/ppermute | solution.py:303
  8.8 1.6 %collective-permute-start.1 = (bf16[528,128]{1,0:T(8,128)(2,1)S(1)}, bf16[528,128]{1,0:T(8,128)(2,1)S(1)}, u32[]{:S(2)}, u32[]{:S(2)}) collective-permute-start(bf16[528,128]{1,0:T(8,128)(2,1)S(1)} %get-tuple-element.29), channel_id=1, source_target_pairs={{0,8},{4,12},{8,0},{12,4},{16,24},{20,28},{24,16},{28,20},{1,9},{5... | collective-permute-start | bytes 405512 | tf_op jit(solution)/shard_map/ppermute | solution.py:303
  10.8 1.3 %collective-permute-done.3.refs_4_ = bf16[128,512]{1,0:T(8,128)(2,1)S(1)} collective-permute-done((bf16[128,512]{1,0:T(8,128)(2,1)S(1)}, bf16[128,512]{1,0:T(8,128)(2,1)S(1)}, u32[]{:S(2)}, u32[]{:S(2)}) %collective-permute-start.3) | collective-permute-done | bytes 131104 | tf_op jit(solution)/shard_map/ppermute | solution.py:309
  12.1 1.7 %collective-permute-start.10 = (bf16[256,512]{1,0:T(8,128)(2,1)S(1)}, bf16[256,512]{1,0:T(8,128)(2,1)S(1)}, u32[]{:S(2)}, u32[]{:S(2)}) collective-permute-start(bf16[256,512]{1,0:T(8,128)(2,1)S(1)} %pad_maximum_fusion.refs_2_), channel_id=1, source_target_pairs={{0,12},{4,8},{8,4},{12,0},{16,28},{20,24},{24,20},{28,16},{1,13},{... | collective-permute-start | bytes 786440 | tf_op jit(solution)/shard_map/ppermute | solution.py:303
  13.8 0.5 %collective-permute-start.8 = (bf16[256,512]{1,0:T(8,128)(2,1)S(1)}, bf16[256,512]{1,0:T(8,128)(2,1)S(1)}, u32[]{:S(2)}, u32[]{:S(2)}) collective-permute-start(bf16[256,512]{1,0:T(8,128)(2,1)S(1)} %pad_maximum_fusion.refs_2_), channel_id=1, source_target_pairs={{0,4},{4,0},{8,12},{12,8},{16,20},{20,16},{24,28},{28,24},{1,5},{5... | collective-permute-start | bytes 786440 | tf_op jit(solution)/shard_map/ppermute | solution.py:303
  14.3 1.4 %collective-permute-start.9 = (bf16[256,512]{1,0:T(8,128)(2,1)S(1)}, bf16[256,512]{1,0:T(8,128)(2,1)S(1)}, u32[]{:S(2)}, u32[]{:S(2)}) collective-permute-start(bf16[256,512]{1,0:T(8,128)(2,1)S(1)} %pad_maximum_fusion.refs_2_), channel_id=1, source_target_pairs={{0,8},{4,12},{8,0},{12,4},{16,24},{20,28},{24,16},{28,20},{1,9},{5... | collective-permute-start | bytes 786440 | tf_op jit(solution)/shard_map/ppermute | solution.py:303
  15.7 3.4 %collective-permute-done.2.refs_3_ = bf16[528,128]{1,0:T(8,128)(2,1)S(1)} collective-permute-done((bf16[528,128]{1,0:T(8,128)(2,1)S(1)}, bf16[528,128]{1,0:T(8,128)(2,1)S(1)}, u32[]{:S(2)}, u32[]{:S(2)}) %collective-permute-start.2) | collective-permute-done | bytes 135200 | tf_op jit(solution)/shard_map/ppermute | solution.py:303
  19.2 0.6 %collective-permute-start.4 = (bf16[528,128]{1,0:T(8,128)(2,1)S(1)}, bf16[528,128]{1,0:T(8,128)(2,1)S(1)}, u32[]{:S(2)}, u32[]{:S(2)}) collective-permute-start(bf16[528,128]{1,0:T(8,128)(2,1)S(1)} %group_state.1), channel_id=1, source_target_pairs={{0,16},{4,20},{8,24},{12,28},{16,0},{20,4},{24,8},{28,12},{1,17},{... | collective-permute-start | bytes 405512 | tf_op jit(solution)/shard_map/ppermute | solution.py:309
  19.8 2.8 %intra_block.1 = (f32[128,2048]{1,0:T(8,128)S(1)}, bf16[128,2048]{1,0:T(8,128)(2,1)S(1)}, f32[128,2048]{1,0:T(8,128)S(1)}, f32[128,16]{1,0:T(8,128)S(1)}) custom-call(f32[128,128]{1,0:T(8,128)S(1)} %get-tuple-element.20.refs_0_, f32[128,128]{1,0:T(8,128)S(1)} %get-tuple-element.21.refs_1_, f32[16,128]{1,0:T(8,128)S(1)} %copy-done.6, ...), custom_call_target="tpu_custom_call" | custom-call | flops 134217728 | bytes 4874240 | tf_op jit(solution)/shard_map/intra_block/pallas_call | solution.py:277
  22.5 7.2 %collective-permute-done.4.refs_4_ = bf16[528,128]{1,0:T(8,128)(2,1)S(1)} collective-permute-done((bf16[528,128]{1,0:T(8,128)(2,1)S(1)}, bf16[528,128]{1,0:T(8,128)(2,1)S(1)}, u32[]{:S(2)}, u32[]{:S(2)}) %collective-permute-start.4) | collective-permute-done | bytes 135200 | tf_op jit(solution)/shard_map/ppermute | solution.py:309
  29.9 0.6 %collective-permute-start.5 = (bf16[512,128]{1,0:T(8,128)(2,1)S(1)}, bf16[512,128]{1,0:T(8,128)(2,1)S(1)}, u32[]{:S(2)}, u32[]{:S(2)}) collective-permute-start(bf16[512,128]{1,0:T(8,128)(2,1)S(1)} %get-tuple-element.32), channel_id=1, source_target_pairs={{0,4},{4,0},{8,12},{12,8},{16,20},{20,16},{24,28},{28,24},{1,5},{5... | collective-permute-start | bytes 393224 | tf_op jit(solution)/shard_map/ppermute | solution.py:303
  30.5 2.6 %collective-permute-start.6 = (bf16[512,128]{1,0:T(8,128)(2,1)S(1)}, bf16[512,128]{1,0:T(8,128)(2,1)S(1)}, u32[]{:S(2)}, u32[]{:S(2)}) collective-permute-start(bf16[512,128]{1,0:T(8,128)(2,1)S(1)} %get-tuple-element.33), channel_id=1, source_target_pairs={{0,8},{4,12},{8,0},{12,4},{16,24},{20,28},{24,16},{28,20},{1,9},{5... | collective-permute-start | bytes 393224 | tf_op jit(solution)/shard_map/ppermute | solution.py:303
  33.1 0.6 %collective-permute-start.7 = (bf16[512,128]{1,0:T(8,128)(2,1)S(1)}, bf16[512,128]{1,0:T(8,128)(2,1)S(1)}, u32[]{:S(2)}, u32[]{:S(2)}) collective-permute-start(bf16[512,128]{1,0:T(8,128)(2,1)S(1)} %get-tuple-element.34), channel_id=1, source_target_pairs={{0,12},{4,8},{8,4},{12,0},{16,28},{20,24},{24,20},{28,16},{1,13},{... | collective-permute-start | bytes 393224 | tf_op jit(solution)/shard_map/ppermute | solution.py:303
  34.4 2.9 %softmax_attention.2.refs_7_.refs_6_ = bf16[128,2048]{1,0:T(8,128)(2,1)} custom-call(s32[1]{0:T(128)S(6)} %copy.15.refs_0_, bf16[128,2048]{1,0:T(8,128)(2,1)S(1)} %copy-done.1, bf16[256,512]{1,0:T(8,128)(2,1)S(1)} %pad_maximum_fusion.refs_2_, bf16[256,512]{1,0:T(8,128)(2,1)S(1)} %collective-permute-done.8.refs_3_, ...), custom_call_target="tpu_custom_call" | custom-call | flops 536870912 | bytes 2097156 | tf_op jit(solution)/shard_map/softmax_attention/pallas_call | solution.py:277
  37.3 2.2 %collective-permute-done.7.refs_6_ = bf16[512,128]{1,0:T(8,128)(2,1)S(1)} collective-permute-done((bf16[512,128]{1,0:T(8,128)(2,1)S(1)}, bf16[512,128]{1,0:T(8,128)(2,1)S(1)}, u32[]{:S(2)}, u32[]{:S(2)}) %collective-permute-start.7) | collective-permute-done | bytes 131104 | tf_op jit(solution)/shard_map/ppermute | solution.py:303
  39.4 1.0 %copy-done = bf16[128,2048]{1,0:T(8,128)(2,1)S(1)} copy-done((bf16[128,2048]{1,0:T(8,128)(2,1)S(1)}, bf16[128,2048]{1,0:T(8,128)(2,1)}, u32[]{:S(2)}) %copy-start) | copy-done | bytes 524312
  40.5 0.7 %inter_block.1 = (f32[128,2048]{1,0:T(8,128)S(1)}, f32[8,128]{1,0:T(8,128)S(1)}) custom-call(f32[128,16]{1,0:T(8,128)S(1)} %get-tuple-element.24.refs_0_, bf16[128,2048]{1,0:T(8,128)(2,1)S(1)} %get-tuple-element.25.refs_1_, f32[128,2048]{1,0:T(8,128)S(1)} %get-tuple-element.26.refs_5_.refs_2_, bf16[512,128]{1,0:T(8,128)(2,1)S(1)} %get-tuple-element.31.refs_3_, ...), custom_call_target="tpu_custom_call" | custom-call | flops 67108864 | bytes 3158016 | tf_op jit(solution)/shard_map/inter_block/pallas_call | solution.py:277
  41.2 1.2 %collective-permute-done.11 = f32[8,128]{1,0:T(8,128)S(1)} collective-permute-done((f32[8,128]{1,0:T(8,128)S(1)}, f32[8,128]{1,0:T(8,128)S(1)}, u32[]{:S(2)}, u32[]{:S(2)}) %collective-permute-start.11) | collective-permute-done | bytes 4128 | tf_op jit(solution)/shard_map/ppermute | solution.py:419
  42.4 1.5 %collective-permute-start.12 = (f32[8,128]{1,0:T(8,128)S(1)}, f32[8,128]{1,0:T(8,128)S(1)}, u32[]{:S(2)}, u32[]{:S(2)}) collective-permute-start(f32[8,128]{1,0:T(8,128)S(1)} %add.3.refs_2_), channel_id=1, source_target_pairs={{0,2},{1,3},{2,0},{3,1},{4,6},{5,7},{6,4},{7,5},{8,10},{9,11},{10,... | collective-permute-start | bytes 12296 | tf_op jit(solution)/shard_map/ppermute | solution.py:419
  43.8 2.9 %softmax_attention.3 = bf16[128,2048]{1,0:T(8,128)(2,1)} custom-call(s32[1]{0:T(128)S(6)} %copy.15.refs_0_, bf16[128,2048]{1,0:T(8,128)(2,1)S(1)} %copy-done.1, bf16[256,512]{1,0:T(8,128)(2,1)S(1)} %pad_maximum_fusion.refs_2_, bf16[256,512]{1,0:T(8,128)(2,1)S(1)} %collective-permute-done.8.refs_3_, ...), custom_call_target="tpu_custom_call", output_to_operand_aliasing={{}: (6, {})} | custom-call | flops 536870912 | bytes 2621444 | tf_op jit(solution)/shard_map/softmax_attention/pallas_call | solution.py:277
  46.7 1.1 %gated_norm.1 = bf16[128,2048]{1,0:T(8,128)(2,1)} custom-call(f32[128,2048]{1,0:T(8,128)S(1)} %get-tuple-element.35.refs_0_, f32[128,2048]{1,0:T(8,128)S(1)} %get-tuple-element.36.refs_1_, f32[8,128]{1,0:T(8,128)S(1)} %add.3.refs_2_, f32[8,128]{1,0:T(8,128)S(1)} %collective-permute-done.12.refs_3_), custom_call_target="tpu_custom_call" | custom-call | flops 1048576 | bytes 2629632 | tf_op jit(solution)/shard_map/gated_norm/pallas_call | solution.py:277
  (33 shorter events, 0.8 us)
Async XLA Ops:
  0.6 0.9 %copy-start.8 = (bf16[128,256]{1,0:T(8,128)(2,1)S(1)}, bf16[128,256]{1,0:T(8,128)(2,1)}, u32[]{:S(2)}) copy-start(bf16[128,256]{1,0:T(8,128)(2,1)} %param.18) | copy-start | bytes 196612
  1.5 4.2 %copy-start.4 = (bf16[128,2048]{1,0:T(8,128)(2,1)S(1)}, bf16[128,2048]{1,0:T(8,128)(2,1)}, u32[]{:S(2)}) copy-start(bf16[128,2048]{1,0:T(8,128)(2,1)} %refs_2_.2) | copy-start | bytes 1572868
  1.5 4.2 %copy-start.5 = (bf16[128,2048]{1,0:T(8,128)(2,1)S(1)}, bf16[128,2048]{1,0:T(8,128)(2,1)}, u32[]{:S(2)}) copy-start(bf16[128,2048]{1,0:T(8,128)(2,1)} %refs_3_.2) | copy-start | bytes 1572868
  1.6 4.2 %copy-start.6 = (f32[16,128]{1,0:T(8,128)S(1)}, f32[16,128]{1,0:T(8,128)}, u32[]{:S(2)}) copy-start(f32[16,128]{1,0:T(8,128)} %refs_2_.3) | copy-start | bytes 24580
  1.6 10.5 %collective-permute-start.3 = (bf16[128,512]{1,0:T(8,128)(2,1)S(1)}, bf16[128,512]{1,0:T(8,128)(2,1)S(1)}, u32[]{:S(2)}, u32[]{:S(2)}) collective-permute-start(bf16[128,512]{1,0:T(8,128)(2,1)S(1)} %constant_dynamic-update-slice_fusion), channel_id=1, source_target_pairs={{0,16},{4,20},{8,24},{12,28},{16,0},{20,4},{24,8},{28,12},{1,17},{... | collective-permute-start | bytes 393224 | tf_op jit(solution)/shard_map/ppermute | solution.py:309
  7.2 7.1 %collective-permute-start = (bf16[528,128]{1,0:T(8,128)(2,1)S(1)}, bf16[528,128]{1,0:T(8,128)(2,1)S(1)}, u32[]{:S(2)}, u32[]{:S(2)}) collective-permute-start(bf16[528,128]{1,0:T(8,128)(2,1)S(1)} %get-tuple-element.28), channel_id=1, source_target_pairs={{0,4},{4,0},{8,12},{12,8},{16,20},{20,16},{24,28},{28,24},{1,5},{5... | collective-permute-start | bytes 405512 | tf_op jit(solution)/shard_map/ppermute | solution.py:303
  8.8 6.8 %collective-permute-start.1 = (bf16[528,128]{1,0:T(8,128)(2,1)S(1)}, bf16[528,128]{1,0:T(8,128)(2,1)S(1)}, u32[]{:S(2)}, u32[]{:S(2)}) collective-permute-start(bf16[528,128]{1,0:T(8,128)(2,1)S(1)} %get-tuple-element.29), channel_id=1, source_target_pairs={{0,8},{4,12},{8,0},{12,4},{16,24},{20,28},{24,16},{28,20},{1,9},{5... | collective-permute-start | bytes 405512 | tf_op jit(solution)/shard_map/ppermute | solution.py:303
  10.4 8.6 %collective-permute-start.2 = (bf16[528,128]{1,0:T(8,128)(2,1)S(1)}, bf16[528,128]{1,0:T(8,128)(2,1)S(1)}, u32[]{:S(2)}, u32[]{:S(2)}) collective-permute-start(bf16[528,128]{1,0:T(8,128)(2,1)S(1)} %get-tuple-element.30), channel_id=1, source_target_pairs={{0,12},{4,8},{8,4},{12,0},{16,28},{20,24},{24,20},{28,16},{1,13},{... | collective-permute-start | bytes 405512 | tf_op jit(solution)/shard_map/ppermute | solution.py:303
  12.1 7.7 %copy-start.3 = (bf16[128,2048]{1,0:T(8,128)(2,1)S(1)}, bf16[128,2048]{1,0:T(8,128)(2,1)}, u32[]{:S(2)}) copy-start(bf16[128,2048]{1,0:T(8,128)(2,1)} %refs_6_.1) | copy-start | bytes 1572868
  12.1 7.7 %copy-start.2 = (bf16[128,2048]{1,0:T(8,128)(2,1)S(1)}, bf16[128,2048]{1,0:T(8,128)(2,1)}, u32[]{:S(2)}) copy-start(bf16[128,2048]{1,0:T(8,128)(2,1)} %refs_3_.3) | copy-start | bytes 1572868
  12.1 20.9 %collective-permute-start.10 = (bf16[256,512]{1,0:T(8,128)(2,1)S(1)}, bf16[256,512]{1,0:T(8,128)(2,1)S(1)}, u32[]{:S(2)}, u32[]{:S(2)}) collective-permute-start(bf16[256,512]{1,0:T(8,128)(2,1)S(1)} %pad_maximum_fusion.refs_2_), channel_id=1, source_target_pairs={{0,12},{4,8},{8,4},{12,0},{16,28},{20,24},{24,20},{28,16},{1,13},{... | collective-permute-start | bytes 786440 | tf_op jit(solution)/shard_map/ppermute | solution.py:303
  13.8 20.6 %collective-permute-start.8 = (bf16[256,512]{1,0:T(8,128)(2,1)S(1)}, bf16[256,512]{1,0:T(8,128)(2,1)S(1)}, u32[]{:S(2)}, u32[]{:S(2)}) collective-permute-start(bf16[256,512]{1,0:T(8,128)(2,1)S(1)} %pad_maximum_fusion.refs_2_), channel_id=1, source_target_pairs={{0,4},{4,0},{8,12},{12,8},{16,20},{20,16},{24,28},{28,24},{1,5},{5... | collective-permute-start | bytes 786440 | tf_op jit(solution)/shard_map/ppermute | solution.py:303
  14.3 20.1 %collective-permute-start.9 = (bf16[256,512]{1,0:T(8,128)(2,1)S(1)}, bf16[256,512]{1,0:T(8,128)(2,1)S(1)}, u32[]{:S(2)}, u32[]{:S(2)}) collective-permute-start(bf16[256,512]{1,0:T(8,128)(2,1)S(1)} %pad_maximum_fusion.refs_2_), channel_id=1, source_target_pairs={{0,8},{4,12},{8,0},{12,4},{16,24},{20,28},{24,16},{28,20},{1,9},{5... | collective-permute-start | bytes 786440 | tf_op jit(solution)/shard_map/ppermute | solution.py:303
  19.0 0.7 %copy-start.7 = (f32[2048]{0:T(1024)S(1)}, f32[2048]{0:T(1024)}, u32[]{:S(2)}) copy-start(f32[2048]{0:T(1024)} %param.15) | copy-start | bytes 24580
  19.2 10.5 %collective-permute-start.4 = (bf16[528,128]{1,0:T(8,128)(2,1)S(1)}, bf16[528,128]{1,0:T(8,128)(2,1)S(1)}, u32[]{:S(2)}, u32[]{:S(2)}) collective-permute-start(bf16[528,128]{1,0:T(8,128)(2,1)S(1)} %group_state.1), channel_id=1, source_target_pairs={{0,16},{4,20},{8,24},{12,28},{16,0},{20,4},{24,8},{28,12},{1,17},{... | collective-permute-start | bytes 405512 | tf_op jit(solution)/shard_map/ppermute | solution.py:309
  29.7 4.6 %copy-start.1 = (bf16[128,2048]{1,0:T(8,128)(2,1)S(1)}, bf16[128,2048]{1,0:T(8,128)(2,1)}, u32[]{:S(2)}) copy-start(bf16[128,2048]{1,0:T(8,128)(2,1)} %refs_1_.5) | copy-start | bytes 1572868
  29.9 7.4 %collective-permute-start.5 = (bf16[512,128]{1,0:T(8,128)(2,1)S(1)}, bf16[512,128]{1,0:T(8,128)(2,1)S(1)}, u32[]{:S(2)}, u32[]{:S(2)}) collective-permute-start(bf16[512,128]{1,0:T(8,128)(2,1)S(1)} %get-tuple-element.32), channel_id=1, source_target_pairs={{0,4},{4,0},{8,12},{12,8},{16,20},{20,16},{24,28},{28,24},{1,5},{5... | collective-permute-start | bytes 393224 | tf_op jit(solution)/shard_map/ppermute | solution.py:303
  30.5 6.8 %collective-permute-start.6 = (bf16[512,128]{1,0:T(8,128)(2,1)S(1)}, bf16[512,128]{1,0:T(8,128)(2,1)S(1)}, u32[]{:S(2)}, u32[]{:S(2)}) collective-permute-start(bf16[512,128]{1,0:T(8,128)(2,1)S(1)} %get-tuple-element.33), channel_id=1, source_target_pairs={{0,8},{4,12},{8,0},{12,4},{16,24},{20,28},{24,16},{28,20},{1,9},{5... | collective-permute-start | bytes 393224 | tf_op jit(solution)/shard_map/ppermute | solution.py:303
  33.1 6.4 %collective-permute-start.7 = (bf16[512,128]{1,0:T(8,128)(2,1)S(1)}, bf16[512,128]{1,0:T(8,128)(2,1)S(1)}, u32[]{:S(2)}, u32[]{:S(2)}) collective-permute-start(bf16[512,128]{1,0:T(8,128)(2,1)S(1)} %get-tuple-element.34), channel_id=1, source_target_pairs={{0,12},{4,8},{8,4},{12,0},{16,28},{20,24},{24,20},{28,16},{1,13},{... | collective-permute-start | bytes 393224 | tf_op jit(solution)/shard_map/ppermute | solution.py:303
  39.4 1.0 %copy-start = (bf16[128,2048]{1,0:T(8,128)(2,1)S(1)}, bf16[128,2048]{1,0:T(8,128)(2,1)}, u32[]{:S(2)}) copy-start(bf16[128,2048]{1,0:T(8,128)(2,1)} %softmax_attention.2.refs_7_.refs_6_) | copy-start | bytes 1572868
  41.2 1.2 %collective-permute-start.11 = (f32[8,128]{1,0:T(8,128)S(1)}, f32[8,128]{1,0:T(8,128)S(1)}, u32[]{:S(2)}, u32[]{:S(2)}) collective-permute-start(f32[8,128]{1,0:T(8,128)S(1)} %get-tuple-element.37), channel_id=1, source_target_pairs={{0,1},{1,0},{2,3},{3,2},{4,5},{5,4},{6,7},{7,6},{8,9},{9,8},{10,11... | collective-permute-start | bytes 12296 | tf_op jit(solution)/shard_map/ppermute | solution.py:419
  42.4 4.4 %collective-permute-start.12 = (f32[8,128]{1,0:T(8,128)S(1)}, f32[8,128]{1,0:T(8,128)S(1)}, u32[]{:S(2)}, u32[]{:S(2)}) collective-permute-start(f32[8,128]{1,0:T(8,128)S(1)} %add.3.refs_2_), channel_id=1, source_target_pairs={{0,2},{1,3},{2,0},{3,1},{4,6},{5,7},{6,4},{7,5},{8,10},{9,11},{10,... | collective-permute-start | bytes 12296 | tf_op jit(solution)/shard_map/ppermute | solution.py:419

commit v4 on v3

--- a/solution.py
+++ b/solution.py
@@ -81,6 +81,12 @@
         outs[s][per * HD :, :] = totals[dyn(dest, 16), :].astype(BF16)
 
 
+def stack_kernel(*refs):
+    tokens = refs[0].shape[0]
+    for i, part in enumerate(refs[:-1]):
+        refs[-1][i * tokens : (i + 1) * tokens, :] = part[...]
+
+
 def decay_row(slots, k, base, j):
     tail = slots[k, base : base + 16, :].astype(F32)
     return tail[j : j + 1] + tail[8 + j : 9 + j]
@@ -174,6 +180,10 @@
     squares_ref[...] = lax.dot_general(ones, acc, NT, precision=HIGH, preferred_element_type=F32)
 
 
+def add_kernel(a_ref, b_ref, out_ref):
+    out_ref[...] = a_ref[...] + b_ref[...]
+
+
 def mixed_kernel(heads, columns, lin_ref, gain_ref, *rest):
     squares, out_ref = rest[:-1], rest[-1]
     total = squares[0][...]
@@ -186,7 +196,8 @@
 
 
 def softmax_kernel(count, group, block, g, kv_heads, order_ref, q_ref, *rest):
-    chunks, (out_ref, kv, bias_ref) = rest[:group], rest[-3:]
+    chunks, (out_ref, done_ref, kv, bias_ref) = rest[:group], rest[-4:]
+    done_ref[...] = jnp.zeros_like(done_ref)
     tokens = q_ref.shape[0]
     heads = q_ref.shape[1] // HD
     me = lax.axis_index("ctx")
@@ -313,7 +324,6 @@
     )
     kv = jnp.concatenate([keys, values], axis=1)
     far = [ahead(kv, d) for d in range(1, groups)]
-    own = jnp.concatenate([kv] + far, axis=0)
 
     *pays, ka, va = call(
         functools.partial(state_kernel, group, heads),
@@ -325,8 +335,6 @@
         exps=2 * tokens * width,
     )
     pays = swap_all(pays)
-    chunks = [own] + [swap(own, s) for s in range(1, group)]
-
     intra, qa, gain, decay = call(
         functools.partial(intra_kernel, heads),
         "intra_block",
@@ -351,7 +359,7 @@
             pays,
             [slots],
             flops=2 * per * HD * HD * group,
-            after=far,
+            after=(intra, *far),
         )
         before = ahead(total, 1)
         shift = 1
@@ -376,10 +384,21 @@
         (*pays, *carry),
         [slots, pltpu.VMEM((group, per * HD, HD), BF16)],
         flops=2 * per * HD * HD * group,
+    )
+    prefixes = swap_all(prefixes)
+
+    (own,) = call(
+        stack_kernel,
+        "stack_keys_values",
+        [shape((groups * tokens, kv.shape[1]), BF16)],
+        (kv, *far),
         after=(intra,),
-    )
-    prefixes = swap_all(prefixes)
-
+        limit=16 + 4 * n * tokens * kv.shape[1] // MIB,
+    )
+    chunks = [own] + [swap(own, s) for s in (1, 2) if s < group]
+    if group == 4:
+        half = own.shape[0] // 2
+        chunks.append(jnp.concatenate([swap(chunks[1][:half], 2), swap(chunks[2][half:], 1)]))
     span = n * tokens
     block = min(span, 1024)
     share = width // kv_heads
@@ -390,19 +409,23 @@
         return call(
             functools.partial(softmax_kernel, n, group, block, g, kv_heads),
             "softmax_attention",
-            [shape((tokens, width), BF16)],
+            [shape((tokens, width), BF16), shape((8, HD), F32)],
             (order, queries, *chunks, *done),
             [pltpu.VMEM((span, 2 * HD), BF16), pltpu.VMEM((tokens, block), F32)],
             flops=4 * tokens * share * span,
             exps=tokens * span * share // HD,
             limit=16 + 6 * span * 2 * kv_width // MIB,
             specs=[pl.BlockSpec(memory_space=pltpu.SMEM), columns, *held, *[HBM for _ in done]],
-            out_specs=[columns],
+            out_specs=[columns, pl.BlockSpec((8, HD), lambda i: (0, 0))],
             grid=(1,),
             input_output_aliases={2 + group: 0} if done else {},
         )
 
-    attended = attend(0)
+    attended, marks = (), []
+    for g in range(kv_heads):
+        *attended, mark = attend(g, *attended)
+        marks.append(mark)
+
     lin, squares = call(
         functools.partial(inter_kernel, group, heads),
         "inter_block",
@@ -410,12 +433,13 @@
         (decay, qa, intra, *prefixes),
         [pltpu.VMEM((heads * HD, HD), BF16)],
         flops=2 * cube,
-        after=attended,
     )
     if nh & (nh - 1) == 0:
         parts, shift = [squares], 1
         while shift < nh:
-            held = parts[0] if len(parts) == 1 else parts[0] + parts[1]
+            held = parts[0]
+            if len(parts) > 1:
+                (held,) = call(add_kernel, "add", [shape((8, tokens), F32)], parts, after=marks[:1])
             parts = [held, lax.ppermute(held, "head", [(i, i ^ shift) for i in range(nh)])]
             shift *= 2
     else:
@@ -427,10 +451,8 @@
         [shape((tokens, width), BF16)],
         (lin, gain, *parts),
         flops=4 * tokens * width,
-    )
-
-    for g in range(1, kv_heads):
-        attended = attend(g, *attended)
+        after=marks,
+    )
     return (mixed, attended[0])
 
 

time: 48 us -> 47.1 us (0.981)
  waiting for transfers between devices: 15.2 us -> 13.7 us
  starting transfers between devices: 17 us -> 18.3 us
  local copies, waits for them, and re-layouts: 1.96 us -> 1.26 us
    ppermute x2, waiting for transfers between devices: 1.2 us -> 0.01 us  [body(): lax.ppermute(held, 'head', [(i, i ^ shift) for i in range(nh)])]
    ppermute x2, waiting for transfers between devices: 8.5 us -> 7.38 us  [ahead(): return lax.ppermute(x, 'ctx', [(c, (c + d * group) % n) for c in range(n)])]
    ppermute x9 -> x10, starting transfers between devices: 10.9 us -> 11.7 us  [swap(): return lax.ppermute(x, 'ctx', [(c, c ^ s) for c in range(n)])]
    ppermute x9 -> x10, waiting for transfers between devices: 5.54 us -> 6.33 us  [swap(): return lax.ppermute(x, 'ctx', [(c, c ^ s) for c in range(n)])]
    unnamed x19 -> x18, local copies, waits for them, and re-layouts: 1.96 us -> 1.23 us
    pallas_call x9 -> x11, Pallas kernels: 12.1 us -> 12.2 us  [call(): pl.pallas_call(run, name=name, out_shape=list(outs), in_specs=specs, scra...]
  transfers between devices with their start and end apart: 13 -> 14, of which waited for: 5 -> 6; matrix products, arithmetic and copies ran while one was open for 0% -> 0% of each run, Pallas kernels for 22% -> 24%
where the time goes in v4:
time: 47.1 us; the launch traced here: 46.9 us
  starting transfers between devices  18.3 us (39%)
  waiting for transfers between devices  13.7 us (29%)
  Pallas kernels  12.2 us (26%)
  between operations  1.45 us (3%)
  local copies, waits for them, and re-layouts  1.26 us (3%)
    pallas_call x11, Pallas kernels, call(): pl.pallas_call(run, name=name, out_shape=list(outs), in_specs=specs, scra...  12.2 us
    ppermute x10, starting transfers between devices, swap(): return lax.ppermute(x, 'ctx', [(c, c ^ s) for c in range(n)])  11.7 us
    ppermute x2, waiting for transfers between devices, ahead(): return lax.ppermute(x, 'ctx', [(c, (c + d * group) % n) for c in range(n)])  7.38 us
    ppermute x10, waiting for transfers between devices, swap(): return lax.ppermute(x, 'ctx', [(c, c ^ s) for c in range(n)])  6.33 us
    ppermute x2, starting transfers between devices, ahead(): return lax.ppermute(x, 'ctx', [(c, (c + d * group) % n) for c in range(n)])  4.72 us
    ppermute x2, starting transfers between devices, body(): lax.ppermute(held, 'head', [(i, i ^ shift) for i in range(nh)])  1.87 us
    unnamed x18, local copies, waits for them, and re-layouts  1.23 us
  transfers between devices with their start and end apart: 14, of which 6 were waited for; matrix products, arithmetic and copies ran while one was open for 0% of the time, Pallas kernels for 24%

profile of v4, /device:TPU:0, one launch (start us, length us, event | category | flops | bytes accessed | tf_op | source)
XLA Modules:
  0.0 46.9 jit_solution(980317196359680655)
XLA Ops:
  0.6 0.9 %constant_dynamic-update-slice_fusion.1 = bf16[128,512]{1,0:T(8,128)(2,1)S(1)} fusion(bf16[128,256]{1,0:T(8,128)(2,1)} %param.17), kind=kLoop, calls=%fused_computation.1 | loop fusion | bytes 131072
  1.6 4.1 %collective-permute-start.3 = (bf16[128,512]{1,0:T(8,128)(2,1)S(1)}, bf16[128,512]{1,0:T(8,128)(2,1)S(1)}, u32[]{:S(2)}, u32[]{:S(2)}) collective-permute-start(bf16[128,512]{1,0:T(8,128)(2,1)S(1)} %constant_dynamic-update-slice_fusion.refs_0_), channel_id=1, source_target_pairs={{0,16},{4,20},{8,24},{12,28},{16,0},{20,4},{24,8},{28,12},{1,17},{... | collective-permute-start | bytes 393224 | tf_op jit(solution)/shard_map/ppermute | solution.py:320
  5.7 1.5 %block_states.1 = (bf16[528,128]{1,0:T(8,128)(2,1)S(1)}, bf16[528,128]{1,0:T(8,128)(2,1)S(1)}, bf16[528,128]{1,0:T(8,128)(2,1)S(1)}, bf16[528,128]{1,0:T(8,128)(...) custom-call(f32[128,128]{1,0:T(8,128)S(1)} %get-tuple-element.24.refs_0_, ...), custom_call_target="tpu_custom_call" | custom-call | flops 134217728 | bytes 2711552 | tf_op jit(solution)/shard_map/block_states/pallas_call | solution.py:288
  7.3 1.6 %collective-permute-start = (bf16[528,128]{1,0:T(8,128)(2,1)S(1)}, bf16[528,128]{1,0:T(8,128)(2,1)S(1)}, u32[]{:S(2)}, u32[]{:S(2)}) collective-permute-start(bf16[528,128]{1,0:T(8,128)(2,1)S(1)} %get-tuple-element.32), channel_id=1, source_target_pairs={{0,4},{4,0},{8,12},{12,8},{16,20},{20,16},{24,28},{28,24},{1,5},{5... | collective-permute-start | bytes 405512 | tf_op jit(solution)/shard_map/ppermute | solution.py:314
  8.9 1.6 %collective-permute-start.1 = (bf16[528,128]{1,0:T(8,128)(2,1)S(1)}, bf16[528,128]{1,0:T(8,128)(2,1)S(1)}, u32[]{:S(2)}, u32[]{:S(2)}) collective-permute-start(bf16[528,128]{1,0:T(8,128)(2,1)S(1)} %get-tuple-element.33), channel_id=1, source_target_pairs={{0,8},{4,12},{8,0},{12,4},{16,24},{20,28},{24,16},{28,20},{1,9},{5... | collective-permute-start | bytes 405512 | tf_op jit(solution)/shard_map/ppermute | solution.py:314
  10.4 0.4 collective-permute-start.2
  10.8 2.8 %intra_block.1 = (f32[128,2048]{1,0:T(8,128)S(1)}, bf16[128,2048]{1,0:T(8,128)(2,1)S(1)}, f32[128,2048]{1,0:T(8,128)S(1)}, f32[128,16]{1,0:T(8,128)S(1)}) custom-call(f32[128,128]{1,0:T(8,128)S(1)} %get-tuple-element.24.refs_0_, f32[128,128]{1,0:T(8,128)S(1)} %get-tuple-element.25.refs_1_, f32[16,128]{1,0:T(8,128)S(1)} %copy-done.5, ...), custom_call_target="tpu_custom_call" | custom-call | flops 134217728 | bytes 4874240 | tf_op jit(solution)/shard_map/intra_block/pallas_call | solution.py:288
  13.6 1.6 %collective-permute-start.9 = (bf16[256,512]{1,0:T(8,128)(2,1)S(1)}, bf16[256,512]{1,0:T(8,128)(2,1)S(1)}, u32[]{:S(2)}, u32[]{:S(2)}) collective-permute-start(bf16[256,512]{1,0:T(8,128)(2,1)S(1)} %stack_keys_values.1.refs_2_), channel_id=1, source_target_pairs={{0,4},{4,0},{8,12},{12,8},{16,20},{20,16},{24,28},{28,24},{1,5},{5... | collective-permute-start | bytes 786440 | tf_op jit(solution)/shard_map/ppermute | solution.py:314
  15.2 1.6 %collective-permute-start.10 = (bf16[256,512]{1,0:T(8,128)(2,1)S(1)}, bf16[256,512]{1,0:T(8,128)(2,1)S(1)}, u32[]{:S(2)}, u32[]{:S(2)}) collective-permute-start(bf16[256,512]{1,0:T(8,128)(2,1)S(1)} %stack_keys_values.1.refs_2_), channel_id=1, source_target_pairs={{0,8},{4,12},{8,0},{12,4},{16,24},{20,28},{24,16},{28,20},{1,9},{5... | collective-permute-start | bytes 786440 | tf_op jit(solution)/shard_map/ppermute | solution.py:314
  16.8 2.2 %collective-permute-done.2.refs_3_ = bf16[528,128]{1,0:T(8,128)(2,1)S(1)} collective-permute-done((bf16[528,128]{1,0:T(8,128)(2,1)S(1)}, bf16[528,128]{1,0:T(8,128)(2,1)S(1)}, u32[]{:S(2)}, u32[]{:S(2)}) %collective-permute-start.2) | collective-permute-done | bytes 135200 | tf_op jit(solution)/shard_map/ppermute | solution.py:314
  19.1 0.6 %collective-permute-start.4 = (bf16[528,128]{1,0:T(8,128)(2,1)S(1)}, bf16[528,128]{1,0:T(8,128)(2,1)S(1)}, u32[]{:S(2)}, u32[]{:S(2)}) collective-permute-start(bf16[528,128]{1,0:T(8,128)(2,1)S(1)} %group_state.1), channel_id=1, source_target_pairs={{0,16},{4,20},{8,24},{12,28},{16,0},{20,4},{24,8},{28,12},{1,17},{... | collective-permute-start | bytes 405512 | tf_op jit(solution)/shard_map/ppermute | solution.py:320
  19.7 7.4 %collective-permute-done.4.refs_4_ = bf16[528,128]{1,0:T(8,128)(2,1)S(1)} collective-permute-done((bf16[528,128]{1,0:T(8,128)(2,1)S(1)}, bf16[528,128]{1,0:T(8,128)(2,1)S(1)}, u32[]{:S(2)}, u32[]{:S(2)}) %collective-permute-start.4) | collective-permute-done | bytes 135200 | tf_op jit(solution)/shard_map/ppermute | solution.py:320
  27.3 1.4 %collective-permute-start.5 = (bf16[512,128]{1,0:T(8,128)(2,1)S(1)}, bf16[512,128]{1,0:T(8,128)(2,1)S(1)}, u32[]{:S(2)}, u32[]{:S(2)}) collective-permute-start(bf16[512,128]{1,0:T(8,128)(2,1)S(1)} %get-tuple-element.36), channel_id=1, source_target_pairs={{0,4},{4,0},{8,12},{12,8},{16,20},{20,16},{24,28},{28,24},{1,5},{5... | collective-permute-start | bytes 393224 | tf_op jit(solution)/shard_map/ppermute | solution.py:314
  28.7 2.2 %collective-permute-start.7 = (bf16[512,128]{1,0:T(8,128)(2,1)S(1)}, bf16[512,128]{1,0:T(8,128)(2,1)S(1)}, u32[]{:S(2)}, u32[]{:S(2)}) collective-permute-start(bf16[512,128]{1,0:T(8,128)(2,1)S(1)} %get-tuple-element.38), channel_id=1, source_target_pairs={{0,12},{4,8},{8,4},{12,0},{16,28},{20,24},{24,20},{28,16},{1,13},{... | collective-permute-start | bytes 393224 | tf_op jit(solution)/shard_map/ppermute | solution.py:314
  31.1 1.2 %collective-permute-start.12 = (bf16[128,512]{1,0:T(8,128)(2,1)S(1)}, bf16[128,512]{1,0:T(8,128)(2,1)S(1)}, u32[]{:S(2)}, u32[]{:S(2)}) collective-permute-start(bf16[128,512]{1,0:T(8,128)(2,1)S(1)} %slice.9), channel_id=1, source_target_pairs={{0,4},{4,0},{8,12},{12,8},{16,20},{20,16},{24,28},{28,24},{1,5},{5... | collective-permute-start | bytes 393224 | tf_op jit(solution)/shard_map/ppermute | solution.py:314
  33.0 1.9 %collective-permute-done.5.refs_4_ = bf16[512,128]{1,0:T(8,128)(2,1)S(1)} collective-permute-done((bf16[512,128]{1,0:T(8,128)(2,1)S(1)}, bf16[512,128]{1,0:T(8,128)(2,1)S(1)}, u32[]{:S(2)}, u32[]{:S(2)}) %collective-permute-start.5) | collective-permute-done | bytes 131104 | tf_op jit(solution)/shard_map/ppermute | solution.py:314
  35.0 1.5 %collective-permute-done.7.refs_6_ = bf16[512,128]{1,0:T(8,128)(2,1)S(1)} collective-permute-done((bf16[512,128]{1,0:T(8,128)(2,1)S(1)}, bf16[512,128]{1,0:T(8,128)(2,1)S(1)}, u32[]{:S(2)}, u32[]{:S(2)}) %collective-permute-start.7) | collective-permute-done | bytes 131104 | tf_op jit(solution)/shard_map/ppermute | solution.py:314
  36.4 0.7 %inter_block.1 = (f32[128,2048]{1,0:T(8,128)S(1)}, f32[8,128]{1,0:T(8,128)S(1)}) custom-call(f32[128,16]{1,0:T(8,128)S(1)} %get-tuple-element.28.refs_0_, bf16[128,2048]{1,0:T(8,128)(2,1)S(1)} %get-tuple-element.29.refs_1_, f32[128,2048]{1,0:T(8,128)S(1)} %get-tuple-element.30.refs_4_.refs_2_, bf16[512,128]{1,0:T(8,128)(2,1)S(1)} %get-tuple-element.35.refs_3_, ...), custom_call_target="tpu_custom_call" | custom-call | flops 67108864 | bytes 3158016 | tf_op jit(solution)/shard_map/inter_block/pallas_call | solution.py:288
  37.1 0.7 %collective-permute-done.11 = bf16[128,512]{1,0:T(8,128)(2,1)S(1)} collective-permute-done((bf16[128,512]{1,0:T(8,128)(2,1)S(1)}, bf16[128,512]{1,0:T(8,128)(2,1)S(1)}, u32[]{:S(2)}, u32[]{:S(2)}) %collective-permute-start.11) | collective-permute-done | bytes 131104 | tf_op jit(solution)/shard_map/ppermute | solution.py:314
  37.9 0.3 copy-done.2
  38.2 2.9 %softmax_attention.2 = (bf16[128,2048]{1,0:T(8,128)(2,1)}, f32[8,128]{1,0:T(8,128)S(1)}) custom-call(s32[1]{0:T(128)S(6)} %copy.16.refs_0_, bf16[128,2048]{1,0:T(8,128)(2,1)S(1)} %copy-done.2, bf16[256,512]{1,0:T(8,128)(2,1)S(1)} %stack_keys_values.1.refs_2_, bf16[256,512]{1,0:T(8,128)(2,1)S(1)} %collective-permute-done.9.refs_3_, ...), custom_call_target="tpu_custom_call" | custom-call | flops 536870912 | bytes 2101252 | tf_op jit(solution)/shard_map/softmax_attention/pallas_call | solution.py:288
  41.1 1.9 %collective-permute-start.13 = (f32[8,128]{1,0:T(8,128)S(1)}, f32[8,128]{1,0:T(8,128)S(1)}, u32[]{:S(2)}, u32[]{:S(2)}) collective-permute-start(f32[8,128]{1,0:T(8,128)S(1)} %add.1.refs_2_), channel_id=1, source_target_pairs={{0,2},{1,3},{2,0},{3,1},{4,6},{5,7},{6,4},{7,5},{8,10},{9,11},{10,... | collective-permute-start | bytes 12296 | tf_op jit(solution)/shard_map/ppermute | solution.py:443
  42.9 2.9 %softmax_attention.3 = (bf16[128,2048]{1,0:T(8,128)(2,1)}, f32[8,128]{1,0:T(8,128)S(1)}) custom-call(s32[1]{0:T(128)S(6)} %copy.16.refs_0_, bf16[128,2048]{1,0:T(8,128)(2,1)S(1)} %copy-done.2, bf16[256,512]{1,0:T(8,128)(2,1)S(1)} %stack_keys_values.1.refs_2_, bf16[256,512]{1,0:T(8,128)(2,1)S(1)} %collective-permute-done.9.refs_3_, ...), custom_call_target="tpu_custom_call", output_to_operand_aliasing={{0}: (6, {})} | custom-call | flops 536870912 | bytes 2625540 | tf_op jit(solution)/shard_map/softmax_attention/pallas_call | solution.py:288
  45.8 1.1 %gated_norm.1 = bf16[128,2048]{1,0:T(8,128)(2,1)} custom-call(f32[128,2048]{1,0:T(8,128)S(1)} %get-tuple-element.39.refs_0_, f32[128,2048]{1,0:T(8,128)S(1)} %get-tuple-element.40.refs_1_, f32[8,128]{1,0:T(8,128)S(1)} %add.1.refs_2_, f32[8,128]{1,0:T(8,128)S(1)} %collective-permute-done.13.refs_3_, f32[8,128]{1,0:T(8,128)S(1)} %get-tuple-element.42.refs_2_.refs_4_, ...), custom_call_target="tpu_custom_call" | custom-call | flops 1048576 | bytes 2629632 | tf_op jit(solution)/shard_map/gated_norm/pallas_call | solution.py:288
  (37 shorter events, 0.8 us)
Async XLA Ops:
  0.6 0.9 %copy-start.7 = (bf16[128,256]{1,0:T(8,128)(2,1)S(1)}, bf16[128,256]{1,0:T(8,128)(2,1)}, u32[]{:S(2)}) copy-start(bf16[128,256]{1,0:T(8,128)(2,1)} %param.18) | copy-start | bytes 196612
  1.5 4.2 %copy-start.3 = (bf16[128,2048]{1,0:T(8,128)(2,1)S(1)}, bf16[128,2048]{1,0:T(8,128)(2,1)}, u32[]{:S(2)}) copy-start(bf16[128,2048]{1,0:T(8,128)(2,1)} %refs_2_.2) | copy-start | bytes 1572868
  1.5 4.2 %copy-start.4 = (bf16[128,2048]{1,0:T(8,128)(2,1)S(1)}, bf16[128,2048]{1,0:T(8,128)(2,1)}, u32[]{:S(2)}) copy-start(bf16[128,2048]{1,0:T(8,128)(2,1)} %refs_3_.2) | copy-start | bytes 1572868
  1.6 4.2 %copy-start.5 = (f32[16,128]{1,0:T(8,128)S(1)}, f32[16,128]{1,0:T(8,128)}, u32[]{:S(2)}) copy-start(f32[16,128]{1,0:T(8,128)} %refs_2_.3) | copy-start | bytes 24580
  1.6 12.0 %collective-permute-start.3 = (bf16[128,512]{1,0:T(8,128)(2,1)S(1)}, bf16[128,512]{1,0:T(8,128)(2,1)S(1)}, u32[]{:S(2)}, u32[]{:S(2)}) collective-permute-start(bf16[128,512]{1,0:T(8,128)(2,1)S(1)} %constant_dynamic-update-slice_fusion.refs_0_), channel_id=1, source_target_pairs={{0,16},{4,20},{8,24},{12,28},{16,0},{20,4},{24,8},{28,12},{1,17},{... | collective-permute-start | bytes 393224 | tf_op jit(solution)/shard_map/ppermute | solution.py:320
  5.7 5.1 %copy-start = (bf16[128,2048]{1,0:T(8,128)(2,1)S(1)}, bf16[128,2048]{1,0:T(8,128)(2,1)}, u32[]{:S(2)}) copy-start(bf16[128,2048]{1,0:T(8,128)(2,1)} %refs_3_.3) | copy-start | bytes 1572868
  5.7 5.1 %copy-start.1 = (bf16[128,2048]{1,0:T(8,128)(2,1)S(1)}, bf16[128,2048]{1,0:T(8,128)(2,1)}, u32[]{:S(2)}) copy-start(bf16[128,2048]{1,0:T(8,128)(2,1)} %refs_6_.1) | copy-start | bytes 1572868
  7.3 3.6 %copy-start.6 = (f32[2048]{0:T(1024)S(1)}, f32[2048]{0:T(1024)}, u32[]{:S(2)}) copy-start(f32[2048]{0:T(1024)} %param.15) | copy-start | bytes 24580
  7.3 9.5 %collective-permute-start = (bf16[528,128]{1,0:T(8,128)(2,1)S(1)}, bf16[528,128]{1,0:T(8,128)(2,1)S(1)}, u32[]{:S(2)}, u32[]{:S(2)}) collective-permute-start(bf16[528,128]{1,0:T(8,128)(2,1)S(1)} %get-tuple-element.32), channel_id=1, source_target_pairs={{0,4},{4,0},{8,12},{12,8},{16,20},{20,16},{24,28},{28,24},{1,5},{5... | collective-permute-start | bytes 405512 | tf_op jit(solution)/shard_map/ppermute | solution.py:314
  8.9 7.9 %collective-permute-start.1 = (bf16[528,128]{1,0:T(8,128)(2,1)S(1)}, bf16[528,128]{1,0:T(8,128)(2,1)S(1)}, u32[]{:S(2)}, u32[]{:S(2)}) collective-permute-start(bf16[528,128]{1,0:T(8,128)(2,1)S(1)} %get-tuple-element.33), channel_id=1, source_target_pairs={{0,8},{4,12},{8,0},{12,4},{16,24},{20,28},{24,16},{28,20},{1,9},{5... | collective-permute-start | bytes 405512 | tf_op jit(solution)/shard_map/ppermute | solution.py:314
  10.4 8.5 %collective-permute-start.2 = (bf16[528,128]{1,0:T(8,128)(2,1)S(1)}, bf16[528,128]{1,0:T(8,128)(2,1)S(1)}, u32[]{:S(2)}, u32[]{:S(2)}) collective-permute-start(bf16[528,128]{1,0:T(8,128)(2,1)S(1)} %get-tuple-element.34), channel_id=1, source_target_pairs={{0,12},{4,8},{8,4},{12,0},{16,28},{20,24},{24,20},{28,16},{1,13},{... | collective-permute-start | bytes 405512 | tf_op jit(solution)/shard_map/ppermute | solution.py:314
  13.6 17.3 %collective-permute-start.9 = (bf16[256,512]{1,0:T(8,128)(2,1)S(1)}, bf16[256,512]{1,0:T(8,128)(2,1)S(1)}, u32[]{:S(2)}, u32[]{:S(2)}) collective-permute-start(bf16[256,512]{1,0:T(8,128)(2,1)S(1)} %stack_keys_values.1.refs_2_), channel_id=1, source_target_pairs={{0,4},{4,0},{8,12},{12,8},{16,20},{20,16},{24,28},{28,24},{1,5},{5... | collective-permute-start | bytes 786440 | tf_op jit(solution)/shard_map/ppermute | solution.py:314
  15.2 15.9 %collective-permute-start.10 = (bf16[256,512]{1,0:T(8,128)(2,1)S(1)}, bf16[256,512]{1,0:T(8,128)(2,1)S(1)}, u32[]{:S(2)}, u32[]{:S(2)}) collective-permute-start(bf16[256,512]{1,0:T(8,128)(2,1)S(1)} %stack_keys_values.1.refs_2_), channel_id=1, source_target_pairs={{0,8},{4,12},{8,0},{12,4},{16,24},{20,28},{24,16},{28,20},{1,9},{5... | collective-permute-start | bytes 786440 | tf_op jit(solution)/shard_map/ppermute | solution.py:314
  19.1 8.0 %collective-permute-start.4 = (bf16[528,128]{1,0:T(8,128)(2,1)S(1)}, bf16[528,128]{1,0:T(8,128)(2,1)S(1)}, u32[]{:S(2)}, u32[]{:S(2)}) collective-permute-start(bf16[528,128]{1,0:T(8,128)(2,1)S(1)} %group_state.1), channel_id=1, source_target_pairs={{0,16},{4,20},{8,24},{12,28},{16,0},{20,4},{24,8},{28,12},{1,17},{... | collective-permute-start | bytes 405512 | tf_op jit(solution)/shard_map/ppermute | solution.py:320
  27.3 7.6 %collective-permute-start.5 = (bf16[512,128]{1,0:T(8,128)(2,1)S(1)}, bf16[512,128]{1,0:T(8,128)(2,1)S(1)}, u32[]{:S(2)}, u32[]{:S(2)}) collective-permute-start(bf16[512,128]{1,0:T(8,128)(2,1)S(1)} %get-tuple-element.36), channel_id=1, source_target_pairs={{0,4},{4,0},{8,12},{12,8},{16,20},{20,16},{24,28},{28,24},{1,5},{5... | collective-permute-start | bytes 393224 | tf_op jit(solution)/shard_map/ppermute | solution.py:314
  28.7 6.3 %collective-permute-start.6 = (bf16[512,128]{1,0:T(8,128)(2,1)S(1)}, bf16[512,128]{1,0:T(8,128)(2,1)S(1)}, u32[]{:S(2)}, u32[]{:S(2)}) collective-permute-start(bf16[512,128]{1,0:T(8,128)(2,1)S(1)} %get-tuple-element.37), channel_id=1, source_target_pairs={{0,8},{4,12},{8,0},{12,4},{16,24},{20,28},{24,16},{28,20},{1,9},{5... | collective-permute-start | bytes 393224 | tf_op jit(solution)/shard_map/ppermute | solution.py:314
  28.7 7.8 %collective-permute-start.7 = (bf16[512,128]{1,0:T(8,128)(2,1)S(1)}, bf16[512,128]{1,0:T(8,128)(2,1)S(1)}, u32[]{:S(2)}, u32[]{:S(2)}) collective-permute-start(bf16[512,128]{1,0:T(8,128)(2,1)S(1)} %get-tuple-element.38), channel_id=1, source_target_pairs={{0,12},{4,8},{8,4},{12,0},{16,28},{20,24},{24,20},{28,16},{1,13},{... | collective-permute-start | bytes 393224 | tf_op jit(solution)/shard_map/ppermute | solution.py:314
  30.9 6.9 %collective-permute-start.11 = (bf16[128,512]{1,0:T(8,128)(2,1)S(1)}, bf16[128,512]{1,0:T(8,128)(2,1)S(1)}, u32[]{:S(2)}, u32[]{:S(2)}) collective-permute-start(bf16[128,512]{1,0:T(8,128)(2,1)S(1)} %slice.8), channel_id=1, source_target_pairs={{0,8},{4,12},{8,0},{12,4},{16,24},{20,28},{24,16},{28,20},{1,9},{5... | collective-permute-start | bytes 393224 | tf_op jit(solution)/shard_map/ppermute | solution.py:314
  31.1 6.7 %collective-permute-start.12 = (bf16[128,512]{1,0:T(8,128)(2,1)S(1)}, bf16[128,512]{1,0:T(8,128)(2,1)S(1)}, u32[]{:S(2)}, u32[]{:S(2)}) collective-permute-start(bf16[128,512]{1,0:T(8,128)(2,1)S(1)} %slice.9), channel_id=1, source_target_pairs={{0,4},{4,0},{8,12},{12,8},{16,20},{20,16},{24,28},{28,24},{1,5},{5... | collective-permute-start | bytes 393224 | tf_op jit(solution)/shard_map/ppermute | solution.py:314
  37.1 1.1 %copy-start.2 = (bf16[128,2048]{1,0:T(8,128)(2,1)S(1)}, bf16[128,2048]{1,0:T(8,128)(2,1)}, u32[]{:S(2)}) copy-start(bf16[128,2048]{1,0:T(8,128)(2,1)} %refs_1_.5) | copy-start | bytes 1572868
  37.1 4.0 %collective-permute-start.8 = (f32[8,128]{1,0:T(8,128)S(1)}, f32[8,128]{1,0:T(8,128)S(1)}, u32[]{:S(2)}, u32[]{:S(2)}) collective-permute-start(f32[8,128]{1,0:T(8,128)S(1)} %get-tuple-element.41.refs_0_), channel_id=1, source_target_pairs={{0,1},{1,0},{2,3},{3,2},{4,5},{5,4},{6,7},{7,6},{8,9},{9,8},{10,11... | collective-permute-start | bytes 12296 | tf_op jit(solution)/shard_map/ppermute | solution.py:443
  41.1 4.8 %collective-permute-start.13 = (f32[8,128]{1,0:T(8,128)S(1)}, f32[8,128]{1,0:T(8,128)S(1)}, u32[]{:S(2)}, u32[]{:S(2)}) collective-permute-start(f32[8,128]{1,0:T(8,128)S(1)} %add.1.refs_2_), channel_id=1, source_target_pairs={{0,2},{1,3},{2,0},{3,1},{4,6},{5,7},{6,4},{7,5},{8,10},{9,11},{10,... | collective-permute-start | bytes 12296 | tf_op jit(solution)/shard_map/ppermute | solution.py:443

commit v5 on v4

--- a/solution.py
+++ b/solution.py
@@ -81,6 +81,12 @@
         outs[s][per * HD :, :] = totals[dyn(dest, 16), :].astype(BF16)
 
 
+def beside_kernel(keys, values, out):
+    width = keys.shape[1]
+    out[:, :width] = keys[...]
+    out[:, width:] = values[...]
+
+
 def stack_kernel(*refs):
     tokens = refs[0].shape[0]
     for i, part in enumerate(refs[:-1]):
@@ -195,83 +201,81 @@
         out_ref[:, cols] = (lin_ref[:, cols] * inv * gain_ref[:, cols]).astype(BF16)
 
 
-def softmax_kernel(count, group, block, g, kv_heads, order_ref, q_ref, *rest):
-    chunks, (out_ref, done_ref, kv, bias_ref) = rest[:group], rest[-4:]
-    done_ref[...] = jnp.zeros_like(done_ref)
-    tokens = q_ref.shape[0]
-    heads = q_ref.shape[1] // HD
+def softmax_bias(group, sides, order_ref, bias):
+    tokens, span = bias.shape[0], bias.shape[1] // 2
+    groups = span // tokens
     me = lax.axis_index("ctx")
     rank, mine = lax.rem(me, group), lax.div(me, group)
-    groups = count // group
-    for i in range(count):
-        s, d = divmod(i, groups)
-        place = lax.rem(mine + groups - d, groups) * group + (rank ^ s)
-        rows = slice(d * tokens, (d + 1) * tokens)
-        kv[dyn(place, tokens), :HD] = chunks[s][rows, head_cols(g)]
-        kv[dyn(place, tokens), HD:] = chunks[s][rows, head_cols(kv_heads + g)]
-    first = order_ref[0] * tokens
-    scale = math.log2(math.e) / math.sqrt(HD)
-    blocks = count * tokens // block
-    pack = 2 if heads % 2 == 0 else 1
-
-    def allowed(start):
-        qpos = first + lax.broadcasted_iota(jnp.int32, (tokens, block), 0)
-        kpos = start + lax.broadcasted_iota(jnp.int32, (tokens, block), 1)
-        return jnp.where(kpos <= qpos, 0.0, -1e30)
-
-    def query(h):
-        return jnp.concatenate([q_ref[:, head_cols(h + i)] for i in range(pack)], axis=0)
-
-    def store(h, value):
-        for i in range(pack):
-            out_ref[:, head_cols(h + i)] = value[i * tokens : (i + 1) * tokens]
-
-    def scores(h, start):
-        keys = kv[pl.ds(start, block), :HD]
-        raw = lax.dot_general(query(h), keys, NT, preferred_element_type=F32)
-        return raw.reshape(pack, tokens, block) + bias_ref[...][None]
-
-    def weigh(start, probs):
-        values = kv[pl.ds(start, block), HD:]
-        flat = probs.astype(BF16).reshape(pack * tokens, block)
-        return jnp.dot(flat, values, preferred_element_type=F32)
-
-    if blocks == 1:
-        bias_ref[...] = allowed(0)
-        for h in range(0, heads, pack):
-            raw = scores(h, 0)
+    qpos = order_ref[0] * tokens + lax.broadcasted_iota(jnp.int32, (tokens, tokens), 0)
+    kpos = lax.broadcasted_iota(jnp.int32, (tokens, tokens), 1)
+    for i, s in enumerate(sides):
+        for d in range(groups):
+            place = lax.rem(mine + groups - d, groups) * group + (rank ^ s)
+            at = i * span + d * tokens
+            bias[:, at : at + tokens] = jnp.where(place * tokens + kpos <= qpos, 0.0, -1e30)
+
+
+def softmax_values(held, g, kv_heads, values):
+    span = held[0].shape[0]
+    values[:, HD:] = jnp.ones((2 * span, HD), BF16)
+    for i, ref in enumerate(held):
+        values[i * span : (i + 1) * span, :HD] = ref[:, head_cols(kv_heads + g)]
+
+
+def softmax_scores(query, held, g, bias):
+    raw = [
+        lax.dot_general(query, ref[:, head_cols(g)], NT, preferred_element_type=F32) for ref in held
+    ]
+    raw = jnp.concatenate(raw, axis=1)
+    raw = raw.reshape(-1, *bias.shape) + bias[...][None]
+    return raw.reshape(-1, bias.shape[1])
+
+
+def stacked(ref, columns):
+    return jnp.concatenate([ref[:, cols] for cols in columns], axis=0)
+
+
+SCORE = math.log2(math.e) / math.sqrt(HD)
+
+
+def softmax_first_kernel(group, sides, kv_heads, pack, order_ref, q_ref, a_ref, b_ref, *rest):
+    acc_ref, tops, (values, bias) = rest[0], rest[1:-2], rest[-2:]
+    tokens = q_ref.shape[0]
+    share = q_ref.shape[1] // HD // kv_heads
+    softmax_bias(group, sides, order_ref, bias)
+    for g in range(kv_heads):
+        softmax_values((a_ref, b_ref), g, kv_heads, values)
+        for j in range(0, share, pack):
+            heads = range(g * share + j, g * share + j + pack)
+            raw = softmax_scores(stacked(q_ref, map(head_cols, heads)), (a_ref, b_ref), g, bias)
             top = jnp.max(raw, axis=-1, keepdims=True)
-            probs = jnp.exp2((raw - top) * scale)
-            den = jnp.sum(probs, axis=-1, keepdims=True).reshape(pack * tokens, 1)
-            store(h, (weigh(0, probs) / den).astype(BF16))
-        return
-
-    reach = lax.div(first + tokens - 1, block) + 1
-    for h in range(0, heads, pack):
-
-        def step(i, carry):
-            top, den, acc = carry
-            start = pl.multiple_of(i * block, block)
-            bias_ref[...] = allowed(start)
-            raw = scores(h, start)
-            new = jnp.maximum(top, jnp.max(raw, axis=-1, keepdims=True))
-            alpha = jnp.exp2((top - new) * scale)
-            probs = jnp.exp2((raw - new) * scale)
-            den = den * alpha + jnp.sum(probs, axis=-1, keepdims=True)
-            acc = acc * alpha.reshape(pack * tokens, 1) + weigh(start, probs)
-            return new, den, acc
-
-        top, den, acc = lax.fori_loop(
-            0,
-            reach,
-            step,
-            (
-                jnp.full((pack, tokens, 1), -1e30, F32),
-                jnp.zeros((pack, tokens, 1), F32),
-                jnp.zeros((pack * tokens, HD), F32),
-            ),
-        )
-        store(h, (acc / den.reshape(pack * tokens, 1)).astype(BF16))
+            probs = jnp.exp2((raw - top) * SCORE).astype(BF16)
+            acc = jnp.dot(probs, values[...], preferred_element_type=F32)
+            for i, h in enumerate(heads):
+                rows = slice(i * tokens, (i + 1) * tokens)
+                acc_ref[:, 2 * h * HD : 2 * (h + 1) * HD] = acc[rows]
+                tops[g][:, j + i : j + i + 1] = top[rows]
+
+
+def softmax_last_kernel(group, sides, g, kv_heads, pack, order_ref, q_ref, a_ref, b_ref, *rest):
+    acc_ref, top_ref = rest[:2]
+    out_ref, done_ref, values, bias = rest[-4:]
+    tokens = q_ref.shape[0]
+    done_ref[...] = jnp.zeros_like(done_ref)
+    softmax_bias(group, sides, order_ref, bias)
+    softmax_values((a_ref, b_ref), g, kv_heads, values)
+    for j in range(0, q_ref.shape[1] // HD, pack):
+        heads = range(j, j + pack)
+        raw = softmax_scores(stacked(q_ref, map(head_cols, heads)), (a_ref, b_ref), g, bias)
+        old = stacked(top_ref, [slice(h, h + 1) for h in heads])
+        top = jnp.maximum(old, jnp.max(raw, axis=-1, keepdims=True))
+        probs = jnp.exp2((raw - top) * SCORE).astype(BF16)
+        acc = jnp.dot(probs, values[...], preferred_element_type=F32)
+        held = stacked(acc_ref, [slice(2 * h * HD, 2 * (h + 1) * HD) for h in heads])
+        acc += held * jnp.exp2((old - top) * SCORE)
+        out = (acc[:, :HD] / acc[:, HD:]).astype(BF16)
+        for i, h in enumerate(heads):
+            out_ref[:, head_cols(h)] = out[i * tokens : (i + 1) * tokens]
 
 
 def call(
@@ -303,7 +307,7 @@
     kv_width = keys.shape[1]
     kv_heads = kv_width // HD
     n, nh = lax.axis_size("ctx"), lax.axis_size("head")
-    group = 4 if n % 4 == 0 else 2 if n % 2 == 0 else 1
+    group = 4
     groups = n // group
     per = heads // group
     rows = per * HD + 16
@@ -322,7 +326,13 @@
     tri, bias = call(
         triangle_kernel, "triangle", [shape((tokens, tokens), F32)] * 2, (), flops=1 << 31
     )
-    kv = jnp.concatenate([keys, values], axis=1)
+    (kv,) = call(
+        beside_kernel,
+        "keys_beside_values",
+        [shape((tokens, 2 * kv_width), BF16)],
+        (keys, values),
+        after=(tri,),
+    )
     far = [ahead(kv, d) for d in range(1, groups)]
 
     *pays, ka, va = call(
@@ -347,6 +357,7 @@
         (tri, bias, log_decay, q_lin, ka, va, gate, norm_gain.reshape(1, width)),
         flops=4 * cube,
         exps=4 * tokens * width,
+        after=far,
     )
 
     slots = pltpu.VMEM((group, rows, HD), BF16)
@@ -359,7 +370,7 @@
             pays,
             [slots],
             flops=2 * per * HD * HD * group,
-            after=(intra, *far),
+            after=(intra,),
         )
         before = ahead(total, 1)
         shift = 1
@@ -383,7 +394,7 @@
         [shape((per * HD, HD), BF16)] * group,
         (*pays, *carry),
         [slots, pltpu.VMEM((group, per * HD, HD), BF16)],
-        flops=2 * per * HD * HD * group,
+        flops=1 << 33,
     )
     prefixes = swap_all(prefixes)
 
@@ -392,38 +403,54 @@
         "stack_keys_values",
         [shape((groups * tokens, kv.shape[1]), BF16)],
         (kv, *far),
-        after=(intra,),
-        limit=16 + 4 * n * tokens * kv.shape[1] // MIB,
-    )
-    chunks = [own] + [swap(own, s) for s in (1, 2) if s < group]
-    if group == 4:
-        half = own.shape[0] // 2
-        chunks.append(jnp.concatenate([swap(chunks[1][:half], 2), swap(chunks[2][half:], 1)]))
-    span = n * tokens
-    block = min(span, 1024)
+        after=(total,) if groups > 1 else (intra,),
+        flops=1 << 32,
+    )
+    near, side = swap(own, 1), swap(own, 2)
+    half = own.shape[0] // 2
+    across = jnp.concatenate([swap(near[:half], 2), swap(side[half:], 1)])
     share = width // kv_heads
-
-    def attend(g, *done):
-        columns = pl.BlockSpec((tokens, share), functools.partial(lambda g, i: (0, g), g))
-        held = [pl.BlockSpec(x.shape, lambda i: (0, 0)) for x in chunks]
-        return call(
-            functools.partial(softmax_kernel, n, group, block, g, kv_heads),
-            "softmax_attention",
+    pack = 2 if share // HD % 2 == 0 else 1
+    span = 2 * own.shape[0]
+    scratch = [pltpu.VMEM((span, 2 * HD), BF16), pltpu.VMEM((tokens, span), F32)]
+    room = 24 + 16 * span * tokens * 4 // MIB
+    smem = pl.BlockSpec(memory_space=pltpu.SMEM)
+    acc, *tops = call(
+        functools.partial(softmax_first_kernel, group, (0, 1), kv_heads, pack),
+        "softmax_first",
+        [shape((tokens, 2 * width), F32)] + [shape((tokens, share // HD), F32)] * kv_heads,
+        (order, queries, own, near),
+        scratch,
+        flops=4 * tokens * width * span,
+        exps=tokens * span * width // HD,
+        limit=room,
+        specs=[smem] + [VMEM] * 3,
+    )
+    attended, marks = (), []
+    for g in range(kv_heads):
+
+        def columns(size, g=g):
+            return pl.BlockSpec((tokens, size), lambda i: (0, g))
+
+        def whole(x):
+            return pl.BlockSpec(x.shape, lambda i: (0, 0))
+
+        *attended, mark = call(
+            functools.partial(softmax_last_kernel, group, (2, 3), g, kv_heads, pack),
+            "softmax_last",
             [shape((tokens, width), BF16), shape((8, HD), F32)],
-            (order, queries, *chunks, *done),
-            [pltpu.VMEM((span, 2 * HD), BF16), pltpu.VMEM((tokens, block), F32)],
+            (order, queries, side, across, acc, tops[g], *attended),
+            scratch,
             flops=4 * tokens * share * span,
             exps=tokens * span * share // HD,
-            limit=16 + 6 * span * 2 * kv_width // MIB,
-            specs=[pl.BlockSpec(memory_space=pltpu.SMEM), columns, *held, *[HBM for _ in done]],
-            out_specs=[columns, pl.BlockSpec((8, HD), lambda i: (0, 0))],
+            limit=room,
+            specs=[smem, columns(share), whole(side), whole(across)]
+            + [columns(2 * share), whole(tops[g])]
+            + [HBM for _ in attended],
+            out_specs=[columns(share), pl.BlockSpec((8, HD), lambda i: (0, 0))],
             grid=(1,),
-            input_output_aliases={2 + group: 0} if done else {},
+            input_output_aliases={6: 0} if attended else {},
         )
-
-    attended, marks = (), []
-    for g in range(kv_heads):
-        *attended, mark = attend(g, *attended)
         marks.append(mark)
 
     lin, squares = call(
@@ -433,6 +460,7 @@
         (decay, qa, intra, *prefixes),
         [pltpu.VMEM((heads * HD, HD), BF16)],
         flops=2 * cube,
+        after=tops[:1],
     )
     if nh & (nh - 1) == 0:
         parts, shift = [squares], 1

time: 47.1 us -> 47 us (level)
  waiting for transfers between devices: 13.7 us -> 11.3 us
  starting transfers between devices: 18.3 us -> 20.6 us
    ppermute x2, waiting for transfers between devices: 7.38 us -> 4.18 us  [ahead(): return lax.ppermute(x, 'ctx', [(c, (c + d * group) % n) for c in range(n)])]
    ppermute x10, starting transfers between devices: 11.7 us -> 13.8 us  [swap(): return lax.ppermute(x, 'ctx', [(c, c ^ s) for c in range(n)])]
    ppermute x10, waiting for transfers between devices: 6.33 us -> 7.15 us  [swap(): return lax.ppermute(x, 'ctx', [(c, c ^ s) for c in range(n)])]
    pallas_call x11 -> x13, Pallas kernels: 12.2 us -> 12.6 us  [call(): pl.pallas_call(run, name=name, out_shape=list(outs), in_specs=specs, scra...]
    unnamed x18 -> x19, local copies, waits for them, and re-layouts: 1.23 us -> 0.82 us
  transfers between devices with their start and end apart: 14 -> 14, of which waited for: 6 -> 7; matrix products, arithmetic and copies ran while one was open for 0% -> 0% of each run, Pallas kernels for 24% -> 24%
where the time goes in v5:
time: 47 us; the launch traced here: 46.8 us
  starting transfers between devices  20.6 us (44%)
  Pallas kernels  12.6 us (27%)
  waiting for transfers between devices  11.3 us (24%)
  between operations  1.47 us (3%)
  local copies, waits for them, and re-layouts  0.85 us (2%)
    ppermute x10, starting transfers between devices, swap(): return lax.ppermute(x, 'ctx', [(c, c ^ s) for c in range(n)])  13.8 us
    pallas_call x13, Pallas kernels, call(): pl.pallas_call(run, name=name, out_shape=list(outs), in_specs=specs, scra...  12.6 us
    ppermute x10, waiting for transfers between devices, swap(): return lax.ppermute(x, 'ctx', [(c, c ^ s) for c in range(n)])  7.15 us
    ppermute x2, starting transfers between devices, ahead(): return lax.ppermute(x, 'ctx', [(c, (c + d * group) % n) for c in range(n)])  4.96 us
    ppermute x2, waiting for transfers between devices, ahead(): return lax.ppermute(x, 'ctx', [(c, (c + d * group) % n) for c in range(n)])  4.18 us
    ppermute x2, starting transfers between devices, body(): lax.ppermute(held, 'head', [(i, i ^ shift) for i in range(nh)])  1.83 us
  transfers between devices with their start and end apart: 14, of which 7 were waited for; matrix products, arithmetic and copies ran while one was open for 0% of the time, Pallas kernels for 24%

profile of v5, /device:TPU:0, one launch (start us, length us, event | category | flops | bytes accessed | tf_op | source)
XLA Modules:
  0.0 46.8 jit_solution(3641739682871937209)
XLA Ops:
  0.7 0.7 %copy-done.6 = bf16[128,256]{1,0:T(8,128)(2,1)S(1)} copy-done((bf16[128,256]{1,0:T(8,128)(2,1)S(1)}, bf16[128,256]{1,0:T(8,128)(2,1)}, u32[]{:S(2)}) %copy-start.6) | copy-done | bytes 65560
  1.5 4.1 %collective-permute-start = (bf16[128,512]{1,0:T(8,128)(2,1)S(1)}, bf16[128,512]{1,0:T(8,128)(2,1)S(1)}, u32[]{:S(2)}, u32[]{:S(2)}) collective-permute-start(bf16[128,512]{1,0:T(8,128)(2,1)S(1)} %keys_beside_values.1.refs_0_), channel_id=1, source_target_pairs={{0,16},{4,20},{8,24},{12,28},{16,0},{20,4},{24,8},{28,12},{1,17},{... | collective-permute-start | bytes 393224 | tf_op jit(solution)/shard_map/ppermute | solution.py:324
  5.6 1.5 %block_states.1 = (bf16[528,128]{1,0:T(8,128)(2,1)S(1)}, bf16[528,128]{1,0:T(8,128)(2,1)S(1)}, bf16[528,128]{1,0:T(8,128)(2,1)S(1)}, bf16[528,128]{1,0:T(8,128)(...) custom-call(f32[128,128]{1,0:T(8,128)S(1)} %get-tuple-element.27.refs_0_.refs_2_, ...), custom_call_target="tpu_custom_call" | custom-call | flops 134217728 | bytes 2711552 | tf_op jit(solution)/shard_map/block_states/pallas_call | solution.py:292
  7.2 1.6 %collective-permute-start.1 = (bf16[528,128]{1,0:T(8,128)(2,1)S(1)}, bf16[528,128]{1,0:T(8,128)(2,1)S(1)}, u32[]{:S(2)}, u32[]{:S(2)}) collective-permute-start(bf16[528,128]{1,0:T(8,128)(2,1)S(1)} %get-tuple-element.35), channel_id=1, source_target_pairs={{0,4},{4,0},{8,12},{12,8},{16,20},{20,16},{24,28},{28,24},{1,5},{5... | collective-permute-start | bytes 405512 | tf_op jit(solution)/shard_map/ppermute | solution.py:318
  8.7 1.6 %collective-permute-start.2 = (bf16[528,128]{1,0:T(8,128)(2,1)S(1)}, bf16[528,128]{1,0:T(8,128)(2,1)S(1)}, u32[]{:S(2)}, u32[]{:S(2)}) collective-permute-start(bf16[528,128]{1,0:T(8,128)(2,1)S(1)} %get-tuple-element.36), channel_id=1, source_target_pairs={{0,8},{4,12},{8,0},{12,4},{16,24},{20,28},{24,16},{28,20},{1,9},{5... | collective-permute-start | bytes 405512 | tf_op jit(solution)/shard_map/ppermute | solution.py:318
  10.7 1.3 %collective-permute-done.refs_8_.refs_1_ = bf16[128,512]{1,0:T(8,128)(2,1)S(1)} collective-permute-done((bf16[128,512]{1,0:T(8,128)(2,1)S(1)}, bf16[128,512]{1,0:T(8,128)(2,1)S(1)}, u32[]{:S(2)}, u32[]{:S(2)}) %collective-permute-start) | collective-permute-done | bytes 131104 | tf_op jit(solution)/shard_map/ppermute | solution.py:324
  12.0 2.8 %intra_block.1 = (f32[128,2048]{1,0:T(8,128)S(1)}, bf16[128,2048]{1,0:T(8,128)(2,1)S(1)}, f32[128,2048]{1,0:T(8,128)S(1)}, f32[128,16]{1,0:T(8,128)S(1)}) custom-call(f32[128,128]{1,0:T(8,128)S(1)} %get-tuple-element.27.refs_0_.refs_2_, f32[128,128]{1,0:T(8,128)S(1)} %get-tuple-element.28.refs_1_, f32[16,128]{1,0:T(8,128)S(1)} %copy-done.7, ...), custom_call_target="tpu_custom_call" | custom-call | flops 134217728 | bytes 4874240 | tf_op jit(solution)/shard_map/intra_block/pallas_call | solution.py:292
  15.3 2.8 %collective-permute-done.3.refs_3_ = bf16[528,128]{1,0:T(8,128)(2,1)S(1)} collective-permute-done((bf16[528,128]{1,0:T(8,128)(2,1)S(1)}, bf16[528,128]{1,0:T(8,128)(2,1)S(1)}, u32[]{:S(2)}, u32[]{:S(2)}) %collective-permute-start.3) | collective-permute-done | bytes 135200 | tf_op jit(solution)/shard_map/ppermute | solution.py:318
  18.2 0.9 %collective-permute-start.4 = (bf16[528,128]{1,0:T(8,128)(2,1)S(1)}, bf16[528,128]{1,0:T(8,128)(2,1)S(1)}, u32[]{:S(2)}, u32[]{:S(2)}) collective-permute-start(bf16[528,128]{1,0:T(8,128)(2,1)S(1)} %group_state.1.refs_2_), channel_id=1, source_target_pairs={{0,16},{4,20},{8,24},{12,28},{16,0},{20,4},{24,8},{28,12},{1,17},{... | collective-permute-start | bytes 405512 | tf_op jit(solution)/shard_map/ppermute | solution.py:324
  19.1 2.5 %collective-permute-start.10 = (bf16[256,512]{1,0:T(8,128)(2,1)S(1)}, bf16[256,512]{1,0:T(8,128)(2,1)S(1)}, u32[]{:S(2)}, u32[]{:S(2)}) collective-permute-start(bf16[256,512]{1,0:T(8,128)(2,1)S(1)} %stack_keys_values.1.refs_2_), channel_id=1, source_target_pairs={{0,8},{4,12},{8,0},{12,4},{16,24},{20,28},{24,16},{28,20},{1,9},{5... | collective-permute-start | bytes 786440 | tf_op jit(solution)/shard_map/ppermute | solution.py:318
  21.6 1.5 %collective-permute-start.8 = (bf16[256,512]{1,0:T(8,128)(2,1)S(1)}, bf16[256,512]{1,0:T(8,128)(2,1)S(1)}, u32[]{:S(2)}, u32[]{:S(2)}) collective-permute-start(bf16[256,512]{1,0:T(8,128)(2,1)S(1)} %stack_keys_values.1.refs_2_), channel_id=1, source_target_pairs={{0,4},{4,0},{8,12},{12,8},{16,20},{20,16},{24,28},{28,24},{1,5},{5... | collective-permute-start | bytes 786440 | tf_op jit(solution)/shard_map/ppermute | solution.py:318
  23.1 2.9 %collective-permute-done.4.refs_4_ = bf16[528,128]{1,0:T(8,128)(2,1)S(1)} collective-permute-done((bf16[528,128]{1,0:T(8,128)(2,1)S(1)}, bf16[528,128]{1,0:T(8,128)(2,1)S(1)}, u32[]{:S(2)}, u32[]{:S(2)}) %collective-permute-start.4) | collective-permute-done | bytes 135200 | tf_op jit(solution)/shard_map/ppermute | solution.py:324
  26.2 2.6 %collective-permute-start.5 = (bf16[512,128]{1,0:T(8,128)(2,1)S(1)}, bf16[512,128]{1,0:T(8,128)(2,1)S(1)}, u32[]{:S(2)}, u32[]{:S(2)}) collective-permute-start(bf16[512,128]{1,0:T(8,128)(2,1)S(1)} %get-tuple-element.39), channel_id=1, source_target_pairs={{0,4},{4,0},{8,12},{12,8},{16,20},{20,16},{24,28},{28,24},{1,5},{5... | collective-permute-start | bytes 393224 | tf_op jit(solution)/shard_map/ppermute | solution.py:318
  28.7 1.5 %collective-permute-start.7 = (bf16[512,128]{1,0:T(8,128)(2,1)S(1)}, bf16[512,128]{1,0:T(8,128)(2,1)S(1)}, u32[]{:S(2)}, u32[]{:S(2)}) collective-permute-start(bf16[512,128]{1,0:T(8,128)(2,1)S(1)} %get-tuple-element.41), channel_id=1, source_target_pairs={{0,12},{4,8},{8,4},{12,0},{16,28},{20,24},{24,20},{28,16},{1,13},{... | collective-permute-start | bytes 393224 | tf_op jit(solution)/shard_map/ppermute | solution.py:318
  30.3 0.6 %collective-permute-start.11 = (bf16[128,512]{1,0:T(8,128)(2,1)S(1)}, bf16[128,512]{1,0:T(8,128)(2,1)S(1)}, u32[]{:S(2)}, u32[]{:S(2)}) collective-permute-start(bf16[128,512]{1,0:T(8,128)(2,1)S(1)} %slice.8), channel_id=1, source_target_pairs={{0,8},{4,12},{8,0},{12,4},{16,24},{20,28},{24,16},{28,20},{1,9},{5... | collective-permute-start | bytes 393224 | tf_op jit(solution)/shard_map/ppermute | solution.py:318
  31.5 1.5 %collective-permute-start.12 = (bf16[128,512]{1,0:T(8,128)(2,1)S(1)}, bf16[128,512]{1,0:T(8,128)(2,1)S(1)}, u32[]{:S(2)}, u32[]{:S(2)}) collective-permute-start(bf16[128,512]{1,0:T(8,128)(2,1)S(1)} %slice.9), channel_id=1, source_target_pairs={{0,4},{4,0},{8,12},{12,8},{16,20},{20,16},{24,28},{28,24},{1,5},{5... | collective-permute-start | bytes 393224 | tf_op jit(solution)/shard_map/ppermute | solution.py:318
  33.1 1.6 %softmax_first.1 = (f32[128,4096]{1,0:T(8,128)S(1)}, f32[128,8]{1,0:T(8,128)S(1)}, f32[128,8]{1,0:T(8,128)S(1)}) custom-call(s32[1]{0:T(128)S(6)} %copy.15.refs_0_, bf16[128,2048]{1,0:T(8,128)(2,1)S(1)} %copy-done, bf16[256,512]{1,0:T(8,128)(2,1)S(1)} %stack_keys_values.1.refs_2_, bf16[256,512]{1,0:T(8,128)(2,1)S(1)} %collective-permute-done.8.refs_3_), custom_call_target="tpu_custom_call" | custom-call | flops 536870912 | bytes 3153924 | tf_op jit(solution)/shard_map/softmax_first/pallas_call | solution.py:292
  35.2 2.3 %collective-permute-done.7.refs_6_ = bf16[512,128]{1,0:T(8,128)(2,1)S(1)} collective-permute-done((bf16[512,128]{1,0:T(8,128)(2,1)S(1)}, bf16[512,128]{1,0:T(8,128)(2,1)S(1)}, u32[]{:S(2)}, u32[]{:S(2)}) %collective-permute-start.7) | collective-permute-done | bytes 131104 | tf_op jit(solution)/shard_map/ppermute | solution.py:318
  37.4 0.7 %inter_block.1 = (f32[128,2048]{1,0:T(8,128)S(1)}, f32[8,128]{1,0:T(8,128)S(1)}) custom-call(f32[128,16]{1,0:T(8,128)S(1)} %get-tuple-element.31.refs_0_, bf16[128,2048]{1,0:T(8,128)(2,1)S(1)} %get-tuple-element.32.refs_1_, f32[128,2048]{1,0:T(8,128)S(1)} %get-tuple-element.33.refs_4_.refs_2_, bf16[512,128]{1,0:T(8,128)(2,1)S(1)} %get-tuple-element.38.refs_3_, ...), custom_call_target="tpu_custom_call" | custom-call | flops 67108864 | bytes 3158016 | tf_op jit(solution)/shard_map/inter_block/pallas_call | solution.py:292
  38.1 1.1 %collective-permute-done.11 = bf16[128,512]{1,0:T(8,128)(2,1)S(1)} collective-permute-done((bf16[128,512]{1,0:T(8,128)(2,1)S(1)}, bf16[128,512]{1,0:T(8,128)(2,1)S(1)}, u32[]{:S(2)}, u32[]{:S(2)}) %collective-permute-start.11) | collective-permute-done | bytes 131104 | tf_op jit(solution)/shard_map/ppermute | solution.py:318
  39.3 2.3 %softmax_last.2 = (bf16[128,2048]{1,0:T(8,128)(2,1)}, f32[8,128]{1,0:T(8,128)S(1)}) custom-call(s32[1]{0:T(128)S(6)} %copy.15.refs_0_, bf16[128,2048]{1,0:T(8,128)(2,1)S(1)} %copy-done, bf16[256,512]{1,0:T(8,128)(2,1)S(1)} %collective-permute-done.10.refs_2_, bf16[256,512]{1,0:T(8,128)(2,1)S(1)} %constant_dynamic-update-slice_fusion.refs_3_, ...), custom_call_target="tpu_custom_call" | custom-call | flops 268435456 | bytes 3678212 | tf_op jit(solution)/shard_map/softmax_last/pallas_call | solution.py:292
  41.6 1.8 %collective-permute-start.13 = (f32[8,128]{1,0:T(8,128)S(1)}, f32[8,128]{1,0:T(8,128)S(1)}, u32[]{:S(2)}, u32[]{:S(2)}) collective-permute-start(f32[8,128]{1,0:T(8,128)S(1)} %add.1.refs_2_), channel_id=1, source_target_pairs={{0,2},{1,3},{2,0},{3,1},{4,6},{5,7},{6,4},{7,5},{8,10},{9,11},{10,... | collective-permute-start | bytes 12296 | tf_op jit(solution)/shard_map/ppermute | solution.py:471
  43.4 2.3 %softmax_last.3 = (bf16[128,2048]{1,0:T(8,128)(2,1)}, f32[8,128]{1,0:T(8,128)S(1)}) custom-call(s32[1]{0:T(128)S(6)} %copy.15.refs_0_, bf16[128,2048]{1,0:T(8,128)(2,1)S(1)} %copy-done, bf16[256,512]{1,0:T(8,128)(2,1)S(1)} %collective-permute-done.10.refs_2_, ...), custom_call_target="tpu_custom_call", output_to_operand_aliasing={{0}: (6, {})} | custom-call | flops 268435456 | bytes 4202500 | tf_op jit(solution)/shard_map/softmax_last/pallas_call | solution.py:292
  45.8 1.1 %gated_norm.1 = bf16[128,2048]{1,0:T(8,128)(2,1)} custom-call(f32[128,2048]{1,0:T(8,128)S(1)} %get-tuple-element.43.refs_0_, f32[128,2048]{1,0:T(8,128)S(1)} %get-tuple-element.44.refs_1_, f32[8,128]{1,0:T(8,128)S(1)} %add.1.refs_2_, f32[8,128]{1,0:T(8,128)S(1)} %collective-permute-done.13.refs_3_, f32[8,128]{1,0:T(8,128)S(1)} %get-tuple-element.47.refs_2_.refs_4_, ...), custom_call_target="tpu_custom_call" | custom-call | flops 1048576 | bytes 2629632 | tf_op jit(solution)/shard_map/gated_norm/pallas_call | solution.py:292
  (39 shorter events, 1.8 us)
Async XLA Ops:
  0.6 0.8 %copy-start.6 = (bf16[128,256]{1,0:T(8,128)(2,1)S(1)}, bf16[128,256]{1,0:T(8,128)(2,1)}, u32[]{:S(2)}) copy-start(bf16[128,256]{1,0:T(8,128)(2,1)} %refs_1_.6) | copy-start | bytes 196612
  0.6 0.9 %copy-start.5 = (bf16[128,256]{1,0:T(8,128)(2,1)S(1)}, bf16[128,256]{1,0:T(8,128)(2,1)}, u32[]{:S(2)}) copy-start(bf16[128,256]{1,0:T(8,128)(2,1)} %refs_0_.4) | copy-start | bytes 196612
  0.7 5.0 %copy-start.7 = (f32[16,128]{1,0:T(8,128)S(1)}, f32[16,128]{1,0:T(8,128)}, u32[]{:S(2)}) copy-start(f32[16,128]{1,0:T(8,128)} %refs_2_.3) | copy-start | bytes 24580
  0.7 5.0 %copy-start.2 = (bf16[128,2048]{1,0:T(8,128)(2,1)S(1)}, bf16[128,2048]{1,0:T(8,128)(2,1)}, u32[]{:S(2)}) copy-start(bf16[128,2048]{1,0:T(8,128)(2,1)} %refs_3_.2) | copy-start | bytes 1572868
  0.7 5.0 %copy-start.1 = (bf16[128,2048]{1,0:T(8,128)(2,1)S(1)}, bf16[128,2048]{1,0:T(8,128)(2,1)}, u32[]{:S(2)}) copy-start(bf16[128,2048]{1,0:T(8,128)(2,1)} %refs_2_.2) | copy-start | bytes 1572868
  0.7 11.4 %copy-start.8 = (f32[2048]{0:T(1024)S(1)}, f32[2048]{0:T(1024)}, u32[]{:S(2)}) copy-start(f32[2048]{0:T(1024)} %param.15) | copy-start | bytes 24580
  0.7 11.3 %copy-start.4 = (bf16[128,2048]{1,0:T(8,128)(2,1)S(1)}, bf16[128,2048]{1,0:T(8,128)(2,1)}, u32[]{:S(2)}) copy-start(bf16[128,2048]{1,0:T(8,128)(2,1)} %refs_6_.1) | copy-start | bytes 1572868
  0.7 11.3 %copy-start.3 = (bf16[128,2048]{1,0:T(8,128)(2,1)S(1)}, bf16[128,2048]{1,0:T(8,128)(2,1)}, u32[]{:S(2)}) copy-start(bf16[128,2048]{1,0:T(8,128)(2,1)} %refs_3_.3) | copy-start | bytes 1572868
  1.5 10.5 %collective-permute-start = (bf16[128,512]{1,0:T(8,128)(2,1)S(1)}, bf16[128,512]{1,0:T(8,128)(2,1)S(1)}, u32[]{:S(2)}, u32[]{:S(2)}) collective-permute-start(bf16[128,512]{1,0:T(8,128)(2,1)S(1)} %keys_beside_values.1.refs_0_), channel_id=1, source_target_pairs={{0,16},{4,20},{8,24},{12,28},{16,0},{20,4},{24,8},{28,12},{1,17},{... | collective-permute-start | bytes 393224 | tf_op jit(solution)/shard_map/ppermute | solution.py:324
  7.2 7.6 %collective-permute-start.1 = (bf16[528,128]{1,0:T(8,128)(2,1)S(1)}, bf16[528,128]{1,0:T(8,128)(2,1)S(1)}, u32[]{:S(2)}, u32[]{:S(2)}) collective-permute-start(bf16[528,128]{1,0:T(8,128)(2,1)S(1)} %get-tuple-element.35), channel_id=1, source_target_pairs={{0,4},{4,0},{8,12},{12,8},{16,20},{20,16},{24,28},{28,24},{1,5},{5... | collective-permute-start | bytes 405512 | tf_op jit(solution)/shard_map/ppermute | solution.py:318
  8.7 6.5 %collective-permute-start.2 = (bf16[528,128]{1,0:T(8,128)(2,1)S(1)}, bf16[528,128]{1,0:T(8,128)(2,1)S(1)}, u32[]{:S(2)}, u32[]{:S(2)}) collective-permute-start(bf16[528,128]{1,0:T(8,128)(2,1)S(1)} %get-tuple-element.36), channel_id=1, source_target_pairs={{0,8},{4,12},{8,0},{12,4},{16,24},{20,28},{24,16},{28,20},{1,9},{5... | collective-permute-start | bytes 405512 | tf_op jit(solution)/shard_map/ppermute | solution.py:318
  10.3 7.7 %collective-permute-start.3 = (bf16[528,128]{1,0:T(8,128)(2,1)S(1)}, bf16[528,128]{1,0:T(8,128)(2,1)S(1)}, u32[]{:S(2)}, u32[]{:S(2)}) collective-permute-start(bf16[528,128]{1,0:T(8,128)(2,1)S(1)} %get-tuple-element.37), channel_id=1, source_target_pairs={{0,12},{4,8},{8,4},{12,0},{16,28},{20,24},{24,20},{28,16},{1,13},{... | collective-permute-start | bytes 405512 | tf_op jit(solution)/shard_map/ppermute | solution.py:318
  18.2 7.8 %collective-permute-start.4 = (bf16[528,128]{1,0:T(8,128)(2,1)S(1)}, bf16[528,128]{1,0:T(8,128)(2,1)S(1)}, u32[]{:S(2)}, u32[]{:S(2)}) collective-permute-start(bf16[528,128]{1,0:T(8,128)(2,1)S(1)} %group_state.1.refs_2_), channel_id=1, source_target_pairs={{0,16},{4,20},{8,24},{12,28},{16,0},{20,4},{24,8},{28,12},{1,17},{... | collective-permute-start | bytes 405512 | tf_op jit(solution)/shard_map/ppermute | solution.py:324
  19.1 14.0 %copy-start = (bf16[128,2048]{1,0:T(8,128)(2,1)S(1)}, bf16[128,2048]{1,0:T(8,128)(2,1)}, u32[]{:S(2)}) copy-start(bf16[128,2048]{1,0:T(8,128)(2,1)} %refs_1_.9) | copy-start | bytes 1572868
  19.1 12.4 %collective-permute-start.10 = (bf16[256,512]{1,0:T(8,128)(2,1)S(1)}, bf16[256,512]{1,0:T(8,128)(2,1)S(1)}, u32[]{:S(2)}, u32[]{:S(2)}) collective-permute-start(bf16[256,512]{1,0:T(8,128)(2,1)S(1)} %stack_keys_values.1.refs_2_), channel_id=1, source_target_pairs={{0,8},{4,12},{8,0},{12,4},{16,24},{20,28},{24,16},{28,20},{1,9},{5... | collective-permute-start | bytes 786440 | tf_op jit(solution)/shard_map/ppermute | solution.py:318
  21.6 8.7 %collective-permute-start.8 = (bf16[256,512]{1,0:T(8,128)(2,1)S(1)}, bf16[256,512]{1,0:T(8,128)(2,1)S(1)}, u32[]{:S(2)}, u32[]{:S(2)}) collective-permute-start(bf16[256,512]{1,0:T(8,128)(2,1)S(1)} %stack_keys_values.1.refs_2_), channel_id=1, source_target_pairs={{0,4},{4,0},{8,12},{12,8},{16,20},{20,16},{24,28},{28,24},{1,5},{5... | collective-permute-start | bytes 786440 | tf_op jit(solution)/shard_map/ppermute | solution.py:318
  26.2 8.5 %collective-permute-start.5 = (bf16[512,128]{1,0:T(8,128)(2,1)S(1)}, bf16[512,128]{1,0:T(8,128)(2,1)S(1)}, u32[]{:S(2)}, u32[]{:S(2)}) collective-permute-start(bf16[512,128]{1,0:T(8,128)(2,1)S(1)} %get-tuple-element.39), channel_id=1, source_target_pairs={{0,4},{4,0},{8,12},{12,8},{16,20},{20,16},{24,28},{28,24},{1,5},{5... | collective-permute-start | bytes 393224 | tf_op jit(solution)/shard_map/ppermute | solution.py:318
  28.7 6.4 %collective-permute-start.6 = (bf16[512,128]{1,0:T(8,128)(2,1)S(1)}, bf16[512,128]{1,0:T(8,128)(2,1)S(1)}, u32[]{:S(2)}, u32[]{:S(2)}) collective-permute-start(bf16[512,128]{1,0:T(8,128)(2,1)S(1)} %get-tuple-element.40), channel_id=1, source_target_pairs={{0,8},{4,12},{8,0},{12,4},{16,24},{20,28},{24,16},{28,20},{1,9},{5... | collective-permute-start | bytes 393224 | tf_op jit(solution)/shard_map/ppermute | solution.py:318
  28.7 8.7 %collective-permute-start.7 = (bf16[512,128]{1,0:T(8,128)(2,1)S(1)}, bf16[512,128]{1,0:T(8,128)(2,1)S(1)}, u32[]{:S(2)}, u32[]{:S(2)}) collective-permute-start(bf16[512,128]{1,0:T(8,128)(2,1)S(1)} %get-tuple-element.41), channel_id=1, source_target_pairs={{0,12},{4,8},{8,4},{12,0},{16,28},{20,24},{24,20},{28,16},{1,13},{... | collective-permute-start | bytes 393224 | tf_op jit(solution)/shard_map/ppermute | solution.py:318
  30.3 9.0 %collective-permute-start.11 = (bf16[128,512]{1,0:T(8,128)(2,1)S(1)}, bf16[128,512]{1,0:T(8,128)(2,1)S(1)}, u32[]{:S(2)}, u32[]{:S(2)}) collective-permute-start(bf16[128,512]{1,0:T(8,128)(2,1)S(1)} %slice.8), channel_id=1, source_target_pairs={{0,8},{4,12},{8,0},{12,4},{16,24},{20,28},{24,16},{28,20},{1,9},{5... | collective-permute-start | bytes 393224 | tf_op jit(solution)/shard_map/ppermute | solution.py:318
  31.5 7.7 %collective-permute-start.12 = (bf16[128,512]{1,0:T(8,128)(2,1)S(1)}, bf16[128,512]{1,0:T(8,128)(2,1)S(1)}, u32[]{:S(2)}, u32[]{:S(2)}) collective-permute-start(bf16[128,512]{1,0:T(8,128)(2,1)S(1)} %slice.9), channel_id=1, source_target_pairs={{0,4},{4,0},{8,12},{12,8},{16,20},{20,16},{24,28},{28,24},{1,5},{5... | collective-permute-start | bytes 393224 | tf_op jit(solution)/shard_map/ppermute | solution.py:318
  38.1 3.5 %collective-permute-start.9 = (f32[8,128]{1,0:T(8,128)S(1)}, f32[8,128]{1,0:T(8,128)S(1)}, u32[]{:S(2)}, u32[]{:S(2)}) collective-permute-start(f32[8,128]{1,0:T(8,128)S(1)} %get-tuple-element.45.refs_0_), channel_id=1, source_target_pairs={{0,1},{1,0},{2,3},{3,2},{4,5},{5,4},{6,7},{7,6},{8,9},{9,8},{10,11... | collective-permute-start | bytes 12296 | tf_op jit(solution)/shard_map/ppermute | solution.py:471
  41.6 4.1 %collective-permute-start.13 = (f32[8,128]{1,0:T(8,128)S(1)}, f32[8,128]{1,0:T(8,128)S(1)}, u32[]{:S(2)}, u32[]{:S(2)}) collective-permute-start(f32[8,128]{1,0:T(8,128)S(1)} %add.1.refs_2_), channel_id=1, source_target_pairs={{0,2},{1,3},{2,0},{3,1},{4,6},{5,7},{6,4},{7,5},{8,10},{9,11},{10,... | collective-permute-start | bytes 12296 | tf_op jit(solution)/shard_map/ppermute | solution.py:471

commit v6 on v5

--- a/solution.py
+++ b/solution.py
@@ -93,14 +93,24 @@
         refs[-1][i * tokens : (i + 1) * tokens, :] = part[...]
 
 
+def halves_kernel(a_ref, b_ref, a_out, b_out):
+    half = a_out.shape[0]
+    a_out[...] = a_ref[:half, :]
+    b_out[...] = b_ref[half:, :]
+
+
 def decay_row(slots, k, base, j):
     tail = slots[k, base : base + 16, :].astype(F32)
     return tail[j : j + 1] + tail[8 + j : 9 + j]
 
 
+def sent(group):
+    return [0, *range(group - 1, 0, -1)]
+
+
 def fill_slots(group, rank, pays, slots):
-    for s in range(group):
-        slots[rank ^ s] = pays[s][...]
+    for s, pay in zip(sent(group), pays):
+        slots[rank ^ s] = pay[...]
 
 
 def total_kernel(group, per, *refs):
@@ -171,8 +181,8 @@
     tokens = qa_ref.shape[0]
     per = heads // group
     rank = my_rank(group)
-    for s in range(group):
-        states[dyn(rank ^ s, per * HD), :] = parts[s][...]
+    for s, part in zip(sent(group), parts):
+        states[dyn(rank ^ s, per * HD), :] = part[...]
     decay = decay_ref[...]
     acc = jnp.zeros((tokens, HD), F32)
     for h in range(heads):
@@ -257,25 +267,26 @@
                 tops[g][:, j + i : j + i + 1] = top[rows]
 
 
-def softmax_last_kernel(group, sides, g, kv_heads, pack, order_ref, q_ref, a_ref, b_ref, *rest):
-    acc_ref, top_ref = rest[:2]
-    out_ref, done_ref, values, bias = rest[-4:]
+def softmax_last_kernel(group, sides, kv_heads, pack, order_ref, q_ref, a_ref, b_ref, *rest):
+    acc_ref, tops, (out_ref, done_ref, values, bias) = rest[0], rest[1:-4], rest[-4:]
     tokens = q_ref.shape[0]
+    share = q_ref.shape[1] // HD // kv_heads
     done_ref[...] = jnp.zeros_like(done_ref)
     softmax_bias(group, sides, order_ref, bias)
-    softmax_values((a_ref, b_ref), g, kv_heads, values)
-    for j in range(0, q_ref.shape[1] // HD, pack):
-        heads = range(j, j + pack)
-        raw = softmax_scores(stacked(q_ref, map(head_cols, heads)), (a_ref, b_ref), g, bias)
-        old = stacked(top_ref, [slice(h, h + 1) for h in heads])
-        top = jnp.maximum(old, jnp.max(raw, axis=-1, keepdims=True))
-        probs = jnp.exp2((raw - top) * SCORE).astype(BF16)
-        acc = jnp.dot(probs, values[...], preferred_element_type=F32)
-        held = stacked(acc_ref, [slice(2 * h * HD, 2 * (h + 1) * HD) for h in heads])
-        acc += held * jnp.exp2((old - top) * SCORE)
-        out = (acc[:, :HD] / acc[:, HD:]).astype(BF16)
-        for i, h in enumerate(heads):
-            out_ref[:, head_cols(h)] = out[i * tokens : (i + 1) * tokens]
+    for g in range(kv_heads):
+        softmax_values((a_ref, b_ref), g, kv_heads, values)
+        for j in range(0, share, pack):
+            heads = range(g * share + j, g * share + j + pack)
+            raw = softmax_scores(stacked(q_ref, map(head_cols, heads)), (a_ref, b_ref), g, bias)
+            old = stacked(tops[g], [slice(j + i, j + i + 1) for i in range(pack)])
+            top = jnp.maximum(old, jnp.max(raw, axis=-1, keepdims=True))
+            probs = jnp.exp2((raw - top) * SCORE).astype(BF16)
+            acc = jnp.dot(probs, values[...], preferred_element_type=F32)
+            held = stacked(acc_ref, [slice(2 * h * HD, 2 * (h + 1) * HD) for h in heads])
+            acc += held * jnp.exp2((old - top) * SCORE)
+            out = (acc[:, :HD] / acc[:, HD:]).astype(BF16)
+            for i, h in enumerate(heads):
+                out_ref[:, head_cols(h)] = out[i * tokens : (i + 1) * tokens]
 
 
 def call(
@@ -318,7 +329,7 @@
         return lax.ppermute(x, "ctx", [(c, c ^ s) for c in range(n)])
 
     def swap_all(xs):
-        return [xs[0]] + [swap(xs[s], s) for s in range(1, group)]
+        return [swap(xs[s], s) if s else xs[s] for s in sent(group)]
 
     def ahead(x, d):
         return lax.ppermute(x, "ctx", [(c, (c + d * group) % n) for c in range(n)])
@@ -407,8 +418,6 @@
         flops=1 << 32,
     )
     near, side = swap(own, 1), swap(own, 2)
-    half = own.shape[0] // 2
-    across = jnp.concatenate([swap(near[:half], 2), swap(side[half:], 1)])
     share = width // kv_heads
     pack = 2 if share // HD % 2 == 0 else 1
     span = 2 * own.shape[0]
@@ -426,32 +435,20 @@
         limit=room,
         specs=[smem] + [VMEM] * 3,
     )
-    attended, marks = (), []
-    for g in range(kv_heads):
-
-        def columns(size, g=g):
-            return pl.BlockSpec((tokens, size), lambda i: (0, g))
-
-        def whole(x):
-            return pl.BlockSpec(x.shape, lambda i: (0, 0))
-
-        *attended, mark = call(
-            functools.partial(softmax_last_kernel, group, (2, 3), g, kv_heads, pack),
-            "softmax_last",
-            [shape((tokens, width), BF16), shape((8, HD), F32)],
-            (order, queries, side, across, acc, tops[g], *attended),
-            scratch,
-            flops=4 * tokens * share * span,
-            exps=tokens * span * share // HD,
-            limit=room,
-            specs=[smem, columns(share), whole(side), whole(across)]
-            + [columns(2 * share), whole(tops[g])]
-            + [HBM for _ in attended],
-            out_specs=[columns(share), pl.BlockSpec((8, HD), lambda i: (0, 0))],
-            grid=(1,),
-            input_output_aliases={6: 0} if attended else {},
-        )
-        marks.append(mark)
+    half = shape((own.shape[0] // 2, own.shape[1]), BF16)
+    upper, under = call(halves_kernel, "sent_on", [half] * 2, (near, side), after=tops[:1])
+    across = jnp.concatenate([swap(upper, 2), swap(under, 1)])
+    attended, mark = call(
+        functools.partial(softmax_last_kernel, group, (2, 3), kv_heads, pack),
+        "softmax_last",
+        [shape((tokens, width), BF16), shape((8, HD), F32)],
+        (order, queries, side, across, acc, *tops),
+        scratch,
+        flops=4 * tokens * width * span,
+        exps=tokens * span * width // HD,
+        limit=room,
+        specs=[smem] + [VMEM] * (4 + kv_heads),
+    )
 
     lin, squares = call(
         functools.partial(inter_kernel, group, heads),
@@ -467,7 +464,7 @@
         while shift < nh:
             held = parts[0]
             if len(parts) > 1:
-                (held,) = call(add_kernel, "add", [shape((8, tokens), F32)], parts, after=marks[:1])
+                (held,) = call(add_kernel, "add", [shape((8, tokens), F32)], parts, after=(mark,))
             parts = [held, lax.ppermute(held, "head", [(i, i ^ shift) for i in range(nh)])]
             shift *= 2
     else:
@@ -479,9 +476,9 @@
         [shape((tokens, width), BF16)],
         (lin, gain, *parts),
         flops=4 * tokens * width,
-        after=marks,
-    )
-    return (mixed, attended[0])
+        after=(mark,),
+    )
+    return (mixed, attended)
 
 
 def solution(mesh):

time: 47 us -> 46.9 us (level)
  waiting for transfers between devices: 11.3 us -> 15.8 us
  starting transfers between devices: 20.6 us -> 17.4 us
  Pallas kernels: 12.6 us -> 11.3 us
    ppermute x10, starting transfers between devices: 13.8 us -> 10.9 us  [swap(): return lax.ppermute(x, 'ctx', [(c, c ^ s) for c in range(n)])]
    ppermute x2, waiting for transfers between devices: 0.01 us -> 2.11 us  [body(): lax.ppermute(held, 'head', [(i, i ^ shift) for i in range(nh)])]
    pallas_call x13, Pallas kernels: 12.6 us -> 11.3 us  [call(): pl.pallas_call(run, name=name, out_shape=list(outs), in_specs=specs, scra...]
    ppermute x2, waiting for transfers between devices: 4.18 us -> 5.43 us  [ahead(): return lax.ppermute(x, 'ctx', [(c, (c + d * group) % n) for c in range(n)])]
    ppermute x10, waiting for transfers between devices: 7.15 us -> 8.23 us  [swap(): return lax.ppermute(x, 'ctx', [(c, c ^ s) for c in range(n)])]
  transfers between devices with their start and end apart: 14 -> 14, of which waited for: 7 -> 9; matrix products, arithmetic and copies ran while one was open for 0% -> 0% of each run, Pallas kernels for 24% -> 22%
where the time goes in v6:
time: 46.9 us; the launch traced here: 46.7 us
  starting transfers between devices  17.4 us (37%)
  waiting for transfers between devices  15.8 us (34%)
  Pallas kernels  11.3 us (24%)
  between operations  1.45 us (3%)
  local copies, waits for them, and re-layouts  0.81 us (2%)
    pallas_call x13, Pallas kernels, call(): pl.pallas_call(run, name=name, out_shape=list(outs), in_specs=specs, scra...  11.3 us
    ppermute x10, starting transfers between devices, swap(): return lax.ppermute(x, 'ctx', [(c, c ^ s) for c in range(n)])  10.9 us
    ppermute x10, waiting for transfers between devices, swap(): return lax.ppermute(x, 'ctx', [(c, c ^ s) for c in range(n)])  8.23 us
    ppermute x2, waiting for transfers between devices, ahead(): return lax.ppermute(x, 'ctx', [(c, (c + d * group) % n) for c in range(n)])  5.43 us
    ppermute x2, starting transfers between devices, ahead(): return lax.ppermute(x, 'ctx', [(c, (c + d * group) % n) for c in range(n)])  4.97 us
    ppermute x2, waiting for transfers between devices, body(): lax.ppermute(held, 'head', [(i, i ^ shift) for i in range(nh)])  2.11 us
    ppermute x2, starting transfers between devices, body(): lax.ppermute(held, 'head', [(i, i ^ shift) for i in range(nh)])  1.5 us
  transfers between devices with their start and end apart: 14, of which 9 were waited for; matrix products, arithmetic and copies ran while one was open for 0% of the time, Pallas kernels for 22%

profile of v6, /device:TPU:0, one launch (start us, length us, event | category | flops | bytes accessed | tf_op | source)
XLA Modules:
  0.0 46.7 jit_solution(4272562749314815864)
XLA Ops:
  0.7 0.7 %copy-done.5 = bf16[128,256]{1,0:T(8,128)(2,1)S(1)} copy-done((bf16[128,256]{1,0:T(8,128)(2,1)S(1)}, bf16[128,256]{1,0:T(8,128)(2,1)}, u32[]{:S(2)}) %copy-start.5) | copy-done | bytes 65560
  1.5 4.1 %collective-permute-start = (bf16[128,512]{1,0:T(8,128)(2,1)S(1)}, bf16[128,512]{1,0:T(8,128)(2,1)S(1)}, u32[]{:S(2)}, u32[]{:S(2)}) collective-permute-start(bf16[128,512]{1,0:T(8,128)(2,1)S(1)} %keys_beside_values.1.refs_0_), channel_id=1, source_target_pairs={{0,16},{4,20},{8,24},{12,28},{16,0},{20,4},{24,8},{28,12},{1,17},{... | collective-permute-start | bytes 393224 | tf_op jit(solution)/shard_map/ppermute | solution.py:335
  5.6 1.5 %block_states.1 = (bf16[528,128]{1,0:T(8,128)(2,1)S(1)}, bf16[528,128]{1,0:T(8,128)(2,1)S(1)}, bf16[528,128]{1,0:T(8,128)(2,1)S(1)}, bf16[528,128]{1,0:T(8,128)(...) custom-call(f32[128,128]{1,0:T(8,128)S(1)} %get-tuple-element.27.refs_0_.refs_2_, ...), custom_call_target="tpu_custom_call" | custom-call | flops 134217728 | bytes 2711552 | tf_op jit(solution)/shard_map/block_states/pallas_call | solution.py:303
  7.2 2.6 %collective-permute-start.1 = (bf16[528,128]{1,0:T(8,128)(2,1)S(1)}, bf16[528,128]{1,0:T(8,128)(2,1)S(1)}, u32[]{:S(2)}, u32[]{:S(2)}) collective-permute-start(bf16[528,128]{1,0:T(8,128)(2,1)S(1)} %get-tuple-element.35), channel_id=1, source_target_pairs={{0,12},{4,8},{8,4},{12,0},{16,28},{20,24},{24,20},{28,16},{1,13},{... | collective-permute-start | bytes 405512 | tf_op jit(solution)/shard_map/ppermute | solution.py:329
  11.4 0.7 %collective-permute-done.refs_8_.refs_1_ = bf16[128,512]{1,0:T(8,128)(2,1)S(1)} collective-permute-done((bf16[128,512]{1,0:T(8,128)(2,1)S(1)}, bf16[128,512]{1,0:T(8,128)(2,1)S(1)}, u32[]{:S(2)}, u32[]{:S(2)}) %collective-permute-start) | collective-permute-done | bytes 131104 | tf_op jit(solution)/shard_map/ppermute | solution.py:335
  12.0 2.8 %intra_block.1 = (f32[128,2048]{1,0:T(8,128)S(1)}, bf16[128,2048]{1,0:T(8,128)(2,1)S(1)}, f32[128,2048]{1,0:T(8,128)S(1)}, f32[128,16]{1,0:T(8,128)S(1)}) custom-call(f32[128,128]{1,0:T(8,128)S(1)} %get-tuple-element.27.refs_0_.refs_2_, f32[128,128]{1,0:T(8,128)S(1)} %get-tuple-element.28.refs_1_, f32[16,128]{1,0:T(8,128)S(1)} %copy-done.7, ...), custom_call_target="tpu_custom_call" | custom-call | flops 134217728 | bytes 4874240 | tf_op jit(solution)/shard_map/intra_block/pallas_call | solution.py:303
  14.8 0.9 %collective-permute-done.1.refs_1_ = bf16[528,128]{1,0:T(8,128)(2,1)S(1)} collective-permute-done((bf16[528,128]{1,0:T(8,128)(2,1)S(1)}, bf16[528,128]{1,0:T(8,128)(2,1)S(1)}, u32[]{:S(2)}, u32[]{:S(2)}) %collective-permute-start.1) | collective-permute-done | bytes 135200 | tf_op jit(solution)/shard_map/ppermute | solution.py:329
  15.7 2.0 %collective-permute-done.2.refs_2_ = bf16[528,128]{1,0:T(8,128)(2,1)S(1)} collective-permute-done((bf16[528,128]{1,0:T(8,128)(2,1)S(1)}, bf16[528,128]{1,0:T(8,128)(2,1)S(1)}, u32[]{:S(2)}, u32[]{:S(2)}) %collective-permute-start.2) | collective-permute-done | bytes 135200 | tf_op jit(solution)/shard_map/ppermute | solution.py:329
  17.9 0.9 %collective-permute-start.4 = (bf16[528,128]{1,0:T(8,128)(2,1)S(1)}, bf16[528,128]{1,0:T(8,128)(2,1)S(1)}, u32[]{:S(2)}, u32[]{:S(2)}) collective-permute-start(bf16[528,128]{1,0:T(8,128)(2,1)S(1)} %group_state.1.refs_2_), channel_id=1, source_target_pairs={{0,16},{4,20},{8,24},{12,28},{16,0},{20,4},{24,8},{28,12},{1,17},{... | collective-permute-start | bytes 405512 | tf_op jit(solution)/shard_map/ppermute | solution.py:335
  19.4 2.5 %collective-permute-start.10 = (bf16[256,512]{1,0:T(8,128)(2,1)S(1)}, bf16[256,512]{1,0:T(8,128)(2,1)S(1)}, u32[]{:S(2)}, u32[]{:S(2)}) collective-permute-start(bf16[256,512]{1,0:T(8,128)(2,1)S(1)} %stack_keys_values.1.refs_2_), channel_id=1, source_target_pairs={{0,8},{4,12},{8,0},{12,4},{16,24},{20,28},{24,16},{28,20},{1,9},{5... | collective-permute-start | bytes 786440 | tf_op jit(solution)/shard_map/ppermute | solution.py:329
  21.8 4.8 %collective-permute-done.4.refs_4_ = bf16[528,128]{1,0:T(8,128)(2,1)S(1)} collective-permute-done((bf16[528,128]{1,0:T(8,128)(2,1)S(1)}, bf16[528,128]{1,0:T(8,128)(2,1)S(1)}, u32[]{:S(2)}, u32[]{:S(2)}) %collective-permute-start.4) | collective-permute-done | bytes 135200 | tf_op jit(solution)/shard_map/ppermute | solution.py:335
  26.9 2.1 %collective-permute-start.6 = (bf16[512,128]{1,0:T(8,128)(2,1)S(1)}, bf16[512,128]{1,0:T(8,128)(2,1)S(1)}, u32[]{:S(2)}, u32[]{:S(2)}) collective-permute-start(bf16[512,128]{1,0:T(8,128)(2,1)S(1)} %get-tuple-element.40), channel_id=1, source_target_pairs={{0,8},{4,12},{8,0},{12,4},{16,24},{20,28},{24,16},{28,20},{1,9},{5... | collective-permute-start | bytes 393224 | tf_op jit(solution)/shard_map/ppermute | solution.py:329
  29.0 1.3 %collective-permute-start.7 = (bf16[512,128]{1,0:T(8,128)(2,1)S(1)}, bf16[512,128]{1,0:T(8,128)(2,1)S(1)}, u32[]{:S(2)}, u32[]{:S(2)}) collective-permute-start(bf16[512,128]{1,0:T(8,128)(2,1)S(1)} %get-tuple-element.41), channel_id=1, source_target_pairs={{0,4},{4,0},{8,12},{12,8},{16,20},{20,16},{24,28},{28,24},{1,5},{5... | collective-permute-start | bytes 393224 | tf_op jit(solution)/shard_map/ppermute | solution.py:329
  30.4 1.6 %softmax_first.1 = (f32[128,4096]{1,0:T(8,128)S(1)}, f32[128,8]{1,0:T(8,128)S(1)}, f32[128,8]{1,0:T(8,128)S(1)}) custom-call(s32[1]{0:T(128)S(6)} %copy.12.refs_0_, bf16[128,2048]{1,0:T(8,128)(2,1)S(1)} %copy-done.4, bf16[256,512]{1,0:T(8,128)(2,1)S(1)} %stack_keys_values.1.refs_2_, bf16[256,512]{1,0:T(8,128)(2,1)S(1)} %collective-permute-done.8.refs_3_.refs_0_), custom_call_target="tpu_custom_call" | custom-call | flops 536870912 | bytes 3153924 | tf_op jit(solution)/shard_map/softmax_first/pallas_call | solution.py:303
  32.1 0.7 %collective-permute-start.12 = (bf16[128,512]{1,0:T(8,128)(2,1)S(1)}, bf16[128,512]{1,0:T(8,128)(2,1)S(1)}, u32[]{:S(2)}, u32[]{:S(2)}) collective-permute-start(bf16[128,512]{1,0:T(8,128)(2,1)S(1)} %get-tuple-element.47), channel_id=1, source_target_pairs={{0,4},{4,0},{8,12},{12,8},{16,20},{20,16},{24,28},{28,24},{1,5},{5... | collective-permute-start | bytes 393224 | tf_op jit(solution)/shard_map/ppermute | solution.py:329
  32.8 1.3 %collective-permute-done.5.refs_4_ = bf16[512,128]{1,0:T(8,128)(2,1)S(1)} collective-permute-done((bf16[512,128]{1,0:T(8,128)(2,1)S(1)}, bf16[512,128]{1,0:T(8,128)(2,1)S(1)}, u32[]{:S(2)}, u32[]{:S(2)}) %collective-permute-start.5) | collective-permute-done | bytes 131104 | tf_op jit(solution)/shard_map/ppermute | solution.py:329
  34.1 2.1 %collective-permute-done.6.refs_5_ = bf16[512,128]{1,0:T(8,128)(2,1)S(1)} collective-permute-done((bf16[512,128]{1,0:T(8,128)(2,1)S(1)}, bf16[512,128]{1,0:T(8,128)(2,1)S(1)}, u32[]{:S(2)}, u32[]{:S(2)}) %collective-permute-start.6) | collective-permute-done | bytes 131104 | tf_op jit(solution)/shard_map/ppermute | solution.py:329
  36.2 0.7 %inter_block.1 = (f32[128,2048]{1,0:T(8,128)S(1)}, f32[8,128]{1,0:T(8,128)S(1)}) custom-call(f32[128,16]{1,0:T(8,128)S(1)} %get-tuple-element.31.refs_0_, bf16[128,2048]{1,0:T(8,128)(2,1)S(1)} %get-tuple-element.32.refs_1_, f32[128,2048]{1,0:T(8,128)S(1)} %get-tuple-element.33.refs_4_.refs_2_, bf16[512,128]{1,0:T(8,128)(2,1)S(1)} %get-tuple-element.38.refs_3_, ...), custom_call_target="tpu_custom_call" | custom-call | flops 67108864 | bytes 3158016 | tf_op jit(solution)/shard_map/inter_block/pallas_call | solution.py:303
  36.9 1.3 %collective-permute-done.11 = bf16[128,512]{1,0:T(8,128)(2,1)S(1)} collective-permute-done((bf16[128,512]{1,0:T(8,128)(2,1)S(1)}, bf16[128,512]{1,0:T(8,128)(2,1)S(1)}, u32[]{:S(2)}, u32[]{:S(2)}) %collective-permute-start.11) | collective-permute-done | bytes 131104 | tf_op jit(solution)/shard_map/ppermute | solution.py:329
  38.2 0.6 %collective-permute-done.12 = bf16[128,512]{1,0:T(8,128)(2,1)S(1)} collective-permute-done((bf16[128,512]{1,0:T(8,128)(2,1)S(1)}, bf16[128,512]{1,0:T(8,128)(2,1)S(1)}, u32[]{:S(2)}, u32[]{:S(2)}) %collective-permute-start.12) | collective-permute-done | bytes 131104 | tf_op jit(solution)/shard_map/ppermute | solution.py:329
  38.8 3.3 %softmax_last.1 = (bf16[128,2048]{1,0:T(8,128)(2,1)}, f32[8,128]{1,0:T(8,128)S(1)}) custom-call(s32[1]{0:T(128)S(6)} %copy.12.refs_0_, bf16[128,2048]{1,0:T(8,128)(2,1)S(1)} %copy-done.4, bf16[256,512]{1,0:T(8,128)(2,1)S(1)} %collective-permute-done.10.refs_1_.refs_2_, bf16[256,512]{1,0:T(8,128)(2,1)S(1)} %pad_maximum_fusion.refs_3_, ...), custom_call_target="tpu_custom_call" | custom-call | flops 536870912 | bytes 3682308 | tf_op jit(solution)/shard_map/softmax_last/pallas_call | solution.py:303
  42.1 1.5 %collective-permute-start.13 = (f32[8,128]{1,0:T(8,128)S(1)}, f32[8,128]{1,0:T(8,128)S(1)}, u32[]{:S(2)}, u32[]{:S(2)}) collective-permute-start(f32[8,128]{1,0:T(8,128)S(1)} %add.1.refs_2_), channel_id=1, source_target_pairs={{0,2},{1,3},{2,0},{3,1},{4,6},{5,7},{6,4},{7,5},{8,10},{9,11},{10,... | collective-permute-start | bytes 12296 | tf_op jit(solution)/shard_map/ppermute | solution.py:468
  43.6 2.1 %collective-permute-done.13.refs_3_ = f32[8,128]{1,0:T(8,128)S(1)} collective-permute-done((f32[8,128]{1,0:T(8,128)S(1)}, f32[8,128]{1,0:T(8,128)S(1)}, u32[]{:S(2)}, u32[]{:S(2)}) %collective-permute-start.13) | collective-permute-done | bytes 4128 | tf_op jit(solution)/shard_map/ppermute | solution.py:468
  45.7 1.1 %gated_norm.1 = bf16[128,2048]{1,0:T(8,128)(2,1)} custom-call(f32[128,2048]{1,0:T(8,128)S(1)} %get-tuple-element.43.refs_0_, f32[128,2048]{1,0:T(8,128)S(1)} %get-tuple-element.44.refs_1_, f32[8,128]{1,0:T(8,128)S(1)} %add.1.refs_2_, f32[8,128]{1,0:T(8,128)S(1)} %collective-permute-done.13.refs_3_, f32[8,128]{1,0:T(8,128)S(1)} %get-tuple-element.50.refs_2_.refs_4_), custom_call_target="tpu_custom_call" | custom-call | flops 1048576 | bytes 2629632 | tf_op jit(solution)/shard_map/gated_norm/pallas_call | solution.py:303
  (36 shorter events, 2.1 us)
Async XLA Ops:
  0.6 0.8 %copy-start.5 = (bf16[128,256]{1,0:T(8,128)(2,1)S(1)}, bf16[128,256]{1,0:T(8,128)(2,1)}, u32[]{:S(2)}) copy-start(bf16[128,256]{1,0:T(8,128)(2,1)} %refs_0_.3) | copy-start | bytes 196612
  0.6 0.9 %copy-start.6 = (bf16[128,256]{1,0:T(8,128)(2,1)S(1)}, bf16[128,256]{1,0:T(8,128)(2,1)}, u32[]{:S(2)}) copy-start(bf16[128,256]{1,0:T(8,128)(2,1)} %refs_1_.5) | copy-start | bytes 196612
  0.7 5.0 %copy-start = (bf16[128,2048]{1,0:T(8,128)(2,1)S(1)}, bf16[128,2048]{1,0:T(8,128)(2,1)}, u32[]{:S(2)}) copy-start(bf16[128,2048]{1,0:T(8,128)(2,1)} %refs_2_.2) | copy-start | bytes 1572868
  0.7 5.0 %copy-start.1 = (bf16[128,2048]{1,0:T(8,128)(2,1)S(1)}, bf16[128,2048]{1,0:T(8,128)(2,1)}, u32[]{:S(2)}) copy-start(bf16[128,2048]{1,0:T(8,128)(2,1)} %refs_3_.2) | copy-start | bytes 1572868
  0.7 5.0 %copy-start.7 = (f32[16,128]{1,0:T(8,128)S(1)}, f32[16,128]{1,0:T(8,128)}, u32[]{:S(2)}) copy-start(f32[16,128]{1,0:T(8,128)} %refs_2_.3) | copy-start | bytes 24580
  0.7 11.3 %copy-start.8 = (f32[2048]{0:T(1024)S(1)}, f32[2048]{0:T(1024)}, u32[]{:S(2)}) copy-start(f32[2048]{0:T(1024)} %param.15) | copy-start | bytes 24580
  0.7 11.3 %copy-start.2 = (bf16[128,2048]{1,0:T(8,128)(2,1)S(1)}, bf16[128,2048]{1,0:T(8,128)(2,1)}, u32[]{:S(2)}) copy-start(bf16[128,2048]{1,0:T(8,128)(2,1)} %refs_3_.3) | copy-start | bytes 1572868
  0.7 11.3 %copy-start.3 = (bf16[128,2048]{1,0:T(8,128)(2,1)S(1)}, bf16[128,2048]{1,0:T(8,128)(2,1)}, u32[]{:S(2)}) copy-start(bf16[128,2048]{1,0:T(8,128)(2,1)} %refs_6_.1) | copy-start | bytes 1572868
  1.5 10.5 %collective-permute-start = (bf16[128,512]{1,0:T(8,128)(2,1)S(1)}, bf16[128,512]{1,0:T(8,128)(2,1)S(1)}, u32[]{:S(2)}, u32[]{:S(2)}) collective-permute-start(bf16[128,512]{1,0:T(8,128)(2,1)S(1)} %keys_beside_values.1.refs_0_), channel_id=1, source_target_pairs={{0,16},{4,20},{8,24},{12,28},{16,0},{20,4},{24,8},{28,12},{1,17},{... | collective-permute-start | bytes 393224 | tf_op jit(solution)/shard_map/ppermute | solution.py:335
  7.2 8.6 %collective-permute-start.1 = (bf16[528,128]{1,0:T(8,128)(2,1)S(1)}, bf16[528,128]{1,0:T(8,128)(2,1)S(1)}, u32[]{:S(2)}, u32[]{:S(2)}) collective-permute-start(bf16[528,128]{1,0:T(8,128)(2,1)S(1)} %get-tuple-element.35), channel_id=1, source_target_pairs={{0,12},{4,8},{8,4},{12,0},{16,28},{20,24},{24,20},{28,16},{1,13},{... | collective-permute-start | bytes 405512 | tf_op jit(solution)/shard_map/ppermute | solution.py:329
  9.8 8.0 %collective-permute-start.2 = (bf16[528,128]{1,0:T(8,128)(2,1)S(1)}, bf16[528,128]{1,0:T(8,128)(2,1)S(1)}, u32[]{:S(2)}, u32[]{:S(2)}) collective-permute-start(bf16[528,128]{1,0:T(8,128)(2,1)S(1)} %get-tuple-element.36), channel_id=1, source_target_pairs={{0,8},{4,12},{8,0},{12,4},{16,24},{20,28},{24,16},{28,20},{1,9},{5... | collective-permute-start | bytes 405512 | tf_op jit(solution)/shard_map/ppermute | solution.py:329
  10.2 7.6 %collective-permute-start.3 = (bf16[528,128]{1,0:T(8,128)(2,1)S(1)}, bf16[528,128]{1,0:T(8,128)(2,1)S(1)}, u32[]{:S(2)}, u32[]{:S(2)}) collective-permute-start(bf16[528,128]{1,0:T(8,128)(2,1)S(1)} %get-tuple-element.37), channel_id=1, source_target_pairs={{0,4},{4,0},{8,12},{12,8},{16,20},{20,16},{24,28},{28,24},{1,5},{5... | collective-permute-start | bytes 405512 | tf_op jit(solution)/shard_map/ppermute | solution.py:329
  17.9 8.7 %collective-permute-start.4 = (bf16[528,128]{1,0:T(8,128)(2,1)S(1)}, bf16[528,128]{1,0:T(8,128)(2,1)S(1)}, u32[]{:S(2)}, u32[]{:S(2)}) collective-permute-start(bf16[528,128]{1,0:T(8,128)(2,1)S(1)} %group_state.1.refs_2_), channel_id=1, source_target_pairs={{0,16},{4,20},{8,24},{12,28},{16,0},{20,4},{24,8},{28,12},{1,17},{... | collective-permute-start | bytes 405512 | tf_op jit(solution)/shard_map/ppermute | solution.py:335
  18.8 11.5 %copy-start.4 = (bf16[128,2048]{1,0:T(8,128)(2,1)S(1)}, bf16[128,2048]{1,0:T(8,128)(2,1)}, u32[]{:S(2)}) copy-start(bf16[128,2048]{1,0:T(8,128)(2,1)} %refs_1_.7) | copy-start | bytes 1572868
  18.8 11.5 %collective-permute-start.8 = (bf16[256,512]{1,0:T(8,128)(2,1)S(1)}, bf16[256,512]{1,0:T(8,128)(2,1)S(1)}, u32[]{:S(2)}, u32[]{:S(2)}) collective-permute-start(bf16[256,512]{1,0:T(8,128)(2,1)S(1)} %stack_keys_values.1.refs_2_), channel_id=1, source_target_pairs={{0,4},{4,0},{8,12},{12,8},{16,20},{20,16},{24,28},{28,24},{1,5},{5... | collective-permute-start | bytes 786440 | tf_op jit(solution)/shard_map/ppermute | solution.py:329
  19.4 12.6 %collective-permute-start.10 = (bf16[256,512]{1,0:T(8,128)(2,1)S(1)}, bf16[256,512]{1,0:T(8,128)(2,1)S(1)}, u32[]{:S(2)}, u32[]{:S(2)}) collective-permute-start(bf16[256,512]{1,0:T(8,128)(2,1)S(1)} %stack_keys_values.1.refs_2_), channel_id=1, source_target_pairs={{0,8},{4,12},{8,0},{12,4},{16,24},{20,28},{24,16},{28,20},{1,9},{5... | collective-permute-start | bytes 786440 | tf_op jit(solution)/shard_map/ppermute | solution.py:329
  26.8 7.3 %collective-permute-start.5 = (bf16[512,128]{1,0:T(8,128)(2,1)S(1)}, bf16[512,128]{1,0:T(8,128)(2,1)S(1)}, u32[]{:S(2)}, u32[]{:S(2)}) collective-permute-start(bf16[512,128]{1,0:T(8,128)(2,1)S(1)} %get-tuple-element.39), channel_id=1, source_target_pairs={{0,12},{4,8},{8,4},{12,0},{16,28},{20,24},{24,20},{28,16},{1,13},{... | collective-permute-start | bytes 393224 | tf_op jit(solution)/shard_map/ppermute | solution.py:329
  26.9 9.3 %collective-permute-start.6 = (bf16[512,128]{1,0:T(8,128)(2,1)S(1)}, bf16[512,128]{1,0:T(8,128)(2,1)S(1)}, u32[]{:S(2)}, u32[]{:S(2)}) collective-permute-start(bf16[512,128]{1,0:T(8,128)(2,1)S(1)} %get-tuple-element.40), channel_id=1, source_target_pairs={{0,8},{4,12},{8,0},{12,4},{16,24},{20,28},{24,16},{28,20},{1,9},{5... | collective-permute-start | bytes 393224 | tf_op jit(solution)/shard_map/ppermute | solution.py:329
  29.0 7.2 %collective-permute-start.7 = (bf16[512,128]{1,0:T(8,128)(2,1)S(1)}, bf16[512,128]{1,0:T(8,128)(2,1)S(1)}, u32[]{:S(2)}, u32[]{:S(2)}) collective-permute-start(bf16[512,128]{1,0:T(8,128)(2,1)S(1)} %get-tuple-element.41), channel_id=1, source_target_pairs={{0,4},{4,0},{8,12},{12,8},{16,20},{20,16},{24,28},{28,24},{1,5},{5... | collective-permute-start | bytes 393224 | tf_op jit(solution)/shard_map/ppermute | solution.py:329
  32.0 6.1 %collective-permute-start.11 = (bf16[128,512]{1,0:T(8,128)(2,1)S(1)}, bf16[128,512]{1,0:T(8,128)(2,1)S(1)}, u32[]{:S(2)}, u32[]{:S(2)}) collective-permute-start(bf16[128,512]{1,0:T(8,128)(2,1)S(1)} %get-tuple-element.46), channel_id=1, source_target_pairs={{0,8},{4,12},{8,0},{12,4},{16,24},{20,28},{24,16},{28,20},{1,9},{5... | collective-permute-start | bytes 393224 | tf_op jit(solution)/shard_map/ppermute | solution.py:329
  32.1 6.7 %collective-permute-start.12 = (bf16[128,512]{1,0:T(8,128)(2,1)S(1)}, bf16[128,512]{1,0:T(8,128)(2,1)S(1)}, u32[]{:S(2)}, u32[]{:S(2)}) collective-permute-start(bf16[128,512]{1,0:T(8,128)(2,1)S(1)} %get-tuple-element.47), channel_id=1, source_target_pairs={{0,4},{4,0},{8,12},{12,8},{16,20},{20,16},{24,28},{28,24},{1,5},{5... | collective-permute-start | bytes 393224 | tf_op jit(solution)/shard_map/ppermute | solution.py:329
  36.9 5.2 %collective-permute-start.9 = (f32[8,128]{1,0:T(8,128)S(1)}, f32[8,128]{1,0:T(8,128)S(1)}, u32[]{:S(2)}, u32[]{:S(2)}) collective-permute-start(f32[8,128]{1,0:T(8,128)S(1)} %get-tuple-element.45.refs_0_), channel_id=1, source_target_pairs={{0,1},{1,0},{2,3},{3,2},{4,5},{5,4},{6,7},{7,6},{8,9},{9,8},{10,11... | collective-permute-start | bytes 12296 | tf_op jit(solution)/shard_map/ppermute | solution.py:468
  42.1 3.6 %collective-permute-start.13 = (f32[8,128]{1,0:T(8,128)S(1)}, f32[8,128]{1,0:T(8,128)S(1)}, u32[]{:S(2)}, u32[]{:S(2)}) collective-permute-start(f32[8,128]{1,0:T(8,128)S(1)} %add.1.refs_2_), channel_id=1, source_target_pairs={{0,2},{1,3},{2,0},{3,1},{4,6},{5,7},{6,4},{7,5},{8,10},{9,11},{10,... | collective-permute-start | bytes 12296 | tf_op jit(solution)/shard_map/ppermute | solution.py:468

commit v7 on v6

--- a/solution.py
+++ b/solution.py
@@ -196,10 +196,6 @@
     squares_ref[...] = lax.dot_general(ones, acc, NT, precision=HIGH, preferred_element_type=F32)
 
 
-def add_kernel(a_ref, b_ref, out_ref):
-    out_ref[...] = a_ref[...] + b_ref[...]
-
-
 def mixed_kernel(heads, columns, lin_ref, gain_ref, *rest):
     squares, out_ref = rest[:-1], rest[-1]
     total = squares[0][...]
@@ -212,7 +208,7 @@
 
 
 def softmax_bias(group, sides, order_ref, bias):
-    tokens, span = bias.shape[0], bias.shape[1] // 2
+    tokens, span = bias.shape[0], bias.shape[1] // len(sides)
     groups = span // tokens
     me = lax.axis_index("ctx")
     rank, mine = lax.rem(me, group), lax.div(me, group)
@@ -227,7 +223,7 @@
 
 def softmax_values(held, g, kv_heads, values):
     span = held[0].shape[0]
-    values[:, HD:] = jnp.ones((2 * span, HD), BF16)
+    values[:, HD:] = jnp.ones((span * len(held), HD), BF16)
     for i, ref in enumerate(held):
         values[i * span : (i + 1) * span, :HD] = ref[:, head_cols(kv_heads + g)]
 
@@ -248,16 +244,17 @@
 SCORE = math.log2(math.e) / math.sqrt(HD)
 
 
-def softmax_first_kernel(group, sides, kv_heads, pack, order_ref, q_ref, a_ref, b_ref, *rest):
+def softmax_first_kernel(group, sides, kv_heads, pack, order_ref, q_ref, *rest):
+    arrays, rest = rest[: len(sides)], rest[len(sides) :]
     acc_ref, tops, (values, bias) = rest[0], rest[1:-2], rest[-2:]
     tokens = q_ref.shape[0]
     share = q_ref.shape[1] // HD // kv_heads
     softmax_bias(group, sides, order_ref, bias)
     for g in range(kv_heads):
-        softmax_values((a_ref, b_ref), g, kv_heads, values)
+        softmax_values(arrays, g, kv_heads, values)
         for j in range(0, share, pack):
             heads = range(g * share + j, g * share + j + pack)
-            raw = softmax_scores(stacked(q_ref, map(head_cols, heads)), (a_ref, b_ref), g, bias)
+            raw = softmax_scores(stacked(q_ref, map(head_cols, heads)), arrays, g, bias)
             top = jnp.max(raw, axis=-1, keepdims=True)
             probs = jnp.exp2((raw - top) * SCORE).astype(BF16)
             acc = jnp.dot(probs, values[...], preferred_element_type=F32)
@@ -267,17 +264,18 @@
                 tops[g][:, j + i : j + i + 1] = top[rows]
 
 
-def softmax_last_kernel(group, sides, kv_heads, pack, order_ref, q_ref, a_ref, b_ref, *rest):
+def softmax_last_kernel(group, sides, kv_heads, pack, order_ref, q_ref, *rest):
+    arrays, rest = rest[: len(sides)], rest[len(sides) :]
     acc_ref, tops, (out_ref, done_ref, values, bias) = rest[0], rest[1:-4], rest[-4:]
     tokens = q_ref.shape[0]
     share = q_ref.shape[1] // HD // kv_heads
     done_ref[...] = jnp.zeros_like(done_ref)
     softmax_bias(group, sides, order_ref, bias)
     for g in range(kv_heads):
-        softmax_values((a_ref, b_ref), g, kv_heads, values)
+        softmax_values(arrays, g, kv_heads, values)
         for j in range(0, share, pack):
             heads = range(g * share + j, g * share + j + pack)
-            raw = softmax_scores(stacked(q_ref, map(head_cols, heads)), (a_ref, b_ref), g, bias)
+            raw = softmax_scores(stacked(q_ref, map(head_cols, heads)), arrays, g, bias)
             old = stacked(tops[g], [slice(j + i, j + i + 1) for i in range(pack)])
             top = jnp.maximum(old, jnp.max(raw, axis=-1, keepdims=True))
             probs = jnp.exp2((raw - top) * SCORE).astype(BF16)
@@ -417,37 +415,41 @@
         after=(total,) if groups > 1 else (intra,),
         flops=1 << 32,
     )
-    near, side = swap(own, 1), swap(own, 2)
+    side, near = swap(own, 2), swap(own, 1)
+    half = shape((own.shape[0] // 2, own.shape[1]), BF16)
+    upper, under = call(halves_kernel, "sent_on", [half] * 2, (side, near))
+    across = jnp.concatenate([swap(upper, 1), swap(under, 2)])
     share = width // kv_heads
     pack = 2 if share // HD % 2 == 0 else 1
-    span = 2 * own.shape[0]
-    scratch = [pltpu.VMEM((span, 2 * HD), BF16), pltpu.VMEM((tokens, span), F32)]
-    room = 24 + 16 * span * tokens * 4 // MIB
+    span = own.shape[0]
+    room = 24 + 48 * span * tokens * 4 // MIB
     smem = pl.BlockSpec(memory_space=pltpu.SMEM)
+
+    def scratch(count):
+        keys = count * span
+        return [pltpu.VMEM((keys, 2 * HD), BF16), pltpu.VMEM((tokens, keys), F32)]
+
     acc, *tops = call(
-        functools.partial(softmax_first_kernel, group, (0, 1), kv_heads, pack),
+        functools.partial(softmax_first_kernel, group, (0, 2, 1), kv_heads, pack),
         "softmax_first",
         [shape((tokens, 2 * width), F32)] + [shape((tokens, share // HD), F32)] * kv_heads,
-        (order, queries, own, near),
-        scratch,
+        (order, queries, own, side, near),
+        scratch(3),
+        flops=12 * tokens * width * span,
+        exps=3 * tokens * span * width // HD,
+        limit=room,
+        specs=[smem] + [VMEM] * 4,
+    )
+    attended, mark = call(
+        functools.partial(softmax_last_kernel, group, (3,), kv_heads, pack),
+        "softmax_last",
+        [shape((tokens, width), BF16), shape((8, HD), F32)],
+        (order, queries, across, acc, *tops),
+        scratch(1),
         flops=4 * tokens * width * span,
         exps=tokens * span * width // HD,
         limit=room,
-        specs=[smem] + [VMEM] * 3,
-    )
-    half = shape((own.shape[0] // 2, own.shape[1]), BF16)
-    upper, under = call(halves_kernel, "sent_on", [half] * 2, (near, side), after=tops[:1])
-    across = jnp.concatenate([swap(upper, 2), swap(under, 1)])
-    attended, mark = call(
-        functools.partial(softmax_last_kernel, group, (2, 3), kv_heads, pack),
-        "softmax_last",
-        [shape((tokens, width), BF16), shape((8, HD), F32)],
-        (order, queries, side, across, acc, *tops),
-        scratch,
-        flops=4 * tokens * width * span,
-        exps=tokens * span * width // HD,
-        limit=room,
-        specs=[smem] + [VMEM] * (4 + kv_heads),
+        specs=[smem] + [VMEM] * (3 + kv_heads),
     )
 
     lin, squares = call(
@@ -460,16 +462,10 @@
         after=tops[:1],
     )
     if nh & (nh - 1) == 0:
-        parts, shift = [squares], 1
-        while shift < nh:
-            held = parts[0]
-            if len(parts) > 1:
-                (held,) = call(add_kernel, "add", [shape((8, tokens), F32)], parts, after=(mark,))
-            parts = [held, lax.ppermute(held, "head", [(i, i ^ shift) for i in range(nh)])]
-            shift *= 2
+        turns = [[(i, i ^ d) for i in range(nh)] for d in range(nh - 1, 0, -1)]
     else:
         turns = [[(i, (i + d) % nh) for i in range(nh)] for d in range(1, nh)]
-        parts = [squares] + [lax.ppermute(squares, "head", turn) for turn in turns]
+    parts = [squares] + [lax.ppermute(squares, "head", turn) for turn in turns]
     (mixed,) = call(
         functools.partial(mixed_kernel, heads, float(width * nh)),
         "gated_norm",

time: 46.9 us -> 43.3 us (0.923)
  waiting for transfers between devices: 15.8 us -> 11.1 us
  Pallas kernels: 11.3 us -> 12 us
    ppermute x10, waiting for transfers between devices: 8.23 us -> 5.02 us  [swap(): return lax.ppermute(x, 'ctx', [(c, c ^ s) for c in range(n)])]
    ppermute x2 -> x3, waiting for transfers between devices: 2.11 us -> 0.01 us  [body(): parts = [squares] + [lax.ppermute(squares, 'head', turn) for turn in turns]]
    pallas_call x13 -> x12, Pallas kernels: 11.3 us -> 12 us  [call(): pl.pallas_call(run, name=name, out_shape=list(outs), in_specs=specs, scra...]
    ppermute x2, waiting for transfers between devices: 5.43 us -> 6.08 us  [ahead(): return lax.ppermute(x, 'ctx', [(c, (c + d * group) % n) for c in range(n)])]
    ppermute x2 -> x3, starting transfers between devices: 1.5 us -> 1.89 us  [body(): parts = [squares] + [lax.ppermute(squares, 'head', turn) for turn in turns]]
  transfers between devices with their start and end apart: 14 -> 15, of which waited for: 9 -> 5; matrix products, arithmetic and copies ran while one was open for 0% -> 0% of each run, Pallas kernels for 22% -> 25%
where the time goes in v7:
time: 43.3 us; the launch traced here: 43.1 us
  starting transfers between devices  17.7 us (41%)
  Pallas kernels  12 us (28%)
  waiting for transfers between devices  11.1 us (26%)
  between operations  1.45 us (3%)
  local copies, waits for them, and re-layouts  0.81 us (2%)
    pallas_call x12, Pallas kernels, call(): pl.pallas_call(run, name=name, out_shape=list(outs), in_specs=specs, scra...  12 us
    ppermute x10, starting transfers between devices, swap(): return lax.ppermute(x, 'ctx', [(c, c ^ s) for c in range(n)])  10.8 us
    ppermute x2, waiting for transfers between devices, ahead(): return lax.ppermute(x, 'ctx', [(c, (c + d * group) % n) for c in range(n)])  6.08 us
    ppermute x10, waiting for transfers between devices, swap(): return lax.ppermute(x, 'ctx', [(c, c ^ s) for c in range(n)])  5.02 us
    ppermute x2, starting transfers between devices, ahead(): return lax.ppermute(x, 'ctx', [(c, (c + d * group) % n) for c in range(n)])  4.97 us
    ppermute x3, starting transfers between devices, body(): parts = [squares] + [lax.ppermute(squares, 'head', turn) for turn in turns]  1.89 us
  transfers between devices with their start and end apart: 15, of which 5 were waited for; matrix products, arithmetic and copies ran while one was open for 0% of the time, Pallas kernels for 25%

profile of v7, /device:TPU:0, one launch (start us, length us, event | category | flops | bytes accessed | tf_op | source)
XLA Modules:
  0.0 43.1 jit_solution(7159191098132672757)
XLA Ops:
  0.7 0.7 %copy-done.5 = bf16[128,256]{1,0:T(8,128)(2,1)S(1)} copy-done((bf16[128,256]{1,0:T(8,128)(2,1)S(1)}, bf16[128,256]{1,0:T(8,128)(2,1)}, u32[]{:S(2)}) %copy-start.5) | copy-done | bytes 65560
  1.5 4.1 %collective-permute-start = (bf16[128,512]{1,0:T(8,128)(2,1)S(1)}, bf16[128,512]{1,0:T(8,128)(2,1)S(1)}, u32[]{:S(2)}, u32[]{:S(2)}) collective-permute-start(bf16[128,512]{1,0:T(8,128)(2,1)S(1)} %keys_beside_values.1.refs_0_), channel_id=1, source_target_pairs={{0,16},{4,20},{8,24},{12,28},{16,0},{20,4},{24,8},{28,12},{1,17},{... | collective-permute-start | bytes 393224 | tf_op jit(solution)/shard_map/ppermute | solution.py:333
  5.6 1.5 %block_states.1 = (bf16[528,128]{1,0:T(8,128)(2,1)S(1)}, bf16[528,128]{1,0:T(8,128)(2,1)S(1)}, bf16[528,128]{1,0:T(8,128)(2,1)S(1)}, bf16[528,128]{1,0:T(8,128)(...) custom-call(f32[128,128]{1,0:T(8,128)S(1)} %get-tuple-element.27.refs_0_.refs_2_, ...), custom_call_target="tpu_custom_call" | custom-call | flops 134217728 | bytes 2711552 | tf_op jit(solution)/shard_map/block_states/pallas_call | solution.py:301
  7.2 2.6 %collective-permute-start.1 = (bf16[528,128]{1,0:T(8,128)(2,1)S(1)}, bf16[528,128]{1,0:T(8,128)(2,1)S(1)}, u32[]{:S(2)}, u32[]{:S(2)}) collective-permute-start(bf16[528,128]{1,0:T(8,128)(2,1)S(1)} %get-tuple-element.35), channel_id=1, source_target_pairs={{0,12},{4,8},{8,4},{12,0},{16,28},{20,24},{24,20},{28,16},{1,13},{... | collective-permute-start | bytes 405512 | tf_op jit(solution)/shard_map/ppermute | solution.py:327
  9.8 0.4 %collective-permute-start.2 = (bf16[528,128]{1,0:T(8,128)(2,1)S(1)}, bf16[528,128]{1,0:T(8,128)(2,1)S(1)}, u32[]{:S(2)}, u32[]{:S(2)}) collective-permute-start(bf16[528,128]{1,0:T(8,128)(2,1)S(1)} %get-tuple-element.36), channel_id=1, source_target_pairs={{0,8},{4,12},{8,0},{12,4},{16,24},{20,28},{24,16},{28,20},{1,9},{5... | collective-permute-start | bytes 405512 | tf_op jit(solution)/shard_map/ppermute | solution.py:327
  10.2 0.5 %collective-permute-start.3 = (bf16[528,128]{1,0:T(8,128)(2,1)S(1)}, bf16[528,128]{1,0:T(8,128)(2,1)S(1)}, u32[]{:S(2)}, u32[]{:S(2)}) collective-permute-start(bf16[528,128]{1,0:T(8,128)(2,1)S(1)} %get-tuple-element.37), channel_id=1, source_target_pairs={{0,4},{4,0},{8,12},{12,8},{16,20},{20,16},{24,28},{28,24},{1,5},{5... | collective-permute-start | bytes 405512 | tf_op jit(solution)/shard_map/ppermute | solution.py:327
  10.7 1.3 %collective-permute-done.refs_8_.refs_1_ = bf16[128,512]{1,0:T(8,128)(2,1)S(1)} collective-permute-done((bf16[128,512]{1,0:T(8,128)(2,1)S(1)}, bf16[128,512]{1,0:T(8,128)(2,1)S(1)}, u32[]{:S(2)}, u32[]{:S(2)}) %collective-permute-start) | collective-permute-done | bytes 131104 | tf_op jit(solution)/shard_map/ppermute | solution.py:333
  12.0 2.8 %intra_block.1 = (f32[128,2048]{1,0:T(8,128)S(1)}, bf16[128,2048]{1,0:T(8,128)(2,1)S(1)}, f32[128,2048]{1,0:T(8,128)S(1)}, f32[128,16]{1,0:T(8,128)S(1)}) custom-call(f32[128,128]{1,0:T(8,128)S(1)} %get-tuple-element.27.refs_0_.refs_2_, f32[128,128]{1,0:T(8,128)S(1)} %get-tuple-element.28.refs_1_, f32[16,128]{1,0:T(8,128)S(1)} %copy-done.7, ...), custom_call_target="tpu_custom_call" | custom-call | flops 134217728 | bytes 4874240 | tf_op jit(solution)/shard_map/intra_block/pallas_call | solution.py:301
  14.8 0.9 %collective-permute-done.1.refs_1_ = bf16[528,128]{1,0:T(8,128)(2,1)S(1)} collective-permute-done((bf16[528,128]{1,0:T(8,128)(2,1)S(1)}, bf16[528,128]{1,0:T(8,128)(2,1)S(1)}, u32[]{:S(2)}, u32[]{:S(2)}) %collective-permute-start.1) | collective-permute-done | bytes 135200 | tf_op jit(solution)/shard_map/ppermute | solution.py:327
  15.7 2.0 %collective-permute-done.2.refs_2_ = bf16[528,128]{1,0:T(8,128)(2,1)S(1)} collective-permute-done((bf16[528,128]{1,0:T(8,128)(2,1)S(1)}, bf16[528,128]{1,0:T(8,128)(2,1)S(1)}, u32[]{:S(2)}, u32[]{:S(2)}) %collective-permute-start.2) | collective-permute-done | bytes 135200 | tf_op jit(solution)/shard_map/ppermute | solution.py:327
  17.9 0.9 %collective-permute-start.4 = (bf16[528,128]{1,0:T(8,128)(2,1)S(1)}, bf16[528,128]{1,0:T(8,128)(2,1)S(1)}, u32[]{:S(2)}, u32[]{:S(2)}) collective-permute-start(bf16[528,128]{1,0:T(8,128)(2,1)S(1)} %group_state.1.refs_2_), channel_id=1, source_target_pairs={{0,16},{4,20},{8,24},{12,28},{16,0},{20,4},{24,8},{28,12},{1,17},{... | collective-permute-start | bytes 405512 | tf_op jit(solution)/shard_map/ppermute | solution.py:333
  18.8 2.5 %collective-permute-start.8 = (bf16[256,512]{1,0:T(8,128)(2,1)S(1)}, bf16[256,512]{1,0:T(8,128)(2,1)S(1)}, u32[]{:S(2)}, u32[]{:S(2)}) collective-permute-start(bf16[256,512]{1,0:T(8,128)(2,1)S(1)} %stack_keys_values.1.refs_2_), channel_id=1, source_target_pairs={{0,8},{4,12},{8,0},{12,4},{16,24},{20,28},{24,16},{28,20},{1,9},{5... | collective-permute-start | bytes 786440 | tf_op jit(solution)/shard_map/ppermute | solution.py:327
  21.4 0.5 %collective-permute-start.9 = (bf16[256,512]{1,0:T(8,128)(2,1)S(1)}, bf16[256,512]{1,0:T(8,128)(2,1)S(1)}, u32[]{:S(2)}, u32[]{:S(2)}) collective-permute-start(bf16[256,512]{1,0:T(8,128)(2,1)S(1)} %stack_keys_values.1.refs_2_), channel_id=1, source_target_pairs={{0,4},{4,0},{8,12},{12,8},{16,20},{20,16},{24,28},{28,24},{1,5},{5... | collective-permute-start | bytes 786440 | tf_op jit(solution)/shard_map/ppermute | solution.py:327
  21.8 4.8 %collective-permute-done.4.refs_4_ = bf16[528,128]{1,0:T(8,128)(2,1)S(1)} collective-permute-done((bf16[528,128]{1,0:T(8,128)(2,1)S(1)}, bf16[528,128]{1,0:T(8,128)(2,1)S(1)}, u32[]{:S(2)}, u32[]{:S(2)}) %collective-permute-start.4) | collective-permute-done | bytes 135200 | tf_op jit(solution)/shard_map/ppermute | solution.py:333
  26.9 2.1 %collective-permute-start.6 = (bf16[512,128]{1,0:T(8,128)(2,1)S(1)}, bf16[512,128]{1,0:T(8,128)(2,1)S(1)}, u32[]{:S(2)}, u32[]{:S(2)}) collective-permute-start(bf16[512,128]{1,0:T(8,128)(2,1)S(1)} %get-tuple-element.40), channel_id=1, source_target_pairs={{0,8},{4,12},{8,0},{12,4},{16,24},{20,28},{24,16},{28,20},{1,9},{5... | collective-permute-start | bytes 393224 | tf_op jit(solution)/shard_map/ppermute | solution.py:327
  29.0 1.4 %collective-permute-start.7 = (bf16[512,128]{1,0:T(8,128)(2,1)S(1)}, bf16[512,128]{1,0:T(8,128)(2,1)S(1)}, u32[]{:S(2)}, u32[]{:S(2)}) collective-permute-start(bf16[512,128]{1,0:T(8,128)(2,1)S(1)} %get-tuple-element.41), channel_id=1, source_target_pairs={{0,4},{4,0},{8,12},{12,8},{16,20},{20,16},{24,28},{28,24},{1,5},{5... | collective-permute-start | bytes 393224 | tf_op jit(solution)/shard_map/ppermute | solution.py:327
  30.4 0.7 %collective-permute-start.13 = (bf16[128,512]{1,0:T(8,128)(2,1)S(1)}, bf16[128,512]{1,0:T(8,128)(2,1)S(1)}, u32[]{:S(2)}, u32[]{:S(2)}) collective-permute-start(bf16[128,512]{1,0:T(8,128)(2,1)S(1)} %get-tuple-element.46), channel_id=1, source_target_pairs={{0,4},{4,0},{8,12},{12,8},{16,20},{20,16},{24,28},{28,24},{1,5},{5... | collective-permute-start | bytes 393224 | tf_op jit(solution)/shard_map/ppermute | solution.py:327
  31.8 2.4 %softmax_first.1 = (f32[128,4096]{1,0:T(8,128)S(1)}, f32[128,8]{1,0:T(8,128)S(1)}, f32[128,8]{1,0:T(8,128)S(1)}) custom-call(s32[1]{0:T(128)S(6)} %copy.12.refs_0_, bf16[128,2048]{1,0:T(8,128)(2,1)S(1)} %copy-done, bf16[256,512]{1,0:T(8,128)(2,1)S(1)} %stack_keys_values.1.refs_2_, bf16[256,512]{1,0:T(8,128)(2,1)S(1)} %collective-permute-done.8.refs_3_.refs_0_, ...), custom_call_target="tpu_custom_call" | custom-call | flops 805306368 | bytes 3416068 | tf_op jit(solution)/shard_map/softmax_first/pallas_call | solution.py:301
  34.2 2.0 %collective-permute-done.6.refs_5_ = bf16[512,128]{1,0:T(8,128)(2,1)S(1)} collective-permute-done((bf16[512,128]{1,0:T(8,128)(2,1)S(1)}, bf16[512,128]{1,0:T(8,128)(2,1)S(1)}, u32[]{:S(2)}, u32[]{:S(2)}) %collective-permute-start.6) | collective-permute-done | bytes 131104 | tf_op jit(solution)/shard_map/ppermute | solution.py:327
  36.2 0.7 %inter_block.1 = (f32[128,2048]{1,0:T(8,128)S(1)}, f32[8,128]{1,0:T(8,128)S(1)}) custom-call(f32[128,16]{1,0:T(8,128)S(1)} %get-tuple-element.31.refs_0_, bf16[128,2048]{1,0:T(8,128)(2,1)S(1)} %get-tuple-element.32.refs_1_, f32[128,2048]{1,0:T(8,128)S(1)} %get-tuple-element.33.refs_4_.refs_2_, bf16[512,128]{1,0:T(8,128)(2,1)S(1)} %get-tuple-element.38.refs_3_, ...), custom_call_target="tpu_custom_call" | custom-call | flops 67108864 | bytes 3158016 | tf_op jit(solution)/shard_map/inter_block/pallas_call | solution.py:301
  36.9 0.7 %collective-permute-start.10 = (f32[8,128]{1,0:T(8,128)S(1)}, f32[8,128]{1,0:T(8,128)S(1)}, u32[]{:S(2)}, u32[]{:S(2)}) collective-permute-start(f32[8,128]{1,0:T(8,128)S(1)} %get-tuple-element.45.refs_2_), channel_id=1, source_target_pairs={{0,3},{1,2},{2,1},{3,0},{4,7},{5,6},{6,5},{7,4},{8,11},{9,10},{10,... | collective-permute-start | bytes 12296 | tf_op jit(solution)/shard_map/ppermute | solution.py:468
  37.6 0.8 %collective-permute-start.11 = (f32[8,128]{1,0:T(8,128)S(1)}, f32[8,128]{1,0:T(8,128)S(1)}, u32[]{:S(2)}, u32[]{:S(2)}) collective-permute-start(f32[8,128]{1,0:T(8,128)S(1)} %get-tuple-element.45.refs_2_), channel_id=1, source_target_pairs={{0,2},{1,3},{2,0},{3,1},{4,6},{5,7},{6,4},{7,5},{8,10},{9,11},{10,... | collective-permute-start | bytes 12296 | tf_op jit(solution)/shard_map/ppermute | solution.py:468
  38.8 3.3 %softmax_last.1 = (bf16[128,2048]{1,0:T(8,128)(2,1)}, f32[8,128]{1,0:T(8,128)S(1)}) custom-call(s32[1]{0:T(128)S(6)} %copy.12.refs_0_, bf16[128,2048]{1,0:T(8,128)(2,1)S(1)} %copy-done, bf16[256,512]{1,0:T(8,128)(2,1)S(1)} %pad_maximum_fusion.refs_2_, f32[128,4096]{1,0:T(8,128)S(1)} %get-tuple-element.48.refs_3_, ...), custom_call_target="tpu_custom_call" | custom-call | flops 268435456 | bytes 3420164 | tf_op jit(solution)/shard_map/softmax_last/pallas_call | solution.py:301
  42.1 1.1 %gated_norm.1 = bf16[128,2048]{1,0:T(8,128)(2,1)} custom-call(f32[128,2048]{1,0:T(8,128)S(1)} %get-tuple-element.43.refs_0_, f32[128,2048]{1,0:T(8,128)S(1)} %get-tuple-element.44.refs_1_, f32[8,128]{1,0:T(8,128)S(1)} %get-tuple-element.45.refs_2_, f32[8,128]{1,0:T(8,128)S(1)} %collective-permute-done.10.refs_3_, ...), custom_call_target="tpu_custom_call" | custom-call | flops 1048576 | bytes 2637824 | tf_op jit(solution)/shard_map/gated_norm/pallas_call | solution.py:301
  (37 shorter events, 0.9 us)
Async XLA Ops:
  0.6 0.8 %copy-start.5 = (bf16[128,256]{1,0:T(8,128)(2,1)S(1)}, bf16[128,256]{1,0:T(8,128)(2,1)}, u32[]{:S(2)}) copy-start(bf16[128,256]{1,0:T(8,128)(2,1)} %refs_0_.3) | copy-start | bytes 196612
  0.6 0.9 %copy-start.6 = (bf16[128,256]{1,0:T(8,128)(2,1)S(1)}, bf16[128,256]{1,0:T(8,128)(2,1)}, u32[]{:S(2)}) copy-start(bf16[128,256]{1,0:T(8,128)(2,1)} %refs_1_.5) | copy-start | bytes 196612
  0.7 5.0 %copy-start.1 = (bf16[128,2048]{1,0:T(8,128)(2,1)S(1)}, bf16[128,2048]{1,0:T(8,128)(2,1)}, u32[]{:S(2)}) copy-start(bf16[128,2048]{1,0:T(8,128)(2,1)} %refs_2_.2) | copy-start | bytes 1572868
  0.7 5.0 %copy-start.2 = (bf16[128,2048]{1,0:T(8,128)(2,1)S(1)}, bf16[128,2048]{1,0:T(8,128)(2,1)}, u32[]{:S(2)}) copy-start(bf16[128,2048]{1,0:T(8,128)(2,1)} %refs_3_.2) | copy-start | bytes 1572868
  0.7 5.0 %copy-start.7 = (f32[16,128]{1,0:T(8,128)S(1)}, f32[16,128]{1,0:T(8,128)}, u32[]{:S(2)}) copy-start(f32[16,128]{1,0:T(8,128)} %refs_2_.3) | copy-start | bytes 24580
  0.7 11.3 %copy-start.8 = (f32[2048]{0:T(1024)S(1)}, f32[2048]{0:T(1024)}, u32[]{:S(2)}) copy-start(f32[2048]{0:T(1024)} %param.15) | copy-start | bytes 24580
  0.7 11.3 %copy-start.3 = (bf16[128,2048]{1,0:T(8,128)(2,1)S(1)}, bf16[128,2048]{1,0:T(8,128)(2,1)}, u32[]{:S(2)}) copy-start(bf16[128,2048]{1,0:T(8,128)(2,1)} %refs_3_.3) | copy-start | bytes 1572868
  0.7 11.3 %copy-start.4 = (bf16[128,2048]{1,0:T(8,128)(2,1)S(1)}, bf16[128,2048]{1,0:T(8,128)(2,1)}, u32[]{:S(2)}) copy-start(bf16[128,2048]{1,0:T(8,128)(2,1)} %refs_6_.1) | copy-start | bytes 1572868
  1.5 10.5 %collective-permute-start = (bf16[128,512]{1,0:T(8,128)(2,1)S(1)}, bf16[128,512]{1,0:T(8,128)(2,1)S(1)}, u32[]{:S(2)}, u32[]{:S(2)}) collective-permute-start(bf16[128,512]{1,0:T(8,128)(2,1)S(1)} %keys_beside_values.1.refs_0_), channel_id=1, source_target_pairs={{0,16},{4,20},{8,24},{12,28},{16,0},{20,4},{24,8},{28,12},{1,17},{... | collective-permute-start | bytes 393224 | tf_op jit(solution)/shard_map/ppermute | solution.py:333
  7.2 8.6 %collective-permute-start.1 = (bf16[528,128]{1,0:T(8,128)(2,1)S(1)}, bf16[528,128]{1,0:T(8,128)(2,1)S(1)}, u32[]{:S(2)}, u32[]{:S(2)}) collective-permute-start(bf16[528,128]{1,0:T(8,128)(2,1)S(1)} %get-tuple-element.35), channel_id=1, source_target_pairs={{0,12},{4,8},{8,4},{12,0},{16,28},{20,24},{24,20},{28,16},{1,13},{... | collective-permute-start | bytes 405512 | tf_op jit(solution)/shard_map/ppermute | solution.py:327
  9.8 8.0 %collective-permute-start.2 = (bf16[528,128]{1,0:T(8,128)(2,1)S(1)}, bf16[528,128]{1,0:T(8,128)(2,1)S(1)}, u32[]{:S(2)}, u32[]{:S(2)}) collective-permute-start(bf16[528,128]{1,0:T(8,128)(2,1)S(1)} %get-tuple-element.36), channel_id=1, source_target_pairs={{0,8},{4,12},{8,0},{12,4},{16,24},{20,28},{24,16},{28,20},{1,9},{5... | collective-permute-start | bytes 405512 | tf_op jit(solution)/shard_map/ppermute | solution.py:327
  10.2 7.6 %collective-permute-start.3 = (bf16[528,128]{1,0:T(8,128)(2,1)S(1)}, bf16[528,128]{1,0:T(8,128)(2,1)S(1)}, u32[]{:S(2)}, u32[]{:S(2)}) collective-permute-start(bf16[528,128]{1,0:T(8,128)(2,1)S(1)} %get-tuple-element.37), channel_id=1, source_target_pairs={{0,4},{4,0},{8,12},{12,8},{16,20},{20,16},{24,28},{28,24},{1,5},{5... | collective-permute-start | bytes 405512 | tf_op jit(solution)/shard_map/ppermute | solution.py:327
  17.9 8.7 %collective-permute-start.4 = (bf16[528,128]{1,0:T(8,128)(2,1)S(1)}, bf16[528,128]{1,0:T(8,128)(2,1)S(1)}, u32[]{:S(2)}, u32[]{:S(2)}) collective-permute-start(bf16[528,128]{1,0:T(8,128)(2,1)S(1)} %group_state.1.refs_2_), channel_id=1, source_target_pairs={{0,16},{4,20},{8,24},{12,28},{16,0},{20,4},{24,8},{28,12},{1,17},{... | collective-permute-start | bytes 405512 | tf_op jit(solution)/shard_map/ppermute | solution.py:333
  18.8 13.0 %copy-start = (bf16[128,2048]{1,0:T(8,128)(2,1)S(1)}, bf16[128,2048]{1,0:T(8,128)(2,1)}, u32[]{:S(2)}) copy-start(bf16[128,2048]{1,0:T(8,128)(2,1)} %refs_1_.7) | copy-start | bytes 1572868
  18.8 11.5 %collective-permute-start.8 = (bf16[256,512]{1,0:T(8,128)(2,1)S(1)}, bf16[256,512]{1,0:T(8,128)(2,1)S(1)}, u32[]{:S(2)}, u32[]{:S(2)}) collective-permute-start(bf16[256,512]{1,0:T(8,128)(2,1)S(1)} %stack_keys_values.1.refs_2_), channel_id=1, source_target_pairs={{0,8},{4,12},{8,0},{12,4},{16,24},{20,28},{24,16},{28,20},{1,9},{5... | collective-permute-start | bytes 786440 | tf_op jit(solution)/shard_map/ppermute | solution.py:327
  21.4 9.0 %collective-permute-start.9 = (bf16[256,512]{1,0:T(8,128)(2,1)S(1)}, bf16[256,512]{1,0:T(8,128)(2,1)S(1)}, u32[]{:S(2)}, u32[]{:S(2)}) collective-permute-start(bf16[256,512]{1,0:T(8,128)(2,1)S(1)} %stack_keys_values.1.refs_2_), channel_id=1, source_target_pairs={{0,4},{4,0},{8,12},{12,8},{16,20},{20,16},{24,28},{28,24},{1,5},{5... | collective-permute-start | bytes 786440 | tf_op jit(solution)/shard_map/ppermute | solution.py:327
  26.8 7.4 %collective-permute-start.5 = (bf16[512,128]{1,0:T(8,128)(2,1)S(1)}, bf16[512,128]{1,0:T(8,128)(2,1)S(1)}, u32[]{:S(2)}, u32[]{:S(2)}) collective-permute-start(bf16[512,128]{1,0:T(8,128)(2,1)S(1)} %get-tuple-element.39), channel_id=1, source_target_pairs={{0,12},{4,8},{8,4},{12,0},{16,28},{20,24},{24,20},{28,16},{1,13},{... | collective-permute-start | bytes 393224 | tf_op jit(solution)/shard_map/ppermute | solution.py:327
  26.9 9.3 %collective-permute-start.6 = (bf16[512,128]{1,0:T(8,128)(2,1)S(1)}, bf16[512,128]{1,0:T(8,128)(2,1)S(1)}, u32[]{:S(2)}, u32[]{:S(2)}) collective-permute-start(bf16[512,128]{1,0:T(8,128)(2,1)S(1)} %get-tuple-element.40), channel_id=1, source_target_pairs={{0,8},{4,12},{8,0},{12,4},{16,24},{20,28},{24,16},{28,20},{1,9},{5... | collective-permute-start | bytes 393224 | tf_op jit(solution)/shard_map/ppermute | solution.py:327
  29.0 7.2 %collective-permute-start.7 = (bf16[512,128]{1,0:T(8,128)(2,1)S(1)}, bf16[512,128]{1,0:T(8,128)(2,1)S(1)}, u32[]{:S(2)}, u32[]{:S(2)}) collective-permute-start(bf16[512,128]{1,0:T(8,128)(2,1)S(1)} %get-tuple-element.41), channel_id=1, source_target_pairs={{0,4},{4,0},{8,12},{12,8},{16,20},{20,16},{24,28},{28,24},{1,5},{5... | collective-permute-start | bytes 393224 | tf_op jit(solution)/shard_map/ppermute | solution.py:327
  30.4 8.4 %collective-permute-start.13 = (bf16[128,512]{1,0:T(8,128)(2,1)S(1)}, bf16[128,512]{1,0:T(8,128)(2,1)S(1)}, u32[]{:S(2)}, u32[]{:S(2)}) collective-permute-start(bf16[128,512]{1,0:T(8,128)(2,1)S(1)} %get-tuple-element.46), channel_id=1, source_target_pairs={{0,4},{4,0},{8,12},{12,8},{16,20},{20,16},{24,28},{28,24},{1,5},{5... | collective-permute-start | bytes 393224 | tf_op jit(solution)/shard_map/ppermute | solution.py:327
  31.1 7.7 %collective-permute-start.14 = (bf16[128,512]{1,0:T(8,128)(2,1)S(1)}, bf16[128,512]{1,0:T(8,128)(2,1)S(1)}, u32[]{:S(2)}, u32[]{:S(2)}) collective-permute-start(bf16[128,512]{1,0:T(8,128)(2,1)S(1)} %get-tuple-element.47), channel_id=1, source_target_pairs={{0,8},{4,12},{8,0},{12,4},{16,24},{20,28},{24,16},{28,20},{1,9},{5... | collective-permute-start | bytes 393224 | tf_op jit(solution)/shard_map/ppermute | solution.py:327
  36.9 5.2 %collective-permute-start.10 = (f32[8,128]{1,0:T(8,128)S(1)}, f32[8,128]{1,0:T(8,128)S(1)}, u32[]{:S(2)}, u32[]{:S(2)}) collective-permute-start(f32[8,128]{1,0:T(8,128)S(1)} %get-tuple-element.45.refs_2_), channel_id=1, source_target_pairs={{0,3},{1,2},{2,1},{3,0},{4,7},{5,6},{6,5},{7,4},{8,11},{9,10},{10,... | collective-permute-start | bytes 12296 | tf_op jit(solution)/shard_map/ppermute | solution.py:468
  37.6 4.4 %collective-permute-start.11 = (f32[8,128]{1,0:T(8,128)S(1)}, f32[8,128]{1,0:T(8,128)S(1)}, u32[]{:S(2)}, u32[]{:S(2)}) collective-permute-start(f32[8,128]{1,0:T(8,128)S(1)} %get-tuple-element.45.refs_2_), channel_id=1, source_target_pairs={{0,2},{1,3},{2,0},{3,1},{4,6},{5,7},{6,4},{7,5},{8,10},{9,11},{10,... | collective-permute-start | bytes 12296 | tf_op jit(solution)/shard_map/ppermute | solution.py:468
  38.4 3.6 %collective-permute-start.12 = (f32[8,128]{1,0:T(8,128)S(1)}, f32[8,128]{1,0:T(8,128)S(1)}, u32[]{:S(2)}, u32[]{:S(2)}) collective-permute-start(f32[8,128]{1,0:T(8,128)S(1)} %get-tuple-element.45.refs_2_), channel_id=1, source_target_pairs={{0,1},{1,0},{2,3},{3,2},{4,5},{5,4},{6,7},{7,6},{8,9},{9,8},{10,11... | collective-permute-start | bytes 12296 | tf_op jit(solution)/shard_map/ppermute | solution.py:468

commit v8 on v7

--- a/solution.py
+++ b/solution.py
@@ -20,9 +20,18 @@
 HBM = pl.BlockSpec(memory_space=pltpu.HBM)
 
 
+def inverse(x):
+    guess = pl.reciprocal(x, approx=True)
+    return guess * (2.0 - x * guess)
+
+
+def sigmoid(x):
+    return inverse(1.0 + jnp.exp(-x))
+
+
 def silu16(x):
     x = x.astype(F32)
-    return (x / (1.0 + jnp.exp(-x))).astype(BF16)
+    return (x * sigmoid(x)).astype(BF16)
 
 
 def lower_ones(size):
@@ -172,8 +181,7 @@
         decay = jnp.exp((cum[:, h : h + 1] - cum_t[h : h + 1, :]) + bias)
         weights = (scores * decay).astype(BF16)
         intra_ref[:, cols] = jnp.dot(weights, va_ref[:, cols], preferred_element_type=F32)
-        gate = 1.0 / (1.0 + jnp.exp(-gate_ref[:, cols].astype(F32)))
-        gain_out[:, cols] = gate * gain_ref[:, cols]
+        gain_out[:, cols] = sigmoid(gate_ref[:, cols].astype(F32)) * gain_ref[:, cols]
 
 
 def inter_kernel(group, heads, decay_ref, qa_ref, intra_ref, *rest):
@@ -196,15 +204,26 @@
     squares_ref[...] = lax.dot_general(ones, acc, NT, precision=HIGH, preferred_element_type=F32)
 
 
-def mixed_kernel(heads, columns, lin_ref, gain_ref, *rest):
-    squares, out_ref = rest[:-1], rest[-1]
+def results_kernel(columns, parts, attended_ref, lin_ref, gain_ref, *rest):
+    squares, (mixed_out, attended_out, mixed_ref, sems) = rest[:-4], rest[-4:]
+    first = pltpu.make_async_copy(attended_ref, attended_out, sems.at[parts])
+    first.start()
     total = squares[0][...]
     for part in squares[1:]:
         total = total + part[...]
     inv = jnp.transpose(lax.rsqrt(total / columns + EPS))[:, 0:1]
-    for h in range(heads):
-        cols = head_cols(h)
-        out_ref[:, cols] = (lin_ref[:, cols] * inv * gain_ref[:, cols]).astype(BF16)
+    width = lin_ref.shape[1] // parts
+    copies = []
+    for i in range(parts):
+        cols = slice(i * width, (i + 1) * width)
+        mixed_ref[:, cols] = (lin_ref[:, cols] * inv * gain_ref[:, cols]).astype(BF16)
+        copies.append(
+            pltpu.make_async_copy(mixed_ref.at[:, cols], mixed_out.at[:, cols], sems.at[i])
+        )
+        copies[-1].start()
+    for copy in copies:
+        copy.wait()
+    first.wait()
 
 
 def softmax_bias(group, sides, order_ref, bias):
@@ -266,10 +285,9 @@
 
 def softmax_last_kernel(group, sides, kv_heads, pack, order_ref, q_ref, *rest):
     arrays, rest = rest[: len(sides)], rest[len(sides) :]
-    acc_ref, tops, (out_ref, done_ref, values, bias) = rest[0], rest[1:-4], rest[-4:]
+    acc_ref, tops, (out_ref, values, bias) = rest[0], rest[1:-3], rest[-3:]
     tokens = q_ref.shape[0]
     share = q_ref.shape[1] // HD // kv_heads
-    done_ref[...] = jnp.zeros_like(done_ref)
     softmax_bias(group, sides, order_ref, bias)
     for g in range(kv_heads):
         softmax_values(arrays, g, kv_heads, values)
@@ -282,7 +300,7 @@
             acc = jnp.dot(probs, values[...], preferred_element_type=F32)
             held = stacked(acc_ref, [slice(2 * h * HD, 2 * (h + 1) * HD) for h in heads])
             acc += held * jnp.exp2((old - top) * SCORE)
-            out = (acc[:, :HD] / acc[:, HD:]).astype(BF16)
+            out = (acc[:, :HD] * inverse(acc[:, HD:])).astype(BF16)
             for i, h in enumerate(heads):
                 out_ref[:, head_cols(h)] = out[i * tokens : (i + 1) * tokens]
 
@@ -440,10 +458,10 @@
         limit=room,
         specs=[smem] + [VMEM] * 4,
     )
-    attended, mark = call(
+    (attended,) = call(
         functools.partial(softmax_last_kernel, group, (3,), kv_heads, pack),
         "softmax_last",
-        [shape((tokens, width), BF16), shape((8, HD), F32)],
+        [shape((tokens, width), BF16)],
         (order, queries, across, acc, *tops),
         scratch(1),
         flops=4 * tokens * width * span,
@@ -466,15 +484,16 @@
     else:
         turns = [[(i, (i + d) % nh) for i in range(nh)] for d in range(1, nh)]
     parts = [squares] + [lax.ppermute(squares, "head", turn) for turn in turns]
-    (mixed,) = call(
-        functools.partial(mixed_kernel, heads, float(width * nh)),
-        "gated_norm",
-        [shape((tokens, width), BF16)],
-        (lin, gain, *parts),
+    pieces = 4 if width % (4 * HD) == 0 else 1
+    return call(
+        functools.partial(results_kernel, float(width * nh), pieces),
+        "results",
+        [shape((tokens, width), BF16)] * 2,
+        (attended, lin, gain, *parts),
+        [pltpu.VMEM((tokens, width), BF16), pltpu.SemaphoreType.DMA((pieces + 1,))],
         flops=4 * tokens * width,
-        after=(mark,),
-    )
-    return (mixed, attended)
+        out_specs=[HBM] * 2,
+    )
 
 
 def solution(mesh):

time: 43.3 us -> 43.1 us (level)
  Pallas kernels: 12 us -> 11.5 us
    pallas_call x12, Pallas kernels: 12 us -> 11.5 us  [call(): pl.pallas_call(run, name=name, out_shape=list(outs), in_specs=specs, scra...]
  transfers between devices with their start and end apart: 15 -> 15, of which waited for: 5 -> 7; matrix products, arithmetic and copies ran while one was open for 0% -> 0% of each run, Pallas kernels for 25% -> 24%
where the time goes in v8:
time: 43.1 us; the launch traced here: 42.9 us
  starting transfers between devices  17.7 us (41%)
  Pallas kernels  11.5 us (27%)
  waiting for transfers between devices  11.4 us (26%)
  between operations  1.46 us (3%)
  local copies, waits for them, and re-layouts  0.81 us (2%)
    pallas_call x12, Pallas kernels, call(): pl.pallas_call(run, name=name, out_shape=list(outs), in_specs=specs, scra...  11.5 us
    ppermute x10, starting transfers between devices, swap(): return lax.ppermute(x, 'ctx', [(c, c ^ s) for c in range(n)])  10.6 us
    ppermute x2, waiting for transfers between devices, ahead(): return lax.ppermute(x, 'ctx', [(c, (c + d * group) % n) for c in range(n)])  6.16 us
    ppermute x2, starting transfers between devices, ahead(): return lax.ppermute(x, 'ctx', [(c, (c + d * group) % n) for c in range(n)])  5.19 us
    ppermute x10, waiting for transfers between devices, swap(): return lax.ppermute(x, 'ctx', [(c, c ^ s) for c in range(n)])  5.16 us
    ppermute x3, starting transfers between devices, body(): parts = [squares] + [lax.ppermute(squares, 'head', turn) for turn in turns]  1.89 us
  transfers between devices with their start and end apart: 15, of which 7 were waited for; matrix products, arithmetic and copies ran while one was open for 0% of the time, Pallas kernels for 24%

profile of v8, /device:TPU:0, one launch (start us, length us, event | category | flops | bytes accessed | tf_op | source)
XLA Modules:
  0.0 42.9 jit_solution(13859755559108238301)
XLA Ops:
  0.7 0.7 %copy-done.5 = bf16[128,256]{1,0:T(8,128)(2,1)S(1)} copy-done((bf16[128,256]{1,0:T(8,128)(2,1)S(1)}, bf16[128,256]{1,0:T(8,128)(2,1)}, u32[]{:S(2)}) %copy-start.5) | copy-done | bytes 65560
  1.5 4.1 %collective-permute-start = (bf16[128,512]{1,0:T(8,128)(2,1)S(1)}, bf16[128,512]{1,0:T(8,128)(2,1)S(1)}, u32[]{:S(2)}, u32[]{:S(2)}) collective-permute-start(bf16[128,512]{1,0:T(8,128)(2,1)S(1)} %keys_beside_values.1.refs_0_), channel_id=1, source_target_pairs={{0,16},{4,20},{8,24},{12,28},{16,0},{20,4},{24,8},{28,12},{1,17},{... | collective-permute-start | bytes 393224 | tf_op jit(solution)/shard_map/ppermute | solution.py:351
  5.6 1.7 %block_states.1 = (bf16[528,128]{1,0:T(8,128)(2,1)S(1)}, bf16[528,128]{1,0:T(8,128)(2,1)S(1)}, bf16[528,128]{1,0:T(8,128)(2,1)S(1)}, bf16[528,128]{1,0:T(8,128)(...) custom-call(f32[128,128]{1,0:T(8,128)S(1)} %get-tuple-element.25.refs_2_.refs_0_, ...), custom_call_target="tpu_custom_call" | custom-call | flops 134217728 | bytes 2711552 | tf_op jit(solution)/shard_map/block_states/pallas_call | solution.py:319
  7.4 2.6 %collective-permute-start.1 = (bf16[528,128]{1,0:T(8,128)(2,1)S(1)}, bf16[528,128]{1,0:T(8,128)(2,1)S(1)}, u32[]{:S(2)}, u32[]{:S(2)}) collective-permute-start(bf16[528,128]{1,0:T(8,128)(2,1)S(1)} %get-tuple-element.27), channel_id=1, source_target_pairs={{0,12},{4,8},{8,4},{12,0},{16,28},{20,24},{24,20},{28,16},{1,13},{... | collective-permute-start | bytes 405512 | tf_op jit(solution)/shard_map/ppermute | solution.py:345
  10.0 0.4 %collective-permute-start.2 = (bf16[528,128]{1,0:T(8,128)(2,1)S(1)}, bf16[528,128]{1,0:T(8,128)(2,1)S(1)}, u32[]{:S(2)}, u32[]{:S(2)}) collective-permute-start(bf16[528,128]{1,0:T(8,128)(2,1)S(1)} %get-tuple-element.28), channel_id=1, source_target_pairs={{0,8},{4,12},{8,0},{12,4},{16,24},{20,28},{24,16},{28,20},{1,9},{5... | collective-permute-start | bytes 405512 | tf_op jit(solution)/shard_map/ppermute | solution.py:345
  10.4 0.5 %collective-permute-start.3 = (bf16[528,128]{1,0:T(8,128)(2,1)S(1)}, bf16[528,128]{1,0:T(8,128)(2,1)S(1)}, u32[]{:S(2)}, u32[]{:S(2)}) collective-permute-start(bf16[528,128]{1,0:T(8,128)(2,1)S(1)} %get-tuple-element.29), channel_id=1, source_target_pairs={{0,4},{4,0},{8,12},{12,8},{16,20},{20,16},{24,28},{28,24},{1,5},{5... | collective-permute-start | bytes 405512 | tf_op jit(solution)/shard_map/ppermute | solution.py:345
  10.9 1.1 %collective-permute-done.refs_8_.refs_1_ = bf16[128,512]{1,0:T(8,128)(2,1)S(1)} collective-permute-done((bf16[128,512]{1,0:T(8,128)(2,1)S(1)}, bf16[128,512]{1,0:T(8,128)(2,1)S(1)}, u32[]{:S(2)}, u32[]{:S(2)}) %collective-permute-start) | collective-permute-done | bytes 131104 | tf_op jit(solution)/shard_map/ppermute | solution.py:351
  12.0 2.8 %intra_block.1 = (f32[128,2048]{1,0:T(8,128)S(1)}, bf16[128,2048]{1,0:T(8,128)(2,1)S(1)}, f32[128,2048]{1,0:T(8,128)S(1)}, f32[128,16]{1,0:T(8,128)S(1)}) custom-call(f32[128,128]{1,0:T(8,128)S(1)} %get-tuple-element.25.refs_2_.refs_0_, f32[128,128]{1,0:T(8,128)S(1)} %get-tuple-element.30.refs_1_, f32[16,128]{1,0:T(8,128)S(1)} %copy-done.7, ...), custom_call_target="tpu_custom_call" | custom-call | flops 134217728 | bytes 4874240 | tf_op jit(solution)/shard_map/intra_block/pallas_call | solution.py:319
  14.8 1.1 %collective-permute-done.1.refs_1_ = bf16[528,128]{1,0:T(8,128)(2,1)S(1)} collective-permute-done((bf16[528,128]{1,0:T(8,128)(2,1)S(1)}, bf16[528,128]{1,0:T(8,128)(2,1)S(1)}, u32[]{:S(2)}, u32[]{:S(2)}) %collective-permute-start.1) | collective-permute-done | bytes 135200 | tf_op jit(solution)/shard_map/ppermute | solution.py:345
  16.0 1.8 %collective-permute-done.2.refs_2_ = bf16[528,128]{1,0:T(8,128)(2,1)S(1)} collective-permute-done((bf16[528,128]{1,0:T(8,128)(2,1)S(1)}, bf16[528,128]{1,0:T(8,128)(2,1)S(1)}, u32[]{:S(2)}, u32[]{:S(2)}) %collective-permute-start.2) | collective-permute-done | bytes 135200 | tf_op jit(solution)/shard_map/ppermute | solution.py:345
  17.9 1.1 %collective-permute-start.8 = (bf16[528,128]{1,0:T(8,128)(2,1)S(1)}, bf16[528,128]{1,0:T(8,128)(2,1)S(1)}, u32[]{:S(2)}, u32[]{:S(2)}) collective-permute-start(bf16[528,128]{1,0:T(8,128)(2,1)S(1)} %group_state.1.refs_2_), channel_id=1, source_target_pairs={{0,16},{4,20},{8,24},{12,28},{16,0},{20,4},{24,8},{28,12},{1,17},{... | collective-permute-start | bytes 405512 | tf_op jit(solution)/shard_map/ppermute | solution.py:351
  19.0 2.5 %collective-permute-start.4 = (bf16[256,512]{1,0:T(8,128)(2,1)S(1)}, bf16[256,512]{1,0:T(8,128)(2,1)S(1)}, u32[]{:S(2)}, u32[]{:S(2)}) collective-permute-start(bf16[256,512]{1,0:T(8,128)(2,1)S(1)} %stack_keys_values.1.refs_2_), channel_id=1, source_target_pairs={{0,8},{4,12},{8,0},{12,4},{16,24},{20,28},{24,16},{28,20},{1,9},{5... | collective-permute-start | bytes 786440 | tf_op jit(solution)/shard_map/ppermute | solution.py:345
  21.6 0.5 %collective-permute-start.5 = (bf16[256,512]{1,0:T(8,128)(2,1)S(1)}, bf16[256,512]{1,0:T(8,128)(2,1)S(1)}, u32[]{:S(2)}, u32[]{:S(2)}) collective-permute-start(bf16[256,512]{1,0:T(8,128)(2,1)S(1)} %stack_keys_values.1.refs_2_), channel_id=1, source_target_pairs={{0,4},{4,0},{8,12},{12,8},{16,20},{20,16},{24,28},{28,24},{1,5},{5... | collective-permute-start | bytes 786440 | tf_op jit(solution)/shard_map/ppermute | solution.py:345
  22.0 5.0 %collective-permute-done.8.refs_4_ = bf16[528,128]{1,0:T(8,128)(2,1)S(1)} collective-permute-done((bf16[528,128]{1,0:T(8,128)(2,1)S(1)}, bf16[528,128]{1,0:T(8,128)(2,1)S(1)}, u32[]{:S(2)}, u32[]{:S(2)}) %collective-permute-start.8) | collective-permute-done | bytes 135200 | tf_op jit(solution)/shard_map/ppermute | solution.py:351
  27.4 1.8 %collective-permute-start.10 = (bf16[512,128]{1,0:T(8,128)(2,1)S(1)}, bf16[512,128]{1,0:T(8,128)(2,1)S(1)}, u32[]{:S(2)}, u32[]{:S(2)}) collective-permute-start(bf16[512,128]{1,0:T(8,128)(2,1)S(1)} %get-tuple-element.43), channel_id=1, source_target_pairs={{0,8},{4,12},{8,0},{12,4},{16,24},{20,28},{24,16},{28,20},{1,9},{5... | collective-permute-start | bytes 393224 | tf_op jit(solution)/shard_map/ppermute | solution.py:345
  29.2 1.7 %collective-permute-start.11 = (bf16[512,128]{1,0:T(8,128)(2,1)S(1)}, bf16[512,128]{1,0:T(8,128)(2,1)S(1)}, u32[]{:S(2)}, u32[]{:S(2)}) collective-permute-start(bf16[512,128]{1,0:T(8,128)(2,1)S(1)} %get-tuple-element.44), channel_id=1, source_target_pairs={{0,4},{4,0},{8,12},{12,8},{16,20},{20,16},{24,28},{28,24},{1,5},{5... | collective-permute-start | bytes 393224 | tf_op jit(solution)/shard_map/ppermute | solution.py:345
  31.1 0.5 %collective-permute-start.6 = (bf16[128,512]{1,0:T(8,128)(2,1)S(1)}, bf16[128,512]{1,0:T(8,128)(2,1)S(1)}, u32[]{:S(2)}, u32[]{:S(2)}) collective-permute-start(bf16[128,512]{1,0:T(8,128)(2,1)S(1)} %get-tuple-element.34), channel_id=1, source_target_pairs={{0,4},{4,0},{8,12},{12,8},{16,20},{20,16},{24,28},{28,24},{1,5},{5... | collective-permute-start | bytes 393224 | tf_op jit(solution)/shard_map/ppermute | solution.py:345
  32.2 2.4 %softmax_first.1 = (f32[128,4096]{1,0:T(8,128)S(1)}, f32[128,8]{1,0:T(8,128)S(1)}, f32[128,8]{1,0:T(8,128)S(1)}) custom-call(s32[1]{0:T(128)S(6)} %copy.12.refs_0_, bf16[128,2048]{1,0:T(8,128)(2,1)S(1)} %copy-done.4, bf16[256,512]{1,0:T(8,128)(2,1)S(1)} %stack_keys_values.1.refs_2_, bf16[256,512]{1,0:T(8,128)(2,1)S(1)} %collective-permute-done.4.refs_0_.refs_3_, ...), custom_call_target="tpu_custom_call" | custom-call | flops 805306368 | bytes 3416068 | tf_op jit(solution)/shard_map/softmax_first/pallas_call | solution.py:319
  34.6 2.0 %collective-permute-done.10.refs_5_ = bf16[512,128]{1,0:T(8,128)(2,1)S(1)} collective-permute-done((bf16[512,128]{1,0:T(8,128)(2,1)S(1)}, bf16[512,128]{1,0:T(8,128)(2,1)S(1)}, u32[]{:S(2)}, u32[]{:S(2)}) %collective-permute-start.10) | collective-permute-done | bytes 131104 | tf_op jit(solution)/shard_map/ppermute | solution.py:345
  36.6 0.7 %inter_block.1 = (f32[128,2048]{1,0:T(8,128)S(1)}, f32[8,128]{1,0:T(8,128)S(1)}) custom-call(f32[128,16]{1,0:T(8,128)S(1)} %get-tuple-element.39.refs_0_, bf16[128,2048]{1,0:T(8,128)(2,1)S(1)} %get-tuple-element.40.refs_1_, f32[128,2048]{1,0:T(8,128)S(1)} %get-tuple-element.33.refs_4_.refs_2_, bf16[512,128]{1,0:T(8,128)(2,1)S(1)} %get-tuple-element.41.refs_3_, ...), custom_call_target="tpu_custom_call" | custom-call | flops 67108864 | bytes 3158016 | tf_op jit(solution)/shard_map/inter_block/pallas_call | solution.py:319
  37.3 0.9 %collective-permute-start.12 = (f32[8,128]{1,0:T(8,128)S(1)}, f32[8,128]{1,0:T(8,128)S(1)}, u32[]{:S(2)}, u32[]{:S(2)}) collective-permute-start(f32[8,128]{1,0:T(8,128)S(1)} %get-tuple-element.47.refs_3_), channel_id=1, source_target_pairs={{0,3},{1,2},{2,1},{3,0},{4,7},{5,6},{6,5},{7,4},{8,11},{9,10},{10,... | collective-permute-start | bytes 12296 | tf_op jit(solution)/shard_map/ppermute | solution.py:486
  38.2 0.6 %collective-permute-start.13 = (f32[8,128]{1,0:T(8,128)S(1)}, f32[8,128]{1,0:T(8,128)S(1)}, u32[]{:S(2)}, u32[]{:S(2)}) collective-permute-start(f32[8,128]{1,0:T(8,128)S(1)} %get-tuple-element.47.refs_3_), channel_id=1, source_target_pairs={{0,2},{1,3},{2,0},{3,1},{4,6},{5,7},{6,4},{7,5},{8,10},{9,11},{10,... | collective-permute-start | bytes 12296 | tf_op jit(solution)/shard_map/ppermute | solution.py:486
  39.2 2.5 %softmax_last.1.refs_0_ = bf16[128,2048]{1,0:T(8,128)(2,1)S(1)} custom-call(s32[1]{0:T(128)S(6)} %copy.12.refs_0_, bf16[128,2048]{1,0:T(8,128)(2,1)S(1)} %copy-done.4, bf16[256,512]{1,0:T(8,128)(2,1)S(1)} %pad_maximum_fusion.refs_2_, f32[128,4096]{1,0:T(8,128)S(1)} %get-tuple-element.36.refs_3_, f32[128,8]{1,0:T(8,128)S(1)} %get-tuple-element.37.refs_4_.refs_7_, ...), custom_call_target="tpu_custom_call" | custom-call | flops 268435456 | bytes 3416068 | tf_op jit(solution)/shard_map/softmax_last/pallas_call | solution.py:319
  41.8 1.1 %results.1 = (bf16[128,2048]{1,0:T(8,128)(2,1)}, bf16[128,2048]{1,0:T(8,128)(2,1)}) custom-call(bf16[128,2048]{1,0:T(8,128)(2,1)S(1)} %softmax_last.1.refs_0_, f32[128,2048]{1,0:T(8,128)S(1)} %get-tuple-element.45.refs_1_, f32[128,2048]{1,0:T(8,128)S(1)} %get-tuple-element.46.refs_2_, f32[8,128]{1,0:T(8,128)S(1)} %get-tuple-element.47.refs_3_, ...), custom_call_target="tpu_custom_call" | custom-call | flops 1048576 | bytes 3686400 | tf_op jit(solution)/shard_map/results/pallas_call | solution.py:319
  (37 shorter events, 1.3 us)
Async XLA Ops:
  0.6 0.8 %copy-start.5 = (bf16[128,256]{1,0:T(8,128)(2,1)S(1)}, bf16[128,256]{1,0:T(8,128)(2,1)}, u32[]{:S(2)}) copy-start(bf16[128,256]{1,0:T(8,128)(2,1)} %refs_0_.3) | copy-start | bytes 196612
  0.6 0.9 %copy-start.6 = (bf16[128,256]{1,0:T(8,128)(2,1)S(1)}, bf16[128,256]{1,0:T(8,128)(2,1)}, u32[]{:S(2)}) copy-start(bf16[128,256]{1,0:T(8,128)(2,1)} %refs_1_.4) | copy-start | bytes 196612
  0.7 5.0 %copy-start.7 = (f32[16,128]{1,0:T(8,128)S(1)}, f32[16,128]{1,0:T(8,128)}, u32[]{:S(2)}) copy-start(f32[16,128]{1,0:T(8,128)} %refs_2_.3) | copy-start | bytes 24580
  0.7 5.0 %copy-start = (bf16[128,2048]{1,0:T(8,128)(2,1)S(1)}, bf16[128,2048]{1,0:T(8,128)(2,1)}, u32[]{:S(2)}) copy-start(bf16[128,2048]{1,0:T(8,128)(2,1)} %refs_2_.2) | copy-start | bytes 1572868
  0.7 5.0 %copy-start.1 = (bf16[128,2048]{1,0:T(8,128)(2,1)S(1)}, bf16[128,2048]{1,0:T(8,128)(2,1)}, u32[]{:S(2)}) copy-start(bf16[128,2048]{1,0:T(8,128)(2,1)} %refs_3_.2) | copy-start | bytes 1572868
  0.7 11.3 %copy-start.2 = (bf16[128,2048]{1,0:T(8,128)(2,1)S(1)}, bf16[128,2048]{1,0:T(8,128)(2,1)}, u32[]{:S(2)}) copy-start(bf16[128,2048]{1,0:T(8,128)(2,1)} %refs_3_.3) | copy-start | bytes 1572868
  0.7 11.3 %copy-start.3 = (bf16[128,2048]{1,0:T(8,128)(2,1)S(1)}, bf16[128,2048]{1,0:T(8,128)(2,1)}, u32[]{:S(2)}) copy-start(bf16[128,2048]{1,0:T(8,128)(2,1)} %refs_6_.1) | copy-start | bytes 1572868
  0.7 11.3 %copy-start.8 = (f32[2048]{0:T(1024)S(1)}, f32[2048]{0:T(1024)}, u32[]{:S(2)}) copy-start(f32[2048]{0:T(1024)} %param.15) | copy-start | bytes 24580
  1.5 10.5 %collective-permute-start = (bf16[128,512]{1,0:T(8,128)(2,1)S(1)}, bf16[128,512]{1,0:T(8,128)(2,1)S(1)}, u32[]{:S(2)}, u32[]{:S(2)}) collective-permute-start(bf16[128,512]{1,0:T(8,128)(2,1)S(1)} %keys_beside_values.1.refs_0_), channel_id=1, source_target_pairs={{0,16},{4,20},{8,24},{12,28},{16,0},{20,4},{24,8},{28,12},{1,17},{... | collective-permute-start | bytes 393224 | tf_op jit(solution)/shard_map/ppermute | solution.py:351
  7.4 8.6 %collective-permute-start.1 = (bf16[528,128]{1,0:T(8,128)(2,1)S(1)}, bf16[528,128]{1,0:T(8,128)(2,1)S(1)}, u32[]{:S(2)}, u32[]{:S(2)}) collective-permute-start(bf16[528,128]{1,0:T(8,128)(2,1)S(1)} %get-tuple-element.27), channel_id=1, source_target_pairs={{0,12},{4,8},{8,4},{12,0},{16,28},{20,24},{24,20},{28,16},{1,13},{... | collective-permute-start | bytes 405512 | tf_op jit(solution)/shard_map/ppermute | solution.py:345
  10.0 7.8 %collective-permute-start.2 = (bf16[528,128]{1,0:T(8,128)(2,1)S(1)}, bf16[528,128]{1,0:T(8,128)(2,1)S(1)}, u32[]{:S(2)}, u32[]{:S(2)}) collective-permute-start(bf16[528,128]{1,0:T(8,128)(2,1)S(1)} %get-tuple-element.28), channel_id=1, source_target_pairs={{0,8},{4,12},{8,0},{12,4},{16,24},{20,28},{24,16},{28,20},{1,9},{5... | collective-permute-start | bytes 405512 | tf_op jit(solution)/shard_map/ppermute | solution.py:345
  10.4 7.4 %collective-permute-start.3 = (bf16[528,128]{1,0:T(8,128)(2,1)S(1)}, bf16[528,128]{1,0:T(8,128)(2,1)S(1)}, u32[]{:S(2)}, u32[]{:S(2)}) collective-permute-start(bf16[528,128]{1,0:T(8,128)(2,1)S(1)} %get-tuple-element.29), channel_id=1, source_target_pairs={{0,4},{4,0},{8,12},{12,8},{16,20},{20,16},{24,28},{28,24},{1,5},{5... | collective-permute-start | bytes 405512 | tf_op jit(solution)/shard_map/ppermute | solution.py:345
  17.9 9.2 %collective-permute-start.8 = (bf16[528,128]{1,0:T(8,128)(2,1)S(1)}, bf16[528,128]{1,0:T(8,128)(2,1)S(1)}, u32[]{:S(2)}, u32[]{:S(2)}) collective-permute-start(bf16[528,128]{1,0:T(8,128)(2,1)S(1)} %group_state.1.refs_2_), channel_id=1, source_target_pairs={{0,16},{4,20},{8,24},{12,28},{16,0},{20,4},{24,8},{28,12},{1,17},{... | collective-permute-start | bytes 405512 | tf_op jit(solution)/shard_map/ppermute | solution.py:351
  19.0 13.2 %copy-start.4 = (bf16[128,2048]{1,0:T(8,128)(2,1)S(1)}, bf16[128,2048]{1,0:T(8,128)(2,1)}, u32[]{:S(2)}) copy-start(bf16[128,2048]{1,0:T(8,128)(2,1)} %refs_1_.7) | copy-start | bytes 1572868
  19.0 11.9 %collective-permute-start.4 = (bf16[256,512]{1,0:T(8,128)(2,1)S(1)}, bf16[256,512]{1,0:T(8,128)(2,1)S(1)}, u32[]{:S(2)}, u32[]{:S(2)}) collective-permute-start(bf16[256,512]{1,0:T(8,128)(2,1)S(1)} %stack_keys_values.1.refs_2_), channel_id=1, source_target_pairs={{0,8},{4,12},{8,0},{12,4},{16,24},{20,28},{24,16},{28,20},{1,9},{5... | collective-permute-start | bytes 786440 | tf_op jit(solution)/shard_map/ppermute | solution.py:345
  21.6 9.4 %collective-permute-start.5 = (bf16[256,512]{1,0:T(8,128)(2,1)S(1)}, bf16[256,512]{1,0:T(8,128)(2,1)S(1)}, u32[]{:S(2)}, u32[]{:S(2)}) collective-permute-start(bf16[256,512]{1,0:T(8,128)(2,1)S(1)} %stack_keys_values.1.refs_2_), channel_id=1, source_target_pairs={{0,4},{4,0},{8,12},{12,8},{16,20},{20,16},{24,28},{28,24},{1,5},{5... | collective-permute-start | bytes 786440 | tf_op jit(solution)/shard_map/ppermute | solution.py:345
  27.3 7.3 %collective-permute-start.9 = (bf16[512,128]{1,0:T(8,128)(2,1)S(1)}, bf16[512,128]{1,0:T(8,128)(2,1)S(1)}, u32[]{:S(2)}, u32[]{:S(2)}) collective-permute-start(bf16[512,128]{1,0:T(8,128)(2,1)S(1)} %get-tuple-element.42), channel_id=1, source_target_pairs={{0,12},{4,8},{8,4},{12,0},{16,28},{20,24},{24,20},{28,16},{1,13},{... | collective-permute-start | bytes 393224 | tf_op jit(solution)/shard_map/ppermute | solution.py:345
  27.4 9.3 %collective-permute-start.10 = (bf16[512,128]{1,0:T(8,128)(2,1)S(1)}, bf16[512,128]{1,0:T(8,128)(2,1)S(1)}, u32[]{:S(2)}, u32[]{:S(2)}) collective-permute-start(bf16[512,128]{1,0:T(8,128)(2,1)S(1)} %get-tuple-element.43), channel_id=1, source_target_pairs={{0,8},{4,12},{8,0},{12,4},{16,24},{20,28},{24,16},{28,20},{1,9},{5... | collective-permute-start | bytes 393224 | tf_op jit(solution)/shard_map/ppermute | solution.py:345
  29.2 7.4 %collective-permute-start.11 = (bf16[512,128]{1,0:T(8,128)(2,1)S(1)}, bf16[512,128]{1,0:T(8,128)(2,1)S(1)}, u32[]{:S(2)}, u32[]{:S(2)}) collective-permute-start(bf16[512,128]{1,0:T(8,128)(2,1)S(1)} %get-tuple-element.44), channel_id=1, source_target_pairs={{0,4},{4,0},{8,12},{12,8},{16,20},{20,16},{24,28},{28,24},{1,5},{5... | collective-permute-start | bytes 393224 | tf_op jit(solution)/shard_map/ppermute | solution.py:345
  31.0 8.2 %collective-permute-start.7 = (bf16[128,512]{1,0:T(8,128)(2,1)S(1)}, bf16[128,512]{1,0:T(8,128)(2,1)S(1)}, u32[]{:S(2)}, u32[]{:S(2)}) collective-permute-start(bf16[128,512]{1,0:T(8,128)(2,1)S(1)} %get-tuple-element.35), channel_id=1, source_target_pairs={{0,8},{4,12},{8,0},{12,4},{16,24},{20,28},{24,16},{28,20},{1,9},{5... | collective-permute-start | bytes 393224 | tf_op jit(solution)/shard_map/ppermute | solution.py:345
  31.1 8.1 %collective-permute-start.6 = (bf16[128,512]{1,0:T(8,128)(2,1)S(1)}, bf16[128,512]{1,0:T(8,128)(2,1)S(1)}, u32[]{:S(2)}, u32[]{:S(2)}) collective-permute-start(bf16[128,512]{1,0:T(8,128)(2,1)S(1)} %get-tuple-element.34), channel_id=1, source_target_pairs={{0,4},{4,0},{8,12},{12,8},{16,20},{20,16},{24,28},{28,24},{1,5},{5... | collective-permute-start | bytes 393224 | tf_op jit(solution)/shard_map/ppermute | solution.py:345
  37.3 4.4 %collective-permute-start.12 = (f32[8,128]{1,0:T(8,128)S(1)}, f32[8,128]{1,0:T(8,128)S(1)}, u32[]{:S(2)}, u32[]{:S(2)}) collective-permute-start(f32[8,128]{1,0:T(8,128)S(1)} %get-tuple-element.47.refs_3_), channel_id=1, source_target_pairs={{0,3},{1,2},{2,1},{3,0},{4,7},{5,6},{6,5},{7,4},{8,11},{9,10},{10,... | collective-permute-start | bytes 12296 | tf_op jit(solution)/shard_map/ppermute | solution.py:486
  38.2 3.6 %collective-permute-start.13 = (f32[8,128]{1,0:T(8,128)S(1)}, f32[8,128]{1,0:T(8,128)S(1)}, u32[]{:S(2)}, u32[]{:S(2)}) collective-permute-start(f32[8,128]{1,0:T(8,128)S(1)} %get-tuple-element.47.refs_3_), channel_id=1, source_target_pairs={{0,2},{1,3},{2,0},{3,1},{4,6},{5,7},{6,4},{7,5},{8,10},{9,11},{10,... | collective-permute-start | bytes 12296 | tf_op jit(solution)/shard_map/ppermute | solution.py:486
  38.8 3.0 %collective-permute-start.14 = (f32[8,128]{1,0:T(8,128)S(1)}, f32[8,128]{1,0:T(8,128)S(1)}, u32[]{:S(2)}, u32[]{:S(2)}) collective-permute-start(f32[8,128]{1,0:T(8,128)S(1)} %get-tuple-element.47.refs_3_), channel_id=1, source_target_pairs={{0,1},{1,0},{2,3},{3,2},{4,5},{5,4},{6,7},{7,6},{8,9},{9,8},{10,11... | collective-permute-start | bytes 12296 | tf_op jit(solution)/shard_map/ppermute | solution.py:486

commit v9 on v8

--- a/solution.py
+++ b/solution.py
@@ -25,13 +25,9 @@
     return guess * (2.0 - x * guess)
 
 
-def sigmoid(x):
-    return inverse(1.0 + jnp.exp(-x))
-
-
 def silu16(x):
     x = x.astype(F32)
-    return (x * sigmoid(x)).astype(BF16)
+    return (x / (1.0 + jnp.exp(-x))).astype(BF16)
 
 
 def lower_ones(size):
@@ -181,7 +177,8 @@
         decay = jnp.exp((cum[:, h : h + 1] - cum_t[h : h + 1, :]) + bias)
         weights = (scores * decay).astype(BF16)
         intra_ref[:, cols] = jnp.dot(weights, va_ref[:, cols], preferred_element_type=F32)
-        gain_out[:, cols] = sigmoid(gate_ref[:, cols].astype(F32)) * gain_ref[:, cols]
+        gate = 1.0 / (1.0 + jnp.exp(-gate_ref[:, cols].astype(F32)))
+        gain_out[:, cols] = gate * gain_ref[:, cols]
 
 
 def inter_kernel(group, heads, decay_ref, qa_ref, intra_ref, *rest):
@@ -421,7 +418,7 @@
         [shape((per * HD, HD), BF16)] * group,
         (*pays, *carry),
         [slots, pltpu.VMEM((group, per * HD, HD), BF16)],
-        flops=1 << 33,
+        flops=2 * per * HD * HD * group,
     )
     prefixes = swap_all(prefixes)
 
@@ -430,8 +427,7 @@
         "stack_keys_values",
         [shape((groups * tokens, kv.shape[1]), BF16)],
         (kv, *far),
-        after=(total,) if groups > 1 else (intra,),
-        flops=1 << 32,
+        after=(intra,),
     )
     side, near = swap(own, 2), swap(own, 1)
     half = shape((own.shape[0] // 2, own.shape[1]), BF16)

time: 43.1 us -> 43.1 us (level)
  starting transfers between devices: 17.7 us -> 23.3 us
  waiting for transfers between devices: 11.4 us -> 6.05 us
    ppermute x10, waiting for transfers between devices: 5.16 us -> 0.8 us  [swap(): return lax.ppermute(x, 'ctx', [(c, c ^ s) for c in range(n)])]
    ppermute x10, starting transfers between devices: 10.6 us -> 14.6 us  [swap(): return lax.ppermute(x, 'ctx', [(c, c ^ s) for c in range(n)])]
    ppermute x2, starting transfers between devices: 5.19 us -> 6.84 us  [ahead(): return lax.ppermute(x, 'ctx', [(c, (c + d * group) % n) for c in range(n)])]
    ppermute x2, waiting for transfers between devices: 6.16 us -> 5.25 us  [ahead(): return lax.ppermute(x, 'ctx', [(c, (c + d * group) % n) for c in range(n)])]
  transfers between devices with their start and end apart: 15 -> 15, of which waited for: 7 -> 3; matrix products, arithmetic and copies ran while one was open for 0% -> 0% of each run, Pallas kernels for 24% -> 24%
where the time goes in v9:
time: 43.1 us; the launch traced here: 42.9 us
  starting transfers between devices  23.3 us (54%)
  Pallas kernels  11.3 us (26%)
  waiting for transfers between devices  6.05 us (14%)
  between operations  1.48 us (3%)
  local copies, waits for them, and re-layouts  0.81 us (2%)
    ppermute x10, starting transfers between devices, swap(): return lax.ppermute(x, 'ctx', [(c, c ^ s) for c in range(n)])  14.6 us
    pallas_call x12, Pallas kernels, call(): pl.pallas_call(run, name=name, out_shape=list(outs), in_specs=specs, scra...  11.3 us
    ppermute x2, starting transfers between devices, ahead(): return lax.ppermute(x, 'ctx', [(c, (c + d * group) % n) for c in range(n)])  6.84 us
    ppermute x2, waiting for transfers between devices, ahead(): return lax.ppermute(x, 'ctx', [(c, (c + d * group) % n) for c in range(n)])  5.25 us
    ppermute x3, starting transfers between devices, body(): parts = [squares] + [lax.ppermute(squares, 'head', turn) for turn in turns]  1.89 us
  transfers between devices with their start and end apart: 15, of which 3 were waited for; matrix products, arithmetic and copies ran while one was open for 0% of the time, Pallas kernels for 24%

profile of v9, /device:TPU:0, one launch (start us, length us, event | category | flops | bytes accessed | tf_op | source)
XLA Modules:
  0.0 42.9 jit_solution(9760860819947003019)
XLA Ops:
  0.7 0.7 %copy-done.5 = bf16[128,256]{1,0:T(8,128)(2,1)S(1)} copy-done((bf16[128,256]{1,0:T(8,128)(2,1)S(1)}, bf16[128,256]{1,0:T(8,128)(2,1)}, u32[]{:S(2)}) %copy-start.5) | copy-done | bytes 65560
  1.5 4.1 %collective-permute-start = (bf16[128,512]{1,0:T(8,128)(2,1)S(1)}, bf16[128,512]{1,0:T(8,128)(2,1)S(1)}, u32[]{:S(2)}, u32[]{:S(2)}) collective-permute-start(bf16[128,512]{1,0:T(8,128)(2,1)S(1)} %keys_beside_values.1.refs_0_), channel_id=1, source_target_pairs={{0,16},{4,20},{8,24},{12,28},{16,0},{20,4},{24,8},{28,12},{1,17},{... | collective-permute-start | bytes 393224 | tf_op jit(solution)/shard_map/ppermute | solution.py:348
  5.6 1.5 %block_states.1 = (bf16[528,128]{1,0:T(8,128)(2,1)S(1)}, bf16[528,128]{1,0:T(8,128)(2,1)S(1)}, bf16[528,128]{1,0:T(8,128)(2,1)S(1)}, bf16[528,128]{1,0:T(8,128)(...) custom-call(f32[128,128]{1,0:T(8,128)S(1)} %get-tuple-element.25.refs_2_.refs_0_, ...), custom_call_target="tpu_custom_call" | custom-call | flops 134217728 | bytes 2711552 | tf_op jit(solution)/shard_map/block_states/pallas_call | solution.py:316
  7.2 2.6 %collective-permute-start.5 = (bf16[528,128]{1,0:T(8,128)(2,1)S(1)}, bf16[528,128]{1,0:T(8,128)(2,1)S(1)}, u32[]{:S(2)}, u32[]{:S(2)}) collective-permute-start(bf16[528,128]{1,0:T(8,128)(2,1)S(1)} %get-tuple-element.38), channel_id=1, source_target_pairs={{0,12},{4,8},{8,4},{12,0},{16,28},{20,24},{24,20},{28,16},{1,13},{... | collective-permute-start | bytes 405512 | tf_op jit(solution)/shard_map/ppermute | solution.py:342
  9.8 0.4 %collective-permute-start.6 = (bf16[528,128]{1,0:T(8,128)(2,1)S(1)}, bf16[528,128]{1,0:T(8,128)(2,1)S(1)}, u32[]{:S(2)}, u32[]{:S(2)}) collective-permute-start(bf16[528,128]{1,0:T(8,128)(2,1)S(1)} %get-tuple-element.39), channel_id=1, source_target_pairs={{0,8},{4,12},{8,0},{12,4},{16,24},{20,28},{24,16},{28,20},{1,9},{5... | collective-permute-start | bytes 405512 | tf_op jit(solution)/shard_map/ppermute | solution.py:342
  10.2 0.5 %collective-permute-start.7 = (bf16[528,128]{1,0:T(8,128)(2,1)S(1)}, bf16[528,128]{1,0:T(8,128)(2,1)S(1)}, u32[]{:S(2)}, u32[]{:S(2)}) collective-permute-start(bf16[528,128]{1,0:T(8,128)(2,1)S(1)} %get-tuple-element.40), channel_id=1, source_target_pairs={{0,4},{4,0},{8,12},{12,8},{16,20},{20,16},{24,28},{28,24},{1,5},{5... | collective-permute-start | bytes 405512 | tf_op jit(solution)/shard_map/ppermute | solution.py:342
  10.7 1.3 %collective-permute-done.refs_8_.refs_1_ = bf16[128,512]{1,0:T(8,128)(2,1)S(1)} collective-permute-done((bf16[128,512]{1,0:T(8,128)(2,1)S(1)}, bf16[128,512]{1,0:T(8,128)(2,1)S(1)}, u32[]{:S(2)}, u32[]{:S(2)}) %collective-permute-start) | collective-permute-done | bytes 131104 | tf_op jit(solution)/shard_map/ppermute | solution.py:348
  12.0 2.8 %intra_block.1 = (f32[128,2048]{1,0:T(8,128)S(1)}, bf16[128,2048]{1,0:T(8,128)(2,1)S(1)}, f32[128,2048]{1,0:T(8,128)S(1)}, f32[128,16]{1,0:T(8,128)S(1)}) custom-call(f32[128,128]{1,0:T(8,128)S(1)} %get-tuple-element.25.refs_2_.refs_0_, f32[128,128]{1,0:T(8,128)S(1)} %get-tuple-element.26.refs_1_, f32[16,128]{1,0:T(8,128)S(1)} %copy-done.7, ...), custom_call_target="tpu_custom_call" | custom-call | flops 134217728 | bytes 4874240 | tf_op jit(solution)/shard_map/intra_block/pallas_call | solution.py:316
  14.8 0.7 %collective-permute-start.1 = (bf16[256,512]{1,0:T(8,128)(2,1)S(1)}, bf16[256,512]{1,0:T(8,128)(2,1)S(1)}, u32[]{:S(2)}, u32[]{:S(2)}) collective-permute-start(bf16[256,512]{1,0:T(8,128)(2,1)S(1)} %stack_keys_values.1.refs_2_), channel_id=1, source_target_pairs={{0,8},{4,12},{8,0},{12,4},{16,24},{20,28},{24,16},{28,20},{1,9},{5... | collective-permute-start | bytes 786440 | tf_op jit(solution)/shard_map/ppermute | solution.py:342
  15.6 1.5 %collective-permute-start.2 = (bf16[256,512]{1,0:T(8,128)(2,1)S(1)}, bf16[256,512]{1,0:T(8,128)(2,1)S(1)}, u32[]{:S(2)}, u32[]{:S(2)}) collective-permute-start(bf16[256,512]{1,0:T(8,128)(2,1)S(1)} %stack_keys_values.1.refs_2_), channel_id=1, source_target_pairs={{0,4},{4,0},{8,12},{12,8},{16,20},{20,16},{24,28},{28,24},{1,5},{5... | collective-permute-start | bytes 786440 | tf_op jit(solution)/shard_map/ppermute | solution.py:342
  17.1 0.8 %collective-permute-done.6.refs_2_ = bf16[528,128]{1,0:T(8,128)(2,1)S(1)} collective-permute-done((bf16[528,128]{1,0:T(8,128)(2,1)S(1)}, bf16[528,128]{1,0:T(8,128)(2,1)S(1)}, u32[]{:S(2)}, u32[]{:S(2)}) %collective-permute-start.6) | collective-permute-done | bytes 135200 | tf_op jit(solution)/shard_map/ppermute | solution.py:342
  18.0 2.7 %collective-permute-start.8 = (bf16[528,128]{1,0:T(8,128)(2,1)S(1)}, bf16[528,128]{1,0:T(8,128)(2,1)S(1)}, u32[]{:S(2)}, u32[]{:S(2)}) collective-permute-start(bf16[528,128]{1,0:T(8,128)(2,1)S(1)} %group_state.1), channel_id=1, source_target_pairs={{0,16},{4,20},{8,24},{12,28},{16,0},{20,4},{24,8},{28,12},{1,17},{... | collective-permute-start | bytes 405512 | tf_op jit(solution)/shard_map/ppermute | solution.py:348
  20.8 3.9 %collective-permute-done.8.refs_4_ = bf16[528,128]{1,0:T(8,128)(2,1)S(1)} collective-permute-done((bf16[528,128]{1,0:T(8,128)(2,1)S(1)}, bf16[528,128]{1,0:T(8,128)(2,1)S(1)}, u32[]{:S(2)}, u32[]{:S(2)}) %collective-permute-start.8) | collective-permute-done | bytes 135200 | tf_op jit(solution)/shard_map/ppermute | solution.py:348
  24.7 0.2 prefix_states.1
  24.9 4.7 %collective-permute-start.9 = (bf16[512,128]{1,0:T(8,128)(2,1)S(1)}, bf16[512,128]{1,0:T(8,128)(2,1)S(1)}, u32[]{:S(2)}, u32[]{:S(2)}) collective-permute-start(bf16[512,128]{1,0:T(8,128)(2,1)S(1)} %get-tuple-element.42), channel_id=1, source_target_pairs={{0,12},{4,8},{8,4},{12,0},{16,28},{20,24},{24,20},{28,16},{1,13},{... | collective-permute-start | bytes 393224 | tf_op jit(solution)/shard_map/ppermute | solution.py:342
  29.6 0.6 %collective-permute-start.11 = (bf16[512,128]{1,0:T(8,128)(2,1)S(1)}, bf16[512,128]{1,0:T(8,128)(2,1)S(1)}, u32[]{:S(2)}, u32[]{:S(2)}) collective-permute-start(bf16[512,128]{1,0:T(8,128)(2,1)S(1)} %get-tuple-element.44), channel_id=1, source_target_pairs={{0,4},{4,0},{8,12},{12,8},{16,20},{20,16},{24,28},{28,24},{1,5},{5... | collective-permute-start | bytes 393224 | tf_op jit(solution)/shard_map/ppermute | solution.py:342
  30.2 2.0 %collective-permute-start.4 = (bf16[128,512]{1,0:T(8,128)(2,1)S(1)}, bf16[128,512]{1,0:T(8,128)(2,1)S(1)}, u32[]{:S(2)}, u32[]{:S(2)}) collective-permute-start(bf16[128,512]{1,0:T(8,128)(2,1)S(1)} %get-tuple-element.31), channel_id=1, source_target_pairs={{0,8},{4,12},{8,0},{12,4},{16,24},{20,28},{24,16},{28,20},{1,9},{5... | collective-permute-start | bytes 393224 | tf_op jit(solution)/shard_map/ppermute | solution.py:342
  32.2 1.5 %collective-permute-start.3 = (bf16[128,512]{1,0:T(8,128)(2,1)S(1)}, bf16[128,512]{1,0:T(8,128)(2,1)S(1)}, u32[]{:S(2)}, u32[]{:S(2)}) collective-permute-start(bf16[128,512]{1,0:T(8,128)(2,1)S(1)} %get-tuple-element.30), channel_id=1, source_target_pairs={{0,4},{4,0},{8,12},{12,8},{16,20},{20,16},{24,28},{28,24},{1,5},{5... | collective-permute-start | bytes 393224 | tf_op jit(solution)/shard_map/ppermute | solution.py:342
  34.4 2.4 %softmax_first.1 = (f32[128,4096]{1,0:T(8,128)S(1)}, f32[128,8]{1,0:T(8,128)S(1)}, f32[128,8]{1,0:T(8,128)S(1)}) custom-call(s32[1]{0:T(128)S(6)} %copy.12.refs_0_, bf16[128,2048]{1,0:T(8,128)(2,1)S(1)} %copy-done.4, bf16[256,512]{1,0:T(8,128)(2,1)S(1)} %stack_keys_values.1.refs_2_, bf16[256,512]{1,0:T(8,128)(2,1)S(1)} %collective-permute-done.1.refs_0_.refs_3_, ...), custom_call_target="tpu_custom_call" | custom-call | flops 805306368 | bytes 3416068 | tf_op jit(solution)/shard_map/softmax_first/pallas_call | solution.py:316
  36.8 0.7 %inter_block.1 = (f32[128,2048]{1,0:T(8,128)S(1)}, f32[8,128]{1,0:T(8,128)S(1)}) custom-call(f32[128,16]{1,0:T(8,128)S(1)} %get-tuple-element.35.refs_0_, bf16[128,2048]{1,0:T(8,128)(2,1)S(1)} %get-tuple-element.36.refs_1_, f32[128,2048]{1,0:T(8,128)S(1)} %get-tuple-element.29.refs_2_.refs_4_, bf16[512,128]{1,0:T(8,128)(2,1)S(1)} %get-tuple-element.41.refs_3_, ...), custom_call_target="tpu_custom_call" | custom-call | flops 67108864 | bytes 3158016 | tf_op jit(solution)/shard_map/inter_block/pallas_call | solution.py:316
  37.5 1.6 %collective-permute-start.13 = (f32[8,128]{1,0:T(8,128)S(1)}, f32[8,128]{1,0:T(8,128)S(1)}, u32[]{:S(2)}, u32[]{:S(2)}) collective-permute-start(f32[8,128]{1,0:T(8,128)S(1)} %get-tuple-element.47.refs_3_), channel_id=1, source_target_pairs={{0,2},{1,3},{2,0},{3,1},{4,6},{5,7},{6,4},{7,5},{8,10},{9,11},{10,... | collective-permute-start | bytes 12296 | tf_op jit(solution)/shard_map/ppermute | solution.py:482
  39.0 0.3 collective-permute-start.14
  39.4 2.5 %softmax_last.1.refs_0_ = bf16[128,2048]{1,0:T(8,128)(2,1)S(1)} custom-call(s32[1]{0:T(128)S(6)} %copy.12.refs_0_, bf16[128,2048]{1,0:T(8,128)(2,1)S(1)} %copy-done.4, bf16[256,512]{1,0:T(8,128)(2,1)S(1)} %pad_maximum_fusion.refs_2_, f32[128,4096]{1,0:T(8,128)S(1)} %get-tuple-element.32.refs_3_, f32[128,8]{1,0:T(8,128)S(1)} %get-tuple-element.33.refs_4_.refs_7_, ...), custom_call_target="tpu_custom_call" | custom-call | flops 268435456 | bytes 3416068 | tf_op jit(solution)/shard_map/softmax_last/pallas_call | solution.py:316
  41.9 1.1 %results.1 = (bf16[128,2048]{1,0:T(8,128)(2,1)}, bf16[128,2048]{1,0:T(8,128)(2,1)}) custom-call(bf16[128,2048]{1,0:T(8,128)(2,1)S(1)} %softmax_last.1.refs_0_, f32[128,2048]{1,0:T(8,128)S(1)} %get-tuple-element.45.refs_1_, f32[128,2048]{1,0:T(8,128)S(1)} %get-tuple-element.46.refs_2_, f32[8,128]{1,0:T(8,128)S(1)} %get-tuple-element.47.refs_3_, ...), custom_call_target="tpu_custom_call" | custom-call | flops 1048576 | bytes 3686400 | tf_op jit(solution)/shard_map/results/pallas_call | solution.py:316
  (37 shorter events, 0.3 us)
Async XLA Ops:
  0.6 0.8 %copy-start.5 = (bf16[128,256]{1,0:T(8,128)(2,1)S(1)}, bf16[128,256]{1,0:T(8,128)(2,1)}, u32[]{:S(2)}) copy-start(bf16[128,256]{1,0:T(8,128)(2,1)} %refs_0_.3) | copy-start | bytes 196612
  0.6 0.9 %copy-start.6 = (bf16[128,256]{1,0:T(8,128)(2,1)S(1)}, bf16[128,256]{1,0:T(8,128)(2,1)}, u32[]{:S(2)}) copy-start(bf16[128,256]{1,0:T(8,128)(2,1)} %refs_1_.4) | copy-start | bytes 196612
  0.7 5.0 %copy-start.7 = (f32[16,128]{1,0:T(8,128)S(1)}, f32[16,128]{1,0:T(8,128)}, u32[]{:S(2)}) copy-start(f32[16,128]{1,0:T(8,128)} %refs_2_.3) | copy-start | bytes 24580
  0.7 5.0 %copy-start = (bf16[128,2048]{1,0:T(8,128)(2,1)S(1)}, bf16[128,2048]{1,0:T(8,128)(2,1)}, u32[]{:S(2)}) copy-start(bf16[128,2048]{1,0:T(8,128)(2,1)} %refs_2_.2) | copy-start | bytes 1572868
  0.7 5.0 %copy-start.1 = (bf16[128,2048]{1,0:T(8,128)(2,1)S(1)}, bf16[128,2048]{1,0:T(8,128)(2,1)}, u32[]{:S(2)}) copy-start(bf16[128,2048]{1,0:T(8,128)(2,1)} %refs_3_.2) | copy-start | bytes 1572868
  0.7 11.3 %copy-start.2 = (bf16[128,2048]{1,0:T(8,128)(2,1)S(1)}, bf16[128,2048]{1,0:T(8,128)(2,1)}, u32[]{:S(2)}) copy-start(bf16[128,2048]{1,0:T(8,128)(2,1)} %refs_3_.3) | copy-start | bytes 1572868
  0.7 11.3 %copy-start.3 = (bf16[128,2048]{1,0:T(8,128)(2,1)S(1)}, bf16[128,2048]{1,0:T(8,128)(2,1)}, u32[]{:S(2)}) copy-start(bf16[128,2048]{1,0:T(8,128)(2,1)} %refs_6_.1) | copy-start | bytes 1572868
  0.7 11.3 %copy-start.8 = (f32[2048]{0:T(1024)S(1)}, f32[2048]{0:T(1024)}, u32[]{:S(2)}) copy-start(f32[2048]{0:T(1024)} %param.15) | copy-start | bytes 24580
  1.5 10.5 %collective-permute-start = (bf16[128,512]{1,0:T(8,128)(2,1)S(1)}, bf16[128,512]{1,0:T(8,128)(2,1)S(1)}, u32[]{:S(2)}, u32[]{:S(2)}) collective-permute-start(bf16[128,512]{1,0:T(8,128)(2,1)S(1)} %keys_beside_values.1.refs_0_), channel_id=1, source_target_pairs={{0,16},{4,20},{8,24},{12,28},{16,0},{20,4},{24,8},{28,12},{1,17},{... | collective-permute-start | bytes 393224 | tf_op jit(solution)/shard_map/ppermute | solution.py:348
  7.2 9.9 %collective-permute-start.5 = (bf16[528,128]{1,0:T(8,128)(2,1)S(1)}, bf16[528,128]{1,0:T(8,128)(2,1)S(1)}, u32[]{:S(2)}, u32[]{:S(2)}) collective-permute-start(bf16[528,128]{1,0:T(8,128)(2,1)S(1)} %get-tuple-element.38), channel_id=1, source_target_pairs={{0,12},{4,8},{8,4},{12,0},{16,28},{20,24},{24,20},{28,16},{1,13},{... | collective-permute-start | bytes 405512 | tf_op jit(solution)/shard_map/ppermute | solution.py:342
  9.8 8.1 %collective-permute-start.6 = (bf16[528,128]{1,0:T(8,128)(2,1)S(1)}, bf16[528,128]{1,0:T(8,128)(2,1)S(1)}, u32[]{:S(2)}, u32[]{:S(2)}) collective-permute-start(bf16[528,128]{1,0:T(8,128)(2,1)S(1)} %get-tuple-element.39), channel_id=1, source_target_pairs={{0,8},{4,12},{8,0},{12,4},{16,24},{20,28},{24,16},{28,20},{1,9},{5... | collective-permute-start | bytes 405512 | tf_op jit(solution)/shard_map/ppermute | solution.py:342
  10.2 7.7 %collective-permute-start.7 = (bf16[528,128]{1,0:T(8,128)(2,1)S(1)}, bf16[528,128]{1,0:T(8,128)(2,1)S(1)}, u32[]{:S(2)}, u32[]{:S(2)}) collective-permute-start(bf16[528,128]{1,0:T(8,128)(2,1)S(1)} %get-tuple-element.40), channel_id=1, source_target_pairs={{0,4},{4,0},{8,12},{12,8},{16,20},{20,16},{24,28},{28,24},{1,5},{5... | collective-permute-start | bytes 405512 | tf_op jit(solution)/shard_map/ppermute | solution.py:342
  14.8 19.6 %copy-start.4 = (bf16[128,2048]{1,0:T(8,128)(2,1)S(1)}, bf16[128,2048]{1,0:T(8,128)(2,1)}, u32[]{:S(2)}) copy-start(bf16[128,2048]{1,0:T(8,128)(2,1)} %refs_1_.7) | copy-start | bytes 1572868
  14.8 15.4 %collective-permute-start.1 = (bf16[256,512]{1,0:T(8,128)(2,1)S(1)}, bf16[256,512]{1,0:T(8,128)(2,1)S(1)}, u32[]{:S(2)}, u32[]{:S(2)}) collective-permute-start(bf16[256,512]{1,0:T(8,128)(2,1)S(1)} %stack_keys_values.1.refs_2_), channel_id=1, source_target_pairs={{0,8},{4,12},{8,0},{12,4},{16,24},{20,28},{24,16},{28,20},{1,9},{5... | collective-permute-start | bytes 786440 | tf_op jit(solution)/shard_map/ppermute | solution.py:342
  15.6 14.6 %collective-permute-start.2 = (bf16[256,512]{1,0:T(8,128)(2,1)S(1)}, bf16[256,512]{1,0:T(8,128)(2,1)S(1)}, u32[]{:S(2)}, u32[]{:S(2)}) collective-permute-start(bf16[256,512]{1,0:T(8,128)(2,1)S(1)} %stack_keys_values.1.refs_2_), channel_id=1, source_target_pairs={{0,4},{4,0},{8,12},{12,8},{16,20},{20,16},{24,28},{28,24},{1,5},{5... | collective-permute-start | bytes 786440 | tf_op jit(solution)/shard_map/ppermute | solution.py:342
  18.0 6.7 %collective-permute-start.8 = (bf16[528,128]{1,0:T(8,128)(2,1)S(1)}, bf16[528,128]{1,0:T(8,128)(2,1)S(1)}, u32[]{:S(2)}, u32[]{:S(2)}) collective-permute-start(bf16[528,128]{1,0:T(8,128)(2,1)S(1)} %group_state.1), channel_id=1, source_target_pairs={{0,16},{4,20},{8,24},{12,28},{16,0},{20,4},{24,8},{28,12},{1,17},{... | collective-permute-start | bytes 405512 | tf_op jit(solution)/shard_map/ppermute | solution.py:348
  24.9 11.9 %collective-permute-start.9 = (bf16[512,128]{1,0:T(8,128)(2,1)S(1)}, bf16[512,128]{1,0:T(8,128)(2,1)S(1)}, u32[]{:S(2)}, u32[]{:S(2)}) collective-permute-start(bf16[512,128]{1,0:T(8,128)(2,1)S(1)} %get-tuple-element.42), channel_id=1, source_target_pairs={{0,12},{4,8},{8,4},{12,0},{16,28},{20,24},{24,20},{28,16},{1,13},{... | collective-permute-start | bytes 393224 | tf_op jit(solution)/shard_map/ppermute | solution.py:342
  29.6 7.2 %collective-permute-start.10 = (bf16[512,128]{1,0:T(8,128)(2,1)S(1)}, bf16[512,128]{1,0:T(8,128)(2,1)S(1)}, u32[]{:S(2)}, u32[]{:S(2)}) collective-permute-start(bf16[512,128]{1,0:T(8,128)(2,1)S(1)} %get-tuple-element.43), channel_id=1, source_target_pairs={{0,8},{4,12},{8,0},{12,4},{16,24},{20,28},{24,16},{28,20},{1,9},{5... | collective-permute-start | bytes 393224 | tf_op jit(solution)/shard_map/ppermute | solution.py:342
  29.6 7.2 %collective-permute-start.11 = (bf16[512,128]{1,0:T(8,128)(2,1)S(1)}, bf16[512,128]{1,0:T(8,128)(2,1)S(1)}, u32[]{:S(2)}, u32[]{:S(2)}) collective-permute-start(bf16[512,128]{1,0:T(8,128)(2,1)S(1)} %get-tuple-element.44), channel_id=1, source_target_pairs={{0,4},{4,0},{8,12},{12,8},{16,20},{20,16},{24,28},{28,24},{1,5},{5... | collective-permute-start | bytes 393224 | tf_op jit(solution)/shard_map/ppermute | solution.py:342
  30.2 9.1 %collective-permute-start.4 = (bf16[128,512]{1,0:T(8,128)(2,1)S(1)}, bf16[128,512]{1,0:T(8,128)(2,1)S(1)}, u32[]{:S(2)}, u32[]{:S(2)}) collective-permute-start(bf16[128,512]{1,0:T(8,128)(2,1)S(1)} %get-tuple-element.31), channel_id=1, source_target_pairs={{0,8},{4,12},{8,0},{12,4},{16,24},{20,28},{24,16},{28,20},{1,9},{5... | collective-permute-start | bytes 393224 | tf_op jit(solution)/shard_map/ppermute | solution.py:342
  32.2 7.2 %collective-permute-start.3 = (bf16[128,512]{1,0:T(8,128)(2,1)S(1)}, bf16[128,512]{1,0:T(8,128)(2,1)S(1)}, u32[]{:S(2)}, u32[]{:S(2)}) collective-permute-start(bf16[128,512]{1,0:T(8,128)(2,1)S(1)} %get-tuple-element.30), channel_id=1, source_target_pairs={{0,4},{4,0},{8,12},{12,8},{16,20},{20,16},{24,28},{28,24},{1,5},{5... | collective-permute-start | bytes 393224 | tf_op jit(solution)/shard_map/ppermute | solution.py:342
  37.5 4.4 %collective-permute-start.12 = (f32[8,128]{1,0:T(8,128)S(1)}, f32[8,128]{1,0:T(8,128)S(1)}, u32[]{:S(2)}, u32[]{:S(2)}) collective-permute-start(f32[8,128]{1,0:T(8,128)S(1)} %get-tuple-element.47.refs_3_), channel_id=1, source_target_pairs={{0,3},{1,2},{2,1},{3,0},{4,7},{5,6},{6,5},{7,4},{8,11},{9,10},{10,... | collective-permute-start | bytes 12296 | tf_op jit(solution)/shard_map/ppermute | solution.py:482
  37.5 4.4 %collective-permute-start.13 = (f32[8,128]{1,0:T(8,128)S(1)}, f32[8,128]{1,0:T(8,128)S(1)}, u32[]{:S(2)}, u32[]{:S(2)}) collective-permute-start(f32[8,128]{1,0:T(8,128)S(1)} %get-tuple-element.47.refs_3_), channel_id=1, source_target_pairs={{0,2},{1,3},{2,0},{3,1},{4,6},{5,7},{6,4},{7,5},{8,10},{9,11},{10,... | collective-permute-start | bytes 12296 | tf_op jit(solution)/shard_map/ppermute | solution.py:482
  39.0 2.9 %collective-permute-start.14 = (f32[8,128]{1,0:T(8,128)S(1)}, f32[8,128]{1,0:T(8,128)S(1)}, u32[]{:S(2)}, u32[]{:S(2)}) collective-permute-start(f32[8,128]{1,0:T(8,128)S(1)} %get-tuple-element.47.refs_3_), channel_id=1, source_target_pairs={{0,1},{1,0},{2,3},{3,2},{4,5},{5,4},{6,7},{7,6},{8,9},{9,8},{10,11... | collective-permute-start | bytes 12296 | tf_op jit(solution)/shard_map/ppermute | solution.py:482

commit v10 on v9

--- a/solution.py
+++ b/solution.py
@@ -381,7 +381,6 @@
         (tri, bias, log_decay, q_lin, ka, va, gate, norm_gain.reshape(1, width)),
         flops=4 * cube,
         exps=4 * tokens * width,
-        after=far,
     )
 
     slots = pltpu.VMEM((group, rows, HD), BF16)
@@ -418,7 +417,7 @@
         [shape((per * HD, HD), BF16)] * group,
         (*pays, *carry),
         [slots, pltpu.VMEM((group, per * HD, HD), BF16)],
-        flops=2 * per * HD * HD * group,
+        flops=1 << 33,
     )
     prefixes = swap_all(prefixes)
 
@@ -427,7 +426,8 @@
         "stack_keys_values",
         [shape((groups * tokens, kv.shape[1]), BF16)],
         (kv, *far),
-        after=(intra,),
+        after=(total,) if groups > 1 else (intra,),
+        flops=1 << 32,
     )
     side, near = swap(own, 2), swap(own, 1)
     half = shape((own.shape[0] // 2, own.shape[1]), BF16)

time: 43.1 us -> 41.4 us (0.961)
  starting transfers between devices: 23.3 us -> 18.4 us
  waiting for transfers between devices: 6.05 us -> 8.92 us
    ppermute x10, waiting for transfers between devices: 0.8 us -> 4.63 us  [swap(): return lax.ppermute(x, 'ctx', [(c, c ^ s) for c in range(n)])]
    ppermute x10, starting transfers between devices: 14.6 us -> 12 us  [swap(): return lax.ppermute(x, 'ctx', [(c, c ^ s) for c in range(n)])]
    ppermute x2, starting transfers between devices: 6.84 us -> 4.45 us  [ahead(): return lax.ppermute(x, 'ctx', [(c, (c + d * group) % n) for c in range(n)])]
    ppermute x2, waiting for transfers between devices: 5.25 us -> 4.29 us  [ahead(): return lax.ppermute(x, 'ctx', [(c, (c + d * group) % n) for c in range(n)])]
  transfers between devices with their start and end apart: 15 -> 15, of which waited for: 3 -> 3; matrix products, arithmetic and copies ran while one was open for 0% -> 0% of each run, Pallas kernels for 24% -> 21%
where the time goes in v10:
time: 41.4 us; the launch traced here: 41.2 us
  starting transfers between devices  18.4 us (44%)
  Pallas kernels  11.3 us (27%)
  waiting for transfers between devices  8.92 us (22%)
  between operations  1.48 us (4%)
  local copies, waits for them, and re-layouts  1.15 us (3%)
    ppermute x10, starting transfers between devices, swap(): return lax.ppermute(x, 'ctx', [(c, c ^ s) for c in range(n)])  12 us
    pallas_call x12, Pallas kernels, call(): pl.pallas_call(run, name=name, out_shape=list(outs), in_specs=specs, scra...  11.3 us
    ppermute x10, waiting for transfers between devices, swap(): return lax.ppermute(x, 'ctx', [(c, c ^ s) for c in range(n)])  4.63 us
    ppermute x2, starting transfers between devices, ahead(): return lax.ppermute(x, 'ctx', [(c, (c + d * group) % n) for c in range(n)])  4.45 us
    ppermute x2, waiting for transfers between devices, ahead(): return lax.ppermute(x, 'ctx', [(c, (c + d * group) % n) for c in range(n)])  4.29 us
    ppermute x3, starting transfers between devices, body(): parts = [squares] + [lax.ppermute(squares, 'head', turn) for turn in turns]  1.89 us
    unnamed x18, local copies, waits for them, and re-layouts  1.15 us
  transfers between devices with their start and end apart: 15, of which 3 were waited for; matrix products, arithmetic and copies ran while one was open for 0% of the time, Pallas kernels for 21%

profile of v10, /device:TPU:0, one launch (start us, length us, event | category | flops | bytes accessed | tf_op | source)
XLA Modules:
  0.0 41.2 jit_solution(10847071291871906463)
XLA Ops:
  0.7 0.6 %copy-done.7 = f32[16,128]{1,0:T(8,128)S(1)} copy-done((f32[16,128]{1,0:T(8,128)S(1)}, f32[16,128]{1,0:T(8,128)}, u32[]{:S(2)}) %copy-start.7) | copy-done | bytes 8216
  1.3 0.4 copy-done.2
  1.8 1.5 %block_states.1 = (bf16[528,128]{1,0:T(8,128)(2,1)S(1)}, bf16[528,128]{1,0:T(8,128)(2,1)S(1)}, bf16[528,128]{1,0:T(8,128)(2,1)S(1)}, bf16[528,128]{1,0:T(8,128)(...) custom-call(f32[128,128]{1,0:T(8,128)S(1)} %get-tuple-element.25.refs_2_.refs_0_, ...), custom_call_target="tpu_custom_call" | custom-call | flops 134217728 | bytes 2711552 | tf_op jit(solution)/shard_map/block_states/pallas_call | solution.py:316
  3.4 4.1 %collective-permute-start.1 = (bf16[528,128]{1,0:T(8,128)(2,1)S(1)}, bf16[528,128]{1,0:T(8,128)(2,1)S(1)}, u32[]{:S(2)}, u32[]{:S(2)}) collective-permute-start(bf16[528,128]{1,0:T(8,128)(2,1)S(1)} %get-tuple-element.27), channel_id=1, source_target_pairs={{0,12},{4,8},{8,4},{12,0},{16,28},{20,24},{24,20},{28,16},{1,13},{... | collective-permute-start | bytes 405512 | tf_op jit(solution)/shard_map/ppermute | solution.py:342
  7.4 0.4 %collective-permute-start.2 = (bf16[528,128]{1,0:T(8,128)(2,1)S(1)}, bf16[528,128]{1,0:T(8,128)(2,1)S(1)}, u32[]{:S(2)}, u32[]{:S(2)}) collective-permute-start(bf16[528,128]{1,0:T(8,128)(2,1)S(1)} %get-tuple-element.28), channel_id=1, source_target_pairs={{0,8},{4,12},{8,0},{12,4},{16,24},{20,28},{24,16},{28,20},{1,9},{5... | collective-permute-start | bytes 405512 | tf_op jit(solution)/shard_map/ppermute | solution.py:342
  7.9 0.2 collective-permute-start.3
  8.1 3.0 %collective-permute-start = (bf16[128,512]{1,0:T(8,128)(2,1)S(1)}, bf16[128,512]{1,0:T(8,128)(2,1)S(1)}, u32[]{:S(2)}, u32[]{:S(2)}) collective-permute-start(bf16[128,512]{1,0:T(8,128)(2,1)S(1)} %keys_beside_values.1.refs_0_), channel_id=1, source_target_pairs={{0,16},{4,20},{8,24},{12,28},{16,0},{20,4},{24,8},{28,12},{1,17},{... | collective-permute-start | bytes 393224 | tf_op jit(solution)/shard_map/ppermute | solution.py:348
  11.1 2.8 %intra_block.1 = (f32[128,2048]{1,0:T(8,128)S(1)}, bf16[128,2048]{1,0:T(8,128)(2,1)S(1)}, f32[128,2048]{1,0:T(8,128)S(1)}, f32[128,16]{1,0:T(8,128)S(1)}) custom-call(f32[128,128]{1,0:T(8,128)S(1)} %get-tuple-element.25.refs_2_.refs_0_, f32[128,128]{1,0:T(8,128)S(1)} %get-tuple-element.30.refs_1_, f32[16,128]{1,0:T(8,128)S(1)} %copy-done.7, ...), custom_call_target="tpu_custom_call" | custom-call | flops 134217728 | bytes 4874240 | tf_op jit(solution)/shard_map/intra_block/pallas_call | solution.py:316
  13.8 3.0 %collective-permute-done.2.refs_2_ = bf16[528,128]{1,0:T(8,128)(2,1)S(1)} collective-permute-done((bf16[528,128]{1,0:T(8,128)(2,1)S(1)}, bf16[528,128]{1,0:T(8,128)(2,1)S(1)}, u32[]{:S(2)}, u32[]{:S(2)}) %collective-permute-start.2) | collective-permute-done | bytes 135200 | tf_op jit(solution)/shard_map/ppermute | solution.py:342
  16.9 0.2 group_state.1.refs_2_
  17.0 1.5 %collective-permute-start.8 = (bf16[528,128]{1,0:T(8,128)(2,1)S(1)}, bf16[528,128]{1,0:T(8,128)(2,1)S(1)}, u32[]{:S(2)}, u32[]{:S(2)}) collective-permute-start(bf16[528,128]{1,0:T(8,128)(2,1)S(1)} %group_state.1.refs_2_), channel_id=1, source_target_pairs={{0,16},{4,20},{8,24},{12,28},{16,0},{20,4},{24,8},{28,12},{1,17},{... | collective-permute-start | bytes 405512 | tf_op jit(solution)/shard_map/ppermute | solution.py:348
  18.6 2.5 %collective-permute-start.4 = (bf16[256,512]{1,0:T(8,128)(2,1)S(1)}, bf16[256,512]{1,0:T(8,128)(2,1)S(1)}, u32[]{:S(2)}, u32[]{:S(2)}) collective-permute-start(bf16[256,512]{1,0:T(8,128)(2,1)S(1)} %stack_keys_values.1.refs_2_), channel_id=1, source_target_pairs={{0,8},{4,12},{8,0},{12,4},{16,24},{20,28},{24,16},{28,20},{1,9},{5... | collective-permute-start | bytes 786440 | tf_op jit(solution)/shard_map/ppermute | solution.py:342
  21.1 4.3 %collective-permute-done.8.refs_4_ = bf16[528,128]{1,0:T(8,128)(2,1)S(1)} collective-permute-done((bf16[528,128]{1,0:T(8,128)(2,1)S(1)}, bf16[528,128]{1,0:T(8,128)(2,1)S(1)}, u32[]{:S(2)}, u32[]{:S(2)}) %collective-permute-start.8) | collective-permute-done | bytes 135200 | tf_op jit(solution)/shard_map/ppermute | solution.py:348
  25.4 0.2 prefix_states.1
  25.7 2.1 %collective-permute-start.10 = (bf16[512,128]{1,0:T(8,128)(2,1)S(1)}, bf16[512,128]{1,0:T(8,128)(2,1)S(1)}, u32[]{:S(2)}, u32[]{:S(2)}) collective-permute-start(bf16[512,128]{1,0:T(8,128)(2,1)S(1)} %get-tuple-element.43), channel_id=1, source_target_pairs={{0,8},{4,12},{8,0},{12,4},{16,24},{20,28},{24,16},{28,20},{1,9},{5... | collective-permute-start | bytes 393224 | tf_op jit(solution)/shard_map/ppermute | solution.py:342
  27.7 1.4 %collective-permute-start.11 = (bf16[512,128]{1,0:T(8,128)(2,1)S(1)}, bf16[512,128]{1,0:T(8,128)(2,1)S(1)}, u32[]{:S(2)}, u32[]{:S(2)}) collective-permute-start(bf16[512,128]{1,0:T(8,128)(2,1)S(1)} %get-tuple-element.44), channel_id=1, source_target_pairs={{0,4},{4,0},{8,12},{12,8},{16,20},{20,16},{24,28},{28,24},{1,5},{5... | collective-permute-start | bytes 393224 | tf_op jit(solution)/shard_map/ppermute | solution.py:342
  29.2 1.2 %collective-permute-start.7 = (bf16[128,512]{1,0:T(8,128)(2,1)S(1)}, bf16[128,512]{1,0:T(8,128)(2,1)S(1)}, u32[]{:S(2)}, u32[]{:S(2)}) collective-permute-start(bf16[128,512]{1,0:T(8,128)(2,1)S(1)} %get-tuple-element.35), channel_id=1, source_target_pairs={{0,8},{4,12},{8,0},{12,4},{16,24},{20,28},{24,16},{28,20},{1,9},{5... | collective-permute-start | bytes 393224 | tf_op jit(solution)/shard_map/ppermute | solution.py:342
  31.1 2.4 %softmax_first.1 = (f32[128,4096]{1,0:T(8,128)S(1)}, f32[128,8]{1,0:T(8,128)S(1)}, f32[128,8]{1,0:T(8,128)S(1)}) custom-call(s32[1]{0:T(128)S(6)} %copy.12.refs_0_, bf16[128,2048]{1,0:T(8,128)(2,1)S(1)} %copy-done.4, bf16[256,512]{1,0:T(8,128)(2,1)S(1)} %stack_keys_values.1.refs_2_, bf16[256,512]{1,0:T(8,128)(2,1)S(1)} %collective-permute-done.4.refs_0_.refs_3_, ...), custom_call_target="tpu_custom_call" | custom-call | flops 805306368 | bytes 3416068 | tf_op jit(solution)/shard_map/softmax_first/pallas_call | solution.py:316
  33.5 1.5 %collective-permute-done.10.refs_5_ = bf16[512,128]{1,0:T(8,128)(2,1)S(1)} collective-permute-done((bf16[512,128]{1,0:T(8,128)(2,1)S(1)}, bf16[512,128]{1,0:T(8,128)(2,1)S(1)}, u32[]{:S(2)}, u32[]{:S(2)}) %collective-permute-start.10) | collective-permute-done | bytes 131104 | tf_op jit(solution)/shard_map/ppermute | solution.py:342
  35.0 0.7 %inter_block.1 = (f32[128,2048]{1,0:T(8,128)S(1)}, f32[8,128]{1,0:T(8,128)S(1)}) custom-call(f32[128,16]{1,0:T(8,128)S(1)} %get-tuple-element.39.refs_0_, bf16[128,2048]{1,0:T(8,128)(2,1)S(1)} %get-tuple-element.40.refs_1_, f32[128,2048]{1,0:T(8,128)S(1)} %get-tuple-element.33.refs_4_.refs_2_, bf16[512,128]{1,0:T(8,128)(2,1)S(1)} %get-tuple-element.41.refs_3_, ...), custom_call_target="tpu_custom_call" | custom-call | flops 67108864 | bytes 3158016 | tf_op jit(solution)/shard_map/inter_block/pallas_call | solution.py:316
  35.7 1.5 %collective-permute-start.13 = (f32[8,128]{1,0:T(8,128)S(1)}, f32[8,128]{1,0:T(8,128)S(1)}, u32[]{:S(2)}, u32[]{:S(2)}) collective-permute-start(f32[8,128]{1,0:T(8,128)S(1)} %get-tuple-element.47.refs_3_), channel_id=1, source_target_pairs={{0,2},{1,3},{2,0},{3,1},{4,6},{5,7},{6,4},{7,5},{8,10},{9,11},{10,... | collective-permute-start | bytes 12296 | tf_op jit(solution)/shard_map/ppermute | solution.py:482
  37.2 0.4 %collective-permute-start.14 = (f32[8,128]{1,0:T(8,128)S(1)}, f32[8,128]{1,0:T(8,128)S(1)}, u32[]{:S(2)}, u32[]{:S(2)}) collective-permute-start(f32[8,128]{1,0:T(8,128)S(1)} %get-tuple-element.47.refs_3_), channel_id=1, source_target_pairs={{0,1},{1,0},{2,3},{3,2},{4,5},{5,4},{6,7},{7,6},{8,9},{9,8},{10,11... | collective-permute-start | bytes 12296 | tf_op jit(solution)/shard_map/ppermute | solution.py:482
  37.6 2.5 %softmax_last.1.refs_0_ = bf16[128,2048]{1,0:T(8,128)(2,1)S(1)} custom-call(s32[1]{0:T(128)S(6)} %copy.12.refs_0_, bf16[128,2048]{1,0:T(8,128)(2,1)S(1)} %copy-done.4, bf16[256,512]{1,0:T(8,128)(2,1)S(1)} %pad_maximum_fusion.refs_2_, f32[128,4096]{1,0:T(8,128)S(1)} %get-tuple-element.36.refs_3_, f32[128,8]{1,0:T(8,128)S(1)} %get-tuple-element.37.refs_4_.refs_7_, ...), custom_call_target="tpu_custom_call" | custom-call | flops 268435456 | bytes 3416068 | tf_op jit(solution)/shard_map/softmax_last/pallas_call | solution.py:316
  40.1 1.1 %results.1 = (bf16[128,2048]{1,0:T(8,128)(2,1)}, bf16[128,2048]{1,0:T(8,128)(2,1)}) custom-call(bf16[128,2048]{1,0:T(8,128)(2,1)S(1)} %softmax_last.1.refs_0_, f32[128,2048]{1,0:T(8,128)S(1)} %get-tuple-element.45.refs_1_, f32[128,2048]{1,0:T(8,128)S(1)} %get-tuple-element.46.refs_2_, f32[8,128]{1,0:T(8,128)S(1)} %get-tuple-element.47.refs_3_, ...), custom_call_target="tpu_custom_call" | custom-call | flops 1048576 | bytes 3686400 | tf_op jit(solution)/shard_map/results/pallas_call | solution.py:316
  (37 shorter events, 0.4 us)
Async XLA Ops:
  0.6 0.7 %copy-start.7 = (f32[16,128]{1,0:T(8,128)S(1)}, f32[16,128]{1,0:T(8,128)}, u32[]{:S(2)}) copy-start(f32[16,128]{1,0:T(8,128)} %refs_2_.3) | copy-start | bytes 24580
  0.6 1.0 %copy-start.2 = (bf16[128,2048]{1,0:T(8,128)(2,1)S(1)}, bf16[128,2048]{1,0:T(8,128)(2,1)}, u32[]{:S(2)}) copy-start(bf16[128,2048]{1,0:T(8,128)(2,1)} %refs_2_.2) | copy-start | bytes 1572868
  0.7 1.2 %copy-start.3 = (bf16[128,2048]{1,0:T(8,128)(2,1)S(1)}, bf16[128,2048]{1,0:T(8,128)(2,1)}, u32[]{:S(2)}) copy-start(bf16[128,2048]{1,0:T(8,128)(2,1)} %refs_3_.2) | copy-start | bytes 1572868
  0.7 7.4 %copy-start.5 = (bf16[128,256]{1,0:T(8,128)(2,1)S(1)}, bf16[128,256]{1,0:T(8,128)(2,1)}, u32[]{:S(2)}) copy-start(bf16[128,256]{1,0:T(8,128)(2,1)} %refs_0_.3) | copy-start | bytes 196612
  0.7 7.4 %copy-start.6 = (bf16[128,256]{1,0:T(8,128)(2,1)S(1)}, bf16[128,256]{1,0:T(8,128)(2,1)}, u32[]{:S(2)}) copy-start(bf16[128,256]{1,0:T(8,128)(2,1)} %refs_1_.4) | copy-start | bytes 196612
  0.7 10.4 %copy-start = (bf16[128,2048]{1,0:T(8,128)(2,1)S(1)}, bf16[128,2048]{1,0:T(8,128)(2,1)}, u32[]{:S(2)}) copy-start(bf16[128,2048]{1,0:T(8,128)(2,1)} %refs_3_.3) | copy-start | bytes 1572868
  0.7 10.4 %copy-start.1 = (bf16[128,2048]{1,0:T(8,128)(2,1)S(1)}, bf16[128,2048]{1,0:T(8,128)(2,1)}, u32[]{:S(2)}) copy-start(bf16[128,2048]{1,0:T(8,128)(2,1)} %refs_6_.1) | copy-start | bytes 1572868
  0.7 10.4 %copy-start.8 = (f32[2048]{0:T(1024)S(1)}, f32[2048]{0:T(1024)}, u32[]{:S(2)}) copy-start(f32[2048]{0:T(1024)} %param.15) | copy-start | bytes 24580
  3.4 10.4 %collective-permute-start.1 = (bf16[528,128]{1,0:T(8,128)(2,1)S(1)}, bf16[528,128]{1,0:T(8,128)(2,1)S(1)}, u32[]{:S(2)}, u32[]{:S(2)}) collective-permute-start(bf16[528,128]{1,0:T(8,128)(2,1)S(1)} %get-tuple-element.27), channel_id=1, source_target_pairs={{0,12},{4,8},{8,4},{12,0},{16,28},{20,24},{24,20},{28,16},{1,13},{... | collective-permute-start | bytes 405512 | tf_op jit(solution)/shard_map/ppermute | solution.py:342
  7.4 9.4 %collective-permute-start.2 = (bf16[528,128]{1,0:T(8,128)(2,1)S(1)}, bf16[528,128]{1,0:T(8,128)(2,1)S(1)}, u32[]{:S(2)}, u32[]{:S(2)}) collective-permute-start(bf16[528,128]{1,0:T(8,128)(2,1)S(1)} %get-tuple-element.28), channel_id=1, source_target_pairs={{0,8},{4,12},{8,0},{12,4},{16,24},{20,28},{24,16},{28,20},{1,9},{5... | collective-permute-start | bytes 405512 | tf_op jit(solution)/shard_map/ppermute | solution.py:342
  7.9 9.0 %collective-permute-start.3 = (bf16[528,128]{1,0:T(8,128)(2,1)S(1)}, bf16[528,128]{1,0:T(8,128)(2,1)S(1)}, u32[]{:S(2)}, u32[]{:S(2)}) collective-permute-start(bf16[528,128]{1,0:T(8,128)(2,1)S(1)} %get-tuple-element.29), channel_id=1, source_target_pairs={{0,4},{4,0},{8,12},{12,8},{16,20},{20,16},{24,28},{28,24},{1,5},{5... | collective-permute-start | bytes 405512 | tf_op jit(solution)/shard_map/ppermute | solution.py:342
  8.1 10.4 %collective-permute-start = (bf16[128,512]{1,0:T(8,128)(2,1)S(1)}, bf16[128,512]{1,0:T(8,128)(2,1)S(1)}, u32[]{:S(2)}, u32[]{:S(2)}) collective-permute-start(bf16[128,512]{1,0:T(8,128)(2,1)S(1)} %keys_beside_values.1.refs_0_), channel_id=1, source_target_pairs={{0,16},{4,20},{8,24},{12,28},{16,0},{20,4},{24,8},{28,12},{1,17},{... | collective-permute-start | bytes 393224 | tf_op jit(solution)/shard_map/ppermute | solution.py:348
  17.0 8.4 %collective-permute-start.8 = (bf16[528,128]{1,0:T(8,128)(2,1)S(1)}, bf16[528,128]{1,0:T(8,128)(2,1)S(1)}, u32[]{:S(2)}, u32[]{:S(2)}) collective-permute-start(bf16[528,128]{1,0:T(8,128)(2,1)S(1)} %group_state.1.refs_2_), channel_id=1, source_target_pairs={{0,16},{4,20},{8,24},{12,28},{16,0},{20,4},{24,8},{28,12},{1,17},{... | collective-permute-start | bytes 405512 | tf_op jit(solution)/shard_map/ppermute | solution.py:348
  18.6 12.5 %copy-start.4 = (bf16[128,2048]{1,0:T(8,128)(2,1)S(1)}, bf16[128,2048]{1,0:T(8,128)(2,1)}, u32[]{:S(2)}) copy-start(bf16[128,2048]{1,0:T(8,128)(2,1)} %refs_1_.7) | copy-start | bytes 1572868
  18.6 10.6 %collective-permute-start.4 = (bf16[256,512]{1,0:T(8,128)(2,1)S(1)}, bf16[256,512]{1,0:T(8,128)(2,1)S(1)}, u32[]{:S(2)}, u32[]{:S(2)}) collective-permute-start(bf16[256,512]{1,0:T(8,128)(2,1)S(1)} %stack_keys_values.1.refs_2_), channel_id=1, source_target_pairs={{0,8},{4,12},{8,0},{12,4},{16,24},{20,28},{24,16},{28,20},{1,9},{5... | collective-permute-start | bytes 786440 | tf_op jit(solution)/shard_map/ppermute | solution.py:342
  21.1 8.1 %collective-permute-start.5 = (bf16[256,512]{1,0:T(8,128)(2,1)S(1)}, bf16[256,512]{1,0:T(8,128)(2,1)S(1)}, u32[]{:S(2)}, u32[]{:S(2)}) collective-permute-start(bf16[256,512]{1,0:T(8,128)(2,1)S(1)} %stack_keys_values.1.refs_2_), channel_id=1, source_target_pairs={{0,4},{4,0},{8,12},{12,8},{16,20},{20,16},{24,28},{28,24},{1,5},{5... | collective-permute-start | bytes 786440 | tf_op jit(solution)/shard_map/ppermute | solution.py:342
  25.6 7.9 %collective-permute-start.9 = (bf16[512,128]{1,0:T(8,128)(2,1)S(1)}, bf16[512,128]{1,0:T(8,128)(2,1)S(1)}, u32[]{:S(2)}, u32[]{:S(2)}) collective-permute-start(bf16[512,128]{1,0:T(8,128)(2,1)S(1)} %get-tuple-element.42), channel_id=1, source_target_pairs={{0,12},{4,8},{8,4},{12,0},{16,28},{20,24},{24,20},{28,16},{1,13},{... | collective-permute-start | bytes 393224 | tf_op jit(solution)/shard_map/ppermute | solution.py:342
  25.7 9.3 %collective-permute-start.10 = (bf16[512,128]{1,0:T(8,128)(2,1)S(1)}, bf16[512,128]{1,0:T(8,128)(2,1)S(1)}, u32[]{:S(2)}, u32[]{:S(2)}) collective-permute-start(bf16[512,128]{1,0:T(8,128)(2,1)S(1)} %get-tuple-element.43), channel_id=1, source_target_pairs={{0,8},{4,12},{8,0},{12,4},{16,24},{20,28},{24,16},{28,20},{1,9},{5... | collective-permute-start | bytes 393224 | tf_op jit(solution)/shard_map/ppermute | solution.py:342
  27.7 7.3 %collective-permute-start.11 = (bf16[512,128]{1,0:T(8,128)(2,1)S(1)}, bf16[512,128]{1,0:T(8,128)(2,1)S(1)}, u32[]{:S(2)}, u32[]{:S(2)}) collective-permute-start(bf16[512,128]{1,0:T(8,128)(2,1)S(1)} %get-tuple-element.44), channel_id=1, source_target_pairs={{0,4},{4,0},{8,12},{12,8},{16,20},{20,16},{24,28},{28,24},{1,5},{5... | collective-permute-start | bytes 393224 | tf_op jit(solution)/shard_map/ppermute | solution.py:342
  29.2 8.4 %collective-permute-start.7 = (bf16[128,512]{1,0:T(8,128)(2,1)S(1)}, bf16[128,512]{1,0:T(8,128)(2,1)S(1)}, u32[]{:S(2)}, u32[]{:S(2)}) collective-permute-start(bf16[128,512]{1,0:T(8,128)(2,1)S(1)} %get-tuple-element.35), channel_id=1, source_target_pairs={{0,8},{4,12},{8,0},{12,4},{16,24},{20,28},{24,16},{28,20},{1,9},{5... | collective-permute-start | bytes 393224 | tf_op jit(solution)/shard_map/ppermute | solution.py:342
  30.4 7.2 %collective-permute-start.6 = (bf16[128,512]{1,0:T(8,128)(2,1)S(1)}, bf16[128,512]{1,0:T(8,128)(2,1)S(1)}, u32[]{:S(2)}, u32[]{:S(2)}) collective-permute-start(bf16[128,512]{1,0:T(8,128)(2,1)S(1)} %get-tuple-element.34), channel_id=1, source_target_pairs={{0,4},{4,0},{8,12},{12,8},{16,20},{20,16},{24,28},{28,24},{1,5},{5... | collective-permute-start | bytes 393224 | tf_op jit(solution)/shard_map/ppermute | solution.py:342
  35.7 4.4 %collective-permute-start.12 = (f32[8,128]{1,0:T(8,128)S(1)}, f32[8,128]{1,0:T(8,128)S(1)}, u32[]{:S(2)}, u32[]{:S(2)}) collective-permute-start(f32[8,128]{1,0:T(8,128)S(1)} %get-tuple-element.47.refs_3_), channel_id=1, source_target_pairs={{0,3},{1,2},{2,1},{3,0},{4,7},{5,6},{6,5},{7,4},{8,11},{9,10},{10,... | collective-permute-start | bytes 12296 | tf_op jit(solution)/shard_map/ppermute | solution.py:482
  35.7 4.4 %collective-permute-start.13 = (f32[8,128]{1,0:T(8,128)S(1)}, f32[8,128]{1,0:T(8,128)S(1)}, u32[]{:S(2)}, u32[]{:S(2)}) collective-permute-start(f32[8,128]{1,0:T(8,128)S(1)} %get-tuple-element.47.refs_3_), channel_id=1, source_target_pairs={{0,2},{1,3},{2,0},{3,1},{4,6},{5,7},{6,4},{7,5},{8,10},{9,11},{10,... | collective-permute-start | bytes 12296 | tf_op jit(solution)/shard_map/ppermute | solution.py:482
  37.2 2.9 %collective-permute-start.14 = (f32[8,128]{1,0:T(8,128)S(1)}, f32[8,128]{1,0:T(8,128)S(1)}, u32[]{:S(2)}, u32[]{:S(2)}) collective-permute-start(f32[8,128]{1,0:T(8,128)S(1)} %get-tuple-element.47.refs_3_), channel_id=1, source_target_pairs={{0,1},{1,0},{2,3},{3,2},{4,5},{5,4},{6,7},{7,6},{8,9},{9,8},{10,11... | collective-permute-start | bytes 12296 | tf_op jit(solution)/shard_map/ppermute | solution.py:482

commit v11 on v10

--- a/solution.py
+++ b/solution.py
@@ -54,36 +54,49 @@
     bias_ref[...] = jnp.where(lower, 0.0, -1e30)
 
 
-def state_kernel(group, heads, tri_ref, ld_ref, k_ref, v_ref, *rest):
-    outs, (ka_ref, va_ref, states, totals) = rest[:group], rest[group:]
-    tokens = k_ref.shape[0]
-    per = heads // group
-    rank = my_rank(group)
+def decay_weights(tri_ref, ld_ref):
     ld = ld_ref[...]
     cum = lax.dot_general(tri_ref[...], ld, NT, precision=HIGH, preferred_element_type=F32)
-    weight = jnp.exp(cum[tokens - 1 : tokens, :] - cum)
-    total = jnp.broadcast_to(jnp.exp(jnp.sum(ld, axis=1, keepdims=True)), (heads, HD))
-    high = total.astype(BF16).astype(F32)
-    low = total - high
-    totals[...] = jnp.zeros_like(totals)
-    for k in range(group):
-        totals[k * 16 : k * 16 + per, :] = high[k * per : (k + 1) * per]
-        totals[k * 16 + 8 : k * 16 + 8 + per, :] = low[k * per : (k + 1) * per]
-    for h in range(heads):
+    return jnp.exp(cum[-1:, :] - cum), jnp.exp(jnp.sum(ld, axis=1, keepdims=True))
+
+
+def owner_states(k, per, weight, total, k_ref, v_ref, out):
+    for j in range(per):
+        h = k * per + j
         ka = silu16(k_ref[:, head_cols(h)])
         va = silu16(v_ref[:, head_cols(h)])
-        ka_ref[:, head_cols(h)] = ka
-        va_ref[:, head_cols(h)] = va
         kdec = ka.astype(F32) * weight[:, h : h + 1]
         khigh = kdec.astype(BF16)
         klow = (kdec - khigh.astype(F32)).astype(BF16)
         state = lax.dot_general(khigh, va, TN, preferred_element_type=F32)
         state += lax.dot_general(klow, va, TN, preferred_element_type=F32)
-        states[h * HD : (h + 1) * HD, :] = state.astype(BF16)
-    for s in range(group):
-        dest = rank ^ s
-        outs[s][: per * HD, :] = states[dyn(dest, per * HD), :]
-        outs[s][per * HD :, :] = totals[dyn(dest, 16), :].astype(BF16)
+        out[j * HD : (j + 1) * HD, :] = state.astype(BF16)
+    mine = jnp.broadcast_to(total[k * per : (k + 1) * per], (per, HD))
+    high = mine.astype(BF16).astype(F32)
+    pad = [jnp.zeros((8 - per, HD), F32)] if per < 8 else []
+    tail = jnp.concatenate([high, *pad, mine - high, *pad], axis=0)
+    out[per * HD :, :] = tail.astype(BF16)
+
+
+def first_state_kernel(group, per, first, tri_ref, ld_ref, k_ref, v_ref, out_ref):
+    weight, total = decay_weights(tri_ref, ld_ref)
+    dest = my_rank(group) ^ first
+    for k in range(group):
+        pl.when(dest == k)(
+            functools.partial(owner_states, k, per, weight, total, k_ref, v_ref, out_ref)
+        )
+
+
+def other_states_kernel(group, per, first, others, tri_ref, ld_ref, k_ref, v_ref, *rest):
+    outs, payloads = rest[:-1], rest[-1]
+    weight, total = decay_weights(tri_ref, ld_ref)
+    rank = my_rank(group)
+    for k in range(group):
+        pl.when((rank ^ first) != k)(
+            functools.partial(owner_states, k, per, weight, total, k_ref, v_ref, payloads.at[k])
+        )
+    for s, out in zip(others, outs):
+        out[...] = payloads[rank ^ s]
 
 
 def beside_kernel(keys, values, out):
@@ -109,18 +122,14 @@
     return tail[j : j + 1] + tail[8 + j : 9 + j]
 
 
-def sent(group):
-    return [0, *range(group - 1, 0, -1)]
-
-
-def fill_slots(group, rank, pays, slots):
-    for s, pay in zip(sent(group), pays):
+def fill_slots(order, rank, pays, slots):
+    for s, pay in zip(order, pays):
         slots[rank ^ s] = pay[...]
 
 
-def total_kernel(group, per, *refs):
+def total_kernel(group, per, order, *refs):
     pays, out, slots = refs[:group], refs[group], refs[group + 1]
-    fill_slots(group, my_rank(group), pays, slots)
+    fill_slots(order, my_rank(group), pays, slots)
     base = per * HD
     tails = []
     for j in range(per):
@@ -138,7 +147,7 @@
     out[base:, :] = jnp.concatenate([high, total - high], axis=0).astype(BF16)
 
 
-def prefix_kernel(group, per, carried, *refs):
+def prefix_kernel(group, per, order, carried, *refs):
     pays, refs = refs[:group], refs[group:]
     carry = None
     if carried:
@@ -146,7 +155,7 @@
     outs, slots, prefixes = refs[:group], refs[group], refs[group + 1]
     rank = my_rank(group)
     later = lax.axis_index("ctx") >= group
-    fill_slots(group, rank, pays, slots)
+    fill_slots(order, rank, pays, slots)
     base = per * HD
     for j in range(per):
         rows = slice(j * HD, (j + 1) * HD)
@@ -161,7 +170,7 @@
         outs[s][...] = prefixes[rank ^ s]
 
 
-def intra_kernel(heads, tri_ref, bias_ref, ld_ref, q_ref, ka_ref, va_ref, gate_ref, gain_ref, *outs):
+def intra_kernel(heads, tri_ref, bias_ref, ld_ref, q_ref, k_ref, v_ref, gate_ref, gain_ref, *outs):
     intra_ref, qa_ref, gain_out, decay_out = outs
     ld = ld_ref[...]
     tri = tri_ref[...]
@@ -173,20 +182,22 @@
         cols = head_cols(h)
         qa = silu16(q_ref[:, cols])
         qa_ref[:, cols] = qa
-        scores = lax.dot_general(qa, ka_ref[:, cols], NT, preferred_element_type=F32)
+        ka = silu16(k_ref[:, cols])
+        va = silu16(v_ref[:, cols])
+        scores = lax.dot_general(qa, ka, NT, preferred_element_type=F32)
         decay = jnp.exp((cum[:, h : h + 1] - cum_t[h : h + 1, :]) + bias)
         weights = (scores * decay).astype(BF16)
-        intra_ref[:, cols] = jnp.dot(weights, va_ref[:, cols], preferred_element_type=F32)
+        intra_ref[:, cols] = jnp.dot(weights, va, preferred_element_type=F32)
         gate = 1.0 / (1.0 + jnp.exp(-gate_ref[:, cols].astype(F32)))
         gain_out[:, cols] = gate * gain_ref[:, cols]
 
 
-def inter_kernel(group, heads, decay_ref, qa_ref, intra_ref, *rest):
+def inter_kernel(group, heads, order, decay_ref, qa_ref, intra_ref, *rest):
     parts, (lin_ref, squares_ref, states) = rest[:group], rest[group:]
     tokens = qa_ref.shape[0]
     per = heads // group
     rank = my_rank(group)
-    for s, part in zip(sent(group), parts):
+    for s, part in zip(order, parts):
         states[dyn(rank ^ s, per * HD), :] = part[...]
     decay = decay_ref[...]
     acc = jnp.zeros((tokens, HD), F32)
@@ -341,9 +352,6 @@
     def swap(x, s):
         return lax.ppermute(x, "ctx", [(c, c ^ s) for c in range(n)])
 
-    def swap_all(xs):
-        return [swap(xs[s], s) if s else xs[s] for s in sent(group)]
-
     def ahead(x, d):
         return lax.ppermute(x, "ctx", [(c, (c + d * group) % n) for c in range(n)])
 
@@ -359,16 +367,29 @@
     )
     far = [ahead(kv, d) for d in range(1, groups)]
 
-    *pays, ka, va = call(
-        functools.partial(state_kernel, group, heads),
-        "block_states",
-        [shape((rows, HD), BF16)] * group + [shape((tokens, width), BF16)] * 2,
+    to, back = (0, 2, 3, 1), (0, 3, 2, 1)
+    others = [s for s in to if s != to[1]]
+    payload = shape((rows, HD), BF16)
+    (early,) = call(
+        functools.partial(first_state_kernel, group, per, to[1]),
+        "first_states",
+        [payload],
         (tri, log_decay, k_lin, v_lin),
-        [pltpu.VMEM((heads * HD, HD), BF16), pltpu.VMEM((group * 16, HD), F32)],
+        flops=4 * cube // group,
+        exps=2 * tokens * width // group,
+    )
+    late = call(
+        functools.partial(other_states_kernel, group, per, to[1], others),
+        "other_states",
+        [payload] * len(others),
+        (tri, log_decay, k_lin, v_lin),
+        [pltpu.VMEM((group, rows, HD), BF16)],
         flops=4 * cube,
         exps=2 * tokens * width,
     )
-    pays = swap_all(pays)
+    pays = {to[1]: early, **dict(zip(others, late))}
+    pays = [swap(pays[s], s) if s else pays[s] for s in to]
+
     intra, qa, gain, decay = call(
         functools.partial(intra_kernel, heads),
         "intra_block",
@@ -378,7 +399,7 @@
             shape((tokens, width), F32),
             shape((tokens, heads), F32),
         ],
-        (tri, bias, log_decay, q_lin, ka, va, gate, norm_gain.reshape(1, width)),
+        (tri, bias, log_decay, q_lin, k_lin, v_lin, gate, norm_gain.reshape(1, width)),
         flops=4 * cube,
         exps=4 * tokens * width,
     )
@@ -387,7 +408,7 @@
     carry = ()
     if groups > 1:
         (total,) = call(
-            functools.partial(total_kernel, group, per),
+            functools.partial(total_kernel, group, per, to),
             "group_state",
             [shape((rows, HD), BF16)],
             pays,
@@ -412,14 +433,14 @@
             shift *= 2
         carry = (before,)
     prefixes = call(
-        functools.partial(prefix_kernel, group, per, bool(carry)),
+        functools.partial(prefix_kernel, group, per, to, bool(carry)),
         "prefix_states",
         [shape((per * HD, HD), BF16)] * group,
         (*pays, *carry),
         [slots, pltpu.VMEM((group, per * HD, HD), BF16)],
         flops=1 << 33,
     )
-    prefixes = swap_all(prefixes)
+    prefixes = [swap(prefixes[s], s) if s else prefixes[s] for s in back]
 
     (own,) = call(
         stack_kernel,
@@ -430,9 +451,6 @@
         flops=1 << 32,
     )
     side, near = swap(own, 2), swap(own, 1)
-    half = shape((own.shape[0] // 2, own.shape[1]), BF16)
-    upper, under = call(halves_kernel, "sent_on", [half] * 2, (side, near))
-    across = jnp.concatenate([swap(upper, 1), swap(under, 2)])
     share = width // kv_heads
     pack = 2 if share // HD % 2 == 0 else 1
     span = own.shape[0]
@@ -454,6 +472,9 @@
         limit=room,
         specs=[smem] + [VMEM] * 4,
     )
+    half = shape((own.shape[0] // 2, own.shape[1]), BF16)
+    upper, under = call(halves_kernel, "sent_on", [half] * 2, (side, near), after=tops[:1])
+    across = jnp.concatenate([swap(upper, 1), swap(under, 2)])
     (attended,) = call(
         functools.partial(softmax_last_kernel, group, (3,), kv_heads, pack),
         "softmax_last",
@@ -467,7 +488,7 @@
     )
 
     lin, squares = call(
-        functools.partial(inter_kernel, group, heads),
+        functools.partial(inter_kernel, group, heads, back),
         "inter_block",
         [shape((tokens, width), F32), shape((8, tokens), F32)],
         (decay, qa, intra, *prefixes),

time: 41.4 us -> 42.3 us (1.022)
  starting transfers between devices: 18.4 us -> 19 us
  Pallas kernels: 11.3 us -> 11.8 us
    ppermute x2, starting transfers between devices: 4.45 us -> 5.61 us  [ahead(): return lax.ppermute(x, 'ctx', [(c, (c + d * group) % n) for c in range(n)])]
    ppermute x10, waiting for transfers between devices: 4.63 us -> 4.03 us  [swap(): return lax.ppermute(x, 'ctx', [(c, c ^ s) for c in range(n)])]
    pallas_call x12 -> x13, Pallas kernels: 11.3 us -> 11.8 us  [call(): pl.pallas_call(run, name=name, out_shape=list(outs), in_specs=specs, scra...]
    ppermute x10, starting transfers between devices: 12 us -> 11.5 us  [swap(): return lax.ppermute(x, 'ctx', [(c, c ^ s) for c in range(n)])]
  transfers between devices with their start and end apart: 15 -> 15, of which waited for: 3 -> 4; matrix products, arithmetic and copies ran while one was open for 0% -> 0% of each run, Pallas kernels for 21% -> 24%
where the time goes in v11:
time: 42.3 us; the launch traced here: 42.1 us
  starting transfers between devices  19 us (45%)
  Pallas kernels  11.8 us (28%)
  waiting for transfers between devices  8.57 us (20%)
  between operations  1.5 us (4%)
  local copies, waits for them, and re-layouts  1.15 us (3%)
    pallas_call x13, Pallas kernels, call(): pl.pallas_call(run, name=name, out_shape=list(outs), in_specs=specs, scra...  11.8 us
    ppermute x10, starting transfers between devices, swap(): return lax.ppermute(x, 'ctx', [(c, c ^ s) for c in range(n)])  11.5 us
    ppermute x2, starting transfers between devices, ahead(): return lax.ppermute(x, 'ctx', [(c, (c + d * group) % n) for c in range(n)])  5.61 us
    ppermute x2, waiting for transfers between devices, ahead(): return lax.ppermute(x, 'ctx', [(c, (c + d * group) % n) for c in range(n)])  4.53 us
    ppermute x10, waiting for transfers between devices, swap(): return lax.ppermute(x, 'ctx', [(c, c ^ s) for c in range(n)])  4.03 us
    ppermute x3, starting transfers between devices, body(): parts = [squares] + [lax.ppermute(squares, 'head', turn) for turn in turns]  1.89 us
    unnamed x18, local copies, waits for them, and re-layouts  1.15 us
  transfers between devices with their start and end apart: 15, of which 4 were waited for; matrix products, arithmetic and copies ran while one was open for 0% of the time, Pallas kernels for 24%

profile of v11, /device:TPU:0, one launch (start us, length us, event | category | flops | bytes accessed | tf_op | source)
XLA Modules:
  0.0 42.1 jit_solution(13620445822395420014)
XLA Ops:
  0.7 0.6 %copy-done.5 = f32[16,128]{1,0:T(8,128)S(1)} copy-done((f32[16,128]{1,0:T(8,128)S(1)}, f32[16,128]{1,0:T(8,128)}, u32[]{:S(2)}) %copy-start.5) | copy-done | bytes 8216
  1.3 0.4 copy-done
  1.8 0.6 %first_states.1 = bf16[528,128]{1,0:T(8,128)(2,1)S(1)} custom-call(f32[128,128]{1,0:T(8,128)S(1)} %get-tuple-element.22.refs_2_.refs_0_, f32[16,128]{1,0:T(8,128)S(1)} %copy-done.5, bf16[128,2048]{1,0:T(8,128)(2,1)S(1)} %copy-done, bf16[128,2048]{1,0:T(8,128)(2,1)S(1)} %copy-done.1), custom_call_target="tpu_custom_call" | custom-call | flops 33554432 | bytes 1257472 | tf_op jit(solution)/shard_map/first_states/pallas_call | solution.py:327
  2.5 3.1 %collective-permute-start.1 = (bf16[528,128]{1,0:T(8,128)(2,1)S(1)}, bf16[528,128]{1,0:T(8,128)(2,1)S(1)}, u32[]{:S(2)}, u32[]{:S(2)}) collective-permute-start(bf16[528,128]{1,0:T(8,128)(2,1)S(1)} %first_states.1), channel_id=1, source_target_pairs={{0,8},{4,12},{8,0},{12,4},{16,24},{20,28},{24,16},{28,20},{1,9},{5... | collective-permute-start | bytes 405512 | tf_op jit(solution)/shard_map/ppermute | solution.py:353
  5.6 1.4 %other_states.1 = (bf16[528,128]{1,0:T(8,128)(2,1)S(1)}, bf16[528,128]{1,0:T(8,128)(2,1)S(1)}, bf16[528,128]{1,0:T(8,128)(2,1)S(1)}) custom-call(f32[128,128]{1,0:T(8,128)S(1)} %get-tuple-element.22.refs_2_.refs_0_, f32[16,128]{1,0:T(8,128)S(1)} %copy-done.5, bf16[128,2048]{1,0:T(8,128)(2,1)S(1)} %copy-done, bf16[128,2048]{1,0:T(8,128)(2,1)S(1)} %copy-done.1), custom_call_target="tpu_custom_call" | custom-call | flops 134217728 | bytes 1527808 | tf_op jit(solution)/shard_map/other_states/pallas_call | solution.py:327
  7.0 1.5 %collective-permute-start.2 = (bf16[528,128]{1,0:T(8,128)(2,1)S(1)}, bf16[528,128]{1,0:T(8,128)(2,1)S(1)}, u32[]{:S(2)}, u32[]{:S(2)}) collective-permute-start(bf16[528,128]{1,0:T(8,128)(2,1)S(1)} %get-tuple-element.24), channel_id=1, source_target_pairs={{0,12},{4,8},{8,4},{12,0},{16,28},{20,24},{24,20},{28,16},{1,13},{... | collective-permute-start | bytes 405512 | tf_op jit(solution)/shard_map/ppermute | solution.py:353
  8.6 3.0 %collective-permute-start = (bf16[128,512]{1,0:T(8,128)(2,1)S(1)}, bf16[128,512]{1,0:T(8,128)(2,1)S(1)}, u32[]{:S(2)}, u32[]{:S(2)}) collective-permute-start(bf16[128,512]{1,0:T(8,128)(2,1)S(1)} %keys_beside_values.1.refs_0_), channel_id=1, source_target_pairs={{0,16},{4,20},{8,24},{12,28},{16,0},{20,4},{24,8},{28,12},{1,17},{... | collective-permute-start | bytes 393224 | tf_op jit(solution)/shard_map/ppermute | solution.py:356
  12.3 2.8 %intra_block.1 = (f32[128,2048]{1,0:T(8,128)S(1)}, bf16[128,2048]{1,0:T(8,128)(2,1)S(1)}, f32[128,2048]{1,0:T(8,128)S(1)}, f32[128,16]{1,0:T(8,128)S(1)}) custom-call(f32[128,128]{1,0:T(8,128)S(1)} %get-tuple-element.22.refs_2_.refs_0_, f32[128,128]{1,0:T(8,128)S(1)} %get-tuple-element.26.refs_1_, f32[16,128]{1,0:T(8,128)S(1)} %copy-done.5, ...), custom_call_target="tpu_custom_call" | custom-call | flops 134217728 | bytes 4874240 | tf_op jit(solution)/shard_map/intra_block/pallas_call | solution.py:327
  15.1 0.9 %collective-permute-done.3.refs_3_ = bf16[528,128]{1,0:T(8,128)(2,1)S(1)} collective-permute-done((bf16[528,128]{1,0:T(8,128)(2,1)S(1)}, bf16[528,128]{1,0:T(8,128)(2,1)S(1)}, u32[]{:S(2)}, u32[]{:S(2)}) %collective-permute-start.3) | collective-permute-done | bytes 135200 | tf_op jit(solution)/shard_map/ppermute | solution.py:353
  16.2 2.7 %collective-permute-start.8 = (bf16[528,128]{1,0:T(8,128)(2,1)S(1)}, bf16[528,128]{1,0:T(8,128)(2,1)S(1)}, u32[]{:S(2)}, u32[]{:S(2)}) collective-permute-start(bf16[528,128]{1,0:T(8,128)(2,1)S(1)} %group_state.1.refs_2_), channel_id=1, source_target_pairs={{0,16},{4,20},{8,24},{12,28},{16,0},{20,4},{24,8},{28,12},{1,17},{... | collective-permute-start | bytes 405512 | tf_op jit(solution)/shard_map/ppermute | solution.py:356
  18.9 1.1 %collective-permute-start.4 = (bf16[256,512]{1,0:T(8,128)(2,1)S(1)}, bf16[256,512]{1,0:T(8,128)(2,1)S(1)}, u32[]{:S(2)}, u32[]{:S(2)}) collective-permute-start(bf16[256,512]{1,0:T(8,128)(2,1)S(1)} %stack_keys_values.1.refs_2_), channel_id=1, source_target_pairs={{0,8},{4,12},{8,0},{12,4},{16,24},{20,28},{24,16},{28,20},{1,9},{5... | collective-permute-start | bytes 786440 | tf_op jit(solution)/shard_map/ppermute | solution.py:353
  20.0 1.0 %collective-permute-start.5 = (bf16[256,512]{1,0:T(8,128)(2,1)S(1)}, bf16[256,512]{1,0:T(8,128)(2,1)S(1)}, u32[]{:S(2)}, u32[]{:S(2)}) collective-permute-start(bf16[256,512]{1,0:T(8,128)(2,1)S(1)} %stack_keys_values.1.refs_2_), channel_id=1, source_target_pairs={{0,4},{4,0},{8,12},{12,8},{16,20},{20,16},{24,28},{28,24},{1,5},{5... | collective-permute-start | bytes 786440 | tf_op jit(solution)/shard_map/ppermute | solution.py:353
  20.9 4.5 %collective-permute-done.8.refs_4_ = bf16[528,128]{1,0:T(8,128)(2,1)S(1)} collective-permute-done((bf16[528,128]{1,0:T(8,128)(2,1)S(1)}, bf16[528,128]{1,0:T(8,128)(2,1)S(1)}, u32[]{:S(2)}, u32[]{:S(2)}) %collective-permute-start.8) | collective-permute-done | bytes 135200 | tf_op jit(solution)/shard_map/ppermute | solution.py:356
  25.8 1.5 %collective-permute-start.10 = (bf16[512,128]{1,0:T(8,128)(2,1)S(1)}, bf16[512,128]{1,0:T(8,128)(2,1)S(1)}, u32[]{:S(2)}, u32[]{:S(2)}) collective-permute-start(bf16[512,128]{1,0:T(8,128)(2,1)S(1)} %get-tuple-element.37), channel_id=1, source_target_pairs={{0,8},{4,12},{8,0},{12,4},{16,24},{20,28},{24,16},{28,20},{1,9},{5... | collective-permute-start | bytes 393224 | tf_op jit(solution)/shard_map/ppermute | solution.py:353
  27.3 1.9 %collective-permute-start.11 = (bf16[512,128]{1,0:T(8,128)(2,1)S(1)}, bf16[512,128]{1,0:T(8,128)(2,1)S(1)}, u32[]{:S(2)}, u32[]{:S(2)}) collective-permute-start(bf16[512,128]{1,0:T(8,128)(2,1)S(1)} %get-tuple-element.38), channel_id=1, source_target_pairs={{0,4},{4,0},{8,12},{12,8},{16,20},{20,16},{24,28},{28,24},{1,5},{5... | collective-permute-start | bytes 393224 | tf_op jit(solution)/shard_map/ppermute | solution.py:353
  29.2 1.0 %collective-permute-done.4.refs_3_.refs_0_ = bf16[256,512]{1,0:T(8,128)(2,1)S(1)} collective-permute-done((bf16[256,512]{1,0:T(8,128)(2,1)S(1)}, bf16[256,512]{1,0:T(8,128)(2,1)S(1)}, u32[]{:S(2)}, u32[]{:S(2)}) %collective-permute-start.4) | collective-permute-done | bytes 262176 | tf_op jit(solution)/shard_map/ppermute | solution.py:353
  30.2 2.4 %softmax_first.1 = (f32[128,4096]{1,0:T(8,128)S(1)}, f32[128,8]{1,0:T(8,128)S(1)}, f32[128,8]{1,0:T(8,128)S(1)}) custom-call(s32[1]{0:T(128)S(6)} %copy.12.refs_0_, bf16[128,2048]{1,0:T(8,128)(2,1)S(1)} %copy-done.4, bf16[256,512]{1,0:T(8,128)(2,1)S(1)} %stack_keys_values.1.refs_2_, bf16[256,512]{1,0:T(8,128)(2,1)S(1)} %collective-permute-done.4.refs_3_.refs_0_, ...), custom_call_target="tpu_custom_call" | custom-call | flops 805306368 | bytes 3416068 | tf_op jit(solution)/shard_map/softmax_first/pallas_call | solution.py:327
  32.7 0.8 %collective-permute-start.7 = (bf16[128,512]{1,0:T(8,128)(2,1)S(1)}, bf16[128,512]{1,0:T(8,128)(2,1)S(1)}, u32[]{:S(2)}, u32[]{:S(2)}) collective-permute-start(bf16[128,512]{1,0:T(8,128)(2,1)S(1)} %get-tuple-element.30), channel_id=1, source_target_pairs={{0,8},{4,12},{8,0},{12,4},{16,24},{20,28},{24,16},{28,20},{1,9},{5... | collective-permute-start | bytes 393224 | tf_op jit(solution)/shard_map/ppermute | solution.py:353
  33.4 0.4 collective-permute-start.6
  33.8 2.1 %collective-permute-done.10.refs_5_ = bf16[512,128]{1,0:T(8,128)(2,1)S(1)} collective-permute-done((bf16[512,128]{1,0:T(8,128)(2,1)S(1)}, bf16[512,128]{1,0:T(8,128)(2,1)S(1)}, u32[]{:S(2)}, u32[]{:S(2)}) %collective-permute-start.10) | collective-permute-done | bytes 131104 | tf_op jit(solution)/shard_map/ppermute | solution.py:353
  35.9 0.7 %inter_block.1 = (f32[128,2048]{1,0:T(8,128)S(1)}, f32[8,128]{1,0:T(8,128)S(1)}) custom-call(f32[128,16]{1,0:T(8,128)S(1)} %get-tuple-element.33.refs_0_, bf16[128,2048]{1,0:T(8,128)(2,1)S(1)} %get-tuple-element.34.refs_1_, f32[128,2048]{1,0:T(8,128)S(1)} %get-tuple-element.27.refs_4_.refs_2_, bf16[512,128]{1,0:T(8,128)(2,1)S(1)} %get-tuple-element.35.refs_3_, ...), custom_call_target="tpu_custom_call" | custom-call | flops 67108864 | bytes 3158016 | tf_op jit(solution)/shard_map/inter_block/pallas_call | solution.py:327
  36.6 1.5 %collective-permute-start.13 = (f32[8,128]{1,0:T(8,128)S(1)}, f32[8,128]{1,0:T(8,128)S(1)}, u32[]{:S(2)}, u32[]{:S(2)}) collective-permute-start(f32[8,128]{1,0:T(8,128)S(1)} %get-tuple-element.41.refs_3_), channel_id=1, source_target_pairs={{0,2},{1,3},{2,0},{3,1},{4,6},{5,7},{6,4},{7,5},{8,10},{9,11},{10,... | collective-permute-start | bytes 12296 | tf_op jit(solution)/shard_map/ppermute | solution.py:503
  38.5 2.5 %softmax_last.1.refs_0_ = bf16[128,2048]{1,0:T(8,128)(2,1)S(1)} custom-call(s32[1]{0:T(128)S(6)} %copy.12.refs_0_, bf16[128,2048]{1,0:T(8,128)(2,1)S(1)} %copy-done.4, bf16[256,512]{1,0:T(8,128)(2,1)S(1)} %pad_maximum_fusion.refs_2_, f32[128,4096]{1,0:T(8,128)S(1)} %get-tuple-element.31.refs_3_, f32[128,8]{1,0:T(8,128)S(1)} %get-tuple-element.28.refs_2_.refs_4_.refs_7_, ...), custom_call_target="tpu_custom_call" | custom-call | flops 268435456 | bytes 3416068 | tf_op jit(solution)/shard_map/softmax_last/pallas_call | solution.py:327
  41.0 1.1 %results.1 = (bf16[128,2048]{1,0:T(8,128)(2,1)}, bf16[128,2048]{1,0:T(8,128)(2,1)}) custom-call(bf16[128,2048]{1,0:T(8,128)(2,1)S(1)} %softmax_last.1.refs_0_, f32[128,2048]{1,0:T(8,128)S(1)} %get-tuple-element.39.refs_1_, f32[128,2048]{1,0:T(8,128)S(1)} %get-tuple-element.40.refs_2_, f32[8,128]{1,0:T(8,128)S(1)} %get-tuple-element.41.refs_3_, ...), custom_call_target="tpu_custom_call" | custom-call | flops 1048576 | bytes 3686400 | tf_op jit(solution)/shard_map/results/pallas_call | solution.py:327
  (38 shorter events, 1.3 us)
Async XLA Ops:
  0.6 0.7 %copy-start.5 = (f32[16,128]{1,0:T(8,128)S(1)}, f32[16,128]{1,0:T(8,128)}, u32[]{:S(2)}) copy-start(f32[16,128]{1,0:T(8,128)} %refs_2_.5) | copy-start | bytes 24580
  0.6 1.0 %copy-start = (bf16[128,2048]{1,0:T(8,128)(2,1)S(1)}, bf16[128,2048]{1,0:T(8,128)(2,1)}, u32[]{:S(2)}) copy-start(bf16[128,2048]{1,0:T(8,128)(2,1)} %refs_4_.1) | copy-start | bytes 1572868
  0.7 1.2 %copy-start.1 = (bf16[128,2048]{1,0:T(8,128)(2,1)S(1)}, bf16[128,2048]{1,0:T(8,128)(2,1)}, u32[]{:S(2)}) copy-start(bf16[128,2048]{1,0:T(8,128)(2,1)} %refs_5_.1) | copy-start | bytes 1572868
  0.7 7.9 %copy-start.6 = (bf16[128,256]{1,0:T(8,128)(2,1)S(1)}, bf16[128,256]{1,0:T(8,128)(2,1)}, u32[]{:S(2)}) copy-start(bf16[128,256]{1,0:T(8,128)(2,1)} %refs_0_.3) | copy-start | bytes 196612
  0.7 7.9 %copy-start.7 = (bf16[128,256]{1,0:T(8,128)(2,1)S(1)}, bf16[128,256]{1,0:T(8,128)(2,1)}, u32[]{:S(2)}) copy-start(bf16[128,256]{1,0:T(8,128)(2,1)} %refs_1_.5) | copy-start | bytes 196612
  0.7 11.6 %copy-start.2 = (bf16[128,2048]{1,0:T(8,128)(2,1)S(1)}, bf16[128,2048]{1,0:T(8,128)(2,1)}, u32[]{:S(2)}) copy-start(bf16[128,2048]{1,0:T(8,128)(2,1)} %refs_3_.5) | copy-start | bytes 1572868
  0.7 11.6 %copy-start.3 = (bf16[128,2048]{1,0:T(8,128)(2,1)S(1)}, bf16[128,2048]{1,0:T(8,128)(2,1)}, u32[]{:S(2)}) copy-start(bf16[128,2048]{1,0:T(8,128)(2,1)} %refs_6_.1) | copy-start | bytes 1572868
  0.7 11.6 %copy-start.8 = (f32[2048]{0:T(1024)S(1)}, f32[2048]{0:T(1024)}, u32[]{:S(2)}) copy-start(f32[2048]{0:T(1024)} %param.15) | copy-start | bytes 24580
  2.5 12.6 %collective-permute-start.1 = (bf16[528,128]{1,0:T(8,128)(2,1)S(1)}, bf16[528,128]{1,0:T(8,128)(2,1)S(1)}, u32[]{:S(2)}, u32[]{:S(2)}) collective-permute-start(bf16[528,128]{1,0:T(8,128)(2,1)S(1)} %first_states.1), channel_id=1, source_target_pairs={{0,8},{4,12},{8,0},{12,4},{16,24},{20,28},{24,16},{28,20},{1,9},{5... | collective-permute-start | bytes 405512 | tf_op jit(solution)/shard_map/ppermute | solution.py:353
  7.0 8.1 %collective-permute-start.2 = (bf16[528,128]{1,0:T(8,128)(2,1)S(1)}, bf16[528,128]{1,0:T(8,128)(2,1)S(1)}, u32[]{:S(2)}, u32[]{:S(2)}) collective-permute-start(bf16[528,128]{1,0:T(8,128)(2,1)S(1)} %get-tuple-element.24), channel_id=1, source_target_pairs={{0,12},{4,8},{8,4},{12,0},{16,28},{20,24},{24,20},{28,16},{1,13},{... | collective-permute-start | bytes 405512 | tf_op jit(solution)/shard_map/ppermute | solution.py:353
  8.4 7.6 %collective-permute-start.3 = (bf16[528,128]{1,0:T(8,128)(2,1)S(1)}, bf16[528,128]{1,0:T(8,128)(2,1)S(1)}, u32[]{:S(2)}, u32[]{:S(2)}) collective-permute-start(bf16[528,128]{1,0:T(8,128)(2,1)S(1)} %get-tuple-element.25), channel_id=1, source_target_pairs={{0,4},{4,0},{8,12},{12,8},{16,20},{20,16},{24,28},{28,24},{1,5},{5... | collective-permute-start | bytes 405512 | tf_op jit(solution)/shard_map/ppermute | solution.py:353
  8.6 10.2 %collective-permute-start = (bf16[128,512]{1,0:T(8,128)(2,1)S(1)}, bf16[128,512]{1,0:T(8,128)(2,1)S(1)}, u32[]{:S(2)}, u32[]{:S(2)}) collective-permute-start(bf16[128,512]{1,0:T(8,128)(2,1)S(1)} %keys_beside_values.1.refs_0_), channel_id=1, source_target_pairs={{0,16},{4,20},{8,24},{12,28},{16,0},{20,4},{24,8},{28,12},{1,17},{... | collective-permute-start | bytes 393224 | tf_op jit(solution)/shard_map/ppermute | solution.py:356
  16.2 9.3 %collective-permute-start.8 = (bf16[528,128]{1,0:T(8,128)(2,1)S(1)}, bf16[528,128]{1,0:T(8,128)(2,1)S(1)}, u32[]{:S(2)}, u32[]{:S(2)}) collective-permute-start(bf16[528,128]{1,0:T(8,128)(2,1)S(1)} %group_state.1.refs_2_), channel_id=1, source_target_pairs={{0,16},{4,20},{8,24},{12,28},{16,0},{20,4},{24,8},{28,12},{1,17},{... | collective-permute-start | bytes 405512 | tf_op jit(solution)/shard_map/ppermute | solution.py:356
  18.8 11.4 %copy-start.4 = (bf16[128,2048]{1,0:T(8,128)(2,1)S(1)}, bf16[128,2048]{1,0:T(8,128)(2,1)}, u32[]{:S(2)}) copy-start(bf16[128,2048]{1,0:T(8,128)(2,1)} %refs_1_.9) | copy-start | bytes 1572868
  18.9 11.4 %collective-permute-start.4 = (bf16[256,512]{1,0:T(8,128)(2,1)S(1)}, bf16[256,512]{1,0:T(8,128)(2,1)S(1)}, u32[]{:S(2)}, u32[]{:S(2)}) collective-permute-start(bf16[256,512]{1,0:T(8,128)(2,1)S(1)} %stack_keys_values.1.refs_2_), channel_id=1, source_target_pairs={{0,8},{4,12},{8,0},{12,4},{16,24},{20,28},{24,16},{28,20},{1,9},{5... | collective-permute-start | bytes 786440 | tf_op jit(solution)/shard_map/ppermute | solution.py:353
  20.0 10.2 %collective-permute-start.5 = (bf16[256,512]{1,0:T(8,128)(2,1)S(1)}, bf16[256,512]{1,0:T(8,128)(2,1)S(1)}, u32[]{:S(2)}, u32[]{:S(2)}) collective-permute-start(bf16[256,512]{1,0:T(8,128)(2,1)S(1)} %stack_keys_values.1.refs_2_), channel_id=1, source_target_pairs={{0,4},{4,0},{8,12},{12,8},{16,20},{20,16},{24,28},{28,24},{1,5},{5... | collective-permute-start | bytes 786440 | tf_op jit(solution)/shard_map/ppermute | solution.py:353
  25.7 8.1 %collective-permute-start.9 = (bf16[512,128]{1,0:T(8,128)(2,1)S(1)}, bf16[512,128]{1,0:T(8,128)(2,1)S(1)}, u32[]{:S(2)}, u32[]{:S(2)}) collective-permute-start(bf16[512,128]{1,0:T(8,128)(2,1)S(1)} %get-tuple-element.36), channel_id=1, source_target_pairs={{0,12},{4,8},{8,4},{12,0},{16,28},{20,24},{24,20},{28,16},{1,13},{... | collective-permute-start | bytes 393224 | tf_op jit(solution)/shard_map/ppermute | solution.py:353
  25.8 10.1 %collective-permute-start.10 = (bf16[512,128]{1,0:T(8,128)(2,1)S(1)}, bf16[512,128]{1,0:T(8,128)(2,1)S(1)}, u32[]{:S(2)}, u32[]{:S(2)}) collective-permute-start(bf16[512,128]{1,0:T(8,128)(2,1)S(1)} %get-tuple-element.37), channel_id=1, source_target_pairs={{0,8},{4,12},{8,0},{12,4},{16,24},{20,28},{24,16},{28,20},{1,9},{5... | collective-permute-start | bytes 393224 | tf_op jit(solution)/shard_map/ppermute | solution.py:353
  27.3 8.6 %collective-permute-start.11 = (bf16[512,128]{1,0:T(8,128)(2,1)S(1)}, bf16[512,128]{1,0:T(8,128)(2,1)S(1)}, u32[]{:S(2)}, u32[]{:S(2)}) collective-permute-start(bf16[512,128]{1,0:T(8,128)(2,1)S(1)} %get-tuple-element.38), channel_id=1, source_target_pairs={{0,4},{4,0},{8,12},{12,8},{16,20},{20,16},{24,28},{28,24},{1,5},{5... | collective-permute-start | bytes 393224 | tf_op jit(solution)/shard_map/ppermute | solution.py:353
  32.7 5.8 %collective-permute-start.7 = (bf16[128,512]{1,0:T(8,128)(2,1)S(1)}, bf16[128,512]{1,0:T(8,128)(2,1)S(1)}, u32[]{:S(2)}, u32[]{:S(2)}) collective-permute-start(bf16[128,512]{1,0:T(8,128)(2,1)S(1)} %get-tuple-element.30), channel_id=1, source_target_pairs={{0,8},{4,12},{8,0},{12,4},{16,24},{20,28},{24,16},{28,20},{1,9},{5... | collective-permute-start | bytes 393224 | tf_op jit(solution)/shard_map/ppermute | solution.py:353
  33.4 5.0 %collective-permute-start.6 = (bf16[128,512]{1,0:T(8,128)(2,1)S(1)}, bf16[128,512]{1,0:T(8,128)(2,1)S(1)}, u32[]{:S(2)}, u32[]{:S(2)}) collective-permute-start(bf16[128,512]{1,0:T(8,128)(2,1)S(1)} %get-tuple-element.29), channel_id=1, source_target_pairs={{0,4},{4,0},{8,12},{12,8},{16,20},{20,16},{24,28},{28,24},{1,5},{5... | collective-permute-start | bytes 393224 | tf_op jit(solution)/shard_map/ppermute | solution.py:353
  36.6 4.4 %collective-permute-start.12 = (f32[8,128]{1,0:T(8,128)S(1)}, f32[8,128]{1,0:T(8,128)S(1)}, u32[]{:S(2)}, u32[]{:S(2)}) collective-permute-start(f32[8,128]{1,0:T(8,128)S(1)} %get-tuple-element.41.refs_3_), channel_id=1, source_target_pairs={{0,3},{1,2},{2,1},{3,0},{4,7},{5,6},{6,5},{7,4},{8,11},{9,10},{10,... | collective-permute-start | bytes 12296 | tf_op jit(solution)/shard_map/ppermute | solution.py:503
  36.6 4.3 %collective-permute-start.13 = (f32[8,128]{1,0:T(8,128)S(1)}, f32[8,128]{1,0:T(8,128)S(1)}, u32[]{:S(2)}, u32[]{:S(2)}) collective-permute-start(f32[8,128]{1,0:T(8,128)S(1)} %get-tuple-element.41.refs_3_), channel_id=1, source_target_pairs={{0,2},{1,3},{2,0},{3,1},{4,6},{5,7},{6,4},{7,5},{8,10},{9,11},{10,... | collective-permute-start | bytes 12296 | tf_op jit(solution)/shard_map/ppermute | solution.py:503
  38.1 2.9 %collective-permute-start.14 = (f32[8,128]{1,0:T(8,128)S(1)}, f32[8,128]{1,0:T(8,128)S(1)}, u32[]{:S(2)}, u32[]{:S(2)}) collective-permute-start(f32[8,128]{1,0:T(8,128)S(1)} %get-tuple-element.41.refs_3_), channel_id=1, source_target_pairs={{0,1},{1,0},{2,3},{3,2},{4,5},{5,4},{6,7},{7,6},{8,9},{9,8},{10,11... | collective-permute-start | bytes 12296 | tf_op jit(solution)/shard_map/ppermute | solution.py:503

commit v12 on v11

--- a/solution.py
+++ b/solution.py
@@ -170,8 +170,8 @@
         outs[s][...] = prefixes[rank ^ s]
 
 
-def intra_kernel(heads, tri_ref, bias_ref, ld_ref, q_ref, k_ref, v_ref, gate_ref, gain_ref, *outs):
-    intra_ref, qa_ref, gain_out, decay_out = outs
+def intra_kernel(heads, tri_ref, bias_ref, ld_ref, q_ref, k_ref, v_ref, *outs):
+    intra_ref, qa_ref, decay_out = outs
     ld = ld_ref[...]
     tri = tri_ref[...]
     bias = bias_ref[...]
@@ -188,8 +188,13 @@
         decay = jnp.exp((cum[:, h : h + 1] - cum_t[h : h + 1, :]) + bias)
         weights = (scores * decay).astype(BF16)
         intra_ref[:, cols] = jnp.dot(weights, va, preferred_element_type=F32)
+
+
+def gate_kernel(heads, gate_ref, gain_ref, out_ref):
+    for h in range(heads):
+        cols = head_cols(h)
         gate = 1.0 / (1.0 + jnp.exp(-gate_ref[:, cols].astype(F32)))
-        gain_out[:, cols] = gate * gain_ref[:, cols]
+        out_ref[:, cols] = gate * gain_ref[:, cols]
 
 
 def inter_kernel(group, heads, order, decay_ref, qa_ref, intra_ref, *rest):
@@ -314,9 +319,21 @@
 
 
 def call(
-    kernel, name, outs, args, scratch=(), flops=0, exps=0, limit=16, specs=None, after=(), **more
+    kernel,
+    name,
+    outs,
+    args,
+    scratch=(),
+    flops=0,
+    exps=0,
+    size=None,
+    limit=16,
+    specs=None,
+    after=(),
+    **more,
 ):
-    size = sum(math.prod(x.shape) * x.dtype.itemsize for x in list(args) + list(outs))
+    if size is None:
+        size = sum(math.prod(x.shape) * x.dtype.itemsize for x in list(args) + list(outs))
     more.setdefault("out_specs", [VMEM for _ in outs])
     specs = list(specs or [VMEM for _ in args]) + [HBM for _ in after]
     count = len(args)
@@ -358,15 +375,6 @@
     tri, bias = call(
         triangle_kernel, "triangle", [shape((tokens, tokens), F32)] * 2, (), flops=1 << 31
     )
-    (kv,) = call(
-        beside_kernel,
-        "keys_beside_values",
-        [shape((tokens, 2 * kv_width), BF16)],
-        (keys, values),
-        after=(tri,),
-    )
-    far = [ahead(kv, d) for d in range(1, groups)]
-
     to, back = (0, 2, 3, 1), (0, 3, 2, 1)
     others = [s for s in to if s != to[1]]
     payload = shape((rows, HD), BF16)
@@ -378,30 +386,35 @@
         flops=4 * cube // group,
         exps=2 * tokens * width // group,
     )
+    (kv,) = call(
+        beside_kernel,
+        "keys_beside_values",
+        [shape((tokens, 2 * kv_width), BF16)],
+        (keys, values),
+        after=(early,),
+    )
+    far = [ahead(kv, d) for d in range(1, groups)]
+
     late = call(
         functools.partial(other_states_kernel, group, per, to[1], others),
         "other_states",
         [payload] * len(others),
         (tri, log_decay, k_lin, v_lin),
         [pltpu.VMEM((group, rows, HD), BF16)],
-        flops=4 * cube,
+        flops=1 << 32,
         exps=2 * tokens * width,
     )
     pays = {to[1]: early, **dict(zip(others, late))}
     pays = [swap(pays[s], s) if s else pays[s] for s in to]
 
-    intra, qa, gain, decay = call(
-        functools.partial(intra_kernel, heads),
-        "intra_block",
-        [
-            shape((tokens, width), F32),
-            shape((tokens, width), BF16),
-            shape((tokens, width), F32),
-            shape((tokens, heads), F32),
-        ],
-        (tri, bias, log_decay, q_lin, k_lin, v_lin, gate, norm_gain.reshape(1, width)),
-        flops=4 * cube,
-        exps=4 * tokens * width,
+    (gain,) = call(
+        functools.partial(gate_kernel, heads),
+        "gate_gain",
+        [shape((tokens, width), F32)],
+        (gate, norm_gain.reshape(1, width)),
+        flops=1 << 32,
+        exps=tokens * width,
+        after=far,
     )
 
     slots = pltpu.VMEM((group, rows, HD), BF16)
@@ -414,7 +427,7 @@
             pays,
             [slots],
             flops=2 * per * HD * HD * group,
-            after=(intra,),
+            after=(gain,),
         )
         before = ahead(total, 1)
         shift = 1
@@ -432,6 +445,15 @@
             before = jnp.concatenate([state, high, pad, both - high, pad], axis=0).astype(BF16)
             shift *= 2
         carry = (before,)
+    intra, qa, decay = call(
+        functools.partial(intra_kernel, heads),
+        "intra_block",
+        [shape((tokens, width), F32), shape((tokens, width), BF16), shape((tokens, heads), F32)],
+        (tri, bias, log_decay, q_lin, k_lin, v_lin),
+        flops=4 * cube,
+        exps=4 * tokens * width,
+        after=(total,) if groups > 1 else (),
+    )
     prefixes = call(
         functools.partial(prefix_kernel, group, per, to, bool(carry)),
         "prefix_states",
@@ -439,6 +461,7 @@
         (*pays, *carry),
         [slots, pltpu.VMEM((group, per * HD, HD), BF16)],
         flops=1 << 33,
+        after=(intra,),
     )
     prefixes = [swap(prefixes[s], s) if s else prefixes[s] for s in back]
 
@@ -447,7 +470,7 @@
         "stack_keys_values",
         [shape((groups * tokens, kv.shape[1]), BF16)],
         (kv, *far),
-        after=(total,) if groups > 1 else (intra,),
+        after=(total,) if groups > 1 else (),
         flops=1 << 32,
     )
     side, near = swap(own, 2), swap(own, 1)
@@ -473,7 +496,7 @@
         specs=[smem] + [VMEM] * 4,
     )
     half = shape((own.shape[0] // 2, own.shape[1]), BF16)
-    upper, under = call(halves_kernel, "sent_on", [half] * 2, (side, near), after=tops[:1])
+    upper, under = call(halves_kernel, "sent_on", [half] * 2, (side, near))
     across = jnp.concatenate([swap(upper, 1), swap(under, 2)])
     (attended,) = call(
         functools.partial(softmax_last_kernel, group, (3,), kv_heads, pack),

time: 42.3 us -> 43.2 us (1.021)
  waiting for transfers between devices: 8.57 us -> 11.7 us
  starting transfers between devices: 19 us -> 16.6 us
    ppermute x10, waiting for transfers between devices: 4.03 us -> 6.5 us  [swap(): return lax.ppermute(x, 'ctx', [(c, c ^ s) for c in range(n)])]
    ppermute x2, starting transfers between devices: 5.61 us -> 3.43 us  [ahead(): return lax.ppermute(x, 'ctx', [(c, (c + d * group) % n) for c in range(n)])]
    ppermute x2, waiting for transfers between devices: 4.53 us -> 5.17 us  [ahead(): return lax.ppermute(x, 'ctx', [(c, (c + d * group) % n) for c in range(n)])]
    pallas_call x13 -> x14, Pallas kernels: 11.8 us -> 12.1 us  [call(): pl.pallas_call(run, name=name, out_shape=list(outs), in_specs=specs, scra...]
  transfers between devices with their start and end apart: 15 -> 15, of which waited for: 4 -> 6; matrix products, arithmetic and copies ran while one was open for 0% -> 0% of each run, Pallas kernels for 24% -> 24%
where the time goes in v12:
time: 43.2 us; the launch traced here: 43 us
  starting transfers between devices  16.6 us (38%)
  Pallas kernels  12.1 us (28%)
  waiting for transfers between devices  11.7 us (27%)
  between operations  1.47 us (3%)
  local copies, waits for them, and re-layouts  1.18 us (3%)
    pallas_call x14, Pallas kernels, call(): pl.pallas_call(run, name=name, out_shape=list(outs), in_specs=specs, scra...  12.1 us
    ppermute x10, starting transfers between devices, swap(): return lax.ppermute(x, 'ctx', [(c, c ^ s) for c in range(n)])  11.3 us
    ppermute x10, waiting for transfers between devices, swap(): return lax.ppermute(x, 'ctx', [(c, c ^ s) for c in range(n)])  6.5 us
    ppermute x2, waiting for transfers between devices, ahead(): return lax.ppermute(x, 'ctx', [(c, (c + d * group) % n) for c in range(n)])  5.17 us
    ppermute x2, starting transfers between devices, ahead(): return lax.ppermute(x, 'ctx', [(c, (c + d * group) % n) for c in range(n)])  3.43 us
    ppermute x3, starting transfers between devices, body(): parts = [squares] + [lax.ppermute(squares, 'head', turn) for turn in turns]  1.89 us
    unnamed x18, local copies, waits for them, and re-layouts  1.18 us
  transfers between devices with their start and end apart: 15, of which 6 were waited for; matrix products, arithmetic and copies ran while one was open for 0% of the time, Pallas kernels for 24%

profile of v12, /device:TPU:0, one launch (start us, length us, event | category | flops | bytes accessed | tf_op | source)
XLA Modules:
  0.0 43.0 jit_solution(5532759071579572767)
XLA Ops:
  0.7 0.6 %copy-done.5 = f32[16,128]{1,0:T(8,128)S(1)} copy-done((f32[16,128]{1,0:T(8,128)S(1)}, f32[16,128]{1,0:T(8,128)}, u32[]{:S(2)}) %copy-start.5) | copy-done | bytes 8216
  1.8 0.6 %first_states.1.refs_2_ = bf16[528,128]{1,0:T(8,128)(2,1)S(1)} custom-call(f32[128,128]{1,0:T(8,128)S(1)} %get-tuple-element.21.refs_0_, f32[16,128]{1,0:T(8,128)S(1)} %copy-done.5, bf16[128,2048]{1,0:T(8,128)(2,1)S(1)} %copy-done, bf16[128,2048]{1,0:T(8,128)(2,1)S(1)} %copy-done.1), custom_call_target="tpu_custom_call" | custom-call | flops 33554432 | bytes 1257472 | tf_op jit(solution)/shard_map/first_states/pallas_call | solution.py:344
  2.5 3.1 %collective-permute-start.1 = (bf16[528,128]{1,0:T(8,128)(2,1)S(1)}, bf16[528,128]{1,0:T(8,128)(2,1)S(1)}, u32[]{:S(2)}, u32[]{:S(2)}) collective-permute-start(bf16[528,128]{1,0:T(8,128)(2,1)S(1)} %first_states.1.refs_2_), channel_id=1, source_target_pairs={{0,8},{4,12},{8,0},{12,4},{16,24},{20,28},{24,16},{28,20},{1,9},{5... | collective-permute-start | bytes 405512 | tf_op jit(solution)/shard_map/ppermute | solution.py:370
  5.6 2.7 %collective-permute-start = (bf16[128,512]{1,0:T(8,128)(2,1)S(1)}, bf16[128,512]{1,0:T(8,128)(2,1)S(1)}, u32[]{:S(2)}, u32[]{:S(2)}) collective-permute-start(bf16[128,512]{1,0:T(8,128)(2,1)S(1)} %keys_beside_values.1.refs_0_), channel_id=1, source_target_pairs={{0,16},{4,20},{8,24},{12,28},{16,0},{20,4},{24,8},{28,12},{1,17},{... | collective-permute-start | bytes 393224 | tf_op jit(solution)/shard_map/ppermute | solution.py:373
  8.2 1.4 %other_states.1 = (bf16[528,128]{1,0:T(8,128)(2,1)S(1)}, bf16[528,128]{1,0:T(8,128)(2,1)S(1)}, bf16[528,128]{1,0:T(8,128)(2,1)S(1)}) custom-call(f32[128,128]{1,0:T(8,128)S(1)} %get-tuple-element.21.refs_0_, f32[16,128]{1,0:T(8,128)S(1)} %copy-done.5, bf16[128,2048]{1,0:T(8,128)(2,1)S(1)} %copy-done, bf16[128,2048]{1,0:T(8,128)(2,1)S(1)} %copy-done.1), custom_call_target="tpu_custom_call" | custom-call | flops 4294967296 | bytes 1527808 | tf_op jit(solution)/shard_map/other_states/pallas_call | solution.py:344
  9.7 1.5 %collective-permute-start.2 = (bf16[528,128]{1,0:T(8,128)(2,1)S(1)}, bf16[528,128]{1,0:T(8,128)(2,1)S(1)}, u32[]{:S(2)}, u32[]{:S(2)}) collective-permute-start(bf16[528,128]{1,0:T(8,128)(2,1)S(1)} %get-tuple-element.23), channel_id=1, source_target_pairs={{0,12},{4,8},{8,4},{12,0},{16,28},{20,24},{24,20},{28,16},{1,13},{... | collective-permute-start | bytes 405512 | tf_op jit(solution)/shard_map/ppermute | solution.py:370
  11.1 0.5 %collective-permute-start.3 = (bf16[528,128]{1,0:T(8,128)(2,1)S(1)}, bf16[528,128]{1,0:T(8,128)(2,1)S(1)}, u32[]{:S(2)}, u32[]{:S(2)}) collective-permute-start(bf16[528,128]{1,0:T(8,128)(2,1)S(1)} %get-tuple-element.24), channel_id=1, source_target_pairs={{0,4},{4,0},{8,12},{12,8},{16,20},{20,16},{24,28},{28,24},{1,5},{5... | collective-permute-start | bytes 405512 | tf_op jit(solution)/shard_map/ppermute | solution.py:370
  11.6 1.8 %collective-permute-done.refs_2_.refs_1_ = bf16[128,512]{1,0:T(8,128)(2,1)S(1)} collective-permute-done((bf16[128,512]{1,0:T(8,128)(2,1)S(1)}, bf16[128,512]{1,0:T(8,128)(2,1)S(1)}, u32[]{:S(2)}, u32[]{:S(2)}) %collective-permute-start) | collective-permute-done | bytes 131104 | tf_op jit(solution)/shard_map/ppermute | solution.py:373
  13.8 2.4 %collective-permute-done.2.refs_2_ = bf16[528,128]{1,0:T(8,128)(2,1)S(1)} collective-permute-done((bf16[528,128]{1,0:T(8,128)(2,1)S(1)}, bf16[528,128]{1,0:T(8,128)(2,1)S(1)}, u32[]{:S(2)}, u32[]{:S(2)}) %collective-permute-start.2) | collective-permute-done | bytes 135200 | tf_op jit(solution)/shard_map/ppermute | solution.py:370
  16.2 2.2 %collective-permute-done.3.refs_3_ = bf16[528,128]{1,0:T(8,128)(2,1)S(1)} collective-permute-done((bf16[528,128]{1,0:T(8,128)(2,1)S(1)}, bf16[528,128]{1,0:T(8,128)(2,1)S(1)}, u32[]{:S(2)}, u32[]{:S(2)}) %collective-permute-start.3) | collective-permute-done | bytes 135200 | tf_op jit(solution)/shard_map/ppermute | solution.py:370
  18.6 0.8 %collective-permute-start.8 = (bf16[528,128]{1,0:T(8,128)(2,1)S(1)}, bf16[528,128]{1,0:T(8,128)(2,1)S(1)}, u32[]{:S(2)}, u32[]{:S(2)}) collective-permute-start(bf16[528,128]{1,0:T(8,128)(2,1)S(1)} %group_state.1.refs_2_.refs_6_), channel_id=1, source_target_pairs={{0,16},{4,20},{8,24},{12,28},{16,0},{20,4},{24,8},{28,12},{1,17},{... | collective-permute-start | bytes 405512 | tf_op jit(solution)/shard_map/ppermute | solution.py:373
  19.4 1.4 %collective-permute-start.4 = (bf16[256,512]{1,0:T(8,128)(2,1)S(1)}, bf16[256,512]{1,0:T(8,128)(2,1)S(1)}, u32[]{:S(2)}, u32[]{:S(2)}) collective-permute-start(bf16[256,512]{1,0:T(8,128)(2,1)S(1)} %stack_keys_values.1.refs_2_), channel_id=1, source_target_pairs={{0,8},{4,12},{8,0},{12,4},{16,24},{20,28},{24,16},{28,20},{1,9},{5... | collective-permute-start | bytes 786440 | tf_op jit(solution)/shard_map/ppermute | solution.py:370
  21.3 2.8 %intra_block.1 = (f32[128,2048]{1,0:T(8,128)S(1)}, bf16[128,2048]{1,0:T(8,128)(2,1)S(1)}, f32[128,16]{1,0:T(8,128)S(1)}) custom-call(f32[128,128]{1,0:T(8,128)S(1)} %get-tuple-element.21.refs_0_, f32[128,128]{1,0:T(8,128)S(1)} %get-tuple-element.30.refs_1_, f32[16,128]{1,0:T(8,128)S(1)} %copy-done.5, bf16[128,2048]{1,0:T(8,128)(2,1)S(1)} %copy-done.7, ...), custom_call_target="tpu_custom_call" | custom-call | flops 134217728 | bytes 3293184 | tf_op jit(solution)/shard_map/intra_block/pallas_call | solution.py:344
  24.0 3.3 %collective-permute-done.8.refs_4_ = bf16[528,128]{1,0:T(8,128)(2,1)S(1)} collective-permute-done((bf16[528,128]{1,0:T(8,128)(2,1)S(1)}, bf16[528,128]{1,0:T(8,128)(2,1)S(1)}, u32[]{:S(2)}, u32[]{:S(2)}) %collective-permute-start.8) | collective-permute-done | bytes 135200 | tf_op jit(solution)/shard_map/ppermute | solution.py:373
  27.8 1.6 %collective-permute-start.10 = (bf16[512,128]{1,0:T(8,128)(2,1)S(1)}, bf16[512,128]{1,0:T(8,128)(2,1)S(1)}, u32[]{:S(2)}, u32[]{:S(2)}) collective-permute-start(bf16[512,128]{1,0:T(8,128)(2,1)S(1)} %get-tuple-element.36), channel_id=1, source_target_pairs={{0,8},{4,12},{8,0},{12,4},{16,24},{20,28},{24,16},{28,20},{1,9},{5... | collective-permute-start | bytes 393224 | tf_op jit(solution)/shard_map/ppermute | solution.py:370
  29.4 1.8 %collective-permute-start.11 = (bf16[512,128]{1,0:T(8,128)(2,1)S(1)}, bf16[512,128]{1,0:T(8,128)(2,1)S(1)}, u32[]{:S(2)}, u32[]{:S(2)}) collective-permute-start(bf16[512,128]{1,0:T(8,128)(2,1)S(1)} %get-tuple-element.37), channel_id=1, source_target_pairs={{0,4},{4,0},{8,12},{12,8},{16,20},{20,16},{24,28},{28,24},{1,5},{5... | collective-permute-start | bytes 393224 | tf_op jit(solution)/shard_map/ppermute | solution.py:370
  31.3 0.6 %collective-permute-start.6 = (bf16[128,512]{1,0:T(8,128)(2,1)S(1)}, bf16[128,512]{1,0:T(8,128)(2,1)S(1)}, u32[]{:S(2)}, u32[]{:S(2)}) collective-permute-start(bf16[128,512]{1,0:T(8,128)(2,1)S(1)} %get-tuple-element.25), channel_id=1, source_target_pairs={{0,4},{4,0},{8,12},{12,8},{16,20},{20,16},{24,28},{28,24},{1,5},{5... | collective-permute-start | bytes 393224 | tf_op jit(solution)/shard_map/ppermute | solution.py:370
  32.6 2.4 %softmax_first.1 = (f32[128,4096]{1,0:T(8,128)S(1)}, f32[128,8]{1,0:T(8,128)S(1)}, f32[128,8]{1,0:T(8,128)S(1)}) custom-call(s32[1]{0:T(128)S(6)} %copy.12.refs_0_, bf16[128,2048]{1,0:T(8,128)(2,1)S(1)} %copy-done.2, bf16[256,512]{1,0:T(8,128)(2,1)S(1)} %stack_keys_values.1.refs_2_, bf16[256,512]{1,0:T(8,128)(2,1)S(1)} %collective-permute-done.4.refs_0_.refs_3_, ...), custom_call_target="tpu_custom_call" | custom-call | flops 805306368 | bytes 3416068 | tf_op jit(solution)/shard_map/softmax_first/pallas_call | solution.py:344
  35.0 1.3 %collective-permute-done.10.refs_5_ = bf16[512,128]{1,0:T(8,128)(2,1)S(1)} collective-permute-done((bf16[512,128]{1,0:T(8,128)(2,1)S(1)}, bf16[512,128]{1,0:T(8,128)(2,1)S(1)}, u32[]{:S(2)}, u32[]{:S(2)}) %collective-permute-start.10) | collective-permute-done | bytes 131104 | tf_op jit(solution)/shard_map/ppermute | solution.py:370
  36.3 0.6 %collective-permute-done.11.refs_6_ = bf16[512,128]{1,0:T(8,128)(2,1)S(1)} collective-permute-done((bf16[512,128]{1,0:T(8,128)(2,1)S(1)}, bf16[512,128]{1,0:T(8,128)(2,1)S(1)}, u32[]{:S(2)}, u32[]{:S(2)}) %collective-permute-start.11) | collective-permute-done | bytes 131104 | tf_op jit(solution)/shard_map/ppermute | solution.py:370
  36.8 0.7 %inter_block.1 = (f32[128,2048]{1,0:T(8,128)S(1)}, f32[8,128]{1,0:T(8,128)S(1)}) custom-call(f32[128,16]{1,0:T(8,128)S(1)} %get-tuple-element.31.refs_0_, bf16[128,2048]{1,0:T(8,128)(2,1)S(1)} %get-tuple-element.32.refs_1_, f32[128,2048]{1,0:T(8,128)S(1)} %get-tuple-element.33.refs_5_.refs_2_, bf16[512,128]{1,0:T(8,128)(2,1)S(1)} %get-tuple-element.34.refs_3_, ...), custom_call_target="tpu_custom_call" | custom-call | flops 67108864 | bytes 3158016 | tf_op jit(solution)/shard_map/inter_block/pallas_call | solution.py:344
  37.5 1.6 %collective-permute-start.13 = (f32[8,128]{1,0:T(8,128)S(1)}, f32[8,128]{1,0:T(8,128)S(1)}, u32[]{:S(2)}, u32[]{:S(2)}) collective-permute-start(f32[8,128]{1,0:T(8,128)S(1)} %get-tuple-element.39.refs_3_), channel_id=1, source_target_pairs={{0,2},{1,3},{2,0},{3,1},{4,6},{5,7},{6,4},{7,5},{8,10},{9,11},{10,... | collective-permute-start | bytes 12296 | tf_op jit(solution)/shard_map/ppermute | solution.py:526
  39.4 2.5 %softmax_last.1.refs_0_ = bf16[128,2048]{1,0:T(8,128)(2,1)S(1)} custom-call(s32[1]{0:T(128)S(6)} %copy.12.refs_0_, bf16[128,2048]{1,0:T(8,128)(2,1)S(1)} %copy-done.2, bf16[256,512]{1,0:T(8,128)(2,1)S(1)} %pad_maximum_fusion.refs_2_, f32[128,4096]{1,0:T(8,128)S(1)} %get-tuple-element.27.refs_3_, f32[128,8]{1,0:T(8,128)S(1)} %get-tuple-element.28.refs_4_.refs_7_, ...), custom_call_target="tpu_custom_call" | custom-call | flops 268435456 | bytes 3416068 | tf_op jit(solution)/shard_map/softmax_last/pallas_call | solution.py:344
  41.9 1.1 %results.1 = (bf16[128,2048]{1,0:T(8,128)(2,1)}, bf16[128,2048]{1,0:T(8,128)(2,1)}) custom-call(bf16[128,2048]{1,0:T(8,128)(2,1)S(1)} %softmax_last.1.refs_0_, f32[128,2048]{1,0:T(8,128)S(1)} %get-tuple-element.38.refs_1_, f32[128,2048]{1,0:T(8,128)S(1)} %gate_gain.1.refs_4_.refs_2_, f32[8,128]{1,0:T(8,128)S(1)} %get-tuple-element.39.refs_3_, ...), custom_call_target="tpu_custom_call" | custom-call | flops 1048576 | bytes 3686400 | tf_op jit(solution)/shard_map/results/pallas_call | solution.py:344
  (39 shorter events, 2.5 us)
Async XLA Ops:
  0.6 0.7 %copy-start.5 = (f32[16,128]{1,0:T(8,128)S(1)}, f32[16,128]{1,0:T(8,128)}, u32[]{:S(2)}) copy-start(f32[16,128]{1,0:T(8,128)} %refs_2_.5) | copy-start | bytes 24580
  0.6 1.0 %copy-start = (bf16[128,2048]{1,0:T(8,128)(2,1)S(1)}, bf16[128,2048]{1,0:T(8,128)(2,1)}, u32[]{:S(2)}) copy-start(bf16[128,2048]{1,0:T(8,128)(2,1)} %refs_4_.1) | copy-start | bytes 1572868
  0.7 1.2 %copy-start.1 = (bf16[128,2048]{1,0:T(8,128)(2,1)S(1)}, bf16[128,2048]{1,0:T(8,128)(2,1)}, u32[]{:S(2)}) copy-start(bf16[128,2048]{1,0:T(8,128)(2,1)} %refs_5_.1) | copy-start | bytes 1572868
  0.7 4.9 %copy-start.3 = (bf16[128,256]{1,0:T(8,128)(2,1)S(1)}, bf16[128,256]{1,0:T(8,128)(2,1)}, u32[]{:S(2)}) copy-start(bf16[128,256]{1,0:T(8,128)(2,1)} %refs_0_.4) | copy-start | bytes 196612
  0.7 4.9 %copy-start.4 = (bf16[128,256]{1,0:T(8,128)(2,1)S(1)}, bf16[128,256]{1,0:T(8,128)(2,1)}, u32[]{:S(2)}) copy-start(bf16[128,256]{1,0:T(8,128)(2,1)} %refs_1_.6) | copy-start | bytes 196612
  2.5 11.3 %collective-permute-start.1 = (bf16[528,128]{1,0:T(8,128)(2,1)S(1)}, bf16[528,128]{1,0:T(8,128)(2,1)S(1)}, u32[]{:S(2)}, u32[]{:S(2)}) collective-permute-start(bf16[528,128]{1,0:T(8,128)(2,1)S(1)} %first_states.1.refs_2_), channel_id=1, source_target_pairs={{0,8},{4,12},{8,0},{12,4},{16,24},{20,28},{24,16},{28,20},{1,9},{5... | collective-permute-start | bytes 405512 | tf_op jit(solution)/shard_map/ppermute | solution.py:370
  5.6 7.9 %copy-start.6 = (bf16[128,2048]{1,0:T(8,128)(2,1)S(1)}, bf16[128,2048]{1,0:T(8,128)(2,1)}, u32[]{:S(2)}) copy-start(bf16[128,2048]{1,0:T(8,128)(2,1)} %refs_0_.5) | copy-start | bytes 1572868
  5.6 7.9 %copy-start.8 = (f32[2048]{0:T(1024)S(1)}, f32[2048]{0:T(1024)}, u32[]{:S(2)}) copy-start(f32[2048]{0:T(1024)} %param.15) | copy-start | bytes 24580
  5.6 7.9 %collective-permute-start = (bf16[128,512]{1,0:T(8,128)(2,1)S(1)}, bf16[128,512]{1,0:T(8,128)(2,1)S(1)}, u32[]{:S(2)}, u32[]{:S(2)}) collective-permute-start(bf16[128,512]{1,0:T(8,128)(2,1)S(1)} %keys_beside_values.1.refs_0_), channel_id=1, source_target_pairs={{0,16},{4,20},{8,24},{12,28},{16,0},{20,4},{24,8},{28,12},{1,17},{... | collective-permute-start | bytes 393224 | tf_op jit(solution)/shard_map/ppermute | solution.py:373
  9.7 6.5 %collective-permute-start.2 = (bf16[528,128]{1,0:T(8,128)(2,1)S(1)}, bf16[528,128]{1,0:T(8,128)(2,1)S(1)}, u32[]{:S(2)}, u32[]{:S(2)}) collective-permute-start(bf16[528,128]{1,0:T(8,128)(2,1)S(1)} %get-tuple-element.23), channel_id=1, source_target_pairs={{0,12},{4,8},{8,4},{12,0},{16,28},{20,24},{24,20},{28,16},{1,13},{... | collective-permute-start | bytes 405512 | tf_op jit(solution)/shard_map/ppermute | solution.py:370
  11.1 7.3 %collective-permute-start.3 = (bf16[528,128]{1,0:T(8,128)(2,1)S(1)}, bf16[528,128]{1,0:T(8,128)(2,1)S(1)}, u32[]{:S(2)}, u32[]{:S(2)}) collective-permute-start(bf16[528,128]{1,0:T(8,128)(2,1)S(1)} %get-tuple-element.24), channel_id=1, source_target_pairs={{0,4},{4,0},{8,12},{12,8},{16,20},{20,16},{24,28},{28,24},{1,5},{5... | collective-permute-start | bytes 405512 | tf_op jit(solution)/shard_map/ppermute | solution.py:370
  18.6 2.7 %copy-start.7 = (bf16[128,2048]{1,0:T(8,128)(2,1)S(1)}, bf16[128,2048]{1,0:T(8,128)(2,1)}, u32[]{:S(2)}) copy-start(bf16[128,2048]{1,0:T(8,128)(2,1)} %refs_3_.5) | copy-start | bytes 1572868
  18.6 8.8 %collective-permute-start.8 = (bf16[528,128]{1,0:T(8,128)(2,1)S(1)}, bf16[528,128]{1,0:T(8,128)(2,1)S(1)}, u32[]{:S(2)}, u32[]{:S(2)}) collective-permute-start(bf16[528,128]{1,0:T(8,128)(2,1)S(1)} %group_state.1.refs_2_.refs_6_), channel_id=1, source_target_pairs={{0,16},{4,20},{8,24},{12,28},{16,0},{20,4},{24,8},{28,12},{1,17},{... | collective-permute-start | bytes 405512 | tf_op jit(solution)/shard_map/ppermute | solution.py:373
  19.4 11.8 %collective-permute-start.4 = (bf16[256,512]{1,0:T(8,128)(2,1)S(1)}, bf16[256,512]{1,0:T(8,128)(2,1)S(1)}, u32[]{:S(2)}, u32[]{:S(2)}) collective-permute-start(bf16[256,512]{1,0:T(8,128)(2,1)S(1)} %stack_keys_values.1.refs_2_), channel_id=1, source_target_pairs={{0,8},{4,12},{8,0},{12,4},{16,24},{20,28},{24,16},{28,20},{1,9},{5... | collective-permute-start | bytes 786440 | tf_op jit(solution)/shard_map/ppermute | solution.py:370
  20.7 10.4 %collective-permute-start.5 = (bf16[256,512]{1,0:T(8,128)(2,1)S(1)}, bf16[256,512]{1,0:T(8,128)(2,1)S(1)}, u32[]{:S(2)}, u32[]{:S(2)}) collective-permute-start(bf16[256,512]{1,0:T(8,128)(2,1)S(1)} %stack_keys_values.1.refs_2_), channel_id=1, source_target_pairs={{0,4},{4,0},{8,12},{12,8},{16,20},{20,16},{24,28},{28,24},{1,5},{5... | collective-permute-start | bytes 786440 | tf_op jit(solution)/shard_map/ppermute | solution.py:370
  27.4 5.2 %copy-start.2 = (bf16[128,2048]{1,0:T(8,128)(2,1)S(1)}, bf16[128,2048]{1,0:T(8,128)(2,1)}, u32[]{:S(2)}) copy-start(bf16[128,2048]{1,0:T(8,128)(2,1)} %refs_1_.9) | copy-start | bytes 1572868
  27.6 7.4 %collective-permute-start.9 = (bf16[512,128]{1,0:T(8,128)(2,1)S(1)}, bf16[512,128]{1,0:T(8,128)(2,1)S(1)}, u32[]{:S(2)}, u32[]{:S(2)}) collective-permute-start(bf16[512,128]{1,0:T(8,128)(2,1)S(1)} %get-tuple-element.35), channel_id=1, source_target_pairs={{0,12},{4,8},{8,4},{12,0},{16,28},{20,24},{24,20},{28,16},{1,13},{... | collective-permute-start | bytes 393224 | tf_op jit(solution)/shard_map/ppermute | solution.py:370
  27.8 8.5 %collective-permute-start.10 = (bf16[512,128]{1,0:T(8,128)(2,1)S(1)}, bf16[512,128]{1,0:T(8,128)(2,1)S(1)}, u32[]{:S(2)}, u32[]{:S(2)}) collective-permute-start(bf16[512,128]{1,0:T(8,128)(2,1)S(1)} %get-tuple-element.36), channel_id=1, source_target_pairs={{0,8},{4,12},{8,0},{12,4},{16,24},{20,28},{24,16},{28,20},{1,9},{5... | collective-permute-start | bytes 393224 | tf_op jit(solution)/shard_map/ppermute | solution.py:370
  29.4 7.5 %collective-permute-start.11 = (bf16[512,128]{1,0:T(8,128)(2,1)S(1)}, bf16[512,128]{1,0:T(8,128)(2,1)S(1)}, u32[]{:S(2)}, u32[]{:S(2)}) collective-permute-start(bf16[512,128]{1,0:T(8,128)(2,1)S(1)} %get-tuple-element.37), channel_id=1, source_target_pairs={{0,4},{4,0},{8,12},{12,8},{16,20},{20,16},{24,28},{28,24},{1,5},{5... | collective-permute-start | bytes 393224 | tf_op jit(solution)/shard_map/ppermute | solution.py:370
  31.2 8.2 %collective-permute-start.7 = (bf16[128,512]{1,0:T(8,128)(2,1)S(1)}, bf16[128,512]{1,0:T(8,128)(2,1)S(1)}, u32[]{:S(2)}, u32[]{:S(2)}) collective-permute-start(bf16[128,512]{1,0:T(8,128)(2,1)S(1)} %get-tuple-element.26), channel_id=1, source_target_pairs={{0,8},{4,12},{8,0},{12,4},{16,24},{20,28},{24,16},{28,20},{1,9},{5... | collective-permute-start | bytes 393224 | tf_op jit(solution)/shard_map/ppermute | solution.py:370
  31.3 8.1 %collective-permute-start.6 = (bf16[128,512]{1,0:T(8,128)(2,1)S(1)}, bf16[128,512]{1,0:T(8,128)(2,1)S(1)}, u32[]{:S(2)}, u32[]{:S(2)}) collective-permute-start(bf16[128,512]{1,0:T(8,128)(2,1)S(1)} %get-tuple-element.25), channel_id=1, source_target_pairs={{0,4},{4,0},{8,12},{12,8},{16,20},{20,16},{24,28},{28,24},{1,5},{5... | collective-permute-start | bytes 393224 | tf_op jit(solution)/shard_map/ppermute | solution.py:370
  37.5 4.4 %collective-permute-start.12 = (f32[8,128]{1,0:T(8,128)S(1)}, f32[8,128]{1,0:T(8,128)S(1)}, u32[]{:S(2)}, u32[]{:S(2)}) collective-permute-start(f32[8,128]{1,0:T(8,128)S(1)} %get-tuple-element.39.refs_3_), channel_id=1, source_target_pairs={{0,3},{1,2},{2,1},{3,0},{4,7},{5,6},{6,5},{7,4},{8,11},{9,10},{10,... | collective-permute-start | bytes 12296 | tf_op jit(solution)/shard_map/ppermute | solution.py:526
  37.5 4.4 %collective-permute-start.13 = (f32[8,128]{1,0:T(8,128)S(1)}, f32[8,128]{1,0:T(8,128)S(1)}, u32[]{:S(2)}, u32[]{:S(2)}) collective-permute-start(f32[8,128]{1,0:T(8,128)S(1)} %get-tuple-element.39.refs_3_), channel_id=1, source_target_pairs={{0,2},{1,3},{2,0},{3,1},{4,6},{5,7},{6,4},{7,5},{8,10},{9,11},{10,... | collective-permute-start | bytes 12296 | tf_op jit(solution)/shard_map/ppermute | solution.py:526
  39.1 2.9 %collective-permute-start.14 = (f32[8,128]{1,0:T(8,128)S(1)}, f32[8,128]{1,0:T(8,128)S(1)}, u32[]{:S(2)}, u32[]{:S(2)}) collective-permute-start(f32[8,128]{1,0:T(8,128)S(1)} %get-tuple-element.39.refs_3_), channel_id=1, source_target_pairs={{0,1},{1,0},{2,3},{3,2},{4,5},{5,4},{6,7},{7,6},{8,9},{9,8},{10,11... | collective-permute-start | bytes 12296 | tf_op jit(solution)/shard_map/ppermute | solution.py:526

commit v13 on v11

--- a/solution.py
+++ b/solution.py
@@ -78,25 +78,13 @@
     out[per * HD :, :] = tail.astype(BF16)
 
 
-def first_state_kernel(group, per, first, tri_ref, ld_ref, k_ref, v_ref, out_ref):
+def state_kernel(group, per, s, tri_ref, ld_ref, k_ref, v_ref, out_ref):
     weight, total = decay_weights(tri_ref, ld_ref)
-    dest = my_rank(group) ^ first
+    dest = my_rank(group) ^ s
     for k in range(group):
         pl.when(dest == k)(
             functools.partial(owner_states, k, per, weight, total, k_ref, v_ref, out_ref)
         )
-
-
-def other_states_kernel(group, per, first, others, tri_ref, ld_ref, k_ref, v_ref, *rest):
-    outs, payloads = rest[:-1], rest[-1]
-    weight, total = decay_weights(tri_ref, ld_ref)
-    rank = my_rank(group)
-    for k in range(group):
-        pl.when((rank ^ first) != k)(
-            functools.partial(owner_states, k, per, weight, total, k_ref, v_ref, payloads.at[k])
-        )
-    for s, out in zip(others, outs):
-        out[...] = payloads[rank ^ s]
 
 
 def beside_kernel(keys, values, out):
@@ -368,27 +356,20 @@
     far = [ahead(kv, d) for d in range(1, groups)]
 
     to, back = (0, 2, 3, 1), (0, 3, 2, 1)
-    others = [s for s in to if s != to[1]]
-    payload = shape((rows, HD), BF16)
-    (early,) = call(
-        functools.partial(first_state_kernel, group, per, to[1]),
-        "first_states",
-        [payload],
-        (tri, log_decay, k_lin, v_lin),
-        flops=4 * cube // group,
-        exps=2 * tokens * width // group,
-    )
-    late = call(
-        functools.partial(other_states_kernel, group, per, to[1], others),
-        "other_states",
-        [payload] * len(others),
-        (tri, log_decay, k_lin, v_lin),
-        [pltpu.VMEM((group, rows, HD), BF16)],
-        flops=4 * cube,
-        exps=2 * tokens * width,
-    )
-    pays = {to[1]: early, **dict(zip(others, late))}
-    pays = [swap(pays[s], s) if s else pays[s] for s in to]
+
+    def states(s):
+        return call(
+            functools.partial(state_kernel, group, per, s),
+            "states_%d" % s,
+            [shape((rows, HD), BF16)],
+            (tri, log_decay, k_lin, v_lin),
+            flops=4 * cube // group,
+            exps=2 * tokens * width // group,
+        )[0]
+
+    pays = {s: swap(states(s), s) for s in to[1:]}
+    pays[0] = states(0)
+    pays = [pays[s] for s in to]
 
     intra, qa, gain, decay = call(
         functools.partial(intra_kernel, heads),
@@ -473,7 +454,7 @@
         specs=[smem] + [VMEM] * 4,
     )
     half = shape((own.shape[0] // 2, own.shape[1]), BF16)
-    upper, under = call(halves_kernel, "sent_on", [half] * 2, (side, near), after=tops[:1])
+    upper, under = call(halves_kernel, "sent_on", [half] * 2, (side, near))
     across = jnp.concatenate([swap(upper, 1), swap(under, 2)])
     (attended,) = call(
         functools.partial(softmax_last_kernel, group, (3,), kv_heads, pack),

time: 42.3 us -> 41.8 us (0.988)
  waiting for transfers between devices: 8.57 us -> 5.15 us
  starting transfers between devices: 19 us -> 21.3 us
  Pallas kernels: 11.8 us -> 12.4 us
    ppermute x10, waiting for transfers between devices: 4.03 us -> 1.08 us  [swap(): return lax.ppermute(x, 'ctx', [(c, c ^ s) for c in range(n)])]
    ppermute x10, starting transfers between devices: 11.5 us -> 13.7 us  [swap(): return lax.ppermute(x, 'ctx', [(c, c ^ s) for c in range(n)])]
    ppermute x2, waiting for transfers between devices: 4.53 us -> 3.97 us  [ahead(): return lax.ppermute(x, 'ctx', [(c, (c + d * group) % n) for c in range(n)])]
    pallas_call x13 -> x15, Pallas kernels: 11.8 us -> 12.4 us  [call(): pl.pallas_call(run, name=name, out_shape=list(outs), in_specs=specs, scra...]
  transfers between devices with their start and end apart: 15 -> 15, of which waited for: 4 -> 6; matrix products, arithmetic and copies ran while one was open for 0% -> 0% of each run, Pallas kernels for 24% -> 26%
where the time goes in v13:
time: 41.8 us; the launch traced here: 41.6 us
  starting transfers between devices  21.3 us (51%)
  Pallas kernels  12.4 us (30%)
  waiting for transfers between devices  5.15 us (12%)
  between operations  1.67 us (4%)
  local copies, waits for them, and re-layouts  1.18 us (3%)
    ppermute x10, starting transfers between devices, swap(): return lax.ppermute(x, 'ctx', [(c, c ^ s) for c in range(n)])  13.7 us
    pallas_call x15, Pallas kernels, call(): pl.pallas_call(run, name=name, out_shape=list(outs), in_specs=specs, scra...  12.4 us
    ppermute x2, starting transfers between devices, ahead(): return lax.ppermute(x, 'ctx', [(c, (c + d * group) % n) for c in range(n)])  5.69 us
    ppermute x2, waiting for transfers between devices, ahead(): return lax.ppermute(x, 'ctx', [(c, (c + d * group) % n) for c in range(n)])  3.97 us
    ppermute x3, starting transfers between devices, body(): parts = [squares] + [lax.ppermute(squares, 'head', turn) for turn in turns]  1.89 us
    unnamed x18, local copies, waits for them, and re-layouts  1.18 us
    ppermute x10, waiting for transfers between devices, swap(): return lax.ppermute(x, 'ctx', [(c, c ^ s) for c in range(n)])  1.08 us
  transfers between devices with their start and end apart: 15, of which 6 were waited for; matrix products, arithmetic and copies ran while one was open for 0% of the time, Pallas kernels for 26%

profile of v13, /device:TPU:0, one launch (start us, length us, event | category | flops | bytes accessed | tf_op | source)
XLA Modules:
  0.0 41.6 jit_solution(12977634431496890474)
XLA Ops:
  0.7 0.6 %copy-done.5 = f32[16,128]{1,0:T(8,128)S(1)} copy-done((f32[16,128]{1,0:T(8,128)S(1)}, f32[16,128]{1,0:T(8,128)}, u32[]{:S(2)}) %copy-start.5) | copy-done | bytes 8216
  1.8 0.6 %states_2.1 = bf16[528,128]{1,0:T(8,128)(2,1)S(1)} custom-call(f32[128,128]{1,0:T(8,128)S(1)} %get-tuple-element.19.refs_2_.refs_0_, f32[16,128]{1,0:T(8,128)S(1)} %copy-done.5, bf16[128,2048]{1,0:T(8,128)(2,1)S(1)} %copy-done, bf16[128,2048]{1,0:T(8,128)(2,1)S(1)} %copy-done.1), custom_call_target="tpu_custom_call" | custom-call | flops 33554432 | bytes 1257472 | tf_op jit(solution)/shard_map/states_2/pallas_call | solution.py:315
  2.5 3.1 %collective-permute-start.1 = (bf16[528,128]{1,0:T(8,128)(2,1)S(1)}, bf16[528,128]{1,0:T(8,128)(2,1)S(1)}, u32[]{:S(2)}, u32[]{:S(2)}) collective-permute-start(bf16[528,128]{1,0:T(8,128)(2,1)S(1)} %states_2.1), channel_id=1, source_target_pairs={{0,8},{4,12},{8,0},{12,4},{16,24},{20,28},{24,16},{28,20},{1,9},{5... | collective-permute-start | bytes 405512 | tf_op jit(solution)/shard_map/ppermute | solution.py:341
  5.6 0.6 %states_3.1 = bf16[528,128]{1,0:T(8,128)(2,1)S(1)} custom-call(f32[128,128]{1,0:T(8,128)S(1)} %get-tuple-element.19.refs_2_.refs_0_, f32[16,128]{1,0:T(8,128)S(1)} %copy-done.5, bf16[128,2048]{1,0:T(8,128)(2,1)S(1)} %copy-done, bf16[128,2048]{1,0:T(8,128)(2,1)S(1)} %copy-done.1), custom_call_target="tpu_custom_call" | custom-call | flops 33554432 | bytes 1257472 | tf_op jit(solution)/shard_map/states_3/pallas_call | solution.py:315
  6.2 1.5 %collective-permute-start.2 = (bf16[528,128]{1,0:T(8,128)(2,1)S(1)}, bf16[528,128]{1,0:T(8,128)(2,1)S(1)}, u32[]{:S(2)}, u32[]{:S(2)}) collective-permute-start(bf16[528,128]{1,0:T(8,128)(2,1)S(1)} %states_3.1), channel_id=1, source_target_pairs={{0,12},{4,8},{8,4},{12,0},{16,28},{20,24},{24,20},{28,16},{1,13},{... | collective-permute-start | bytes 405512 | tf_op jit(solution)/shard_map/ppermute | solution.py:341
  7.7 0.6 %states_1.1 = bf16[528,128]{1,0:T(8,128)(2,1)S(1)} custom-call(f32[128,128]{1,0:T(8,128)S(1)} %get-tuple-element.19.refs_2_.refs_0_, f32[16,128]{1,0:T(8,128)S(1)} %copy-done.5, bf16[128,2048]{1,0:T(8,128)(2,1)S(1)} %copy-done, bf16[128,2048]{1,0:T(8,128)(2,1)S(1)} %copy-done.1), custom_call_target="tpu_custom_call" | custom-call | flops 33554432 | bytes 1257472 | tf_op jit(solution)/shard_map/states_1/pallas_call | solution.py:315
  8.5 3.0 %collective-permute-start = (bf16[128,512]{1,0:T(8,128)(2,1)S(1)}, bf16[128,512]{1,0:T(8,128)(2,1)S(1)}, u32[]{:S(2)}, u32[]{:S(2)}) collective-permute-start(bf16[128,512]{1,0:T(8,128)(2,1)S(1)} %keys_beside_values.1.refs_0_), channel_id=1, source_target_pairs={{0,16},{4,20},{8,24},{12,28},{16,0},{20,4},{24,8},{28,12},{1,17},{... | collective-permute-start | bytes 393224 | tf_op jit(solution)/shard_map/ppermute | solution.py:344
  11.5 0.8 %states_0.1.refs_0_ = bf16[528,128]{1,0:T(8,128)(2,1)S(1)} custom-call(f32[128,128]{1,0:T(8,128)S(1)} %get-tuple-element.19.refs_2_.refs_0_, f32[16,128]{1,0:T(8,128)S(1)} %copy-done.5, bf16[128,2048]{1,0:T(8,128)(2,1)S(1)} %copy-done, bf16[128,2048]{1,0:T(8,128)(2,1)S(1)} %copy-done.1), custom_call_target="tpu_custom_call" | custom-call | flops 33554432 | bytes 1257472 | tf_op jit(solution)/shard_map/states_0/pallas_call | solution.py:315
  12.4 2.8 %intra_block.1 = (f32[128,2048]{1,0:T(8,128)S(1)}, bf16[128,2048]{1,0:T(8,128)(2,1)S(1)}, f32[128,2048]{1,0:T(8,128)S(1)}, f32[128,16]{1,0:T(8,128)S(1)}) custom-call(f32[128,128]{1,0:T(8,128)S(1)} %get-tuple-element.19.refs_2_.refs_0_, f32[128,128]{1,0:T(8,128)S(1)} %get-tuple-element.20.refs_1_, f32[16,128]{1,0:T(8,128)S(1)} %copy-done.5, ...), custom_call_target="tpu_custom_call" | custom-call | flops 134217728 | bytes 4874240 | tf_op jit(solution)/shard_map/intra_block/pallas_call | solution.py:315
  15.7 2.7 %collective-permute-start.8 = (bf16[528,128]{1,0:T(8,128)(2,1)S(1)}, bf16[528,128]{1,0:T(8,128)(2,1)S(1)}, u32[]{:S(2)}, u32[]{:S(2)}) collective-permute-start(bf16[528,128]{1,0:T(8,128)(2,1)S(1)} %group_state.1.refs_2_), channel_id=1, source_target_pairs={{0,16},{4,20},{8,24},{12,28},{16,0},{20,4},{24,8},{28,12},{1,17},{... | collective-permute-start | bytes 405512 | tf_op jit(solution)/shard_map/ppermute | solution.py:344
  18.4 1.6 %collective-permute-start.4 = (bf16[256,512]{1,0:T(8,128)(2,1)S(1)}, bf16[256,512]{1,0:T(8,128)(2,1)S(1)}, u32[]{:S(2)}, u32[]{:S(2)}) collective-permute-start(bf16[256,512]{1,0:T(8,128)(2,1)S(1)} %stack_keys_values.1.refs_2_), channel_id=1, source_target_pairs={{0,8},{4,12},{8,0},{12,4},{16,24},{20,28},{24,16},{28,20},{1,9},{5... | collective-permute-start | bytes 786440 | tf_op jit(solution)/shard_map/ppermute | solution.py:341
  20.0 0.5 %collective-permute-start.5 = (bf16[256,512]{1,0:T(8,128)(2,1)S(1)}, bf16[256,512]{1,0:T(8,128)(2,1)S(1)}, u32[]{:S(2)}, u32[]{:S(2)}) collective-permute-start(bf16[256,512]{1,0:T(8,128)(2,1)S(1)} %stack_keys_values.1.refs_2_), channel_id=1, source_target_pairs={{0,4},{4,0},{8,12},{12,8},{16,20},{20,16},{24,28},{28,24},{1,5},{5... | collective-permute-start | bytes 786440 | tf_op jit(solution)/shard_map/ppermute | solution.py:341
  20.5 4.0 %collective-permute-done.8.refs_4_ = bf16[528,128]{1,0:T(8,128)(2,1)S(1)} collective-permute-done((bf16[528,128]{1,0:T(8,128)(2,1)S(1)}, bf16[528,128]{1,0:T(8,128)(2,1)S(1)}, u32[]{:S(2)}, u32[]{:S(2)}) %collective-permute-start.8) | collective-permute-done | bytes 135200 | tf_op jit(solution)/shard_map/ppermute | solution.py:344
  24.6 0.9 %collective-permute-start.9 = (bf16[512,128]{1,0:T(8,128)(2,1)S(1)}, bf16[512,128]{1,0:T(8,128)(2,1)S(1)}, u32[]{:S(2)}, u32[]{:S(2)}) collective-permute-start(bf16[512,128]{1,0:T(8,128)(2,1)S(1)} %get-tuple-element.30), channel_id=1, source_target_pairs={{0,12},{4,8},{8,4},{12,0},{16,28},{20,24},{24,20},{28,16},{1,13},{... | collective-permute-start | bytes 393224 | tf_op jit(solution)/shard_map/ppermute | solution.py:341
  25.5 2.1 %collective-permute-start.10 = (bf16[512,128]{1,0:T(8,128)(2,1)S(1)}, bf16[512,128]{1,0:T(8,128)(2,1)S(1)}, u32[]{:S(2)}, u32[]{:S(2)}) collective-permute-start(bf16[512,128]{1,0:T(8,128)(2,1)S(1)} %get-tuple-element.31), channel_id=1, source_target_pairs={{0,8},{4,12},{8,0},{12,4},{16,24},{20,28},{24,16},{28,20},{1,9},{5... | collective-permute-start | bytes 393224 | tf_op jit(solution)/shard_map/ppermute | solution.py:341
  27.7 0.5 %collective-permute-start.11 = (bf16[512,128]{1,0:T(8,128)(2,1)S(1)}, bf16[512,128]{1,0:T(8,128)(2,1)S(1)}, u32[]{:S(2)}, u32[]{:S(2)}) collective-permute-start(bf16[512,128]{1,0:T(8,128)(2,1)S(1)} %get-tuple-element.32), channel_id=1, source_target_pairs={{0,4},{4,0},{8,12},{12,8},{16,20},{20,16},{24,28},{28,24},{1,5},{5... | collective-permute-start | bytes 393224 | tf_op jit(solution)/shard_map/ppermute | solution.py:341
  28.2 2.4 %collective-permute-start.7 = (bf16[128,512]{1,0:T(8,128)(2,1)S(1)}, bf16[128,512]{1,0:T(8,128)(2,1)S(1)}, u32[]{:S(2)}, u32[]{:S(2)}) collective-permute-start(bf16[128,512]{1,0:T(8,128)(2,1)S(1)} %get-tuple-element.23), channel_id=1, source_target_pairs={{0,8},{4,12},{8,0},{12,4},{16,24},{20,28},{24,16},{28,20},{1,9},{5... | collective-permute-start | bytes 393224 | tf_op jit(solution)/shard_map/ppermute | solution.py:341
  30.6 0.9 %collective-permute-start.6 = (bf16[128,512]{1,0:T(8,128)(2,1)S(1)}, bf16[128,512]{1,0:T(8,128)(2,1)S(1)}, u32[]{:S(2)}, u32[]{:S(2)}) collective-permute-start(bf16[128,512]{1,0:T(8,128)(2,1)S(1)} %get-tuple-element.22), channel_id=1, source_target_pairs={{0,4},{4,0},{8,12},{12,8},{16,20},{20,16},{24,28},{28,24},{1,5},{5... | collective-permute-start | bytes 393224 | tf_op jit(solution)/shard_map/ppermute | solution.py:341
  32.2 2.4 %softmax_first.1 = (f32[128,4096]{1,0:T(8,128)S(1)}, f32[128,8]{1,0:T(8,128)S(1)}, f32[128,8]{1,0:T(8,128)S(1)}) custom-call(s32[1]{0:T(128)S(6)} %copy.12.refs_0_, bf16[128,2048]{1,0:T(8,128)(2,1)S(1)} %copy-done.4, bf16[256,512]{1,0:T(8,128)(2,1)S(1)} %stack_keys_values.1.refs_2_, bf16[256,512]{1,0:T(8,128)(2,1)S(1)} %collective-permute-done.4.refs_0_.refs_3_, ...), custom_call_target="tpu_custom_call" | custom-call | flops 805306368 | bytes 3416068 | tf_op jit(solution)/shard_map/softmax_first/pallas_call | solution.py:315
  35.2 0.7 %inter_block.1 = (f32[128,2048]{1,0:T(8,128)S(1)}, f32[8,128]{1,0:T(8,128)S(1)}) custom-call(f32[128,16]{1,0:T(8,128)S(1)} %get-tuple-element.27.refs_0_, bf16[128,2048]{1,0:T(8,128)(2,1)S(1)} %get-tuple-element.28.refs_1_, f32[128,2048]{1,0:T(8,128)S(1)} %get-tuple-element.21.refs_4_.refs_2_, bf16[512,128]{1,0:T(8,128)(2,1)S(1)} %get-tuple-element.29.refs_3_, ...), custom_call_target="tpu_custom_call" | custom-call | flops 67108864 | bytes 3158016 | tf_op jit(solution)/shard_map/inter_block/pallas_call | solution.py:315
  35.8 1.0 %collective-permute-start.12 = (f32[8,128]{1,0:T(8,128)S(1)}, f32[8,128]{1,0:T(8,128)S(1)}, u32[]{:S(2)}, u32[]{:S(2)}) collective-permute-start(f32[8,128]{1,0:T(8,128)S(1)} %get-tuple-element.35.refs_3_), channel_id=1, source_target_pairs={{0,3},{1,2},{2,1},{3,0},{4,7},{5,6},{6,5},{7,4},{8,11},{9,10},{10,... | collective-permute-start | bytes 12296 | tf_op jit(solution)/shard_map/ppermute | solution.py:484
  36.8 0.6 %collective-permute-start.13 = (f32[8,128]{1,0:T(8,128)S(1)}, f32[8,128]{1,0:T(8,128)S(1)}, u32[]{:S(2)}, u32[]{:S(2)}) collective-permute-start(f32[8,128]{1,0:T(8,128)S(1)} %get-tuple-element.35.refs_3_), channel_id=1, source_target_pairs={{0,2},{1,3},{2,0},{3,1},{4,6},{5,7},{6,4},{7,5},{8,10},{9,11},{10,... | collective-permute-start | bytes 12296 | tf_op jit(solution)/shard_map/ppermute | solution.py:484
  37.8 2.5 %softmax_last.1.refs_0_ = bf16[128,2048]{1,0:T(8,128)(2,1)S(1)} custom-call(s32[1]{0:T(128)S(6)} %copy.12.refs_0_, bf16[128,2048]{1,0:T(8,128)(2,1)S(1)} %copy-done.4, bf16[256,512]{1,0:T(8,128)(2,1)S(1)} %pad_maximum_fusion.refs_2_, f32[128,4096]{1,0:T(8,128)S(1)} %get-tuple-element.24.refs_3_, f32[128,8]{1,0:T(8,128)S(1)} %get-tuple-element.25.refs_4_.refs_7_, ...), custom_call_target="tpu_custom_call" | custom-call | flops 268435456 | bytes 3416068 | tf_op jit(solution)/shard_map/softmax_last/pallas_call | solution.py:315
  40.4 1.1 %results.1 = (bf16[128,2048]{1,0:T(8,128)(2,1)}, bf16[128,2048]{1,0:T(8,128)(2,1)}) custom-call(bf16[128,2048]{1,0:T(8,128)(2,1)S(1)} %softmax_last.1.refs_0_, f32[128,2048]{1,0:T(8,128)S(1)} %get-tuple-element.33.refs_1_, f32[128,2048]{1,0:T(8,128)S(1)} %get-tuple-element.34.refs_2_, f32[8,128]{1,0:T(8,128)S(1)} %get-tuple-element.35.refs_3_, ...), custom_call_target="tpu_custom_call" | custom-call | flops 1048576 | bytes 3686400 | tf_op jit(solution)/shard_map/results/pallas_call | solution.py:315
  (40 shorter events, 2.7 us)
Async XLA Ops:
  0.6 0.7 %copy-start.5 = (f32[16,128]{1,0:T(8,128)S(1)}, f32[16,128]{1,0:T(8,128)}, u32[]{:S(2)}) copy-start(f32[16,128]{1,0:T(8,128)} %refs_2_.9) | copy-start | bytes 24580
  0.6 1.0 %copy-start = (bf16[128,2048]{1,0:T(8,128)(2,1)S(1)}, bf16[128,2048]{1,0:T(8,128)(2,1)}, u32[]{:S(2)}) copy-start(bf16[128,2048]{1,0:T(8,128)(2,1)} %refs_4_.1) | copy-start | bytes 1572868
  0.7 1.2 %copy-start.1 = (bf16[128,2048]{1,0:T(8,128)(2,1)S(1)}, bf16[128,2048]{1,0:T(8,128)(2,1)}, u32[]{:S(2)}) copy-start(bf16[128,2048]{1,0:T(8,128)(2,1)} %refs_5_.1) | copy-start | bytes 1572868
  0.7 7.8 %copy-start.6 = (bf16[128,256]{1,0:T(8,128)(2,1)S(1)}, bf16[128,256]{1,0:T(8,128)(2,1)}, u32[]{:S(2)}) copy-start(bf16[128,256]{1,0:T(8,128)(2,1)} %refs_0_.3) | copy-start | bytes 196612
  0.7 7.8 %copy-start.7 = (bf16[128,256]{1,0:T(8,128)(2,1)S(1)}, bf16[128,256]{1,0:T(8,128)(2,1)}, u32[]{:S(2)}) copy-start(bf16[128,256]{1,0:T(8,128)(2,1)} %refs_1_.7) | copy-start | bytes 196612
  2.5 9.9 %copy-start.2 = (bf16[128,2048]{1,0:T(8,128)(2,1)S(1)}, bf16[128,2048]{1,0:T(8,128)(2,1)}, u32[]{:S(2)}) copy-start(bf16[128,2048]{1,0:T(8,128)(2,1)} %refs_3_.9) | copy-start | bytes 1572868
  2.5 9.9 %copy-start.3 = (bf16[128,2048]{1,0:T(8,128)(2,1)S(1)}, bf16[128,2048]{1,0:T(8,128)(2,1)}, u32[]{:S(2)}) copy-start(bf16[128,2048]{1,0:T(8,128)(2,1)} %refs_6_.1) | copy-start | bytes 1572868
  2.5 9.9 %copy-start.8 = (f32[2048]{0:T(1024)S(1)}, f32[2048]{0:T(1024)}, u32[]{:S(2)}) copy-start(f32[2048]{0:T(1024)} %param.15) | copy-start | bytes 24580
  2.5 12.6 %collective-permute-start.1 = (bf16[528,128]{1,0:T(8,128)(2,1)S(1)}, bf16[528,128]{1,0:T(8,128)(2,1)S(1)}, u32[]{:S(2)}, u32[]{:S(2)}) collective-permute-start(bf16[528,128]{1,0:T(8,128)(2,1)S(1)} %states_2.1), channel_id=1, source_target_pairs={{0,8},{4,12},{8,0},{12,4},{16,24},{20,28},{24,16},{28,20},{1,9},{5... | collective-permute-start | bytes 405512 | tf_op jit(solution)/shard_map/ppermute | solution.py:341
  6.2 9.0 %collective-permute-start.2 = (bf16[528,128]{1,0:T(8,128)(2,1)S(1)}, bf16[528,128]{1,0:T(8,128)(2,1)S(1)}, u32[]{:S(2)}, u32[]{:S(2)}) collective-permute-start(bf16[528,128]{1,0:T(8,128)(2,1)S(1)} %states_3.1), channel_id=1, source_target_pairs={{0,12},{4,8},{8,4},{12,0},{16,28},{20,24},{24,20},{28,16},{1,13},{... | collective-permute-start | bytes 405512 | tf_op jit(solution)/shard_map/ppermute | solution.py:341
  8.3 7.3 %collective-permute-start.3 = (bf16[528,128]{1,0:T(8,128)(2,1)S(1)}, bf16[528,128]{1,0:T(8,128)(2,1)S(1)}, u32[]{:S(2)}, u32[]{:S(2)}) collective-permute-start(bf16[528,128]{1,0:T(8,128)(2,1)S(1)} %states_1.1), channel_id=1, source_target_pairs={{0,4},{4,0},{8,12},{12,8},{16,20},{20,16},{24,28},{28,24},{1,5},{5... | collective-permute-start | bytes 405512 | tf_op jit(solution)/shard_map/ppermute | solution.py:341
  8.5 9.9 %collective-permute-start = (bf16[128,512]{1,0:T(8,128)(2,1)S(1)}, bf16[128,512]{1,0:T(8,128)(2,1)S(1)}, u32[]{:S(2)}, u32[]{:S(2)}) collective-permute-start(bf16[128,512]{1,0:T(8,128)(2,1)S(1)} %keys_beside_values.1.refs_0_), channel_id=1, source_target_pairs={{0,16},{4,20},{8,24},{12,28},{16,0},{20,4},{24,8},{28,12},{1,17},{... | collective-permute-start | bytes 393224 | tf_op jit(solution)/shard_map/ppermute | solution.py:344
  15.7 8.7 %collective-permute-start.8 = (bf16[528,128]{1,0:T(8,128)(2,1)S(1)}, bf16[528,128]{1,0:T(8,128)(2,1)S(1)}, u32[]{:S(2)}, u32[]{:S(2)}) collective-permute-start(bf16[528,128]{1,0:T(8,128)(2,1)S(1)} %group_state.1.refs_2_), channel_id=1, source_target_pairs={{0,16},{4,20},{8,24},{12,28},{16,0},{20,4},{24,8},{28,12},{1,17},{... | collective-permute-start | bytes 405512 | tf_op jit(solution)/shard_map/ppermute | solution.py:344
  18.4 13.8 %copy-start.4 = (bf16[128,2048]{1,0:T(8,128)(2,1)S(1)}, bf16[128,2048]{1,0:T(8,128)(2,1)}, u32[]{:S(2)}) copy-start(bf16[128,2048]{1,0:T(8,128)(2,1)} %refs_1_.13) | copy-start | bytes 1572868
  18.4 9.8 %collective-permute-start.4 = (bf16[256,512]{1,0:T(8,128)(2,1)S(1)}, bf16[256,512]{1,0:T(8,128)(2,1)S(1)}, u32[]{:S(2)}, u32[]{:S(2)}) collective-permute-start(bf16[256,512]{1,0:T(8,128)(2,1)S(1)} %stack_keys_values.1.refs_2_), channel_id=1, source_target_pairs={{0,8},{4,12},{8,0},{12,4},{16,24},{20,28},{24,16},{28,20},{1,9},{5... | collective-permute-start | bytes 786440 | tf_op jit(solution)/shard_map/ppermute | solution.py:341
  20.0 8.2 %collective-permute-start.5 = (bf16[256,512]{1,0:T(8,128)(2,1)S(1)}, bf16[256,512]{1,0:T(8,128)(2,1)S(1)}, u32[]{:S(2)}, u32[]{:S(2)}) collective-permute-start(bf16[256,512]{1,0:T(8,128)(2,1)S(1)} %stack_keys_values.1.refs_2_), channel_id=1, source_target_pairs={{0,4},{4,0},{8,12},{12,8},{16,20},{20,16},{24,28},{28,24},{1,5},{5... | collective-permute-start | bytes 786440 | tf_op jit(solution)/shard_map/ppermute | solution.py:341
  24.6 9.9 %collective-permute-start.9 = (bf16[512,128]{1,0:T(8,128)(2,1)S(1)}, bf16[512,128]{1,0:T(8,128)(2,1)S(1)}, u32[]{:S(2)}, u32[]{:S(2)}) collective-permute-start(bf16[512,128]{1,0:T(8,128)(2,1)S(1)} %get-tuple-element.30), channel_id=1, source_target_pairs={{0,12},{4,8},{8,4},{12,0},{16,28},{20,24},{24,20},{28,16},{1,13},{... | collective-permute-start | bytes 393224 | tf_op jit(solution)/shard_map/ppermute | solution.py:341
  25.5 9.3 %collective-permute-start.10 = (bf16[512,128]{1,0:T(8,128)(2,1)S(1)}, bf16[512,128]{1,0:T(8,128)(2,1)S(1)}, u32[]{:S(2)}, u32[]{:S(2)}) collective-permute-start(bf16[512,128]{1,0:T(8,128)(2,1)S(1)} %get-tuple-element.31), channel_id=1, source_target_pairs={{0,8},{4,12},{8,0},{12,4},{16,24},{20,28},{24,16},{28,20},{1,9},{5... | collective-permute-start | bytes 393224 | tf_op jit(solution)/shard_map/ppermute | solution.py:341
  27.7 7.5 %collective-permute-start.11 = (bf16[512,128]{1,0:T(8,128)(2,1)S(1)}, bf16[512,128]{1,0:T(8,128)(2,1)S(1)}, u32[]{:S(2)}, u32[]{:S(2)}) collective-permute-start(bf16[512,128]{1,0:T(8,128)(2,1)S(1)} %get-tuple-element.32), channel_id=1, source_target_pairs={{0,4},{4,0},{8,12},{12,8},{16,20},{20,16},{24,28},{28,24},{1,5},{5... | collective-permute-start | bytes 393224 | tf_op jit(solution)/shard_map/ppermute | solution.py:341
  28.2 9.5 %collective-permute-start.7 = (bf16[128,512]{1,0:T(8,128)(2,1)S(1)}, bf16[128,512]{1,0:T(8,128)(2,1)S(1)}, u32[]{:S(2)}, u32[]{:S(2)}) collective-permute-start(bf16[128,512]{1,0:T(8,128)(2,1)S(1)} %get-tuple-element.23), channel_id=1, source_target_pairs={{0,8},{4,12},{8,0},{12,4},{16,24},{20,28},{24,16},{28,20},{1,9},{5... | collective-permute-start | bytes 393224 | tf_op jit(solution)/shard_map/ppermute | solution.py:341
  30.6 7.2 %collective-permute-start.6 = (bf16[128,512]{1,0:T(8,128)(2,1)S(1)}, bf16[128,512]{1,0:T(8,128)(2,1)S(1)}, u32[]{:S(2)}, u32[]{:S(2)}) collective-permute-start(bf16[128,512]{1,0:T(8,128)(2,1)S(1)} %get-tuple-element.22), channel_id=1, source_target_pairs={{0,4},{4,0},{8,12},{12,8},{16,20},{20,16},{24,28},{28,24},{1,5},{5... | collective-permute-start | bytes 393224 | tf_op jit(solution)/shard_map/ppermute | solution.py:341
  35.8 4.5 %collective-permute-start.12 = (f32[8,128]{1,0:T(8,128)S(1)}, f32[8,128]{1,0:T(8,128)S(1)}, u32[]{:S(2)}, u32[]{:S(2)}) collective-permute-start(f32[8,128]{1,0:T(8,128)S(1)} %get-tuple-element.35.refs_3_), channel_id=1, source_target_pairs={{0,3},{1,2},{2,1},{3,0},{4,7},{5,6},{6,5},{7,4},{8,11},{9,10},{10,... | collective-permute-start | bytes 12296 | tf_op jit(solution)/shard_map/ppermute | solution.py:484
  36.8 3.6 %collective-permute-start.13 = (f32[8,128]{1,0:T(8,128)S(1)}, f32[8,128]{1,0:T(8,128)S(1)}, u32[]{:S(2)}, u32[]{:S(2)}) collective-permute-start(f32[8,128]{1,0:T(8,128)S(1)} %get-tuple-element.35.refs_3_), channel_id=1, source_target_pairs={{0,2},{1,3},{2,0},{3,1},{4,6},{5,7},{6,4},{7,5},{8,10},{9,11},{10,... | collective-permute-start | bytes 12296 | tf_op jit(solution)/shard_map/ppermute | solution.py:484
  37.4 3.0 %collective-permute-start.14 = (f32[8,128]{1,0:T(8,128)S(1)}, f32[8,128]{1,0:T(8,128)S(1)}, u32[]{:S(2)}, u32[]{:S(2)}) collective-permute-start(f32[8,128]{1,0:T(8,128)S(1)} %get-tuple-element.35.refs_3_), channel_id=1, source_target_pairs={{0,1},{1,0},{2,3},{3,2},{4,5},{5,4},{6,7},{7,6},{8,9},{9,8},{10,11... | collective-permute-start | bytes 12296 | tf_op jit(solution)/shard_map/ppermute | solution.py:484

commit v14 on v13

--- a/solution.py
+++ b/solution.py
@@ -355,7 +355,7 @@
     )
     far = [ahead(kv, d) for d in range(1, groups)]
 
-    to, back = (0, 2, 3, 1), (0, 3, 2, 1)
+    to, back = (0, 2, 1, 3), (0, 3, 2, 1)
 
     def states(s):
         return call(

time: 41.8 us -> 43 us (1.029)
  the two profiles are of different devices: /device:TPU:0 before, /device:TPU:25 now
where the time goes in v14:
time: 43 us; the launch traced here: 42.8 us
  starting transfers between devices  22.2 us (52%)
  Pallas kernels  12.4 us (29%)
  waiting for transfers between devices  5.34 us (12%)
  between operations  1.71 us (4%)
  local copies, waits for them, and re-layouts  1.18 us (3%)
    pallas_call x15, Pallas kernels, call(): pl.pallas_call(run, name=name, out_shape=list(outs), in_specs=specs, scra...  12.4 us
    ppermute x10, starting transfers between devices, swap(): return lax.ppermute(x, 'ctx', [(c, c ^ s) for c in range(n)])  11.5 us
    ppermute x3, starting transfers between devices, body(): parts = [squares] + [lax.ppermute(squares, 'head', turn) for turn in turns]  8.12 us
    ppermute x2, waiting for transfers between devices, ahead(): return lax.ppermute(x, 'ctx', [(c, (c + d * group) % n) for c in range(n)])  3.91 us
    ppermute x2, starting transfers between devices, ahead(): return lax.ppermute(x, 'ctx', [(c, (c + d * group) % n) for c in range(n)])  2.49 us
    ppermute x10, waiting for transfers between devices, swap(): return lax.ppermute(x, 'ctx', [(c, c ^ s) for c in range(n)])  1.43 us
    unnamed x18, local copies, waits for them, and re-layouts  1.18 us
  transfers between devices with their start and end apart: 15, of which 4 were waited for; matrix products, arithmetic and copies ran while one was open for 0% of the time, Pallas kernels for 25%

profile of v14, /device:TPU:25, one launch (start us, length us, event | category | flops | bytes accessed | tf_op | source)
XLA Modules:
  0.0 42.8 jit_solution(13797719330316447933)
XLA Ops:
  0.7 0.6 %copy-done.5 = f32[16,128]{1,0:T(8,128)S(1)} copy-done((f32[16,128]{1,0:T(8,128)S(1)}, f32[16,128]{1,0:T(8,128)}, u32[]{:S(2)}) %copy-start.5) | copy-done | bytes 8216
  1.3 0.4 copy-done
  1.8 0.6 %states_2.1 = bf16[528,128]{1,0:T(8,128)(2,1)S(1)} custom-call(f32[128,128]{1,0:T(8,128)S(1)} %get-tuple-element.19.refs_2_.refs_0_, f32[16,128]{1,0:T(8,128)S(1)} %copy-done.5, bf16[128,2048]{1,0:T(8,128)(2,1)S(1)} %copy-done, bf16[128,2048]{1,0:T(8,128)(2,1)S(1)} %copy-done.1), custom_call_target="tpu_custom_call" | custom-call | flops 33554432 | bytes 1257472 | tf_op jit(solution)/shard_map/states_2/pallas_call | solution.py:315
  2.5 0.2 collective-permute-start.1
  2.7 0.6 %states_1.1 = bf16[528,128]{1,0:T(8,128)(2,1)S(1)} custom-call(f32[128,128]{1,0:T(8,128)S(1)} %get-tuple-element.19.refs_2_.refs_0_, f32[16,128]{1,0:T(8,128)S(1)} %copy-done.5, bf16[128,2048]{1,0:T(8,128)(2,1)S(1)} %copy-done, bf16[128,2048]{1,0:T(8,128)(2,1)S(1)} %copy-done.1), custom_call_target="tpu_custom_call" | custom-call | flops 33554432 | bytes 1257472 | tf_op jit(solution)/shard_map/states_1/pallas_call | solution.py:315
  3.3 1.3 %collective-permute-start.2 = (bf16[528,128]{1,0:T(8,128)(2,1)S(1)}, bf16[528,128]{1,0:T(8,128)(2,1)S(1)}, u32[]{:S(2)}, u32[]{:S(2)}) collective-permute-start(bf16[528,128]{1,0:T(8,128)(2,1)S(1)} %states_1.1), channel_id=1, source_target_pairs={{0,4},{4,0},{8,12},{12,8},{16,20},{20,16},{24,28},{28,24},{1,5},{5... | collective-permute-start | bytes 405512 | tf_op jit(solution)/shard_map/ppermute | solution.py:341
  4.6 0.6 %states_3.1 = bf16[528,128]{1,0:T(8,128)(2,1)S(1)} custom-call(f32[128,128]{1,0:T(8,128)S(1)} %get-tuple-element.19.refs_2_.refs_0_, f32[16,128]{1,0:T(8,128)S(1)} %copy-done.5, bf16[128,2048]{1,0:T(8,128)(2,1)S(1)} %copy-done, bf16[128,2048]{1,0:T(8,128)(2,1)S(1)} %copy-done.1), custom_call_target="tpu_custom_call" | custom-call | flops 33554432 | bytes 1257472 | tf_op jit(solution)/shard_map/states_3/pallas_call | solution.py:315
  5.2 1.3 %collective-permute-start.3 = (bf16[528,128]{1,0:T(8,128)(2,1)S(1)}, bf16[528,128]{1,0:T(8,128)(2,1)S(1)}, u32[]{:S(2)}, u32[]{:S(2)}) collective-permute-start(bf16[528,128]{1,0:T(8,128)(2,1)S(1)} %states_3.1), channel_id=1, source_target_pairs={{0,12},{4,8},{8,4},{12,0},{16,28},{20,24},{24,20},{28,16},{1,13},{... | collective-permute-start | bytes 405512 | tf_op jit(solution)/shard_map/ppermute | solution.py:341
  6.7 0.8 %states_0.1.refs_0_ = bf16[528,128]{1,0:T(8,128)(2,1)S(1)} custom-call(f32[128,128]{1,0:T(8,128)S(1)} %get-tuple-element.19.refs_2_.refs_0_, f32[16,128]{1,0:T(8,128)S(1)} %copy-done.5, bf16[128,2048]{1,0:T(8,128)(2,1)S(1)} %copy-done, bf16[128,2048]{1,0:T(8,128)(2,1)S(1)} %copy-done.1), custom_call_target="tpu_custom_call" | custom-call | flops 33554432 | bytes 1257472 | tf_op jit(solution)/shard_map/states_0/pallas_call | solution.py:315
  7.5 2.8 %intra_block.1 = (f32[128,2048]{1,0:T(8,128)S(1)}, bf16[128,2048]{1,0:T(8,128)(2,1)S(1)}, f32[128,2048]{1,0:T(8,128)S(1)}, f32[128,16]{1,0:T(8,128)S(1)}) custom-call(f32[128,128]{1,0:T(8,128)S(1)} %get-tuple-element.19.refs_2_.refs_0_, f32[128,128]{1,0:T(8,128)S(1)} %get-tuple-element.20.refs_1_, f32[16,128]{1,0:T(8,128)S(1)} %copy-done.5, ...), custom_call_target="tpu_custom_call" | custom-call | flops 134217728 | bytes 4874240 | tf_op jit(solution)/shard_map/intra_block/pallas_call | solution.py:315
  10.5 2.4 %collective-permute-start.8 = (bf16[528,128]{1,0:T(8,128)(2,1)S(1)}, bf16[528,128]{1,0:T(8,128)(2,1)S(1)}, u32[]{:S(2)}, u32[]{:S(2)}) collective-permute-start(bf16[528,128]{1,0:T(8,128)(2,1)S(1)} %group_state.1.refs_2_), channel_id=1, source_target_pairs={{0,16},{4,20},{8,24},{12,28},{16,0},{20,4},{24,8},{28,12},{1,17},{... | collective-permute-start | bytes 405512 | tf_op jit(solution)/shard_map/ppermute | solution.py:344
  12.9 2.1 %collective-permute-done.refs_1_ = bf16[128,512]{1,0:T(8,128)(2,1)S(1)} collective-permute-done((bf16[128,512]{1,0:T(8,128)(2,1)S(1)}, bf16[128,512]{1,0:T(8,128)(2,1)S(1)}, u32[]{:S(2)}, u32[]{:S(2)}) %collective-permute-start) | collective-permute-done | bytes 131104 | tf_op jit(solution)/shard_map/ppermute | solution.py:344
  15.1 2.7 %collective-permute-start.5 = (bf16[256,512]{1,0:T(8,128)(2,1)S(1)}, bf16[256,512]{1,0:T(8,128)(2,1)S(1)}, u32[]{:S(2)}, u32[]{:S(2)}) collective-permute-start(bf16[256,512]{1,0:T(8,128)(2,1)S(1)} %stack_keys_values.1.refs_2_), channel_id=1, source_target_pairs={{0,4},{4,0},{8,12},{12,8},{16,20},{20,16},{24,28},{28,24},{1,5},{5... | collective-permute-start | bytes 786440 | tf_op jit(solution)/shard_map/ppermute | solution.py:341
  17.8 1.8 %collective-permute-done.8.refs_4_ = bf16[528,128]{1,0:T(8,128)(2,1)S(1)} collective-permute-done((bf16[528,128]{1,0:T(8,128)(2,1)S(1)}, bf16[528,128]{1,0:T(8,128)(2,1)S(1)}, u32[]{:S(2)}, u32[]{:S(2)}) %collective-permute-start.8) | collective-permute-done | bytes 135200 | tf_op jit(solution)/shard_map/ppermute | solution.py:344
  19.9 3.4 %collective-permute-start.10 = (bf16[512,128]{1,0:T(8,128)(2,1)S(1)}, bf16[512,128]{1,0:T(8,128)(2,1)S(1)}, u32[]{:S(2)}, u32[]{:S(2)}) collective-permute-start(bf16[512,128]{1,0:T(8,128)(2,1)S(1)} %get-tuple-element.31), channel_id=1, source_target_pairs={{0,8},{4,12},{8,0},{12,4},{16,24},{20,28},{24,16},{28,20},{1,9},{5... | collective-permute-start | bytes 393224 | tf_op jit(solution)/shard_map/ppermute | solution.py:341
  23.3 0.8 %collective-permute-done.4.refs_0_.refs_3_ = bf16[256,512]{1,0:T(8,128)(2,1)S(1)} collective-permute-done((bf16[256,512]{1,0:T(8,128)(2,1)S(1)}, bf16[256,512]{1,0:T(8,128)(2,1)S(1)}, u32[]{:S(2)}, u32[]{:S(2)}) %collective-permute-start.4) | collective-permute-done | bytes 262176 | tf_op jit(solution)/shard_map/ppermute | solution.py:341
  24.2 2.3 %collective-permute-start.6 = (bf16[128,512]{1,0:T(8,128)(2,1)S(1)}, bf16[128,512]{1,0:T(8,128)(2,1)S(1)}, u32[]{:S(2)}, u32[]{:S(2)}) collective-permute-start(bf16[128,512]{1,0:T(8,128)(2,1)S(1)} %get-tuple-element.22), channel_id=1, source_target_pairs={{0,4},{4,0},{8,12},{12,8},{16,20},{20,16},{24,28},{28,24},{1,5},{5... | collective-permute-start | bytes 393224 | tf_op jit(solution)/shard_map/ppermute | solution.py:341
  27.2 2.4 %softmax_first.1 = (f32[128,4096]{1,0:T(8,128)S(1)}, f32[128,8]{1,0:T(8,128)S(1)}, f32[128,8]{1,0:T(8,128)S(1)}) custom-call(s32[1]{0:T(128)S(6)} %copy.12.refs_0_, bf16[128,2048]{1,0:T(8,128)(2,1)S(1)} %copy-done.4, bf16[256,512]{1,0:T(8,128)(2,1)S(1)} %stack_keys_values.1.refs_2_, bf16[256,512]{1,0:T(8,128)(2,1)S(1)} %collective-permute-done.4.refs_0_.refs_3_, ...), custom_call_target="tpu_custom_call" | custom-call | flops 805306368 | bytes 3416068 | tf_op jit(solution)/shard_map/softmax_first/pallas_call | solution.py:315
  29.6 0.6 %collective-permute-done.10.refs_5_ = bf16[512,128]{1,0:T(8,128)(2,1)S(1)} collective-permute-done((bf16[512,128]{1,0:T(8,128)(2,1)S(1)}, bf16[512,128]{1,0:T(8,128)(2,1)S(1)}, u32[]{:S(2)}, u32[]{:S(2)}) %collective-permute-start.10) | collective-permute-done | bytes 131104 | tf_op jit(solution)/shard_map/ppermute | solution.py:341
  30.2 0.7 %inter_block.1 = (f32[128,2048]{1,0:T(8,128)S(1)}, f32[8,128]{1,0:T(8,128)S(1)}) custom-call(f32[128,16]{1,0:T(8,128)S(1)} %get-tuple-element.27.refs_0_, bf16[128,2048]{1,0:T(8,128)(2,1)S(1)} %get-tuple-element.28.refs_1_, f32[128,2048]{1,0:T(8,128)S(1)} %get-tuple-element.21.refs_4_.refs_2_, bf16[512,128]{1,0:T(8,128)(2,1)S(1)} %get-tuple-element.29.refs_3_, ...), custom_call_target="tpu_custom_call" | custom-call | flops 67108864 | bytes 3158016 | tf_op jit(solution)/shard_map/inter_block/pallas_call | solution.py:315
  30.9 7.7 %collective-permute-start.12 = (f32[8,128]{1,0:T(8,128)S(1)}, f32[8,128]{1,0:T(8,128)S(1)}, u32[]{:S(2)}, u32[]{:S(2)}) collective-permute-start(f32[8,128]{1,0:T(8,128)S(1)} %get-tuple-element.35.refs_3_), channel_id=1, source_target_pairs={{0,3},{1,2},{2,1},{3,0},{4,7},{5,6},{6,5},{7,4},{8,11},{9,10},{10,... | collective-permute-start | bytes 12296 | tf_op jit(solution)/shard_map/ppermute | solution.py:484
  38.6 0.3 collective-permute-start.13
  39.0 2.5 %softmax_last.1.refs_0_ = bf16[128,2048]{1,0:T(8,128)(2,1)S(1)} custom-call(s32[1]{0:T(128)S(6)} %copy.12.refs_0_, bf16[128,2048]{1,0:T(8,128)(2,1)S(1)} %copy-done.4, bf16[256,512]{1,0:T(8,128)(2,1)S(1)} %pad_maximum_fusion.refs_2_, f32[128,4096]{1,0:T(8,128)S(1)} %get-tuple-element.24.refs_3_, f32[128,8]{1,0:T(8,128)S(1)} %get-tuple-element.25.refs_4_.refs_7_, ...), custom_call_target="tpu_custom_call" | custom-call | flops 268435456 | bytes 3416068 | tf_op jit(solution)/shard_map/softmax_last/pallas_call | solution.py:315
  41.5 1.1 %results.1 = (bf16[128,2048]{1,0:T(8,128)(2,1)}, bf16[128,2048]{1,0:T(8,128)(2,1)}) custom-call(bf16[128,2048]{1,0:T(8,128)(2,1)S(1)} %softmax_last.1.refs_0_, f32[128,2048]{1,0:T(8,128)S(1)} %get-tuple-element.33.refs_1_, f32[128,2048]{1,0:T(8,128)S(1)} %get-tuple-element.34.refs_2_, f32[8,128]{1,0:T(8,128)S(1)} %get-tuple-element.35.refs_3_, ...), custom_call_target="tpu_custom_call" | custom-call | flops 1048576 | bytes 3686400 | tf_op jit(solution)/shard_map/results/pallas_call | solution.py:315
  (40 shorter events, 1.2 us)
Async XLA Ops:
  0.6 0.7 %copy-start.5 = (f32[16,128]{1,0:T(8,128)S(1)}, f32[16,128]{1,0:T(8,128)}, u32[]{:S(2)}) copy-start(f32[16,128]{1,0:T(8,128)} %refs_2_.9) | copy-start | bytes 24580
  0.6 1.0 %copy-start = (bf16[128,2048]{1,0:T(8,128)(2,1)S(1)}, bf16[128,2048]{1,0:T(8,128)(2,1)}, u32[]{:S(2)}) copy-start(bf16[128,2048]{1,0:T(8,128)(2,1)} %refs_4_.1) | copy-start | bytes 1572868
  0.7 1.2 %copy-start.1 = (bf16[128,2048]{1,0:T(8,128)(2,1)S(1)}, bf16[128,2048]{1,0:T(8,128)(2,1)}, u32[]{:S(2)}) copy-start(bf16[128,2048]{1,0:T(8,128)(2,1)} %refs_5_.1) | copy-start | bytes 1572868
  0.7 5.9 %copy-start.6 = (bf16[128,256]{1,0:T(8,128)(2,1)S(1)}, bf16[128,256]{1,0:T(8,128)(2,1)}, u32[]{:S(2)}) copy-start(bf16[128,256]{1,0:T(8,128)(2,1)} %refs_0_.3) | copy-start | bytes 196612
  0.7 5.9 %copy-start.7 = (bf16[128,256]{1,0:T(8,128)(2,1)S(1)}, bf16[128,256]{1,0:T(8,128)(2,1)}, u32[]{:S(2)}) copy-start(bf16[128,256]{1,0:T(8,128)(2,1)} %refs_1_.7) | copy-start | bytes 196612
  2.5 5.0 %copy-start.2 = (bf16[128,2048]{1,0:T(8,128)(2,1)S(1)}, bf16[128,2048]{1,0:T(8,128)(2,1)}, u32[]{:S(2)}) copy-start(bf16[128,2048]{1,0:T(8,128)(2,1)} %refs_3_.9) | copy-start | bytes 1572868
  2.5 5.0 %copy-start.3 = (bf16[128,2048]{1,0:T(8,128)(2,1)S(1)}, bf16[128,2048]{1,0:T(8,128)(2,1)}, u32[]{:S(2)}) copy-start(bf16[128,2048]{1,0:T(8,128)(2,1)} %refs_6_.1) | copy-start | bytes 1572868
  2.5 5.0 %copy-start.8 = (f32[2048]{0:T(1024)S(1)}, f32[2048]{0:T(1024)}, u32[]{:S(2)}) copy-start(f32[2048]{0:T(1024)} %param.15) | copy-start | bytes 24580
  2.5 7.8 %collective-permute-start.1 = (bf16[528,128]{1,0:T(8,128)(2,1)S(1)}, bf16[528,128]{1,0:T(8,128)(2,1)S(1)}, u32[]{:S(2)}, u32[]{:S(2)}) collective-permute-start(bf16[528,128]{1,0:T(8,128)(2,1)S(1)} %states_2.1), channel_id=1, source_target_pairs={{0,8},{4,12},{8,0},{12,4},{16,24},{20,28},{24,16},{28,20},{1,9},{5... | collective-permute-start | bytes 405512 | tf_op jit(solution)/shard_map/ppermute | solution.py:341
  3.3 7.0 %collective-permute-start.2 = (bf16[528,128]{1,0:T(8,128)(2,1)S(1)}, bf16[528,128]{1,0:T(8,128)(2,1)S(1)}, u32[]{:S(2)}, u32[]{:S(2)}) collective-permute-start(bf16[528,128]{1,0:T(8,128)(2,1)S(1)} %states_1.1), channel_id=1, source_target_pairs={{0,4},{4,0},{8,12},{12,8},{16,20},{20,16},{24,28},{28,24},{1,5},{5... | collective-permute-start | bytes 405512 | tf_op jit(solution)/shard_map/ppermute | solution.py:341
  5.2 5.1 %collective-permute-start.3 = (bf16[528,128]{1,0:T(8,128)(2,1)S(1)}, bf16[528,128]{1,0:T(8,128)(2,1)S(1)}, u32[]{:S(2)}, u32[]{:S(2)}) collective-permute-start(bf16[528,128]{1,0:T(8,128)(2,1)S(1)} %states_3.1), channel_id=1, source_target_pairs={{0,12},{4,8},{8,4},{12,0},{16,28},{20,24},{24,20},{28,16},{1,13},{... | collective-permute-start | bytes 405512 | tf_op jit(solution)/shard_map/ppermute | solution.py:341
  6.6 8.4 %collective-permute-start = (bf16[128,512]{1,0:T(8,128)(2,1)S(1)}, bf16[128,512]{1,0:T(8,128)(2,1)S(1)}, u32[]{:S(2)}, u32[]{:S(2)}) collective-permute-start(bf16[128,512]{1,0:T(8,128)(2,1)S(1)} %keys_beside_values.1.refs_0_), channel_id=1, source_target_pairs={{0,16},{4,20},{8,24},{12,28},{16,0},{20,4},{24,8},{28,12},{1,17},{... | collective-permute-start | bytes 393224 | tf_op jit(solution)/shard_map/ppermute | solution.py:344
  10.5 9.1 %collective-permute-start.8 = (bf16[528,128]{1,0:T(8,128)(2,1)S(1)}, bf16[528,128]{1,0:T(8,128)(2,1)S(1)}, u32[]{:S(2)}, u32[]{:S(2)}) collective-permute-start(bf16[528,128]{1,0:T(8,128)(2,1)S(1)} %group_state.1.refs_2_), channel_id=1, source_target_pairs={{0,16},{4,20},{8,24},{12,28},{16,0},{20,4},{24,8},{28,12},{1,17},{... | collective-permute-start | bytes 405512 | tf_op jit(solution)/shard_map/ppermute | solution.py:344
  15.0 12.2 %copy-start.4 = (bf16[128,2048]{1,0:T(8,128)(2,1)S(1)}, bf16[128,2048]{1,0:T(8,128)(2,1)}, u32[]{:S(2)}) copy-start(bf16[128,2048]{1,0:T(8,128)(2,1)} %refs_1_.13) | copy-start | bytes 1572868
  15.0 9.1 %collective-permute-start.4 = (bf16[256,512]{1,0:T(8,128)(2,1)S(1)}, bf16[256,512]{1,0:T(8,128)(2,1)S(1)}, u32[]{:S(2)}, u32[]{:S(2)}) collective-permute-start(bf16[256,512]{1,0:T(8,128)(2,1)S(1)} %stack_keys_values.1.refs_2_), channel_id=1, source_target_pairs={{0,8},{4,12},{8,0},{12,4},{16,24},{20,28},{24,16},{28,20},{1,9},{5... | collective-permute-start | bytes 786440 | tf_op jit(solution)/shard_map/ppermute | solution.py:341
  15.1 9.0 %collective-permute-start.5 = (bf16[256,512]{1,0:T(8,128)(2,1)S(1)}, bf16[256,512]{1,0:T(8,128)(2,1)S(1)}, u32[]{:S(2)}, u32[]{:S(2)}) collective-permute-start(bf16[256,512]{1,0:T(8,128)(2,1)S(1)} %stack_keys_values.1.refs_2_), channel_id=1, source_target_pairs={{0,4},{4,0},{8,12},{12,8},{16,20},{20,16},{24,28},{28,24},{1,5},{5... | collective-permute-start | bytes 786440 | tf_op jit(solution)/shard_map/ppermute | solution.py:341
  19.8 9.8 %collective-permute-start.9 = (bf16[512,128]{1,0:T(8,128)(2,1)S(1)}, bf16[512,128]{1,0:T(8,128)(2,1)S(1)}, u32[]{:S(2)}, u32[]{:S(2)}) collective-permute-start(bf16[512,128]{1,0:T(8,128)(2,1)S(1)} %get-tuple-element.30), channel_id=1, source_target_pairs={{0,12},{4,8},{8,4},{12,0},{16,28},{20,24},{24,20},{28,16},{1,13},{... | collective-permute-start | bytes 393224 | tf_op jit(solution)/shard_map/ppermute | solution.py:341
  19.9 10.4 %collective-permute-start.10 = (bf16[512,128]{1,0:T(8,128)(2,1)S(1)}, bf16[512,128]{1,0:T(8,128)(2,1)S(1)}, u32[]{:S(2)}, u32[]{:S(2)}) collective-permute-start(bf16[512,128]{1,0:T(8,128)(2,1)S(1)} %get-tuple-element.31), channel_id=1, source_target_pairs={{0,8},{4,12},{8,0},{12,4},{16,24},{20,28},{24,16},{28,20},{1,9},{5... | collective-permute-start | bytes 393224 | tf_op jit(solution)/shard_map/ppermute | solution.py:341
  23.3 6.9 %collective-permute-start.11 = (bf16[512,128]{1,0:T(8,128)(2,1)S(1)}, bf16[512,128]{1,0:T(8,128)(2,1)S(1)}, u32[]{:S(2)}, u32[]{:S(2)}) collective-permute-start(bf16[512,128]{1,0:T(8,128)(2,1)S(1)} %get-tuple-element.32), channel_id=1, source_target_pairs={{0,4},{4,0},{8,12},{12,8},{16,20},{20,16},{24,28},{28,24},{1,5},{5... | collective-permute-start | bytes 393224 | tf_op jit(solution)/shard_map/ppermute | solution.py:341
  24.1 14.9 %collective-permute-start.7 = (bf16[128,512]{1,0:T(8,128)(2,1)S(1)}, bf16[128,512]{1,0:T(8,128)(2,1)S(1)}, u32[]{:S(2)}, u32[]{:S(2)}) collective-permute-start(bf16[128,512]{1,0:T(8,128)(2,1)S(1)} %get-tuple-element.23), channel_id=1, source_target_pairs={{0,8},{4,12},{8,0},{12,4},{16,24},{20,28},{24,16},{28,20},{1,9},{5... | collective-permute-start | bytes 393224 | tf_op jit(solution)/shard_map/ppermute | solution.py:341
  24.2 14.8 %collective-permute-start.6 = (bf16[128,512]{1,0:T(8,128)(2,1)S(1)}, bf16[128,512]{1,0:T(8,128)(2,1)S(1)}, u32[]{:S(2)}, u32[]{:S(2)}) collective-permute-start(bf16[128,512]{1,0:T(8,128)(2,1)S(1)} %get-tuple-element.22), channel_id=1, source_target_pairs={{0,4},{4,0},{8,12},{12,8},{16,20},{20,16},{24,28},{28,24},{1,5},{5... | collective-permute-start | bytes 393224 | tf_op jit(solution)/shard_map/ppermute | solution.py:341
  30.9 10.6 %collective-permute-start.12 = (f32[8,128]{1,0:T(8,128)S(1)}, f32[8,128]{1,0:T(8,128)S(1)}, u32[]{:S(2)}, u32[]{:S(2)}) collective-permute-start(f32[8,128]{1,0:T(8,128)S(1)} %get-tuple-element.35.refs_3_), channel_id=1, source_target_pairs={{0,3},{1,2},{2,1},{3,0},{4,7},{5,6},{6,5},{7,4},{8,11},{9,10},{10,... | collective-permute-start | bytes 12296 | tf_op jit(solution)/shard_map/ppermute | solution.py:484
  38.6 2.9 %collective-permute-start.13 = (f32[8,128]{1,0:T(8,128)S(1)}, f32[8,128]{1,0:T(8,128)S(1)}, u32[]{:S(2)}, u32[]{:S(2)}) collective-permute-start(f32[8,128]{1,0:T(8,128)S(1)} %get-tuple-element.35.refs_3_), channel_id=1, source_target_pairs={{0,2},{1,3},{2,0},{3,1},{4,6},{5,7},{6,4},{7,5},{8,10},{9,11},{10,... | collective-permute-start | bytes 12296 | tf_op jit(solution)/shard_map/ppermute | solution.py:484
  38.8 2.7 %collective-permute-start.14 = (f32[8,128]{1,0:T(8,128)S(1)}, f32[8,128]{1,0:T(8,128)S(1)}, u32[]{:S(2)}, u32[]{:S(2)}) collective-permute-start(f32[8,128]{1,0:T(8,128)S(1)} %get-tuple-element.35.refs_3_), channel_id=1, source_target_pairs={{0,1},{1,0},{2,3},{3,2},{4,5},{5,4},{6,7},{7,6},{8,9},{9,8},{10,11... | collective-permute-start | bytes 12296 | tf_op jit(solution)/shard_map/ppermute | solution.py:484

commit v15 on v14

--- a/solution.py
+++ b/solution.py
@@ -383,6 +383,7 @@
         (tri, bias, log_decay, q_lin, k_lin, v_lin, gate, norm_gain.reshape(1, width)),
         flops=4 * cube,
         exps=4 * tokens * width,
+        after=far,
     )
 
     slots = pltpu.VMEM((group, rows, HD), BF16)

time: 43 us -> 41.7 us (0.970)
  the two profiles are of different devices: /device:TPU:25 before, /device:TPU:0 now
where the time goes in v15:
time: 41.7 us; the launch traced here: 41.6 us
  starting transfers between devices  17.7 us (42%)
  Pallas kernels  12.4 us (30%)
  waiting for transfers between devices  9 us (22%)
  between operations  1.66 us (4%)
  local copies, waits for them, and re-layouts  0.84 us (2%)
    pallas_call x15, Pallas kernels, call(): pl.pallas_call(run, name=name, out_shape=list(outs), in_specs=specs, scra...  12.4 us
    ppermute x10, starting transfers between devices, swap(): return lax.ppermute(x, 'ctx', [(c, c ^ s) for c in range(n)])  11 us
    ppermute x2, starting transfers between devices, ahead(): return lax.ppermute(x, 'ctx', [(c, (c + d * group) % n) for c in range(n)])  4.77 us
    ppermute x10, waiting for transfers between devices, swap(): return lax.ppermute(x, 'ctx', [(c, c ^ s) for c in range(n)])  4.67 us
    ppermute x2, waiting for transfers between devices, ahead(): return lax.ppermute(x, 'ctx', [(c, (c + d * group) % n) for c in range(n)])  4.33 us
    ppermute x3, starting transfers between devices, body(): parts = [squares] + [lax.ppermute(squares, 'head', turn) for turn in turns]  1.89 us
    unnamed x18, local copies, waits for them, and re-layouts  0.84 us
  transfers between devices with their start and end apart: 15, of which 6 were waited for; matrix products, arithmetic and copies ran while one was open for 0% of the time, Pallas kernels for 27%

profile of v15, /device:TPU:0, one launch (start us, length us, event | category | flops | bytes accessed | tf_op | source)
XLA Modules:
  0.0 41.6 jit_solution(10701055436719162039)
XLA Ops:
  0.7 0.8 %copy-done.6 = bf16[128,256]{1,0:T(8,128)(2,1)S(1)} copy-done((bf16[128,256]{1,0:T(8,128)(2,1)S(1)}, bf16[128,256]{1,0:T(8,128)(2,1)}, u32[]{:S(2)}) %copy-start.6) | copy-done | bytes 65560
  1.5 4.1 %collective-permute-start = (bf16[128,512]{1,0:T(8,128)(2,1)S(1)}, bf16[128,512]{1,0:T(8,128)(2,1)S(1)}, u32[]{:S(2)}, u32[]{:S(2)}) collective-permute-start(bf16[128,512]{1,0:T(8,128)(2,1)S(1)} %keys_beside_values.1.refs_0_), channel_id=1, source_target_pairs={{0,16},{4,20},{8,24},{12,28},{16,0},{20,4},{24,8},{28,12},{1,17},{... | collective-permute-start | bytes 393224 | tf_op jit(solution)/shard_map/ppermute | solution.py:344
  5.6 0.6 %states_2.1 = bf16[528,128]{1,0:T(8,128)(2,1)S(1)} custom-call(f32[128,128]{1,0:T(8,128)S(1)} %get-tuple-element.19.refs_2_.refs_0_, f32[16,128]{1,0:T(8,128)S(1)} %copy-done.5, bf16[128,2048]{1,0:T(8,128)(2,1)S(1)} %copy-done, bf16[128,2048]{1,0:T(8,128)(2,1)S(1)} %copy-done.1), custom_call_target="tpu_custom_call" | custom-call | flops 33554432 | bytes 1257472 | tf_op jit(solution)/shard_map/states_2/pallas_call | solution.py:315
  6.3 1.6 %collective-permute-start.1 = (bf16[528,128]{1,0:T(8,128)(2,1)S(1)}, bf16[528,128]{1,0:T(8,128)(2,1)S(1)}, u32[]{:S(2)}, u32[]{:S(2)}) collective-permute-start(bf16[528,128]{1,0:T(8,128)(2,1)S(1)} %states_2.1), channel_id=1, source_target_pairs={{0,8},{4,12},{8,0},{12,4},{16,24},{20,28},{24,16},{28,20},{1,9},{5... | collective-permute-start | bytes 405512 | tf_op jit(solution)/shard_map/ppermute | solution.py:341
  7.9 0.6 %states_1.1 = bf16[528,128]{1,0:T(8,128)(2,1)S(1)} custom-call(f32[128,128]{1,0:T(8,128)S(1)} %get-tuple-element.19.refs_2_.refs_0_, f32[16,128]{1,0:T(8,128)S(1)} %copy-done.5, bf16[128,2048]{1,0:T(8,128)(2,1)S(1)} %copy-done, bf16[128,2048]{1,0:T(8,128)(2,1)S(1)} %copy-done.1), custom_call_target="tpu_custom_call" | custom-call | flops 33554432 | bytes 1257472 | tf_op jit(solution)/shard_map/states_1/pallas_call | solution.py:315
  8.5 1.6 %collective-permute-start.2 = (bf16[528,128]{1,0:T(8,128)(2,1)S(1)}, bf16[528,128]{1,0:T(8,128)(2,1)S(1)}, u32[]{:S(2)}, u32[]{:S(2)}) collective-permute-start(bf16[528,128]{1,0:T(8,128)(2,1)S(1)} %states_1.1), channel_id=1, source_target_pairs={{0,4},{4,0},{8,12},{12,8},{16,20},{20,16},{24,28},{28,24},{1,5},{5... | collective-permute-start | bytes 405512 | tf_op jit(solution)/shard_map/ppermute | solution.py:341
  10.1 0.6 %states_3.1 = bf16[528,128]{1,0:T(8,128)(2,1)S(1)} custom-call(f32[128,128]{1,0:T(8,128)S(1)} %get-tuple-element.19.refs_2_.refs_0_, f32[16,128]{1,0:T(8,128)S(1)} %copy-done.5, bf16[128,2048]{1,0:T(8,128)(2,1)S(1)} %copy-done, bf16[128,2048]{1,0:T(8,128)(2,1)S(1)} %copy-done.1), custom_call_target="tpu_custom_call" | custom-call | flops 33554432 | bytes 1257472 | tf_op jit(solution)/shard_map/states_3/pallas_call | solution.py:315
  11.2 0.8 %states_0.1.refs_0_ = bf16[528,128]{1,0:T(8,128)(2,1)S(1)} custom-call(f32[128,128]{1,0:T(8,128)S(1)} %get-tuple-element.19.refs_2_.refs_0_, f32[16,128]{1,0:T(8,128)S(1)} %copy-done.5, bf16[128,2048]{1,0:T(8,128)(2,1)S(1)} %copy-done, bf16[128,2048]{1,0:T(8,128)(2,1)S(1)} %copy-done.1), custom_call_target="tpu_custom_call" | custom-call | flops 33554432 | bytes 1257472 | tf_op jit(solution)/shard_map/states_0/pallas_call | solution.py:315
  12.0 2.8 %intra_block.1 = (f32[128,2048]{1,0:T(8,128)S(1)}, bf16[128,2048]{1,0:T(8,128)(2,1)S(1)}, f32[128,2048]{1,0:T(8,128)S(1)}, f32[128,16]{1,0:T(8,128)S(1)}) custom-call(f32[128,128]{1,0:T(8,128)S(1)} %get-tuple-element.19.refs_2_.refs_0_, f32[128,128]{1,0:T(8,128)S(1)} %get-tuple-element.20.refs_1_, f32[16,128]{1,0:T(8,128)S(1)} %copy-done.5, ...), custom_call_target="tpu_custom_call" | custom-call | flops 134217728 | bytes 4874240 | tf_op jit(solution)/shard_map/intra_block/pallas_call | solution.py:315
  14.8 0.7 %collective-permute-done.2.refs_2_ = bf16[528,128]{1,0:T(8,128)(2,1)S(1)} collective-permute-done((bf16[528,128]{1,0:T(8,128)(2,1)S(1)}, bf16[528,128]{1,0:T(8,128)(2,1)S(1)}, u32[]{:S(2)}, u32[]{:S(2)}) %collective-permute-start.2) | collective-permute-done | bytes 135200 | tf_op jit(solution)/shard_map/ppermute | solution.py:341
  15.6 1.4 %collective-permute-done.3.refs_3_ = bf16[528,128]{1,0:T(8,128)(2,1)S(1)} collective-permute-done((bf16[528,128]{1,0:T(8,128)(2,1)S(1)}, bf16[528,128]{1,0:T(8,128)(2,1)S(1)}, u32[]{:S(2)}, u32[]{:S(2)}) %collective-permute-start.3) | collective-permute-done | bytes 135200 | tf_op jit(solution)/shard_map/ppermute | solution.py:341
  17.1 0.7 %collective-permute-start.8 = (bf16[528,128]{1,0:T(8,128)(2,1)S(1)}, bf16[528,128]{1,0:T(8,128)(2,1)S(1)}, u32[]{:S(2)}, u32[]{:S(2)}) collective-permute-start(bf16[528,128]{1,0:T(8,128)(2,1)S(1)} %group_state.1.refs_2_), channel_id=1, source_target_pairs={{0,16},{4,20},{8,24},{12,28},{16,0},{20,4},{24,8},{28,12},{1,17},{... | collective-permute-start | bytes 405512 | tf_op jit(solution)/shard_map/ppermute | solution.py:344
  17.8 2.8 %collective-permute-start.4 = (bf16[256,512]{1,0:T(8,128)(2,1)S(1)}, bf16[256,512]{1,0:T(8,128)(2,1)S(1)}, u32[]{:S(2)}, u32[]{:S(2)}) collective-permute-start(bf16[256,512]{1,0:T(8,128)(2,1)S(1)} %stack_keys_values.1.refs_2_), channel_id=1, source_target_pairs={{0,8},{4,12},{8,0},{12,4},{16,24},{20,28},{24,16},{28,20},{1,9},{5... | collective-permute-start | bytes 786440 | tf_op jit(solution)/shard_map/ppermute | solution.py:341
  20.6 0.5 %collective-permute-start.5 = (bf16[256,512]{1,0:T(8,128)(2,1)S(1)}, bf16[256,512]{1,0:T(8,128)(2,1)S(1)}, u32[]{:S(2)}, u32[]{:S(2)}) collective-permute-start(bf16[256,512]{1,0:T(8,128)(2,1)S(1)} %stack_keys_values.1.refs_2_), channel_id=1, source_target_pairs={{0,4},{4,0},{8,12},{12,8},{16,20},{20,16},{24,28},{28,24},{1,5},{5... | collective-permute-start | bytes 786440 | tf_op jit(solution)/shard_map/ppermute | solution.py:341
  21.1 4.3 %collective-permute-done.8.refs_4_ = bf16[528,128]{1,0:T(8,128)(2,1)S(1)} collective-permute-done((bf16[528,128]{1,0:T(8,128)(2,1)S(1)}, bf16[528,128]{1,0:T(8,128)(2,1)S(1)}, u32[]{:S(2)}, u32[]{:S(2)}) %collective-permute-start.8) | collective-permute-done | bytes 135200 | tf_op jit(solution)/shard_map/ppermute | solution.py:344
  25.8 1.6 %collective-permute-start.10 = (bf16[512,128]{1,0:T(8,128)(2,1)S(1)}, bf16[512,128]{1,0:T(8,128)(2,1)S(1)}, u32[]{:S(2)}, u32[]{:S(2)}) collective-permute-start(bf16[512,128]{1,0:T(8,128)(2,1)S(1)} %get-tuple-element.31), channel_id=1, source_target_pairs={{0,8},{4,12},{8,0},{12,4},{16,24},{20,28},{24,16},{28,20},{1,9},{5... | collective-permute-start | bytes 393224 | tf_op jit(solution)/shard_map/ppermute | solution.py:341
  27.4 1.7 %collective-permute-start.11 = (bf16[512,128]{1,0:T(8,128)(2,1)S(1)}, bf16[512,128]{1,0:T(8,128)(2,1)S(1)}, u32[]{:S(2)}, u32[]{:S(2)}) collective-permute-start(bf16[512,128]{1,0:T(8,128)(2,1)S(1)} %get-tuple-element.32), channel_id=1, source_target_pairs={{0,4},{4,0},{8,12},{12,8},{16,20},{20,16},{24,28},{28,24},{1,5},{5... | collective-permute-start | bytes 393224 | tf_op jit(solution)/shard_map/ppermute | solution.py:341
  29.1 0.5 %collective-permute-done.4.refs_0_.refs_3_ = bf16[256,512]{1,0:T(8,128)(2,1)S(1)} collective-permute-done((bf16[256,512]{1,0:T(8,128)(2,1)S(1)}, bf16[256,512]{1,0:T(8,128)(2,1)S(1)}, u32[]{:S(2)}, u32[]{:S(2)}) %collective-permute-start.4) | collective-permute-done | bytes 262176 | tf_op jit(solution)/shard_map/ppermute | solution.py:341
  30.8 2.4 %softmax_first.1 = (f32[128,4096]{1,0:T(8,128)S(1)}, f32[128,8]{1,0:T(8,128)S(1)}, f32[128,8]{1,0:T(8,128)S(1)}) custom-call(s32[1]{0:T(128)S(6)} %copy.12.refs_0_, bf16[128,2048]{1,0:T(8,128)(2,1)S(1)} %copy-done.4, bf16[256,512]{1,0:T(8,128)(2,1)S(1)} %stack_keys_values.1.refs_2_, bf16[256,512]{1,0:T(8,128)(2,1)S(1)} %collective-permute-done.4.refs_0_.refs_3_, ...), custom_call_target="tpu_custom_call" | custom-call | flops 805306368 | bytes 3416068 | tf_op jit(solution)/shard_map/softmax_first/pallas_call | solution.py:315
  33.2 2.0 %collective-permute-done.10.refs_5_ = bf16[512,128]{1,0:T(8,128)(2,1)S(1)} collective-permute-done((bf16[512,128]{1,0:T(8,128)(2,1)S(1)}, bf16[512,128]{1,0:T(8,128)(2,1)S(1)}, u32[]{:S(2)}, u32[]{:S(2)}) %collective-permute-start.10) | collective-permute-done | bytes 131104 | tf_op jit(solution)/shard_map/ppermute | solution.py:341
  35.2 0.7 %inter_block.1 = (f32[128,2048]{1,0:T(8,128)S(1)}, f32[8,128]{1,0:T(8,128)S(1)}) custom-call(f32[128,16]{1,0:T(8,128)S(1)} %get-tuple-element.27.refs_0_, bf16[128,2048]{1,0:T(8,128)(2,1)S(1)} %get-tuple-element.28.refs_1_, f32[128,2048]{1,0:T(8,128)S(1)} %get-tuple-element.21.refs_4_.refs_2_, bf16[512,128]{1,0:T(8,128)(2,1)S(1)} %get-tuple-element.29.refs_3_, ...), custom_call_target="tpu_custom_call" | custom-call | flops 67108864 | bytes 3158016 | tf_op jit(solution)/shard_map/inter_block/pallas_call | solution.py:315
  35.9 1.5 %collective-permute-start.13 = (f32[8,128]{1,0:T(8,128)S(1)}, f32[8,128]{1,0:T(8,128)S(1)}, u32[]{:S(2)}, u32[]{:S(2)}) collective-permute-start(f32[8,128]{1,0:T(8,128)S(1)} %get-tuple-element.35.refs_3_), channel_id=1, source_target_pairs={{0,2},{1,3},{2,0},{3,1},{4,6},{5,7},{6,4},{7,5},{8,10},{9,11},{10,... | collective-permute-start | bytes 12296 | tf_op jit(solution)/shard_map/ppermute | solution.py:485
  37.8 2.5 %softmax_last.1.refs_0_ = bf16[128,2048]{1,0:T(8,128)(2,1)S(1)} custom-call(s32[1]{0:T(128)S(6)} %copy.12.refs_0_, bf16[128,2048]{1,0:T(8,128)(2,1)S(1)} %copy-done.4, bf16[256,512]{1,0:T(8,128)(2,1)S(1)} %pad_maximum_fusion.refs_2_, f32[128,4096]{1,0:T(8,128)S(1)} %get-tuple-element.24.refs_3_, f32[128,8]{1,0:T(8,128)S(1)} %get-tuple-element.25.refs_4_.refs_7_, ...), custom_call_target="tpu_custom_call" | custom-call | flops 268435456 | bytes 3416068 | tf_op jit(solution)/shard_map/softmax_last/pallas_call | solution.py:315
  40.3 1.1 %results.1 = (bf16[128,2048]{1,0:T(8,128)(2,1)}, bf16[128,2048]{1,0:T(8,128)(2,1)}) custom-call(bf16[128,2048]{1,0:T(8,128)(2,1)S(1)} %softmax_last.1.refs_0_, f32[128,2048]{1,0:T(8,128)S(1)} %get-tuple-element.33.refs_1_, f32[128,2048]{1,0:T(8,128)S(1)} %get-tuple-element.34.refs_2_, f32[8,128]{1,0:T(8,128)S(1)} %get-tuple-element.35.refs_3_, ...), custom_call_target="tpu_custom_call" | custom-call | flops 1048576 | bytes 3686400 | tf_op jit(solution)/shard_map/results/pallas_call | solution.py:315
  (40 shorter events, 2.2 us)
Async XLA Ops:
  0.6 0.8 %copy-start.6 = (bf16[128,256]{1,0:T(8,128)(2,1)S(1)}, bf16[128,256]{1,0:T(8,128)(2,1)}, u32[]{:S(2)}) copy-start(bf16[128,256]{1,0:T(8,128)(2,1)} %refs_0_.3) | copy-start | bytes 196612
  0.6 0.9 %copy-start.7 = (bf16[128,256]{1,0:T(8,128)(2,1)S(1)}, bf16[128,256]{1,0:T(8,128)(2,1)}, u32[]{:S(2)}) copy-start(bf16[128,256]{1,0:T(8,128)(2,1)} %refs_1_.7) | copy-start | bytes 196612
  0.7 5.0 %copy-start.5 = (f32[16,128]{1,0:T(8,128)S(1)}, f32[16,128]{1,0:T(8,128)}, u32[]{:S(2)}) copy-start(f32[16,128]{1,0:T(8,128)} %refs_2_.9) | copy-start | bytes 24580
  0.7 5.0 %copy-start = (bf16[128,2048]{1,0:T(8,128)(2,1)S(1)}, bf16[128,2048]{1,0:T(8,128)(2,1)}, u32[]{:S(2)}) copy-start(bf16[128,2048]{1,0:T(8,128)(2,1)} %refs_4_.1) | copy-start | bytes 1572868
  0.7 5.0 %copy-start.1 = (bf16[128,2048]{1,0:T(8,128)(2,1)S(1)}, bf16[128,2048]{1,0:T(8,128)(2,1)}, u32[]{:S(2)}) copy-start(bf16[128,2048]{1,0:T(8,128)(2,1)} %refs_5_.1) | copy-start | bytes 1572868
  1.5 10.5 %collective-permute-start = (bf16[128,512]{1,0:T(8,128)(2,1)S(1)}, bf16[128,512]{1,0:T(8,128)(2,1)S(1)}, u32[]{:S(2)}, u32[]{:S(2)}) collective-permute-start(bf16[128,512]{1,0:T(8,128)(2,1)S(1)} %keys_beside_values.1.refs_0_), channel_id=1, source_target_pairs={{0,16},{4,20},{8,24},{12,28},{16,0},{20,4},{24,8},{28,12},{1,17},{... | collective-permute-start | bytes 393224 | tf_op jit(solution)/shard_map/ppermute | solution.py:344
  6.2 5.8 %copy-start.2 = (bf16[128,2048]{1,0:T(8,128)(2,1)S(1)}, bf16[128,2048]{1,0:T(8,128)(2,1)}, u32[]{:S(2)}) copy-start(bf16[128,2048]{1,0:T(8,128)(2,1)} %refs_3_.9) | copy-start | bytes 1572868
  6.2 5.8 %copy-start.3 = (bf16[128,2048]{1,0:T(8,128)(2,1)S(1)}, bf16[128,2048]{1,0:T(8,128)(2,1)}, u32[]{:S(2)}) copy-start(bf16[128,2048]{1,0:T(8,128)(2,1)} %refs_6_.1) | copy-start | bytes 1572868
  6.3 5.8 %copy-start.8 = (f32[2048]{0:T(1024)S(1)}, f32[2048]{0:T(1024)}, u32[]{:S(2)}) copy-start(f32[2048]{0:T(1024)} %param.15) | copy-start | bytes 24580
  6.3 8.6 %collective-permute-start.1 = (bf16[528,128]{1,0:T(8,128)(2,1)S(1)}, bf16[528,128]{1,0:T(8,128)(2,1)S(1)}, u32[]{:S(2)}, u32[]{:S(2)}) collective-permute-start(bf16[528,128]{1,0:T(8,128)(2,1)S(1)} %states_2.1), channel_id=1, source_target_pairs={{0,8},{4,12},{8,0},{12,4},{16,24},{20,28},{24,16},{28,20},{1,9},{5... | collective-permute-start | bytes 405512 | tf_op jit(solution)/shard_map/ppermute | solution.py:341
  8.5 7.0 %collective-permute-start.2 = (bf16[528,128]{1,0:T(8,128)(2,1)S(1)}, bf16[528,128]{1,0:T(8,128)(2,1)S(1)}, u32[]{:S(2)}, u32[]{:S(2)}) collective-permute-start(bf16[528,128]{1,0:T(8,128)(2,1)S(1)} %states_1.1), channel_id=1, source_target_pairs={{0,4},{4,0},{8,12},{12,8},{16,20},{20,16},{24,28},{28,24},{1,5},{5... | collective-permute-start | bytes 405512 | tf_op jit(solution)/shard_map/ppermute | solution.py:341
  10.7 6.2 %collective-permute-start.3 = (bf16[528,128]{1,0:T(8,128)(2,1)S(1)}, bf16[528,128]{1,0:T(8,128)(2,1)S(1)}, u32[]{:S(2)}, u32[]{:S(2)}) collective-permute-start(bf16[528,128]{1,0:T(8,128)(2,1)S(1)} %states_3.1), channel_id=1, source_target_pairs={{0,12},{4,8},{8,4},{12,0},{16,28},{20,24},{24,20},{28,16},{1,13},{... | collective-permute-start | bytes 405512 | tf_op jit(solution)/shard_map/ppermute | solution.py:341
  17.1 8.2 %collective-permute-start.8 = (bf16[528,128]{1,0:T(8,128)(2,1)S(1)}, bf16[528,128]{1,0:T(8,128)(2,1)S(1)}, u32[]{:S(2)}, u32[]{:S(2)}) collective-permute-start(bf16[528,128]{1,0:T(8,128)(2,1)S(1)} %group_state.1.refs_2_), channel_id=1, source_target_pairs={{0,16},{4,20},{8,24},{12,28},{16,0},{20,4},{24,8},{28,12},{1,17},{... | collective-permute-start | bytes 405512 | tf_op jit(solution)/shard_map/ppermute | solution.py:344
  17.8 13.0 %copy-start.4 = (bf16[128,2048]{1,0:T(8,128)(2,1)S(1)}, bf16[128,2048]{1,0:T(8,128)(2,1)}, u32[]{:S(2)}) copy-start(bf16[128,2048]{1,0:T(8,128)(2,1)} %refs_1_.13) | copy-start | bytes 1572868
  17.8 11.8 %collective-permute-start.4 = (bf16[256,512]{1,0:T(8,128)(2,1)S(1)}, bf16[256,512]{1,0:T(8,128)(2,1)S(1)}, u32[]{:S(2)}, u32[]{:S(2)}) collective-permute-start(bf16[256,512]{1,0:T(8,128)(2,1)S(1)} %stack_keys_values.1.refs_2_), channel_id=1, source_target_pairs={{0,8},{4,12},{8,0},{12,4},{16,24},{20,28},{24,16},{28,20},{1,9},{5... | collective-permute-start | bytes 786440 | tf_op jit(solution)/shard_map/ppermute | solution.py:341
  20.6 9.1 %collective-permute-start.5 = (bf16[256,512]{1,0:T(8,128)(2,1)S(1)}, bf16[256,512]{1,0:T(8,128)(2,1)S(1)}, u32[]{:S(2)}, u32[]{:S(2)}) collective-permute-start(bf16[256,512]{1,0:T(8,128)(2,1)S(1)} %stack_keys_values.1.refs_2_), channel_id=1, source_target_pairs={{0,4},{4,0},{8,12},{12,8},{16,20},{20,16},{24,28},{28,24},{1,5},{5... | collective-permute-start | bytes 786440 | tf_op jit(solution)/shard_map/ppermute | solution.py:341
  25.5 7.7 %collective-permute-start.9 = (bf16[512,128]{1,0:T(8,128)(2,1)S(1)}, bf16[512,128]{1,0:T(8,128)(2,1)S(1)}, u32[]{:S(2)}, u32[]{:S(2)}) collective-permute-start(bf16[512,128]{1,0:T(8,128)(2,1)S(1)} %get-tuple-element.30), channel_id=1, source_target_pairs={{0,12},{4,8},{8,4},{12,0},{16,28},{20,24},{24,20},{28,16},{1,13},{... | collective-permute-start | bytes 393224 | tf_op jit(solution)/shard_map/ppermute | solution.py:341
  25.8 9.4 %collective-permute-start.10 = (bf16[512,128]{1,0:T(8,128)(2,1)S(1)}, bf16[512,128]{1,0:T(8,128)(2,1)S(1)}, u32[]{:S(2)}, u32[]{:S(2)}) collective-permute-start(bf16[512,128]{1,0:T(8,128)(2,1)S(1)} %get-tuple-element.31), channel_id=1, source_target_pairs={{0,8},{4,12},{8,0},{12,4},{16,24},{20,28},{24,16},{28,20},{1,9},{5... | collective-permute-start | bytes 393224 | tf_op jit(solution)/shard_map/ppermute | solution.py:341
  27.4 7.8 %collective-permute-start.11 = (bf16[512,128]{1,0:T(8,128)(2,1)S(1)}, bf16[512,128]{1,0:T(8,128)(2,1)S(1)}, u32[]{:S(2)}, u32[]{:S(2)}) collective-permute-start(bf16[512,128]{1,0:T(8,128)(2,1)S(1)} %get-tuple-element.32), channel_id=1, source_target_pairs={{0,4},{4,0},{8,12},{12,8},{16,20},{20,16},{24,28},{28,24},{1,5},{5... | collective-permute-start | bytes 393224 | tf_op jit(solution)/shard_map/ppermute | solution.py:341
  29.7 8.2 %collective-permute-start.7 = (bf16[128,512]{1,0:T(8,128)(2,1)S(1)}, bf16[128,512]{1,0:T(8,128)(2,1)S(1)}, u32[]{:S(2)}, u32[]{:S(2)}) collective-permute-start(bf16[128,512]{1,0:T(8,128)(2,1)S(1)} %get-tuple-element.23), channel_id=1, source_target_pairs={{0,8},{4,12},{8,0},{12,4},{16,24},{20,28},{24,16},{28,20},{1,9},{5... | collective-permute-start | bytes 393224 | tf_op jit(solution)/shard_map/ppermute | solution.py:341
  29.7 8.1 %collective-permute-start.6 = (bf16[128,512]{1,0:T(8,128)(2,1)S(1)}, bf16[128,512]{1,0:T(8,128)(2,1)S(1)}, u32[]{:S(2)}, u32[]{:S(2)}) collective-permute-start(bf16[128,512]{1,0:T(8,128)(2,1)S(1)} %get-tuple-element.22), channel_id=1, source_target_pairs={{0,4},{4,0},{8,12},{12,8},{16,20},{20,16},{24,28},{28,24},{1,5},{5... | collective-permute-start | bytes 393224 | tf_op jit(solution)/shard_map/ppermute | solution.py:341
  35.9 4.4 %collective-permute-start.12 = (f32[8,128]{1,0:T(8,128)S(1)}, f32[8,128]{1,0:T(8,128)S(1)}, u32[]{:S(2)}, u32[]{:S(2)}) collective-permute-start(f32[8,128]{1,0:T(8,128)S(1)} %get-tuple-element.35.refs_3_), channel_id=1, source_target_pairs={{0,3},{1,2},{2,1},{3,0},{4,7},{5,6},{6,5},{7,4},{8,11},{9,10},{10,... | collective-permute-start | bytes 12296 | tf_op jit(solution)/shard_map/ppermute | solution.py:485
  35.9 4.4 %collective-permute-start.13 = (f32[8,128]{1,0:T(8,128)S(1)}, f32[8,128]{1,0:T(8,128)S(1)}, u32[]{:S(2)}, u32[]{:S(2)}) collective-permute-start(f32[8,128]{1,0:T(8,128)S(1)} %get-tuple-element.35.refs_3_), channel_id=1, source_target_pairs={{0,2},{1,3},{2,0},{3,1},{4,6},{5,7},{6,4},{7,5},{8,10},{9,11},{10,... | collective-permute-start | bytes 12296 | tf_op jit(solution)/shard_map/ppermute | solution.py:485
  37.5 2.9 %collective-permute-start.14 = (f32[8,128]{1,0:T(8,128)S(1)}, f32[8,128]{1,0:T(8,128)S(1)}, u32[]{:S(2)}, u32[]{:S(2)}) collective-permute-start(f32[8,128]{1,0:T(8,128)S(1)} %get-tuple-element.35.refs_3_), channel_id=1, source_target_pairs={{0,1},{1,0},{2,3},{3,2},{4,5},{5,4},{6,7},{7,6},{8,9},{9,8},{10,11... | collective-permute-start | bytes 12296 | tf_op jit(solution)/shard_map/ppermute | solution.py:485

commit v16 on v15

--- a/solution.py
+++ b/solution.py
@@ -137,6 +137,9 @@
 
 def prefix_kernel(group, per, order, carried, *refs):
     pays, refs = refs[:group], refs[group:]
+    ends = []
+    if carried:
+        ends, refs = refs[: group - 1], refs[group - 1 :]
     carry = None
     if carried:
         carry, refs = refs[0], refs[1:]
@@ -144,6 +147,9 @@
     rank = my_rank(group)
     later = lax.axis_index("ctx") >= group
     fill_slots(order, rank, pays, slots)
+    if carried:
+        last = lax.axis_index("ctx") >= lax.axis_size("ctx") - group
+        pl.when(last)(functools.partial(fill_slots, order[1:], rank, ends, slots))
     base = per * HD
     for j in range(per):
         rows = slice(j * HD, (j + 1) * HD)
@@ -158,8 +164,8 @@
         outs[s][...] = prefixes[rank ^ s]
 
 
-def intra_kernel(heads, tri_ref, bias_ref, ld_ref, q_ref, k_ref, v_ref, gate_ref, gain_ref, *outs):
-    intra_ref, qa_ref, gain_out, decay_out = outs
+def intra_kernel(heads, tri_ref, bias_ref, ld_ref, q_ref, k_ref, v_ref, *outs):
+    intra_ref, qa_ref, decay_out = outs
     ld = ld_ref[...]
     tri = tri_ref[...]
     bias = bias_ref[...]
@@ -176,8 +182,13 @@
         decay = jnp.exp((cum[:, h : h + 1] - cum_t[h : h + 1, :]) + bias)
         weights = (scores * decay).astype(BF16)
         intra_ref[:, cols] = jnp.dot(weights, va, preferred_element_type=F32)
+
+
+def gate_kernel(heads, gate_ref, gain_ref, out_ref):
+    for h in range(heads):
+        cols = head_cols(h)
         gate = 1.0 / (1.0 + jnp.exp(-gate_ref[:, cols].astype(F32)))
-        gain_out[:, cols] = gate * gain_ref[:, cols]
+        out_ref[:, cols] = gate * gain_ref[:, cols]
 
 
 def inter_kernel(group, heads, order, decay_ref, qa_ref, intra_ref, *rest):
@@ -367,22 +378,23 @@
             exps=2 * tokens * width // group,
         )[0]
 
-    pays = {s: swap(states(s), s) for s in to[1:]}
-    pays[0] = states(0)
-    pays = [pays[s] for s in to]
-
-    intra, qa, gain, decay = call(
-        functools.partial(intra_kernel, heads),
-        "intra_block",
-        [
-            shape((tokens, width), F32),
-            shape((tokens, width), BF16),
-            shape((tokens, width), F32),
-            shape((tokens, heads), F32),
-        ],
-        (tri, bias, log_decay, q_lin, k_lin, v_lin, gate, norm_gain.reshape(1, width)),
-        flops=4 * cube,
-        exps=4 * tokens * width,
+    split = n - group if groups > 1 else n
+
+    def swap_among(x, s, first, last):
+        return lax.ppermute(x, "ctx", [(c, c ^ s) for c in range(first, last)])
+
+    added = {s: states(s) for s in to[1:]}
+    mine = states(0)
+    pays = [mine] + [swap_among(added[s], s, 0, split) for s in to[1:]]
+    ends = [swap_among(added[s], s, split, n) for s in to[1:]] if groups > 1 else []
+
+    (gain,) = call(
+        functools.partial(gate_kernel, heads),
+        "gate_gain",
+        [shape((tokens, width), F32)],
+        (gate, norm_gain.reshape(1, width)),
+        flops=1 << 30,
+        exps=tokens * width,
         after=far,
     )
 
@@ -396,7 +408,7 @@
             pays,
             [slots],
             flops=2 * per * HD * HD * group,
-            after=(intra,),
+            after=(gain,),
         )
         before = ahead(total, 1)
         shift = 1
@@ -414,13 +426,23 @@
             before = jnp.concatenate([state, high, pad, both - high, pad], axis=0).astype(BF16)
             shift *= 2
         carry = (before,)
+    intra, qa, decay = call(
+        functools.partial(intra_kernel, heads),
+        "intra_block",
+        [shape((tokens, width), F32), shape((tokens, width), BF16), shape((tokens, heads), F32)],
+        (tri, bias, log_decay, q_lin, k_lin, v_lin),
+        flops=4 * cube,
+        exps=4 * tokens * width,
+        after=(total,) if groups > 1 else (),
+    )
     prefixes = call(
         functools.partial(prefix_kernel, group, per, to, bool(carry)),
         "prefix_states",
         [shape((per * HD, HD), BF16)] * group,
-        (*pays, *carry),
+        (*pays, *ends, *carry),
         [slots, pltpu.VMEM((group, per * HD, HD), BF16)],
         flops=1 << 33,
+        after=(intra,),
     )
     prefixes = [swap(prefixes[s], s) if s else prefixes[s] for s in back]
 
@@ -429,7 +451,7 @@
         "stack_keys_values",
         [shape((groups * tokens, kv.shape[1]), BF16)],
         (kv, *far),
-        after=(total,) if groups > 1 else (intra,),
+        after=(total,) if groups > 1 else (),
         flops=1 << 32,
     )
     side, near = swap(own, 2), swap(own, 1)

time: 41.7 us -> 50.1 us (1.20)
  starting transfers between devices: 17.7 us -> 25.8 us
  waiting for transfers between devices: 9 us -> 8.29 us
    ppermute x0 -> x6, starting transfers between devices: none -> 11.4 us  [swap_among(): return lax.ppermute(x, 'ctx', [(c, c ^ s) for c in range(first, last)])]
    ppermute x10 -> x7, starting transfers between devices: 11 us -> 8.42 us  [swap(): return lax.ppermute(x, 'ctx', [(c, c ^ s) for c in range(n)])]
    ppermute x0 -> x6, waiting for transfers between devices: none -> 2.53 us  [swap_among(): return lax.ppermute(x, 'ctx', [(c, c ^ s) for c in range(first, last)])]
    ppermute x10 -> x7, waiting for transfers between devices: 4.67 us -> 2.77 us  [swap(): return lax.ppermute(x, 'ctx', [(c, c ^ s) for c in range(n)])]
    ppermute x2, waiting for transfers between devices: 4.33 us -> 2.99 us  [ahead(): return lax.ppermute(x, 'ctx', [(c, (c + d * group) % n) for c in range(n)])]
    ppermute x2, starting transfers between devices: 4.77 us -> 4.17 us  [ahead(): return lax.ppermute(x, 'ctx', [(c, (c + d * group) % n) for c in range(n)])]
    pallas_call x15 -> x16, Pallas kernels: 12.4 us -> 12.7 us  [call(): pl.pallas_call(run, name=name, out_shape=list(outs), in_specs=specs, scra...]
  transfers between devices with their start and end apart: 15 -> 18, of which waited for: 6 -> 4; matrix products, arithmetic and copies ran while one was open for 0% -> 0% of each run, Pallas kernels for 27% -> 23%
where the time goes in v16:
time: 50.1 us; the launch traced here: 49.8 us
  starting transfers between devices  25.8 us (51%)
  Pallas kernels  12.7 us (25%)
  waiting for transfers between devices  8.29 us (17%)
  between operations  1.77 us (4%)
  local copies, waits for them, and re-layouts  1.25 us (2%)
    pallas_call x16, Pallas kernels, call(): pl.pallas_call(run, name=name, out_shape=list(outs), in_specs=specs, scra...  12.7 us
    ppermute x6, starting transfers between devices, swap_among(): return lax.ppermute(x, 'ctx', [(c, c ^ s) for c in range(first, last)])  11.4 us
    ppermute x7, starting transfers between devices, swap(): return lax.ppermute(x, 'ctx', [(c, c ^ s) for c in range(n)])  8.42 us
    ppermute x2, starting transfers between devices, ahead(): return lax.ppermute(x, 'ctx', [(c, (c + d * group) % n) for c in range(n)])  4.17 us
    ppermute x2, waiting for transfers between devices, ahead(): return lax.ppermute(x, 'ctx', [(c, (c + d * group) % n) for c in range(n)])  2.99 us
    ppermute x7, waiting for transfers between devices, swap(): return lax.ppermute(x, 'ctx', [(c, c ^ s) for c in range(n)])  2.77 us
    ppermute x6, waiting for transfers between devices, swap_among(): return lax.ppermute(x, 'ctx', [(c, c ^ s) for c in range(first, last)])  2.53 us
    ppermute x3, starting transfers between devices, body(): parts = [squares] + [lax.ppermute(squares, 'head', turn) for turn in turns]  1.89 us
  transfers between devices with their start and end apart: 18, of which 4 were waited for; matrix products, arithmetic and copies ran while one was open for 0% of the time, Pallas kernels for 23%

profile of v16, /device:TPU:0, one launch (start us, length us, event | category | flops | bytes accessed | tf_op | source)
XLA Modules:
  0.0 49.8 jit_solution(17539531479950008969)
XLA Ops:
  0.7 0.8 %copy-done.4 = bf16[128,256]{1,0:T(8,128)(2,1)S(1)} copy-done((bf16[128,256]{1,0:T(8,128)(2,1)S(1)}, bf16[128,256]{1,0:T(8,128)(2,1)}, u32[]{:S(2)}) %copy-start.4) | copy-done | bytes 65560
  1.5 4.1 %collective-permute-start = (bf16[128,512]{1,0:T(8,128)(2,1)S(1)}, bf16[128,512]{1,0:T(8,128)(2,1)S(1)}, u32[]{:S(2)}, u32[]{:S(2)}) collective-permute-start(bf16[128,512]{1,0:T(8,128)(2,1)S(1)} %keys_beside_values.1.refs_0_), channel_id=1, source_target_pairs={{0,16},{4,20},{8,24},{12,28},{16,0},{20,4},{24,8},{28,12},{1,17},{... | collective-permute-start | bytes 393224 | tf_op jit(solution)/shard_map/ppermute | solution.py:355
  6.3 3.6 %collective-permute-start.1 = (bf16[528,128]{1,0:T(8,128)(2,1)S(1)}, bf16[528,128]{1,0:T(8,128)(2,1)S(1)}, u32[]{:S(2)}, u32[]{:S(2)}) collective-permute-start(bf16[528,128]{1,0:T(8,128)(2,1)S(1)} %states_2.1), channel_id=1, source_target_pairs={{0,8},{4,12},{8,0},{12,4},{1,9},{5,13},{9,1},{13,5},{2,10},{6,14},... | collective-permute-start | bytes 405512 | tf_op jit(solution)/shard_map/ppermute | solution.py:384
  9.9 0.6 %states_1.1 = bf16[528,128]{1,0:T(8,128)(2,1)S(1)} custom-call(f32[128,128]{1,0:T(8,128)S(1)} %get-tuple-element.18.refs_2_.refs_0_, f32[16,128]{1,0:T(8,128)S(1)} %copy-done.3, bf16[128,2048]{1,0:T(8,128)(2,1)S(1)} %copy-done, bf16[128,2048]{1,0:T(8,128)(2,1)S(1)} %copy-done.1), custom_call_target="tpu_custom_call" | custom-call | flops 33554432 | bytes 1257472 | tf_op jit(solution)/shard_map/states_1/pallas_call | solution.py:326
  10.5 3.4 %collective-permute-start.2 = (bf16[528,128]{1,0:T(8,128)(2,1)S(1)}, bf16[528,128]{1,0:T(8,128)(2,1)S(1)}, u32[]{:S(2)}, u32[]{:S(2)}) collective-permute-start(bf16[528,128]{1,0:T(8,128)(2,1)S(1)} %states_1.1), channel_id=1, source_target_pairs={{0,4},{4,0},{8,12},{12,8},{1,5},{5,1},{9,13},{13,9},{2,6},{6,2},{1... | collective-permute-start | bytes 405512 | tf_op jit(solution)/shard_map/ppermute | solution.py:384
  13.9 0.6 %states_3.1 = bf16[528,128]{1,0:T(8,128)(2,1)S(1)} custom-call(f32[128,128]{1,0:T(8,128)S(1)} %get-tuple-element.18.refs_2_.refs_0_, f32[16,128]{1,0:T(8,128)S(1)} %copy-done.3, bf16[128,2048]{1,0:T(8,128)(2,1)S(1)} %copy-done, bf16[128,2048]{1,0:T(8,128)(2,1)S(1)} %copy-done.1), custom_call_target="tpu_custom_call" | custom-call | flops 33554432 | bytes 1257472 | tf_op jit(solution)/shard_map/states_3/pallas_call | solution.py:326
  14.6 2.3 %collective-permute-start.3 = (bf16[528,128]{1,0:T(8,128)(2,1)S(1)}, bf16[528,128]{1,0:T(8,128)(2,1)S(1)}, u32[]{:S(2)}, u32[]{:S(2)}) collective-permute-start(bf16[528,128]{1,0:T(8,128)(2,1)S(1)} %states_3.1), channel_id=1, source_target_pairs={{0,12},{4,8},{8,4},{12,0},{1,13},{5,9},{9,5},{13,1},{2,14},{6,10},... | collective-permute-start | bytes 405512 | tf_op jit(solution)/shard_map/ppermute | solution.py:384
  16.9 0.7 %collective-permute-start.8 = (bf16[528,128]{1,0:T(8,128)(2,1)S(1)}, bf16[528,128]{1,0:T(8,128)(2,1)S(1)}, u32[]{:S(2)}, u32[]{:S(2)}) collective-permute-start(bf16[528,128]{1,0:T(8,128)(2,1)S(1)} %states_2.1), channel_id=1, source_target_pairs={{16,24},{20,28},{24,16},{28,20},{17,25},{21,29},{25,17},{29,21},{1... | collective-permute-start | bytes 405512 | tf_op jit(solution)/shard_map/ppermute | solution.py:384
  17.5 0.6 %states_0.1.refs_0_ = bf16[528,128]{1,0:T(8,128)(2,1)S(1)} custom-call(f32[128,128]{1,0:T(8,128)S(1)} %get-tuple-element.18.refs_2_.refs_0_, f32[16,128]{1,0:T(8,128)S(1)} %copy-done.3, bf16[128,2048]{1,0:T(8,128)(2,1)S(1)} %copy-done, bf16[128,2048]{1,0:T(8,128)(2,1)S(1)} %copy-done.1), custom_call_target="tpu_custom_call" | custom-call | flops 33554432 | bytes 1257472 | tf_op jit(solution)/shard_map/states_0/pallas_call | solution.py:326
  18.2 0.7 %collective-permute-start.9 = (bf16[528,128]{1,0:T(8,128)(2,1)S(1)}, bf16[528,128]{1,0:T(8,128)(2,1)S(1)}, u32[]{:S(2)}, u32[]{:S(2)}) collective-permute-start(bf16[528,128]{1,0:T(8,128)(2,1)S(1)} %states_1.1), channel_id=1, source_target_pairs={{16,20},{20,16},{24,28},{28,24},{17,21},{21,17},{25,29},{29,25},{1... | collective-permute-start | bytes 405512 | tf_op jit(solution)/shard_map/ppermute | solution.py:384
  19.2 0.7 %collective-permute-start.10 = (bf16[528,128]{1,0:T(8,128)(2,1)S(1)}, bf16[528,128]{1,0:T(8,128)(2,1)S(1)}, u32[]{:S(2)}, u32[]{:S(2)}) collective-permute-start(bf16[528,128]{1,0:T(8,128)(2,1)S(1)} %states_3.1), channel_id=1, source_target_pairs={{16,28},{20,24},{24,20},{28,16},{17,29},{21,25},{25,21},{29,17},{1... | collective-permute-start | bytes 405512 | tf_op jit(solution)/shard_map/ppermute | solution.py:384
  19.8 2.5 %collective-permute-done.3.refs_3_ = bf16[528,128]{1,0:T(8,128)(2,1)S(1)} collective-permute-done((bf16[528,128]{1,0:T(8,128)(2,1)S(1)}, bf16[528,128]{1,0:T(8,128)(2,1)S(1)}, u32[]{:S(2)}, u32[]{:S(2)}) %collective-permute-start.3) | collective-permute-done | bytes 135200 | tf_op jit(solution)/shard_map/ppermute | solution.py:384
  23.6 2.8 %intra_block.1 = (f32[128,2048]{1,0:T(8,128)S(1)}, bf16[128,2048]{1,0:T(8,128)(2,1)S(1)}, f32[128,16]{1,0:T(8,128)S(1)}) custom-call(f32[128,128]{1,0:T(8,128)S(1)} %get-tuple-element.18.refs_2_.refs_0_, f32[128,128]{1,0:T(8,128)S(1)} %get-tuple-element.24.refs_1_, f32[16,128]{1,0:T(8,128)S(1)} %copy-done.3, bf16[128,2048]{1,0:T(8,128)(2,1)S(1)} %copy-done.7, ...), custom_call_target="tpu_custom_call" | custom-call | flops 134217728 | bytes 3293184 | tf_op jit(solution)/shard_map/intra_block/pallas_call | solution.py:326
  26.9 3.0 %collective-permute-done.11.refs_7_ = bf16[528,128]{1,0:T(8,128)(2,1)S(1)} collective-permute-done((bf16[528,128]{1,0:T(8,128)(2,1)S(1)}, bf16[528,128]{1,0:T(8,128)(2,1)S(1)}, u32[]{:S(2)}, u32[]{:S(2)}) %collective-permute-start.11) | collective-permute-done | bytes 135200 | tf_op jit(solution)/shard_map/ppermute | solution.py:355
  30.9 1.5 %collective-permute-start.13 = (bf16[512,128]{1,0:T(8,128)(2,1)S(1)}, bf16[512,128]{1,0:T(8,128)(2,1)S(1)}, u32[]{:S(2)}, u32[]{:S(2)}) collective-permute-start(bf16[512,128]{1,0:T(8,128)(2,1)S(1)} %get-tuple-element.30), channel_id=1, source_target_pairs={{0,8},{4,12},{8,0},{12,4},{16,24},{20,28},{24,16},{28,20},{1,9},{5... | collective-permute-start | bytes 393224 | tf_op jit(solution)/shard_map/ppermute | solution.py:352
  32.3 1.5 %collective-permute-start.14 = (bf16[512,128]{1,0:T(8,128)(2,1)S(1)}, bf16[512,128]{1,0:T(8,128)(2,1)S(1)}, u32[]{:S(2)}, u32[]{:S(2)}) collective-permute-start(bf16[512,128]{1,0:T(8,128)(2,1)S(1)} %get-tuple-element.31), channel_id=1, source_target_pairs={{0,4},{4,0},{8,12},{12,8},{16,20},{20,16},{24,28},{28,24},{1,5},{5... | collective-permute-start | bytes 393224 | tf_op jit(solution)/shard_map/ppermute | solution.py:352
  34.0 2.6 %collective-permute-done.5.refs_1_.refs_4_ = bf16[256,512]{1,0:T(8,128)(2,1)S(1)} collective-permute-done((bf16[256,512]{1,0:T(8,128)(2,1)S(1)}, bf16[256,512]{1,0:T(8,128)(2,1)S(1)}, u32[]{:S(2)}, u32[]{:S(2)}) %collective-permute-start.5) | collective-permute-done | bytes 262176 | tf_op jit(solution)/shard_map/ppermute | solution.py:352
  36.6 2.6 %collective-permute-start.7 = (bf16[128,512]{1,0:T(8,128)(2,1)S(1)}, bf16[128,512]{1,0:T(8,128)(2,1)S(1)}, u32[]{:S(2)}, u32[]{:S(2)}) collective-permute-start(bf16[128,512]{1,0:T(8,128)(2,1)S(1)} %get-tuple-element.20), channel_id=1, source_target_pairs={{0,8},{4,12},{8,0},{12,4},{16,24},{20,28},{24,16},{28,20},{1,9},{5... | collective-permute-start | bytes 393224 | tf_op jit(solution)/shard_map/ppermute | solution.py:352
  39.3 1.1 %collective-permute-start.6 = (bf16[128,512]{1,0:T(8,128)(2,1)S(1)}, bf16[128,512]{1,0:T(8,128)(2,1)S(1)}, u32[]{:S(2)}, u32[]{:S(2)}) collective-permute-start(bf16[128,512]{1,0:T(8,128)(2,1)S(1)} %get-tuple-element.19), channel_id=1, source_target_pairs={{0,4},{4,0},{8,12},{12,8},{16,20},{20,16},{24,28},{28,24},{1,5},{5... | collective-permute-start | bytes 393224 | tf_op jit(solution)/shard_map/ppermute | solution.py:352
  41.1 2.4 %softmax_first.1 = (f32[128,4096]{1,0:T(8,128)S(1)}, f32[128,8]{1,0:T(8,128)S(1)}, f32[128,8]{1,0:T(8,128)S(1)}) custom-call(s32[1]{0:T(128)S(6)} %copy.12.refs_0_, bf16[128,2048]{1,0:T(8,128)(2,1)S(1)} %copy-done.2, bf16[256,512]{1,0:T(8,128)(2,1)S(1)} %stack_keys_values.1.refs_2_, bf16[256,512]{1,0:T(8,128)(2,1)S(1)} %collective-permute-done.4.refs_0_.refs_3_, ...), custom_call_target="tpu_custom_call" | custom-call | flops 805306368 | bytes 3416068 | tf_op jit(solution)/shard_map/softmax_first/pallas_call | solution.py:326
  43.5 0.7 %inter_block.1 = (f32[128,2048]{1,0:T(8,128)S(1)}, f32[8,128]{1,0:T(8,128)S(1)}) custom-call(f32[128,16]{1,0:T(8,128)S(1)} %get-tuple-element.25.refs_0_, bf16[128,2048]{1,0:T(8,128)(2,1)S(1)} %get-tuple-element.26.refs_1_, f32[128,2048]{1,0:T(8,128)S(1)} %get-tuple-element.27.refs_8_.refs_2_, bf16[512,128]{1,0:T(8,128)(2,1)S(1)} %get-tuple-element.28.refs_3_, ...), custom_call_target="tpu_custom_call" | custom-call | flops 67108864 | bytes 3158016 | tf_op jit(solution)/shard_map/inter_block/pallas_call | solution.py:326
  44.2 1.6 %collective-permute-start.16 = (f32[8,128]{1,0:T(8,128)S(1)}, f32[8,128]{1,0:T(8,128)S(1)}, u32[]{:S(2)}, u32[]{:S(2)}) collective-permute-start(f32[8,128]{1,0:T(8,128)S(1)} %get-tuple-element.33.refs_3_), channel_id=1, source_target_pairs={{0,2},{1,3},{2,0},{3,1},{4,6},{5,7},{6,4},{7,5},{8,10},{9,11},{10,... | collective-permute-start | bytes 12296 | tf_op jit(solution)/shard_map/ppermute | solution.py:507
  46.1 2.5 %softmax_last.1.refs_0_ = bf16[128,2048]{1,0:T(8,128)(2,1)S(1)} custom-call(s32[1]{0:T(128)S(6)} %copy.12.refs_0_, bf16[128,2048]{1,0:T(8,128)(2,1)S(1)} %copy-done.2, bf16[256,512]{1,0:T(8,128)(2,1)S(1)} %pad_maximum_fusion.refs_2_, f32[128,4096]{1,0:T(8,128)S(1)} %get-tuple-element.21.refs_3_, f32[128,8]{1,0:T(8,128)S(1)} %get-tuple-element.22.refs_4_.refs_7_, ...), custom_call_target="tpu_custom_call" | custom-call | flops 268435456 | bytes 3416068 | tf_op jit(solution)/shard_map/softmax_last/pallas_call | solution.py:326
  48.6 1.1 %results.1 = (bf16[128,2048]{1,0:T(8,128)(2,1)}, bf16[128,2048]{1,0:T(8,128)(2,1)}) custom-call(bf16[128,2048]{1,0:T(8,128)(2,1)S(1)} %softmax_last.1.refs_0_, f32[128,2048]{1,0:T(8,128)S(1)} %get-tuple-element.32.refs_1_, f32[128,2048]{1,0:T(8,128)S(1)} %gate_gain.1.refs_4_.refs_2_, f32[8,128]{1,0:T(8,128)S(1)} %get-tuple-element.33.refs_3_, ...), custom_call_target="tpu_custom_call" | custom-call | flops 1048576 | bytes 3686400 | tf_op jit(solution)/shard_map/results/pallas_call | solution.py:326
  (47 shorter events, 4.2 us)
Async XLA Ops:
  0.7 5.0 %copy-start.3 = (f32[16,128]{1,0:T(8,128)S(1)}, f32[16,128]{1,0:T(8,128)}, u32[]{:S(2)}) copy-start(f32[16,128]{1,0:T(8,128)} %refs_2_.9) | copy-start | bytes 24580
  0.7 5.0 %copy-start = (bf16[128,2048]{1,0:T(8,128)(2,1)S(1)}, bf16[128,2048]{1,0:T(8,128)(2,1)}, u32[]{:S(2)}) copy-start(bf16[128,2048]{1,0:T(8,128)(2,1)} %refs_4_.1) | copy-start | bytes 1572868
  0.7 5.0 %copy-start.1 = (bf16[128,2048]{1,0:T(8,128)(2,1)S(1)}, bf16[128,2048]{1,0:T(8,128)(2,1)}, u32[]{:S(2)}) copy-start(bf16[128,2048]{1,0:T(8,128)(2,1)} %refs_5_.1) | copy-start | bytes 1572868
  1.5 16.6 %collective-permute-start = (bf16[128,512]{1,0:T(8,128)(2,1)S(1)}, bf16[128,512]{1,0:T(8,128)(2,1)S(1)}, u32[]{:S(2)}, u32[]{:S(2)}) collective-permute-start(bf16[128,512]{1,0:T(8,128)(2,1)S(1)} %keys_beside_values.1.refs_0_), channel_id=1, source_target_pairs={{0,16},{4,20},{8,24},{12,28},{16,0},{20,4},{24,8},{28,12},{1,17},{... | collective-permute-start | bytes 393224 | tf_op jit(solution)/shard_map/ppermute | solution.py:355
  6.2 12.6 %copy-start.6 = (bf16[128,2048]{1,0:T(8,128)(2,1)S(1)}, bf16[128,2048]{1,0:T(8,128)(2,1)}, u32[]{:S(2)}) copy-start(bf16[128,2048]{1,0:T(8,128)(2,1)} %refs_0_.5) | copy-start | bytes 1572868
  6.2 12.6 %copy-start.8 = (f32[2048]{0:T(1024)S(1)}, f32[2048]{0:T(1024)}, u32[]{:S(2)}) copy-start(f32[2048]{0:T(1024)} %param.15) | copy-start | bytes 24580
  6.3 12.9 %collective-permute-start.1 = (bf16[528,128]{1,0:T(8,128)(2,1)S(1)}, bf16[528,128]{1,0:T(8,128)(2,1)S(1)}, u32[]{:S(2)}, u32[]{:S(2)}) collective-permute-start(bf16[528,128]{1,0:T(8,128)(2,1)S(1)} %states_2.1), channel_id=1, source_target_pairs={{0,8},{4,12},{8,0},{12,4},{1,9},{5,13},{9,1},{13,5},{2,10},{6,14},... | collective-permute-start | bytes 405512 | tf_op jit(solution)/shard_map/ppermute | solution.py:384
  10.5 9.3 %collective-permute-start.2 = (bf16[528,128]{1,0:T(8,128)(2,1)S(1)}, bf16[528,128]{1,0:T(8,128)(2,1)S(1)}, u32[]{:S(2)}, u32[]{:S(2)}) collective-permute-start(bf16[528,128]{1,0:T(8,128)(2,1)S(1)} %states_1.1), channel_id=1, source_target_pairs={{0,4},{4,0},{8,12},{12,8},{1,5},{5,1},{9,13},{13,9},{2,6},{6,2},{1... | collective-permute-start | bytes 405512 | tf_op jit(solution)/shard_map/ppermute | solution.py:384
  14.6 7.8 %collective-permute-start.3 = (bf16[528,128]{1,0:T(8,128)(2,1)S(1)}, bf16[528,128]{1,0:T(8,128)(2,1)S(1)}, u32[]{:S(2)}, u32[]{:S(2)}) collective-permute-start(bf16[528,128]{1,0:T(8,128)(2,1)S(1)} %states_3.1), channel_id=1, source_target_pairs={{0,12},{4,8},{8,4},{12,0},{1,13},{5,9},{9,5},{13,1},{2,14},{6,10},... | collective-permute-start | bytes 405512 | tf_op jit(solution)/shard_map/ppermute | solution.py:384
  16.9 9.5 %collective-permute-start.8 = (bf16[528,128]{1,0:T(8,128)(2,1)S(1)}, bf16[528,128]{1,0:T(8,128)(2,1)S(1)}, u32[]{:S(2)}, u32[]{:S(2)}) collective-permute-start(bf16[528,128]{1,0:T(8,128)(2,1)S(1)} %states_2.1), channel_id=1, source_target_pairs={{16,24},{20,28},{24,16},{28,20},{17,25},{21,29},{25,17},{29,21},{1... | collective-permute-start | bytes 405512 | tf_op jit(solution)/shard_map/ppermute | solution.py:384
  18.2 8.8 %collective-permute-start.9 = (bf16[528,128]{1,0:T(8,128)(2,1)S(1)}, bf16[528,128]{1,0:T(8,128)(2,1)S(1)}, u32[]{:S(2)}, u32[]{:S(2)}) collective-permute-start(bf16[528,128]{1,0:T(8,128)(2,1)S(1)} %states_1.1), channel_id=1, source_target_pairs={{16,20},{20,16},{24,28},{28,24},{17,21},{21,17},{25,29},{29,25},{1... | collective-permute-start | bytes 405512 | tf_op jit(solution)/shard_map/ppermute | solution.py:384
  19.2 7.8 %collective-permute-start.10 = (bf16[528,128]{1,0:T(8,128)(2,1)S(1)}, bf16[528,128]{1,0:T(8,128)(2,1)S(1)}, u32[]{:S(2)}, u32[]{:S(2)}) collective-permute-start(bf16[528,128]{1,0:T(8,128)(2,1)S(1)} %states_3.1), channel_id=1, source_target_pairs={{16,28},{20,24},{24,20},{28,16},{17,29},{21,25},{25,21},{29,17},{1... | collective-permute-start | bytes 405512 | tf_op jit(solution)/shard_map/ppermute | solution.py:384
  22.5 7.4 %collective-permute-start.11 = (bf16[528,128]{1,0:T(8,128)(2,1)S(1)}, bf16[528,128]{1,0:T(8,128)(2,1)S(1)}, u32[]{:S(2)}, u32[]{:S(2)}) collective-permute-start(bf16[528,128]{1,0:T(8,128)(2,1)S(1)} %group_state.1.refs_2_.refs_6_), channel_id=1, source_target_pairs={{0,16},{4,20},{8,24},{12,28},{16,0},{20,4},{24,8},{28,12},{1,17},{... | collective-permute-start | bytes 405512 | tf_op jit(solution)/shard_map/ppermute | solution.py:355
  22.6 11.4 %collective-permute-start.4 = (bf16[256,512]{1,0:T(8,128)(2,1)S(1)}, bf16[256,512]{1,0:T(8,128)(2,1)S(1)}, u32[]{:S(2)}, u32[]{:S(2)}) collective-permute-start(bf16[256,512]{1,0:T(8,128)(2,1)S(1)} %stack_keys_values.1.refs_2_), channel_id=1, source_target_pairs={{0,8},{4,12},{8,0},{12,4},{16,24},{20,28},{24,16},{28,20},{1,9},{5... | collective-permute-start | bytes 786440 | tf_op jit(solution)/shard_map/ppermute | solution.py:352
  26.4 10.3 %collective-permute-start.5 = (bf16[256,512]{1,0:T(8,128)(2,1)S(1)}, bf16[256,512]{1,0:T(8,128)(2,1)S(1)}, u32[]{:S(2)}, u32[]{:S(2)}) collective-permute-start(bf16[256,512]{1,0:T(8,128)(2,1)S(1)} %stack_keys_values.1.refs_2_), channel_id=1, source_target_pairs={{0,4},{4,0},{8,12},{12,8},{16,20},{20,16},{24,28},{28,24},{1,5},{5... | collective-permute-start | bytes 786440 | tf_op jit(solution)/shard_map/ppermute | solution.py:352
  29.9 11.2 %copy-start.2 = (bf16[128,2048]{1,0:T(8,128)(2,1)S(1)}, bf16[128,2048]{1,0:T(8,128)(2,1)}, u32[]{:S(2)}) copy-start(bf16[128,2048]{1,0:T(8,128)(2,1)} %refs_1_.13) | copy-start | bytes 1572868
  30.3 13.2 %collective-permute-start.12 = (bf16[512,128]{1,0:T(8,128)(2,1)S(1)}, bf16[512,128]{1,0:T(8,128)(2,1)S(1)}, u32[]{:S(2)}, u32[]{:S(2)}) collective-permute-start(bf16[512,128]{1,0:T(8,128)(2,1)S(1)} %get-tuple-element.29), channel_id=1, source_target_pairs={{0,12},{4,8},{8,4},{12,0},{16,28},{20,24},{24,20},{28,16},{1,13},{... | collective-permute-start | bytes 393224 | tf_op jit(solution)/shard_map/ppermute | solution.py:352
  30.9 12.6 %collective-permute-start.13 = (bf16[512,128]{1,0:T(8,128)(2,1)S(1)}, bf16[512,128]{1,0:T(8,128)(2,1)S(1)}, u32[]{:S(2)}, u32[]{:S(2)}) collective-permute-start(bf16[512,128]{1,0:T(8,128)(2,1)S(1)} %get-tuple-element.30), channel_id=1, source_target_pairs={{0,8},{4,12},{8,0},{12,4},{16,24},{20,28},{24,16},{28,20},{1,9},{5... | collective-permute-start | bytes 393224 | tf_op jit(solution)/shard_map/ppermute | solution.py:352
  32.3 11.1 %collective-permute-start.14 = (bf16[512,128]{1,0:T(8,128)(2,1)S(1)}, bf16[512,128]{1,0:T(8,128)(2,1)S(1)}, u32[]{:S(2)}, u32[]{:S(2)}) collective-permute-start(bf16[512,128]{1,0:T(8,128)(2,1)S(1)} %get-tuple-element.31), channel_id=1, source_target_pairs={{0,4},{4,0},{8,12},{12,8},{16,20},{20,16},{24,28},{28,24},{1,5},{5... | collective-permute-start | bytes 393224 | tf_op jit(solution)/shard_map/ppermute | solution.py:352
  36.6 9.4 %collective-permute-start.7 = (bf16[128,512]{1,0:T(8,128)(2,1)S(1)}, bf16[128,512]{1,0:T(8,128)(2,1)S(1)}, u32[]{:S(2)}, u32[]{:S(2)}) collective-permute-start(bf16[128,512]{1,0:T(8,128)(2,1)S(1)} %get-tuple-element.20), channel_id=1, source_target_pairs={{0,8},{4,12},{8,0},{12,4},{16,24},{20,28},{24,16},{28,20},{1,9},{5... | collective-permute-start | bytes 393224 | tf_op jit(solution)/shard_map/ppermute | solution.py:352
  39.3 6.8 %collective-permute-start.6 = (bf16[128,512]{1,0:T(8,128)(2,1)S(1)}, bf16[128,512]{1,0:T(8,128)(2,1)S(1)}, u32[]{:S(2)}, u32[]{:S(2)}) collective-permute-start(bf16[128,512]{1,0:T(8,128)(2,1)S(1)} %get-tuple-element.19), channel_id=1, source_target_pairs={{0,4},{4,0},{8,12},{12,8},{16,20},{20,16},{24,28},{28,24},{1,5},{5... | collective-permute-start | bytes 393224 | tf_op jit(solution)/shard_map/ppermute | solution.py:352
  44.2 4.4 %collective-permute-start.15 = (f32[8,128]{1,0:T(8,128)S(1)}, f32[8,128]{1,0:T(8,128)S(1)}, u32[]{:S(2)}, u32[]{:S(2)}) collective-permute-start(f32[8,128]{1,0:T(8,128)S(1)} %get-tuple-element.33.refs_3_), channel_id=1, source_target_pairs={{0,3},{1,2},{2,1},{3,0},{4,7},{5,6},{6,5},{7,4},{8,11},{9,10},{10,... | collective-permute-start | bytes 12296 | tf_op jit(solution)/shard_map/ppermute | solution.py:507
  44.2 4.4 %collective-permute-start.16 = (f32[8,128]{1,0:T(8,128)S(1)}, f32[8,128]{1,0:T(8,128)S(1)}, u32[]{:S(2)}, u32[]{:S(2)}) collective-permute-start(f32[8,128]{1,0:T(8,128)S(1)} %get-tuple-element.33.refs_3_), channel_id=1, source_target_pairs={{0,2},{1,3},{2,0},{3,1},{4,6},{5,7},{6,4},{7,5},{8,10},{9,11},{10,... | collective-permute-start | bytes 12296 | tf_op jit(solution)/shard_map/ppermute | solution.py:507
  45.7 2.9 %collective-permute-start.17 = (f32[8,128]{1,0:T(8,128)S(1)}, f32[8,128]{1,0:T(8,128)S(1)}, u32[]{:S(2)}, u32[]{:S(2)}) collective-permute-start(f32[8,128]{1,0:T(8,128)S(1)} %get-tuple-element.33.refs_3_), channel_id=1, source_target_pairs={{0,1},{1,0},{2,3},{3,2},{4,5},{5,4},{6,7},{7,6},{8,9},{9,8},{10,11... | collective-permute-start | bytes 12296 | tf_op jit(solution)/shard_map/ppermute | solution.py:507
  (3 other events, 2.7 us)

commit v17 on v13

--- a/solution.py
+++ b/solution.py
@@ -383,6 +383,7 @@
         (tri, bias, log_decay, q_lin, k_lin, v_lin, gate, norm_gain.reshape(1, width)),
         flops=4 * cube,
         exps=4 * tokens * width,
+        after=far,
     )
 
     slots = pltpu.VMEM((group, rows, HD), BF16)

time: 41.8 us -> 41.6 us (level)
  waiting for transfers between devices: 5.15 us -> 8.62 us
  starting transfers between devices: 21.3 us -> 18 us
    ppermute x10, waiting for transfers between devices: 1.08 us -> 4.03 us  [swap(): return lax.ppermute(x, 'ctx', [(c, c ^ s) for c in range(n)])]
    ppermute x10, starting transfers between devices: 13.7 us -> 11.3 us  [swap(): return lax.ppermute(x, 'ctx', [(c, c ^ s) for c in range(n)])]
    ppermute x2, starting transfers between devices: 5.69 us -> 4.79 us  [ahead(): return lax.ppermute(x, 'ctx', [(c, (c + d * group) % n) for c in range(n)])]
    ppermute x2, waiting for transfers between devices: 3.97 us -> 4.58 us  [ahead(): return lax.ppermute(x, 'ctx', [(c, (c + d * group) % n) for c in range(n)])]
  transfers between devices with their start and end apart: 15 -> 15, of which waited for: 6 -> 6; matrix products, arithmetic and copies ran while one was open for 0% -> 0% of each run, Pallas kernels for 26% -> 27%
where the time goes in v17:
time: 41.6 us; the launch traced here: 41.5 us
  starting transfers between devices  18 us (43%)
  Pallas kernels  12.4 us (30%)
  waiting for transfers between devices  8.62 us (21%)
  between operations  1.65 us (4%)
  local copies, waits for them, and re-layouts  0.84 us (2%)
    pallas_call x15, Pallas kernels, call(): pl.pallas_call(run, name=name, out_shape=list(outs), in_specs=specs, scra...  12.4 us
    ppermute x10, starting transfers between devices, swap(): return lax.ppermute(x, 'ctx', [(c, c ^ s) for c in range(n)])  11.3 us
    ppermute x2, starting transfers between devices, ahead(): return lax.ppermute(x, 'ctx', [(c, (c + d * group) % n) for c in range(n)])  4.79 us
    ppermute x2, waiting for transfers between devices, ahead(): return lax.ppermute(x, 'ctx', [(c, (c + d * group) % n) for c in range(n)])  4.58 us
    ppermute x10, waiting for transfers between devices, swap(): return lax.ppermute(x, 'ctx', [(c, c ^ s) for c in range(n)])  4.03 us
    ppermute x3, starting transfers between devices, body(): parts = [squares] + [lax.ppermute(squares, 'head', turn) for turn in turns]  1.89 us
    unnamed x18, local copies, waits for them, and re-layouts  0.84 us
  transfers between devices with their start and end apart: 15, of which 6 were waited for; matrix products, arithmetic and copies ran while one was open for 0% of the time, Pallas kernels for 27%

profile of v17, /device:TPU:0, one launch (start us, length us, event | category | flops | bytes accessed | tf_op | source)
XLA Modules:
  0.0 41.5 jit_solution(5334514620881609047)
XLA Ops:
  0.7 0.8 %copy-done.6 = bf16[128,256]{1,0:T(8,128)(2,1)S(1)} copy-done((bf16[128,256]{1,0:T(8,128)(2,1)S(1)}, bf16[128,256]{1,0:T(8,128)(2,1)}, u32[]{:S(2)}) %copy-start.6) | copy-done | bytes 65560
  1.5 4.1 %collective-permute-start = (bf16[128,512]{1,0:T(8,128)(2,1)S(1)}, bf16[128,512]{1,0:T(8,128)(2,1)S(1)}, u32[]{:S(2)}, u32[]{:S(2)}) collective-permute-start(bf16[128,512]{1,0:T(8,128)(2,1)S(1)} %keys_beside_values.1.refs_0_), channel_id=1, source_target_pairs={{0,16},{4,20},{8,24},{12,28},{16,0},{20,4},{24,8},{28,12},{1,17},{... | collective-permute-start | bytes 393224 | tf_op jit(solution)/shard_map/ppermute | solution.py:344
  5.6 0.6 %states_2.1 = bf16[528,128]{1,0:T(8,128)(2,1)S(1)} custom-call(f32[128,128]{1,0:T(8,128)S(1)} %get-tuple-element.19.refs_2_.refs_0_, f32[16,128]{1,0:T(8,128)S(1)} %copy-done.5, bf16[128,2048]{1,0:T(8,128)(2,1)S(1)} %copy-done, bf16[128,2048]{1,0:T(8,128)(2,1)S(1)} %copy-done.1), custom_call_target="tpu_custom_call" | custom-call | flops 33554432 | bytes 1257472 | tf_op jit(solution)/shard_map/states_2/pallas_call | solution.py:315
  6.3 1.6 %collective-permute-start.1 = (bf16[528,128]{1,0:T(8,128)(2,1)S(1)}, bf16[528,128]{1,0:T(8,128)(2,1)S(1)}, u32[]{:S(2)}, u32[]{:S(2)}) collective-permute-start(bf16[528,128]{1,0:T(8,128)(2,1)S(1)} %states_2.1), channel_id=1, source_target_pairs={{0,8},{4,12},{8,0},{12,4},{16,24},{20,28},{24,16},{28,20},{1,9},{5... | collective-permute-start | bytes 405512 | tf_op jit(solution)/shard_map/ppermute | solution.py:341
  7.9 0.6 %states_3.1 = bf16[528,128]{1,0:T(8,128)(2,1)S(1)} custom-call(f32[128,128]{1,0:T(8,128)S(1)} %get-tuple-element.19.refs_2_.refs_0_, f32[16,128]{1,0:T(8,128)S(1)} %copy-done.5, bf16[128,2048]{1,0:T(8,128)(2,1)S(1)} %copy-done, bf16[128,2048]{1,0:T(8,128)(2,1)S(1)} %copy-done.1), custom_call_target="tpu_custom_call" | custom-call | flops 33554432 | bytes 1257472 | tf_op jit(solution)/shard_map/states_3/pallas_call | solution.py:315
  8.5 1.5 %collective-permute-start.2 = (bf16[528,128]{1,0:T(8,128)(2,1)S(1)}, bf16[528,128]{1,0:T(8,128)(2,1)S(1)}, u32[]{:S(2)}, u32[]{:S(2)}) collective-permute-start(bf16[528,128]{1,0:T(8,128)(2,1)S(1)} %states_3.1), channel_id=1, source_target_pairs={{0,12},{4,8},{8,4},{12,0},{16,28},{20,24},{24,20},{28,16},{1,13},{... | collective-permute-start | bytes 405512 | tf_op jit(solution)/shard_map/ppermute | solution.py:341
  10.0 0.6 %states_1.1 = bf16[528,128]{1,0:T(8,128)(2,1)S(1)} custom-call(f32[128,128]{1,0:T(8,128)S(1)} %get-tuple-element.19.refs_2_.refs_0_, f32[16,128]{1,0:T(8,128)S(1)} %copy-done.5, bf16[128,2048]{1,0:T(8,128)(2,1)S(1)} %copy-done, bf16[128,2048]{1,0:T(8,128)(2,1)S(1)} %copy-done.1), custom_call_target="tpu_custom_call" | custom-call | flops 33554432 | bytes 1257472 | tf_op jit(solution)/shard_map/states_1/pallas_call | solution.py:315
  10.6 0.6 %collective-permute-start.3 = (bf16[528,128]{1,0:T(8,128)(2,1)S(1)}, bf16[528,128]{1,0:T(8,128)(2,1)S(1)}, u32[]{:S(2)}, u32[]{:S(2)}) collective-permute-start(bf16[528,128]{1,0:T(8,128)(2,1)S(1)} %states_1.1), channel_id=1, source_target_pairs={{0,4},{4,0},{8,12},{12,8},{16,20},{20,16},{24,28},{28,24},{1,5},{5... | collective-permute-start | bytes 405512 | tf_op jit(solution)/shard_map/ppermute | solution.py:341
  11.2 0.8 %states_0.1.refs_0_ = bf16[528,128]{1,0:T(8,128)(2,1)S(1)} custom-call(f32[128,128]{1,0:T(8,128)S(1)} %get-tuple-element.19.refs_2_.refs_0_, f32[16,128]{1,0:T(8,128)S(1)} %copy-done.5, bf16[128,2048]{1,0:T(8,128)(2,1)S(1)} %copy-done, bf16[128,2048]{1,0:T(8,128)(2,1)S(1)} %copy-done.1), custom_call_target="tpu_custom_call" | custom-call | flops 33554432 | bytes 1257472 | tf_op jit(solution)/shard_map/states_0/pallas_call | solution.py:315
  12.0 2.8 %intra_block.1 = (f32[128,2048]{1,0:T(8,128)S(1)}, bf16[128,2048]{1,0:T(8,128)(2,1)S(1)}, f32[128,2048]{1,0:T(8,128)S(1)}, f32[128,16]{1,0:T(8,128)S(1)}) custom-call(f32[128,128]{1,0:T(8,128)S(1)} %get-tuple-element.19.refs_2_.refs_0_, f32[128,128]{1,0:T(8,128)S(1)} %get-tuple-element.20.refs_1_, f32[16,128]{1,0:T(8,128)S(1)} %copy-done.5, ...), custom_call_target="tpu_custom_call" | custom-call | flops 134217728 | bytes 4874240 | tf_op jit(solution)/shard_map/intra_block/pallas_call | solution.py:315
  14.8 2.2 %collective-permute-done.2.refs_2_ = bf16[528,128]{1,0:T(8,128)(2,1)S(1)} collective-permute-done((bf16[528,128]{1,0:T(8,128)(2,1)S(1)}, bf16[528,128]{1,0:T(8,128)(2,1)S(1)}, u32[]{:S(2)}, u32[]{:S(2)}) %collective-permute-start.2) | collective-permute-done | bytes 135200 | tf_op jit(solution)/shard_map/ppermute | solution.py:341
  17.0 1.0 %collective-permute-done.3.refs_3_ = bf16[528,128]{1,0:T(8,128)(2,1)S(1)} collective-permute-done((bf16[528,128]{1,0:T(8,128)(2,1)S(1)}, bf16[528,128]{1,0:T(8,128)(2,1)S(1)}, u32[]{:S(2)}, u32[]{:S(2)}) %collective-permute-start.3) | collective-permute-done | bytes 135200 | tf_op jit(solution)/shard_map/ppermute | solution.py:341
  18.2 0.7 %collective-permute-start.8 = (bf16[528,128]{1,0:T(8,128)(2,1)S(1)}, bf16[528,128]{1,0:T(8,128)(2,1)S(1)}, u32[]{:S(2)}, u32[]{:S(2)}) collective-permute-start(bf16[528,128]{1,0:T(8,128)(2,1)S(1)} %group_state.1.refs_2_), channel_id=1, source_target_pairs={{0,16},{4,20},{8,24},{12,28},{16,0},{20,4},{24,8},{28,12},{1,17},{... | collective-permute-start | bytes 405512 | tf_op jit(solution)/shard_map/ppermute | solution.py:344
  18.9 1.6 %collective-permute-start.4 = (bf16[256,512]{1,0:T(8,128)(2,1)S(1)}, bf16[256,512]{1,0:T(8,128)(2,1)S(1)}, u32[]{:S(2)}, u32[]{:S(2)}) collective-permute-start(bf16[256,512]{1,0:T(8,128)(2,1)S(1)} %stack_keys_values.1.refs_2_), channel_id=1, source_target_pairs={{0,8},{4,12},{8,0},{12,4},{16,24},{20,28},{24,16},{28,20},{1,9},{5... | collective-permute-start | bytes 786440 | tf_op jit(solution)/shard_map/ppermute | solution.py:341
  21.1 4.5 %collective-permute-done.8.refs_4_ = bf16[528,128]{1,0:T(8,128)(2,1)S(1)} collective-permute-done((bf16[528,128]{1,0:T(8,128)(2,1)S(1)}, bf16[528,128]{1,0:T(8,128)(2,1)S(1)}, u32[]{:S(2)}, u32[]{:S(2)}) %collective-permute-start.8) | collective-permute-done | bytes 135200 | tf_op jit(solution)/shard_map/ppermute | solution.py:344
  25.8 1.7 %collective-permute-start.9 = (bf16[512,128]{1,0:T(8,128)(2,1)S(1)}, bf16[512,128]{1,0:T(8,128)(2,1)S(1)}, u32[]{:S(2)}, u32[]{:S(2)}) collective-permute-start(bf16[512,128]{1,0:T(8,128)(2,1)S(1)} %get-tuple-element.30), channel_id=1, source_target_pairs={{0,12},{4,8},{8,4},{12,0},{16,28},{20,24},{24,20},{28,16},{1,13},{... | collective-permute-start | bytes 393224 | tf_op jit(solution)/shard_map/ppermute | solution.py:341
  27.8 1.5 %collective-permute-start.11 = (bf16[512,128]{1,0:T(8,128)(2,1)S(1)}, bf16[512,128]{1,0:T(8,128)(2,1)S(1)}, u32[]{:S(2)}, u32[]{:S(2)}) collective-permute-start(bf16[512,128]{1,0:T(8,128)(2,1)S(1)} %get-tuple-element.32), channel_id=1, source_target_pairs={{0,4},{4,0},{8,12},{12,8},{16,20},{20,16},{24,28},{28,24},{1,5},{5... | collective-permute-start | bytes 393224 | tf_op jit(solution)/shard_map/ppermute | solution.py:341
  29.7 1.4 %collective-permute-start.7 = (bf16[128,512]{1,0:T(8,128)(2,1)S(1)}, bf16[128,512]{1,0:T(8,128)(2,1)S(1)}, u32[]{:S(2)}, u32[]{:S(2)}) collective-permute-start(bf16[128,512]{1,0:T(8,128)(2,1)S(1)} %get-tuple-element.23), channel_id=1, source_target_pairs={{0,8},{4,12},{8,0},{12,4},{16,24},{20,28},{24,16},{28,20},{1,9},{5... | collective-permute-start | bytes 393224 | tf_op jit(solution)/shard_map/ppermute | solution.py:341
  31.1 0.5 %collective-permute-start.6 = (bf16[128,512]{1,0:T(8,128)(2,1)S(1)}, bf16[128,512]{1,0:T(8,128)(2,1)S(1)}, u32[]{:S(2)}, u32[]{:S(2)}) collective-permute-start(bf16[128,512]{1,0:T(8,128)(2,1)S(1)} %get-tuple-element.22), channel_id=1, source_target_pairs={{0,4},{4,0},{8,12},{12,8},{16,20},{20,16},{24,28},{28,24},{1,5},{5... | collective-permute-start | bytes 393224 | tf_op jit(solution)/shard_map/ppermute | solution.py:341
  32.3 2.4 %softmax_first.1 = (f32[128,4096]{1,0:T(8,128)S(1)}, f32[128,8]{1,0:T(8,128)S(1)}, f32[128,8]{1,0:T(8,128)S(1)}) custom-call(s32[1]{0:T(128)S(6)} %copy.12.refs_0_, bf16[128,2048]{1,0:T(8,128)(2,1)S(1)} %copy-done.4, bf16[256,512]{1,0:T(8,128)(2,1)S(1)} %stack_keys_values.1.refs_2_, bf16[256,512]{1,0:T(8,128)(2,1)S(1)} %collective-permute-done.4.refs_0_.refs_3_, ...), custom_call_target="tpu_custom_call" | custom-call | flops 805306368 | bytes 3416068 | tf_op jit(solution)/shard_map/softmax_first/pallas_call | solution.py:315
  35.2 0.7 %inter_block.1 = (f32[128,2048]{1,0:T(8,128)S(1)}, f32[8,128]{1,0:T(8,128)S(1)}) custom-call(f32[128,16]{1,0:T(8,128)S(1)} %get-tuple-element.27.refs_0_, bf16[128,2048]{1,0:T(8,128)(2,1)S(1)} %get-tuple-element.28.refs_1_, f32[128,2048]{1,0:T(8,128)S(1)} %get-tuple-element.21.refs_4_.refs_2_, bf16[512,128]{1,0:T(8,128)(2,1)S(1)} %get-tuple-element.29.refs_3_, ...), custom_call_target="tpu_custom_call" | custom-call | flops 67108864 | bytes 3158016 | tf_op jit(solution)/shard_map/inter_block/pallas_call | solution.py:315
  35.8 1.6 %collective-permute-start.13 = (f32[8,128]{1,0:T(8,128)S(1)}, f32[8,128]{1,0:T(8,128)S(1)}, u32[]{:S(2)}, u32[]{:S(2)}) collective-permute-start(f32[8,128]{1,0:T(8,128)S(1)} %get-tuple-element.35.refs_3_), channel_id=1, source_target_pairs={{0,2},{1,3},{2,0},{3,1},{4,6},{5,7},{6,4},{7,5},{8,10},{9,11},{10,... | collective-permute-start | bytes 12296 | tf_op jit(solution)/shard_map/ppermute | solution.py:485
  37.8 2.5 %softmax_last.1.refs_0_ = bf16[128,2048]{1,0:T(8,128)(2,1)S(1)} custom-call(s32[1]{0:T(128)S(6)} %copy.12.refs_0_, bf16[128,2048]{1,0:T(8,128)(2,1)S(1)} %copy-done.4, bf16[256,512]{1,0:T(8,128)(2,1)S(1)} %pad_maximum_fusion.refs_2_, f32[128,4096]{1,0:T(8,128)S(1)} %get-tuple-element.24.refs_3_, f32[128,8]{1,0:T(8,128)S(1)} %get-tuple-element.25.refs_4_.refs_7_, ...), custom_call_target="tpu_custom_call" | custom-call | flops 268435456 | bytes 3416068 | tf_op jit(solution)/shard_map/softmax_last/pallas_call | solution.py:315
  40.2 1.1 %results.1 = (bf16[128,2048]{1,0:T(8,128)(2,1)}, bf16[128,2048]{1,0:T(8,128)(2,1)}) custom-call(bf16[128,2048]{1,0:T(8,128)(2,1)S(1)} %softmax_last.1.refs_0_, f32[128,2048]{1,0:T(8,128)S(1)} %get-tuple-element.33.refs_1_, f32[128,2048]{1,0:T(8,128)S(1)} %get-tuple-element.34.refs_2_, f32[8,128]{1,0:T(8,128)S(1)} %get-tuple-element.35.refs_3_, ...), custom_call_target="tpu_custom_call" | custom-call | flops 1048576 | bytes 3686400 | tf_op jit(solution)/shard_map/results/pallas_call | solution.py:315
  (40 shorter events, 2.6 us)
Async XLA Ops:
  0.6 0.8 %copy-start.6 = (bf16[128,256]{1,0:T(8,128)(2,1)S(1)}, bf16[128,256]{1,0:T(8,128)(2,1)}, u32[]{:S(2)}) copy-start(bf16[128,256]{1,0:T(8,128)(2,1)} %refs_0_.3) | copy-start | bytes 196612
  0.6 0.9 %copy-start.7 = (bf16[128,256]{1,0:T(8,128)(2,1)S(1)}, bf16[128,256]{1,0:T(8,128)(2,1)}, u32[]{:S(2)}) copy-start(bf16[128,256]{1,0:T(8,128)(2,1)} %refs_1_.7) | copy-start | bytes 196612
  0.7 5.0 %copy-start.5 = (f32[16,128]{1,0:T(8,128)S(1)}, f32[16,128]{1,0:T(8,128)}, u32[]{:S(2)}) copy-start(f32[16,128]{1,0:T(8,128)} %refs_2_.9) | copy-start | bytes 24580
  0.7 5.0 %copy-start = (bf16[128,2048]{1,0:T(8,128)(2,1)S(1)}, bf16[128,2048]{1,0:T(8,128)(2,1)}, u32[]{:S(2)}) copy-start(bf16[128,2048]{1,0:T(8,128)(2,1)} %refs_4_.1) | copy-start | bytes 1572868
  0.7 5.0 %copy-start.1 = (bf16[128,2048]{1,0:T(8,128)(2,1)S(1)}, bf16[128,2048]{1,0:T(8,128)(2,1)}, u32[]{:S(2)}) copy-start(bf16[128,2048]{1,0:T(8,128)(2,1)} %refs_5_.1) | copy-start | bytes 1572868
  1.5 10.5 %collective-permute-start = (bf16[128,512]{1,0:T(8,128)(2,1)S(1)}, bf16[128,512]{1,0:T(8,128)(2,1)S(1)}, u32[]{:S(2)}, u32[]{:S(2)}) collective-permute-start(bf16[128,512]{1,0:T(8,128)(2,1)S(1)} %keys_beside_values.1.refs_0_), channel_id=1, source_target_pairs={{0,16},{4,20},{8,24},{12,28},{16,0},{20,4},{24,8},{28,12},{1,17},{... | collective-permute-start | bytes 393224 | tf_op jit(solution)/shard_map/ppermute | solution.py:344
  6.2 5.8 %copy-start.2 = (bf16[128,2048]{1,0:T(8,128)(2,1)S(1)}, bf16[128,2048]{1,0:T(8,128)(2,1)}, u32[]{:S(2)}) copy-start(bf16[128,2048]{1,0:T(8,128)(2,1)} %refs_3_.9) | copy-start | bytes 1572868
  6.2 5.8 %copy-start.3 = (bf16[128,2048]{1,0:T(8,128)(2,1)S(1)}, bf16[128,2048]{1,0:T(8,128)(2,1)}, u32[]{:S(2)}) copy-start(bf16[128,2048]{1,0:T(8,128)(2,1)} %refs_6_.1) | copy-start | bytes 1572868
  6.3 5.8 %copy-start.8 = (f32[2048]{0:T(1024)S(1)}, f32[2048]{0:T(1024)}, u32[]{:S(2)}) copy-start(f32[2048]{0:T(1024)} %param.15) | copy-start | bytes 24580
  6.3 8.6 %collective-permute-start.1 = (bf16[528,128]{1,0:T(8,128)(2,1)S(1)}, bf16[528,128]{1,0:T(8,128)(2,1)S(1)}, u32[]{:S(2)}, u32[]{:S(2)}) collective-permute-start(bf16[528,128]{1,0:T(8,128)(2,1)S(1)} %states_2.1), channel_id=1, source_target_pairs={{0,8},{4,12},{8,0},{12,4},{16,24},{20,28},{24,16},{28,20},{1,9},{5... | collective-permute-start | bytes 405512 | tf_op jit(solution)/shard_map/ppermute | solution.py:341
  8.5 8.5 %collective-permute-start.2 = (bf16[528,128]{1,0:T(8,128)(2,1)S(1)}, bf16[528,128]{1,0:T(8,128)(2,1)S(1)}, u32[]{:S(2)}, u32[]{:S(2)}) collective-permute-start(bf16[528,128]{1,0:T(8,128)(2,1)S(1)} %states_3.1), channel_id=1, source_target_pairs={{0,12},{4,8},{8,4},{12,0},{16,28},{20,24},{24,20},{28,16},{1,13},{... | collective-permute-start | bytes 405512 | tf_op jit(solution)/shard_map/ppermute | solution.py:341
  10.6 7.4 %collective-permute-start.3 = (bf16[528,128]{1,0:T(8,128)(2,1)S(1)}, bf16[528,128]{1,0:T(8,128)(2,1)S(1)}, u32[]{:S(2)}, u32[]{:S(2)}) collective-permute-start(bf16[528,128]{1,0:T(8,128)(2,1)S(1)} %states_1.1), channel_id=1, source_target_pairs={{0,4},{4,0},{8,12},{12,8},{16,20},{20,16},{24,28},{28,24},{1,5},{5... | collective-permute-start | bytes 405512 | tf_op jit(solution)/shard_map/ppermute | solution.py:341
  18.2 7.4 %collective-permute-start.8 = (bf16[528,128]{1,0:T(8,128)(2,1)S(1)}, bf16[528,128]{1,0:T(8,128)(2,1)S(1)}, u32[]{:S(2)}, u32[]{:S(2)}) collective-permute-start(bf16[528,128]{1,0:T(8,128)(2,1)S(1)} %group_state.1.refs_2_), channel_id=1, source_target_pairs={{0,16},{4,20},{8,24},{12,28},{16,0},{20,4},{24,8},{28,12},{1,17},{... | collective-permute-start | bytes 405512 | tf_op jit(solution)/shard_map/ppermute | solution.py:344
  18.9 13.4 %copy-start.4 = (bf16[128,2048]{1,0:T(8,128)(2,1)S(1)}, bf16[128,2048]{1,0:T(8,128)(2,1)}, u32[]{:S(2)}) copy-start(bf16[128,2048]{1,0:T(8,128)(2,1)} %refs_1_.13) | copy-start | bytes 1572868
  18.9 10.8 %collective-permute-start.4 = (bf16[256,512]{1,0:T(8,128)(2,1)S(1)}, bf16[256,512]{1,0:T(8,128)(2,1)S(1)}, u32[]{:S(2)}, u32[]{:S(2)}) collective-permute-start(bf16[256,512]{1,0:T(8,128)(2,1)S(1)} %stack_keys_values.1.refs_2_), channel_id=1, source_target_pairs={{0,8},{4,12},{8,0},{12,4},{16,24},{20,28},{24,16},{28,20},{1,9},{5... | collective-permute-start | bytes 786440 | tf_op jit(solution)/shard_map/ppermute | solution.py:341
  20.6 9.1 %collective-permute-start.5 = (bf16[256,512]{1,0:T(8,128)(2,1)S(1)}, bf16[256,512]{1,0:T(8,128)(2,1)S(1)}, u32[]{:S(2)}, u32[]{:S(2)}) collective-permute-start(bf16[256,512]{1,0:T(8,128)(2,1)S(1)} %stack_keys_values.1.refs_2_), channel_id=1, source_target_pairs={{0,4},{4,0},{8,12},{12,8},{16,20},{20,16},{24,28},{28,24},{1,5},{5... | collective-permute-start | bytes 786440 | tf_op jit(solution)/shard_map/ppermute | solution.py:341
  25.8 8.9 %collective-permute-start.9 = (bf16[512,128]{1,0:T(8,128)(2,1)S(1)}, bf16[512,128]{1,0:T(8,128)(2,1)S(1)}, u32[]{:S(2)}, u32[]{:S(2)}) collective-permute-start(bf16[512,128]{1,0:T(8,128)(2,1)S(1)} %get-tuple-element.30), channel_id=1, source_target_pairs={{0,12},{4,8},{8,4},{12,0},{16,28},{20,24},{24,20},{28,16},{1,13},{... | collective-permute-start | bytes 393224 | tf_op jit(solution)/shard_map/ppermute | solution.py:341
  27.5 7.7 %collective-permute-start.10 = (bf16[512,128]{1,0:T(8,128)(2,1)S(1)}, bf16[512,128]{1,0:T(8,128)(2,1)S(1)}, u32[]{:S(2)}, u32[]{:S(2)}) collective-permute-start(bf16[512,128]{1,0:T(8,128)(2,1)S(1)} %get-tuple-element.31), channel_id=1, source_target_pairs={{0,8},{4,12},{8,0},{12,4},{16,24},{20,28},{24,16},{28,20},{1,9},{5... | collective-permute-start | bytes 393224 | tf_op jit(solution)/shard_map/ppermute | solution.py:341
  27.8 7.3 %collective-permute-start.11 = (bf16[512,128]{1,0:T(8,128)(2,1)S(1)}, bf16[512,128]{1,0:T(8,128)(2,1)S(1)}, u32[]{:S(2)}, u32[]{:S(2)}) collective-permute-start(bf16[512,128]{1,0:T(8,128)(2,1)S(1)} %get-tuple-element.32), channel_id=1, source_target_pairs={{0,4},{4,0},{8,12},{12,8},{16,20},{20,16},{24,28},{28,24},{1,5},{5... | collective-permute-start | bytes 393224 | tf_op jit(solution)/shard_map/ppermute | solution.py:341
  29.7 8.0 %collective-permute-start.7 = (bf16[128,512]{1,0:T(8,128)(2,1)S(1)}, bf16[128,512]{1,0:T(8,128)(2,1)S(1)}, u32[]{:S(2)}, u32[]{:S(2)}) collective-permute-start(bf16[128,512]{1,0:T(8,128)(2,1)S(1)} %get-tuple-element.23), channel_id=1, source_target_pairs={{0,8},{4,12},{8,0},{12,4},{16,24},{20,28},{24,16},{28,20},{1,9},{5... | collective-permute-start | bytes 393224 | tf_op jit(solution)/shard_map/ppermute | solution.py:341
  31.1 6.6 %collective-permute-start.6 = (bf16[128,512]{1,0:T(8,128)(2,1)S(1)}, bf16[128,512]{1,0:T(8,128)(2,1)S(1)}, u32[]{:S(2)}, u32[]{:S(2)}) collective-permute-start(bf16[128,512]{1,0:T(8,128)(2,1)S(1)} %get-tuple-element.22), channel_id=1, source_target_pairs={{0,4},{4,0},{8,12},{12,8},{16,20},{20,16},{24,28},{28,24},{1,5},{5... | collective-permute-start | bytes 393224 | tf_op jit(solution)/shard_map/ppermute | solution.py:341
  35.8 4.4 %collective-permute-start.12 = (f32[8,128]{1,0:T(8,128)S(1)}, f32[8,128]{1,0:T(8,128)S(1)}, u32[]{:S(2)}, u32[]{:S(2)}) collective-permute-start(f32[8,128]{1,0:T(8,128)S(1)} %get-tuple-element.35.refs_3_), channel_id=1, source_target_pairs={{0,3},{1,2},{2,1},{3,0},{4,7},{5,6},{6,5},{7,4},{8,11},{9,10},{10,... | collective-permute-start | bytes 12296 | tf_op jit(solution)/shard_map/ppermute | solution.py:485
  35.8 4.4 %collective-permute-start.13 = (f32[8,128]{1,0:T(8,128)S(1)}, f32[8,128]{1,0:T(8,128)S(1)}, u32[]{:S(2)}, u32[]{:S(2)}) collective-permute-start(f32[8,128]{1,0:T(8,128)S(1)} %get-tuple-element.35.refs_3_), channel_id=1, source_target_pairs={{0,2},{1,3},{2,0},{3,1},{4,6},{5,7},{6,4},{7,5},{8,10},{9,11},{10,... | collective-permute-start | bytes 12296 | tf_op jit(solution)/shard_map/ppermute | solution.py:485
  37.4 2.9 %collective-permute-start.14 = (f32[8,128]{1,0:T(8,128)S(1)}, f32[8,128]{1,0:T(8,128)S(1)}, u32[]{:S(2)}, u32[]{:S(2)}) collective-permute-start(f32[8,128]{1,0:T(8,128)S(1)} %get-tuple-element.35.refs_3_), channel_id=1, source_target_pairs={{0,1},{1,0},{2,3},{3,2},{4,5},{5,4},{6,7},{7,6},{8,9},{9,8},{10,11... | collective-permute-start | bytes 12296 | tf_op jit(solution)/shard_map/ppermute | solution.py:485

commit v18 on v10

--- a/solution.py
+++ b/solution.py
@@ -277,7 +277,7 @@
             for i, h in enumerate(heads):
                 rows = slice(i * tokens, (i + 1) * tokens)
                 acc_ref[:, 2 * h * HD : 2 * (h + 1) * HD] = acc[rows]
-                tops[g][:, j + i : j + i + 1] = top[rows]
+                tops[g][:, head_cols(j + i)] = jnp.broadcast_to(top[rows], (tokens, HD))
 
 
 def softmax_last_kernel(group, sides, kv_heads, pack, order_ref, q_ref, *rest):
@@ -291,12 +291,14 @@
         for j in range(0, share, pack):
             heads = range(g * share + j, g * share + j + pack)
             raw = softmax_scores(stacked(q_ref, map(head_cols, heads)), arrays, g, bias)
-            old = stacked(tops[g], [slice(j + i, j + i + 1) for i in range(pack)])
+            old = stacked(tops[g], map(head_cols, range(j, j + pack)))
             top = jnp.maximum(old, jnp.max(raw, axis=-1, keepdims=True))
-            probs = jnp.exp2((raw - top) * SCORE).astype(BF16)
+            spread = jnp.concatenate([top] * (raw.shape[1] // HD), axis=1)
+            probs = jnp.exp2((raw - spread) * SCORE).astype(BF16)
             acc = jnp.dot(probs, values[...], preferred_element_type=F32)
             held = stacked(acc_ref, [slice(2 * h * HD, 2 * (h + 1) * HD) for h in heads])
-            acc += held * jnp.exp2((old - top) * SCORE)
+            alpha = jnp.exp2((old - top) * SCORE)
+            acc += held * jnp.concatenate([alpha, alpha], axis=1)
             out = (acc[:, :HD] * inverse(acc[:, HD:])).astype(BF16)
             for i, h in enumerate(heads):
                 out_ref[:, head_cols(h)] = out[i * tokens : (i + 1) * tokens]
@@ -446,7 +448,7 @@
     acc, *tops = call(
         functools.partial(softmax_first_kernel, group, (0, 2, 1), kv_heads, pack),
         "softmax_first",
-        [shape((tokens, 2 * width), F32)] + [shape((tokens, share // HD), F32)] * kv_heads,
+        [shape((tokens, 2 * width), F32)] + [shape((tokens, share), F32)] * kv_heads,
         (order, queries, own, side, near),
         scratch(3),
         flops=12 * tokens * width * span,

time: 41.4 us -> 40.7 us (0.983)
  Pallas kernels: 11.3 us -> 9.98 us
  waiting for transfers between devices: 8.92 us -> 9.48 us
    pallas_call x12, Pallas kernels: 11.3 us -> 9.98 us  [call(): pl.pallas_call(run, name=name, out_shape=list(outs), in_specs=specs, scra...]
    ppermute x3, waiting for transfers between devices: 0.01 us -> 0.57 us  [body(): parts = [squares] + [lax.ppermute(squares, 'head', turn) for turn in turns]]
  transfers between devices with their start and end apart: 15 -> 15, of which waited for: 3 -> 4; matrix products, arithmetic and copies ran while one was open for 0% -> 0% of each run, Pallas kernels for 21% -> 18%
where the time goes in v18:
time: 40.7 us; the launch traced here: 40.4 us
  starting transfers between devices  18.4 us (45%)
  Pallas kernels  9.98 us (25%)
  waiting for transfers between devices  9.48 us (23%)
  between operations  1.47 us (4%)
  local copies, waits for them, and re-layouts  1.15 us (3%)
    ppermute x10, starting transfers between devices, swap(): return lax.ppermute(x, 'ctx', [(c, c ^ s) for c in range(n)])  12 us
    pallas_call x12, Pallas kernels, call(): pl.pallas_call(run, name=name, out_shape=list(outs), in_specs=specs, scra...  9.98 us
    ppermute x10, waiting for transfers between devices, swap(): return lax.ppermute(x, 'ctx', [(c, c ^ s) for c in range(n)])  4.62 us
    ppermute x2, starting transfers between devices, ahead(): return lax.ppermute(x, 'ctx', [(c, (c + d * group) % n) for c in range(n)])  4.45 us
    ppermute x2, waiting for transfers between devices, ahead(): return lax.ppermute(x, 'ctx', [(c, (c + d * group) % n) for c in range(n)])  4.29 us
    ppermute x3, starting transfers between devices, body(): parts = [squares] + [lax.ppermute(squares, 'head', turn) for turn in turns]  1.89 us
    unnamed x18, local copies, waits for them, and re-layouts  1.15 us
  transfers between devices with their start and end apart: 15, of which 4 were waited for; matrix products, arithmetic and copies ran while one was open for 0% of the time, Pallas kernels for 18%

profile of v18, /device:TPU:0, one launch (start us, length us, event | category | flops | bytes accessed | tf_op | source)
XLA Modules:
  0.0 40.4 jit_solution(2321419623904418148)
XLA Ops:
  0.7 0.6 %copy-done.7 = f32[16,128]{1,0:T(8,128)S(1)} copy-done((f32[16,128]{1,0:T(8,128)S(1)}, f32[16,128]{1,0:T(8,128)}, u32[]{:S(2)}) %copy-start.7) | copy-done | bytes 8216
  1.3 0.4 copy-done.3
  1.8 1.5 %block_states.1 = (bf16[528,128]{1,0:T(8,128)(2,1)S(1)}, bf16[528,128]{1,0:T(8,128)(2,1)S(1)}, bf16[528,128]{1,0:T(8,128)(2,1)S(1)}, bf16[528,128]{1,0:T(8,128)(...) custom-call(f32[128,128]{1,0:T(8,128)S(1)} %get-tuple-element.25.refs_2_.refs_0_, ...), custom_call_target="tpu_custom_call" | custom-call | flops 134217728 | bytes 2711552 | tf_op jit(solution)/shard_map/block_states/pallas_call | solution.py:318
  3.4 4.1 %collective-permute-start.1 = (bf16[528,128]{1,0:T(8,128)(2,1)S(1)}, bf16[528,128]{1,0:T(8,128)(2,1)S(1)}, u32[]{:S(2)}, u32[]{:S(2)}) collective-permute-start(bf16[528,128]{1,0:T(8,128)(2,1)S(1)} %get-tuple-element.27), channel_id=1, source_target_pairs={{0,12},{4,8},{8,4},{12,0},{16,28},{20,24},{24,20},{28,16},{1,13},{... | collective-permute-start | bytes 405512 | tf_op jit(solution)/shard_map/ppermute | solution.py:344
  7.4 0.4 %collective-permute-start.2 = (bf16[528,128]{1,0:T(8,128)(2,1)S(1)}, bf16[528,128]{1,0:T(8,128)(2,1)S(1)}, u32[]{:S(2)}, u32[]{:S(2)}) collective-permute-start(bf16[528,128]{1,0:T(8,128)(2,1)S(1)} %get-tuple-element.28), channel_id=1, source_target_pairs={{0,8},{4,12},{8,0},{12,4},{16,24},{20,28},{24,16},{28,20},{1,9},{5... | collective-permute-start | bytes 405512 | tf_op jit(solution)/shard_map/ppermute | solution.py:344
  7.9 0.2 collective-permute-start.3
  8.1 3.0 %collective-permute-start = (bf16[128,512]{1,0:T(8,128)(2,1)S(1)}, bf16[128,512]{1,0:T(8,128)(2,1)S(1)}, u32[]{:S(2)}, u32[]{:S(2)}) collective-permute-start(bf16[128,512]{1,0:T(8,128)(2,1)S(1)} %keys_beside_values.1.refs_0_), channel_id=1, source_target_pairs={{0,16},{4,20},{8,24},{12,28},{16,0},{20,4},{24,8},{28,12},{1,17},{... | collective-permute-start | bytes 393224 | tf_op jit(solution)/shard_map/ppermute | solution.py:350
  11.1 2.8 %intra_block.1 = (f32[128,2048]{1,0:T(8,128)S(1)}, bf16[128,2048]{1,0:T(8,128)(2,1)S(1)}, f32[128,2048]{1,0:T(8,128)S(1)}, f32[128,16]{1,0:T(8,128)S(1)}) custom-call(f32[128,128]{1,0:T(8,128)S(1)} %get-tuple-element.25.refs_2_.refs_0_, f32[128,128]{1,0:T(8,128)S(1)} %get-tuple-element.30.refs_1_, f32[16,128]{1,0:T(8,128)S(1)} %copy-done.7, ...), custom_call_target="tpu_custom_call" | custom-call | flops 134217728 | bytes 4874240 | tf_op jit(solution)/shard_map/intra_block/pallas_call | solution.py:318
  13.8 3.0 %collective-permute-done.2.refs_2_ = bf16[528,128]{1,0:T(8,128)(2,1)S(1)} collective-permute-done((bf16[528,128]{1,0:T(8,128)(2,1)S(1)}, bf16[528,128]{1,0:T(8,128)(2,1)S(1)}, u32[]{:S(2)}, u32[]{:S(2)}) %collective-permute-start.2) | collective-permute-done | bytes 135200 | tf_op jit(solution)/shard_map/ppermute | solution.py:344
  17.0 1.5 %collective-permute-start.8 = (bf16[528,128]{1,0:T(8,128)(2,1)S(1)}, bf16[528,128]{1,0:T(8,128)(2,1)S(1)}, u32[]{:S(2)}, u32[]{:S(2)}) collective-permute-start(bf16[528,128]{1,0:T(8,128)(2,1)S(1)} %group_state.1.refs_2_), channel_id=1, source_target_pairs={{0,16},{4,20},{8,24},{12,28},{16,0},{20,4},{24,8},{28,12},{1,17},{... | collective-permute-start | bytes 405512 | tf_op jit(solution)/shard_map/ppermute | solution.py:350
  18.6 2.5 %collective-permute-start.4 = (bf16[256,512]{1,0:T(8,128)(2,1)S(1)}, bf16[256,512]{1,0:T(8,128)(2,1)S(1)}, u32[]{:S(2)}, u32[]{:S(2)}) collective-permute-start(bf16[256,512]{1,0:T(8,128)(2,1)S(1)} %stack_keys_values.1.refs_2_), channel_id=1, source_target_pairs={{0,8},{4,12},{8,0},{12,4},{16,24},{20,28},{24,16},{28,20},{1,9},{5... | collective-permute-start | bytes 786440 | tf_op jit(solution)/shard_map/ppermute | solution.py:344
  21.1 4.3 %collective-permute-done.8.refs_4_ = bf16[528,128]{1,0:T(8,128)(2,1)S(1)} collective-permute-done((bf16[528,128]{1,0:T(8,128)(2,1)S(1)}, bf16[528,128]{1,0:T(8,128)(2,1)S(1)}, u32[]{:S(2)}, u32[]{:S(2)}) %collective-permute-start.8) | collective-permute-done | bytes 135200 | tf_op jit(solution)/shard_map/ppermute | solution.py:350
  25.4 0.2 prefix_states.1
  25.7 2.1 %collective-permute-start.10 = (bf16[512,128]{1,0:T(8,128)(2,1)S(1)}, bf16[512,128]{1,0:T(8,128)(2,1)S(1)}, u32[]{:S(2)}, u32[]{:S(2)}) collective-permute-start(bf16[512,128]{1,0:T(8,128)(2,1)S(1)} %get-tuple-element.43), channel_id=1, source_target_pairs={{0,8},{4,12},{8,0},{12,4},{16,24},{20,28},{24,16},{28,20},{1,9},{5... | collective-permute-start | bytes 393224 | tf_op jit(solution)/shard_map/ppermute | solution.py:344
  27.7 1.4 %collective-permute-start.11 = (bf16[512,128]{1,0:T(8,128)(2,1)S(1)}, bf16[512,128]{1,0:T(8,128)(2,1)S(1)}, u32[]{:S(2)}, u32[]{:S(2)}) collective-permute-start(bf16[512,128]{1,0:T(8,128)(2,1)S(1)} %get-tuple-element.44), channel_id=1, source_target_pairs={{0,4},{4,0},{8,12},{12,8},{16,20},{20,16},{24,28},{28,24},{1,5},{5... | collective-permute-start | bytes 393224 | tf_op jit(solution)/shard_map/ppermute | solution.py:344
  29.2 1.2 %collective-permute-start.7 = (bf16[128,512]{1,0:T(8,128)(2,1)S(1)}, bf16[128,512]{1,0:T(8,128)(2,1)S(1)}, u32[]{:S(2)}, u32[]{:S(2)}) collective-permute-start(bf16[128,512]{1,0:T(8,128)(2,1)S(1)} %get-tuple-element.35), channel_id=1, source_target_pairs={{0,8},{4,12},{8,0},{12,4},{16,24},{20,28},{24,16},{28,20},{1,9},{5... | collective-permute-start | bytes 393224 | tf_op jit(solution)/shard_map/ppermute | solution.py:344
  31.1 2.4 %softmax_first.1 = (f32[128,4096]{1,0:T(8,128)S(1)}, f32[128,1024]{1,0:T(8,128)S(1)}, f32[128,1024]{1,0:T(8,128)S(1)}) custom-call(s32[1]{0:T(128)S(6)} %copy.12.refs_0_, bf16[128,2048]{1,0:T(8,128)(2,1)S(1)} %copy-done.2, bf16[256,512]{1,0:T(8,128)(2,1)S(1)} %stack_keys_values.1.refs_2_, bf16[256,512]{1,0:T(8,128)(2,1)S(1)} %collective-permute-done.4.refs_0_.refs_3_, ...), custom_call_target="tpu_custom_call" | custom-call | flops 805306368 | bytes 4456452 | tf_op jit(solution)/shard_map/softmax_first/pallas_call | solution.py:318
  33.5 1.5 %collective-permute-done.10.refs_5_ = bf16[512,128]{1,0:T(8,128)(2,1)S(1)} collective-permute-done((bf16[512,128]{1,0:T(8,128)(2,1)S(1)}, bf16[512,128]{1,0:T(8,128)(2,1)S(1)}, u32[]{:S(2)}, u32[]{:S(2)}) %collective-permute-start.10) | collective-permute-done | bytes 131104 | tf_op jit(solution)/shard_map/ppermute | solution.py:344
  35.0 0.7 %inter_block.1 = (f32[128,2048]{1,0:T(8,128)S(1)}, f32[8,128]{1,0:T(8,128)S(1)}) custom-call(f32[128,16]{1,0:T(8,128)S(1)} %get-tuple-element.39.refs_0_, bf16[128,2048]{1,0:T(8,128)(2,1)S(1)} %get-tuple-element.40.refs_1_, f32[128,2048]{1,0:T(8,128)S(1)} %get-tuple-element.33.refs_4_.refs_2_, bf16[512,128]{1,0:T(8,128)(2,1)S(1)} %get-tuple-element.41.refs_3_, ...), custom_call_target="tpu_custom_call" | custom-call | flops 67108864 | bytes 3158016 | tf_op jit(solution)/shard_map/inter_block/pallas_call | solution.py:318
  35.7 1.5 %collective-permute-start.13 = (f32[8,128]{1,0:T(8,128)S(1)}, f32[8,128]{1,0:T(8,128)S(1)}, u32[]{:S(2)}, u32[]{:S(2)}) collective-permute-start(f32[8,128]{1,0:T(8,128)S(1)} %get-tuple-element.47.refs_3_), channel_id=1, source_target_pairs={{0,2},{1,3},{2,0},{3,1},{4,6},{5,7},{6,4},{7,5},{8,10},{9,11},{10,... | collective-permute-start | bytes 12296 | tf_op jit(solution)/shard_map/ppermute | solution.py:484
  37.2 0.4 %collective-permute-start.14 = (f32[8,128]{1,0:T(8,128)S(1)}, f32[8,128]{1,0:T(8,128)S(1)}, u32[]{:S(2)}, u32[]{:S(2)}) collective-permute-start(f32[8,128]{1,0:T(8,128)S(1)} %get-tuple-element.47.refs_3_), channel_id=1, source_target_pairs={{0,1},{1,0},{2,3},{3,2},{4,5},{5,4},{6,7},{7,6},{8,9},{9,8},{10,11... | collective-permute-start | bytes 12296 | tf_op jit(solution)/shard_map/ppermute | solution.py:484
  37.6 1.2 %softmax_last.1.refs_0_ = bf16[128,2048]{1,0:T(8,128)(2,1)S(1)} custom-call(s32[1]{0:T(128)S(6)} %copy.12.refs_0_, bf16[128,2048]{1,0:T(8,128)(2,1)S(1)} %copy-done.2, bf16[256,512]{1,0:T(8,128)(2,1)S(1)} %pad_maximum_fusion.refs_2_, f32[128,4096]{1,0:T(8,128)S(1)} %get-tuple-element.36.refs_3_, f32[128,1024]{1,0:T(8,128)S(1)} %get-tuple-element.37.refs_4_.refs_7_, ...), custom_call_target="tpu_custom_call" | custom-call | flops 268435456 | bytes 4456452 | tf_op jit(solution)/shard_map/softmax_last/pallas_call | solution.py:318
  38.8 0.6 %collective-permute-done.13.refs_5_ = f32[8,128]{1,0:T(8,128)S(1)} collective-permute-done((f32[8,128]{1,0:T(8,128)S(1)}, f32[8,128]{1,0:T(8,128)S(1)}, u32[]{:S(2)}, u32[]{:S(2)}) %collective-permute-start.13) | collective-permute-done | bytes 4128 | tf_op jit(solution)/shard_map/ppermute | solution.py:484
  39.4 1.1 %results.1 = (bf16[128,2048]{1,0:T(8,128)(2,1)}, bf16[128,2048]{1,0:T(8,128)(2,1)}) custom-call(bf16[128,2048]{1,0:T(8,128)(2,1)S(1)} %softmax_last.1.refs_0_, f32[128,2048]{1,0:T(8,128)S(1)} %get-tuple-element.45.refs_1_, f32[128,2048]{1,0:T(8,128)S(1)} %get-tuple-element.46.refs_2_, f32[8,128]{1,0:T(8,128)S(1)} %get-tuple-element.47.refs_3_, ...), custom_call_target="tpu_custom_call" | custom-call | flops 1048576 | bytes 3686400 | tf_op jit(solution)/shard_map/results/pallas_call | solution.py:318
  (37 shorter events, 0.6 us)
Async XLA Ops:
  0.6 0.7 %copy-start.7 = (f32[16,128]{1,0:T(8,128)S(1)}, f32[16,128]{1,0:T(8,128)}, u32[]{:S(2)}) copy-start(f32[16,128]{1,0:T(8,128)} %refs_2_.3) | copy-start | bytes 24580
  0.6 1.0 %copy-start.3 = (bf16[128,2048]{1,0:T(8,128)(2,1)S(1)}, bf16[128,2048]{1,0:T(8,128)(2,1)}, u32[]{:S(2)}) copy-start(bf16[128,2048]{1,0:T(8,128)(2,1)} %refs_2_.2) | copy-start | bytes 1572868
  0.7 1.2 %copy-start.4 = (bf16[128,2048]{1,0:T(8,128)(2,1)S(1)}, bf16[128,2048]{1,0:T(8,128)(2,1)}, u32[]{:S(2)}) copy-start(bf16[128,2048]{1,0:T(8,128)(2,1)} %refs_3_.2) | copy-start | bytes 1572868
  0.7 7.4 %copy-start.5 = (bf16[128,256]{1,0:T(8,128)(2,1)S(1)}, bf16[128,256]{1,0:T(8,128)(2,1)}, u32[]{:S(2)}) copy-start(bf16[128,256]{1,0:T(8,128)(2,1)} %refs_0_.3) | copy-start | bytes 196612
  0.7 7.4 %copy-start.6 = (bf16[128,256]{1,0:T(8,128)(2,1)S(1)}, bf16[128,256]{1,0:T(8,128)(2,1)}, u32[]{:S(2)}) copy-start(bf16[128,256]{1,0:T(8,128)(2,1)} %refs_1_.4) | copy-start | bytes 196612
  0.7 10.4 %copy-start = (bf16[128,2048]{1,0:T(8,128)(2,1)S(1)}, bf16[128,2048]{1,0:T(8,128)(2,1)}, u32[]{:S(2)}) copy-start(bf16[128,2048]{1,0:T(8,128)(2,1)} %refs_3_.3) | copy-start | bytes 1572868
  0.7 10.4 %copy-start.1 = (bf16[128,2048]{1,0:T(8,128)(2,1)S(1)}, bf16[128,2048]{1,0:T(8,128)(2,1)}, u32[]{:S(2)}) copy-start(bf16[128,2048]{1,0:T(8,128)(2,1)} %refs_6_.1) | copy-start | bytes 1572868
  0.7 10.4 %copy-start.8 = (f32[2048]{0:T(1024)S(1)}, f32[2048]{0:T(1024)}, u32[]{:S(2)}) copy-start(f32[2048]{0:T(1024)} %param.15) | copy-start | bytes 24580
  3.4 10.4 %collective-permute-start.1 = (bf16[528,128]{1,0:T(8,128)(2,1)S(1)}, bf16[528,128]{1,0:T(8,128)(2,1)S(1)}, u32[]{:S(2)}, u32[]{:S(2)}) collective-permute-start(bf16[528,128]{1,0:T(8,128)(2,1)S(1)} %get-tuple-element.27), channel_id=1, source_target_pairs={{0,12},{4,8},{8,4},{12,0},{16,28},{20,24},{24,20},{28,16},{1,13},{... | collective-permute-start | bytes 405512 | tf_op jit(solution)/shard_map/ppermute | solution.py:344
  7.4 9.4 %collective-permute-start.2 = (bf16[528,128]{1,0:T(8,128)(2,1)S(1)}, bf16[528,128]{1,0:T(8,128)(2,1)S(1)}, u32[]{:S(2)}, u32[]{:S(2)}) collective-permute-start(bf16[528,128]{1,0:T(8,128)(2,1)S(1)} %get-tuple-element.28), channel_id=1, source_target_pairs={{0,8},{4,12},{8,0},{12,4},{16,24},{20,28},{24,16},{28,20},{1,9},{5... | collective-permute-start | bytes 405512 | tf_op jit(solution)/shard_map/ppermute | solution.py:344
  7.9 9.0 %collective-permute-start.3 = (bf16[528,128]{1,0:T(8,128)(2,1)S(1)}, bf16[528,128]{1,0:T(8,128)(2,1)S(1)}, u32[]{:S(2)}, u32[]{:S(2)}) collective-permute-start(bf16[528,128]{1,0:T(8,128)(2,1)S(1)} %get-tuple-element.29), channel_id=1, source_target_pairs={{0,4},{4,0},{8,12},{12,8},{16,20},{20,16},{24,28},{28,24},{1,5},{5... | collective-permute-start | bytes 405512 | tf_op jit(solution)/shard_map/ppermute | solution.py:344
  8.1 10.4 %collective-permute-start = (bf16[128,512]{1,0:T(8,128)(2,1)S(1)}, bf16[128,512]{1,0:T(8,128)(2,1)S(1)}, u32[]{:S(2)}, u32[]{:S(2)}) collective-permute-start(bf16[128,512]{1,0:T(8,128)(2,1)S(1)} %keys_beside_values.1.refs_0_), channel_id=1, source_target_pairs={{0,16},{4,20},{8,24},{12,28},{16,0},{20,4},{24,8},{28,12},{1,17},{... | collective-permute-start | bytes 393224 | tf_op jit(solution)/shard_map/ppermute | solution.py:350
  17.0 8.4 %collective-permute-start.8 = (bf16[528,128]{1,0:T(8,128)(2,1)S(1)}, bf16[528,128]{1,0:T(8,128)(2,1)S(1)}, u32[]{:S(2)}, u32[]{:S(2)}) collective-permute-start(bf16[528,128]{1,0:T(8,128)(2,1)S(1)} %group_state.1.refs_2_), channel_id=1, source_target_pairs={{0,16},{4,20},{8,24},{12,28},{16,0},{20,4},{24,8},{28,12},{1,17},{... | collective-permute-start | bytes 405512 | tf_op jit(solution)/shard_map/ppermute | solution.py:350
  18.6 12.5 %copy-start.2 = (bf16[128,2048]{1,0:T(8,128)(2,1)S(1)}, bf16[128,2048]{1,0:T(8,128)(2,1)}, u32[]{:S(2)}) copy-start(bf16[128,2048]{1,0:T(8,128)(2,1)} %refs_1_.7) | copy-start | bytes 1572868
  18.6 10.6 %collective-permute-start.4 = (bf16[256,512]{1,0:T(8,128)(2,1)S(1)}, bf16[256,512]{1,0:T(8,128)(2,1)S(1)}, u32[]{:S(2)}, u32[]{:S(2)}) collective-permute-start(bf16[256,512]{1,0:T(8,128)(2,1)S(1)} %stack_keys_values.1.refs_2_), channel_id=1, source_target_pairs={{0,8},{4,12},{8,0},{12,4},{16,24},{20,28},{24,16},{28,20},{1,9},{5... | collective-permute-start | bytes 786440 | tf_op jit(solution)/shard_map/ppermute | solution.py:344
  21.1 8.1 %collective-permute-start.5 = (bf16[256,512]{1,0:T(8,128)(2,1)S(1)}, bf16[256,512]{1,0:T(8,128)(2,1)S(1)}, u32[]{:S(2)}, u32[]{:S(2)}) collective-permute-start(bf16[256,512]{1,0:T(8,128)(2,1)S(1)} %stack_keys_values.1.refs_2_), channel_id=1, source_target_pairs={{0,4},{4,0},{8,12},{12,8},{16,20},{20,16},{24,28},{28,24},{1,5},{5... | collective-permute-start | bytes 786440 | tf_op jit(solution)/shard_map/ppermute | solution.py:344
  25.6 7.9 %collective-permute-start.9 = (bf16[512,128]{1,0:T(8,128)(2,1)S(1)}, bf16[512,128]{1,0:T(8,128)(2,1)S(1)}, u32[]{:S(2)}, u32[]{:S(2)}) collective-permute-start(bf16[512,128]{1,0:T(8,128)(2,1)S(1)} %get-tuple-element.42), channel_id=1, source_target_pairs={{0,12},{4,8},{8,4},{12,0},{16,28},{20,24},{24,20},{28,16},{1,13},{... | collective-permute-start | bytes 393224 | tf_op jit(solution)/shard_map/ppermute | solution.py:344
  25.7 9.3 %collective-permute-start.10 = (bf16[512,128]{1,0:T(8,128)(2,1)S(1)}, bf16[512,128]{1,0:T(8,128)(2,1)S(1)}, u32[]{:S(2)}, u32[]{:S(2)}) collective-permute-start(bf16[512,128]{1,0:T(8,128)(2,1)S(1)} %get-tuple-element.43), channel_id=1, source_target_pairs={{0,8},{4,12},{8,0},{12,4},{16,24},{20,28},{24,16},{28,20},{1,9},{5... | collective-permute-start | bytes 393224 | tf_op jit(solution)/shard_map/ppermute | solution.py:344
  27.7 7.3 %collective-permute-start.11 = (bf16[512,128]{1,0:T(8,128)(2,1)S(1)}, bf16[512,128]{1,0:T(8,128)(2,1)S(1)}, u32[]{:S(2)}, u32[]{:S(2)}) collective-permute-start(bf16[512,128]{1,0:T(8,128)(2,1)S(1)} %get-tuple-element.44), channel_id=1, source_target_pairs={{0,4},{4,0},{8,12},{12,8},{16,20},{20,16},{24,28},{28,24},{1,5},{5... | collective-permute-start | bytes 393224 | tf_op jit(solution)/shard_map/ppermute | solution.py:344
  29.2 8.4 %collective-permute-start.7 = (bf16[128,512]{1,0:T(8,128)(2,1)S(1)}, bf16[128,512]{1,0:T(8,128)(2,1)S(1)}, u32[]{:S(2)}, u32[]{:S(2)}) collective-permute-start(bf16[128,512]{1,0:T(8,128)(2,1)S(1)} %get-tuple-element.35), channel_id=1, source_target_pairs={{0,8},{4,12},{8,0},{12,4},{16,24},{20,28},{24,16},{28,20},{1,9},{5... | collective-permute-start | bytes 393224 | tf_op jit(solution)/shard_map/ppermute | solution.py:344
  30.4 7.2 %collective-permute-start.6 = (bf16[128,512]{1,0:T(8,128)(2,1)S(1)}, bf16[128,512]{1,0:T(8,128)(2,1)S(1)}, u32[]{:S(2)}, u32[]{:S(2)}) collective-permute-start(bf16[128,512]{1,0:T(8,128)(2,1)S(1)} %get-tuple-element.34), channel_id=1, source_target_pairs={{0,4},{4,0},{8,12},{12,8},{16,20},{20,16},{24,28},{28,24},{1,5},{5... | collective-permute-start | bytes 393224 | tf_op jit(solution)/shard_map/ppermute | solution.py:344
  35.7 3.1 %collective-permute-start.12 = (f32[8,128]{1,0:T(8,128)S(1)}, f32[8,128]{1,0:T(8,128)S(1)}, u32[]{:S(2)}, u32[]{:S(2)}) collective-permute-start(f32[8,128]{1,0:T(8,128)S(1)} %get-tuple-element.47.refs_3_), channel_id=1, source_target_pairs={{0,3},{1,2},{2,1},{3,0},{4,7},{5,6},{6,5},{7,4},{8,11},{9,10},{10,... | collective-permute-start | bytes 12296 | tf_op jit(solution)/shard_map/ppermute | solution.py:484
  35.7 3.7 %collective-permute-start.13 = (f32[8,128]{1,0:T(8,128)S(1)}, f32[8,128]{1,0:T(8,128)S(1)}, u32[]{:S(2)}, u32[]{:S(2)}) collective-permute-start(f32[8,128]{1,0:T(8,128)S(1)} %get-tuple-element.47.refs_3_), channel_id=1, source_target_pairs={{0,2},{1,3},{2,0},{3,1},{4,6},{5,7},{6,4},{7,5},{8,10},{9,11},{10,... | collective-permute-start | bytes 12296 | tf_op jit(solution)/shard_map/ppermute | solution.py:484
  37.2 2.2 %collective-permute-start.14 = (f32[8,128]{1,0:T(8,128)S(1)}, f32[8,128]{1,0:T(8,128)S(1)}, u32[]{:S(2)}, u32[]{:S(2)}) collective-permute-start(f32[8,128]{1,0:T(8,128)S(1)} %get-tuple-element.47.refs_3_), channel_id=1, source_target_pairs={{0,1},{1,0},{2,3},{3,2},{4,5},{5,4},{6,7},{7,6},{8,9},{9,8},{10,11... | collective-permute-start | bytes 12296 | tf_op jit(solution)/shard_map/ppermute | solution.py:484

commit v19 on v18

--- a/solution.py
+++ b/solution.py
@@ -14,7 +14,6 @@
 F32 = jnp.float32
 BF16 = jnp.bfloat16
 NT = (((1,), (1,)), ((), ()))
-TN = (((0,), (0,)), ((), ()))
 MIB = 1 << 20
 VMEM = pl.BlockSpec(memory_space=pltpu.VMEM)
 HBM = pl.BlockSpec(memory_space=pltpu.HBM)
@@ -60,8 +59,8 @@
     per = heads // group
     rank = my_rank(group)
     ld = ld_ref[...]
-    cum = lax.dot_general(tri_ref[...], ld, NT, precision=HIGH, preferred_element_type=F32)
-    weight = jnp.exp(cum[tokens - 1 : tokens, :] - cum)
+    cum = lax.dot_general(ld, tri_ref[...], NT, precision=HIGH, preferred_element_type=F32)
+    weight = jnp.exp(cum[:, tokens - 1 : tokens] - cum)
     total = jnp.broadcast_to(jnp.exp(jnp.sum(ld, axis=1, keepdims=True)), (heads, HD))
     high = total.astype(BF16).astype(F32)
     low = total - high
@@ -74,11 +73,11 @@
         va = silu16(v_ref[:, head_cols(h)])
         ka_ref[:, head_cols(h)] = ka
         va_ref[:, head_cols(h)] = va
-        kdec = ka.astype(F32) * weight[:, h : h + 1]
+        kdec = jnp.transpose(ka).astype(F32) * weight[h : h + 1, :]
         khigh = kdec.astype(BF16)
         klow = (kdec - khigh.astype(F32)).astype(BF16)
-        state = lax.dot_general(khigh, va, TN, preferred_element_type=F32)
-        state += lax.dot_general(klow, va, TN, preferred_element_type=F32)
+        state = jnp.dot(khigh, va, preferred_element_type=F32)
+        state += jnp.dot(klow, va, preferred_element_type=F32)
         states[h * HD : (h + 1) * HD, :] = state.astype(BF16)
     for s in range(group):
         dest = rank ^ s
@@ -168,11 +167,11 @@
     bias = bias_ref[...]
     cum = lax.dot_general(tri, ld, NT, precision=HIGH, preferred_element_type=F32)
     cum_t = lax.dot_general(ld, tri, NT, precision=HIGH, preferred_element_type=F32)
-    decay_out[...] = jnp.exp(cum)
     for h in range(heads):
         cols = head_cols(h)
         qa = silu16(q_ref[:, cols])
         qa_ref[:, cols] = qa
+        decay_out[:, cols] = jnp.exp(jnp.broadcast_to(cum[:, h : h + 1], qa.shape))
         scores = lax.dot_general(qa, ka_ref[:, cols], NT, preferred_element_type=F32)
         decay = jnp.exp((cum[:, h : h + 1] - cum_t[h : h + 1, :]) + bias)
         weights = (scores * decay).astype(BF16)
@@ -188,13 +187,12 @@
     rank = my_rank(group)
     for s, part in zip(sent(group), parts):
         states[dyn(rank ^ s, per * HD), :] = part[...]
-    decay = decay_ref[...]
     acc = jnp.zeros((tokens, HD), F32)
     for h in range(heads):
         cols = head_cols(h)
         state = states[h * HD : (h + 1) * HD, :]
         inter = jnp.dot(qa_ref[:, cols], state, preferred_element_type=F32)
-        lin = intra_ref[:, cols] + inter * decay[:, h : h + 1]
+        lin = intra_ref[:, cols] + inter * decay_ref[:, cols]
         lin_ref[:, cols] = lin
         acc += lin * lin
     ones = jnp.ones((8, HD), F32)
@@ -378,7 +376,7 @@
             shape((tokens, width), F32),
             shape((tokens, width), BF16),
             shape((tokens, width), F32),
-            shape((tokens, heads), F32),
+            shape((tokens, width), F32),
         ],
         (tri, bias, log_decay, q_lin, ka, va, gate, norm_gain.reshape(1, width)),
         flops=4 * cube,

time: 40.7 us -> 40.3 us (level)
  no operation moved by 1% of the time
where the time goes in v19:
time: 40.3 us; the launch traced here: 40 us
  starting transfers between devices  18.4 us (46%)
  Pallas kernels  9.65 us (24%)
  waiting for transfers between devices  9.39 us (23%)
  between operations  1.47 us (4%)
  local copies, waits for them, and re-layouts  1.15 us (3%)
    ppermute x10, starting transfers between devices, swap(): return lax.ppermute(x, 'ctx', [(c, c ^ s) for c in range(n)])  12 us
    pallas_call x12, Pallas kernels, call(): pl.pallas_call(run, name=name, out_shape=list(outs), in_specs=specs, scra...  9.65 us
    ppermute x10, waiting for transfers between devices, swap(): return lax.ppermute(x, 'ctx', [(c, c ^ s) for c in range(n)])  4.54 us
    ppermute x2, starting transfers between devices, ahead(): return lax.ppermute(x, 'ctx', [(c, (c + d * group) % n) for c in range(n)])  4.45 us
    ppermute x2, waiting for transfers between devices, ahead(): return lax.ppermute(x, 'ctx', [(c, (c + d * group) % n) for c in range(n)])  4.28 us
    ppermute x3, starting transfers between devices, body(): parts = [squares] + [lax.ppermute(squares, 'head', turn) for turn in turns]  1.89 us
    unnamed x18, local copies, waits for them, and re-layouts  1.15 us
  transfers between devices with their start and end apart: 15, of which 4 were waited for; matrix products, arithmetic and copies ran while one was open for 0% of the time, Pallas kernels for 18%

profile of v19, /device:TPU:0, one launch (start us, length us, event | category | flops | bytes accessed | tf_op | source)
XLA Modules:
  0.0 40.0 jit_solution(6937158234233245620)
XLA Ops:
  0.7 0.6 %copy-done.7 = f32[16,128]{1,0:T(8,128)S(1)} copy-done((f32[16,128]{1,0:T(8,128)S(1)}, f32[16,128]{1,0:T(8,128)}, u32[]{:S(2)}) %copy-start.7) | copy-done | bytes 8216
  1.3 0.4 copy-done.3
  1.8 1.2 %block_states.1 = (bf16[528,128]{1,0:T(8,128)(2,1)S(1)}, bf16[528,128]{1,0:T(8,128)(2,1)S(1)}, bf16[528,128]{1,0:T(8,128)(2,1)S(1)}, bf16[528,128]{1,0:T(8,128)(...) custom-call(f32[128,128]{1,0:T(8,128)S(1)} %get-tuple-element.25.refs_2_.refs_0_, ...), custom_call_target="tpu_custom_call" | custom-call | flops 134217728 | bytes 2711552 | tf_op jit(solution)/shard_map/block_states/pallas_call | solution.py:316
  3.1 4.1 %collective-permute-start.1 = (bf16[528,128]{1,0:T(8,128)(2,1)S(1)}, bf16[528,128]{1,0:T(8,128)(2,1)S(1)}, u32[]{:S(2)}, u32[]{:S(2)}) collective-permute-start(bf16[528,128]{1,0:T(8,128)(2,1)S(1)} %get-tuple-element.27), channel_id=1, source_target_pairs={{0,12},{4,8},{8,4},{12,0},{16,28},{20,24},{24,20},{28,16},{1,13},{... | collective-permute-start | bytes 405512 | tf_op jit(solution)/shard_map/ppermute | solution.py:342
  7.2 0.4 %collective-permute-start.2 = (bf16[528,128]{1,0:T(8,128)(2,1)S(1)}, bf16[528,128]{1,0:T(8,128)(2,1)S(1)}, u32[]{:S(2)}, u32[]{:S(2)}) collective-permute-start(bf16[528,128]{1,0:T(8,128)(2,1)S(1)} %get-tuple-element.28), channel_id=1, source_target_pairs={{0,8},{4,12},{8,0},{12,4},{16,24},{20,28},{24,16},{28,20},{1,9},{5... | collective-permute-start | bytes 405512 | tf_op jit(solution)/shard_map/ppermute | solution.py:342
  7.6 0.2 collective-permute-start.3
  7.8 3.0 %collective-permute-start = (bf16[128,512]{1,0:T(8,128)(2,1)S(1)}, bf16[128,512]{1,0:T(8,128)(2,1)S(1)}, u32[]{:S(2)}, u32[]{:S(2)}) collective-permute-start(bf16[128,512]{1,0:T(8,128)(2,1)S(1)} %keys_beside_values.1.refs_0_), channel_id=1, source_target_pairs={{0,16},{4,20},{8,24},{12,28},{16,0},{20,4},{24,8},{28,12},{1,17},{... | collective-permute-start | bytes 393224 | tf_op jit(solution)/shard_map/ppermute | solution.py:348
  10.8 2.8 %intra_block.1 = (f32[128,2048]{1,0:T(8,128)S(1)}, bf16[128,2048]{1,0:T(8,128)(2,1)S(1)}, f32[128,2048]{1,0:T(8,128)S(1)}, f32[128,2048]{1,0:T(8,128)S(1)}) custom-call(f32[128,128]{1,0:T(8,128)S(1)} %get-tuple-element.25.refs_2_.refs_0_, f32[128,128]{1,0:T(8,128)S(1)} %get-tuple-element.30.refs_1_, f32[16,128]{1,0:T(8,128)S(1)} %copy-done.7, ...), custom_call_target="tpu_custom_call" | custom-call | flops 134217728 | bytes 5914624 | tf_op jit(solution)/shard_map/intra_block/pallas_call | solution.py:316
  13.6 3.0 %collective-permute-done.2.refs_2_ = bf16[528,128]{1,0:T(8,128)(2,1)S(1)} collective-permute-done((bf16[528,128]{1,0:T(8,128)(2,1)S(1)}, bf16[528,128]{1,0:T(8,128)(2,1)S(1)}, u32[]{:S(2)}, u32[]{:S(2)}) %collective-permute-start.2) | collective-permute-done | bytes 135200 | tf_op jit(solution)/shard_map/ppermute | solution.py:342
  16.8 1.5 %collective-permute-start.8 = (bf16[528,128]{1,0:T(8,128)(2,1)S(1)}, bf16[528,128]{1,0:T(8,128)(2,1)S(1)}, u32[]{:S(2)}, u32[]{:S(2)}) collective-permute-start(bf16[528,128]{1,0:T(8,128)(2,1)S(1)} %group_state.1.refs_2_), channel_id=1, source_target_pairs={{0,16},{4,20},{8,24},{12,28},{16,0},{20,4},{24,8},{28,12},{1,17},{... | collective-permute-start | bytes 405512 | tf_op jit(solution)/shard_map/ppermute | solution.py:348
  18.3 2.5 %collective-permute-start.4 = (bf16[256,512]{1,0:T(8,128)(2,1)S(1)}, bf16[256,512]{1,0:T(8,128)(2,1)S(1)}, u32[]{:S(2)}, u32[]{:S(2)}) collective-permute-start(bf16[256,512]{1,0:T(8,128)(2,1)S(1)} %stack_keys_values.1.refs_2_), channel_id=1, source_target_pairs={{0,8},{4,12},{8,0},{12,4},{16,24},{20,28},{24,16},{28,20},{1,9},{5... | collective-permute-start | bytes 786440 | tf_op jit(solution)/shard_map/ppermute | solution.py:342
  20.9 4.3 %collective-permute-done.8.refs_4_ = bf16[528,128]{1,0:T(8,128)(2,1)S(1)} collective-permute-done((bf16[528,128]{1,0:T(8,128)(2,1)S(1)}, bf16[528,128]{1,0:T(8,128)(2,1)S(1)}, u32[]{:S(2)}, u32[]{:S(2)}) %collective-permute-start.8) | collective-permute-done | bytes 135200 | tf_op jit(solution)/shard_map/ppermute | solution.py:348
  25.1 0.2 prefix_states.1
  25.4 2.1 %collective-permute-start.10 = (bf16[512,128]{1,0:T(8,128)(2,1)S(1)}, bf16[512,128]{1,0:T(8,128)(2,1)S(1)}, u32[]{:S(2)}, u32[]{:S(2)}) collective-permute-start(bf16[512,128]{1,0:T(8,128)(2,1)S(1)} %get-tuple-element.43), channel_id=1, source_target_pairs={{0,8},{4,12},{8,0},{12,4},{16,24},{20,28},{24,16},{28,20},{1,9},{5... | collective-permute-start | bytes 393224 | tf_op jit(solution)/shard_map/ppermute | solution.py:342
  27.5 1.4 %collective-permute-start.11 = (bf16[512,128]{1,0:T(8,128)(2,1)S(1)}, bf16[512,128]{1,0:T(8,128)(2,1)S(1)}, u32[]{:S(2)}, u32[]{:S(2)}) collective-permute-start(bf16[512,128]{1,0:T(8,128)(2,1)S(1)} %get-tuple-element.44), channel_id=1, source_target_pairs={{0,4},{4,0},{8,12},{12,8},{16,20},{20,16},{24,28},{28,24},{1,5},{5... | collective-permute-start | bytes 393224 | tf_op jit(solution)/shard_map/ppermute | solution.py:342
  28.9 1.2 %collective-permute-start.7 = (bf16[128,512]{1,0:T(8,128)(2,1)S(1)}, bf16[128,512]{1,0:T(8,128)(2,1)S(1)}, u32[]{:S(2)}, u32[]{:S(2)}) collective-permute-start(bf16[128,512]{1,0:T(8,128)(2,1)S(1)} %get-tuple-element.35), channel_id=1, source_target_pairs={{0,8},{4,12},{8,0},{12,4},{16,24},{20,28},{24,16},{28,20},{1,9},{5... | collective-permute-start | bytes 393224 | tf_op jit(solution)/shard_map/ppermute | solution.py:342
  30.8 2.4 %softmax_first.1 = (f32[128,4096]{1,0:T(8,128)S(1)}, f32[128,1024]{1,0:T(8,128)S(1)}, f32[128,1024]{1,0:T(8,128)S(1)}) custom-call(s32[1]{0:T(128)S(6)} %copy.12.refs_0_, bf16[128,2048]{1,0:T(8,128)(2,1)S(1)} %copy-done.2, bf16[256,512]{1,0:T(8,128)(2,1)S(1)} %stack_keys_values.1.refs_2_, bf16[256,512]{1,0:T(8,128)(2,1)S(1)} %collective-permute-done.4.refs_0_.refs_3_, ...), custom_call_target="tpu_custom_call" | custom-call | flops 805306368 | bytes 4456452 | tf_op jit(solution)/shard_map/softmax_first/pallas_call | solution.py:316
  33.2 1.5 %collective-permute-done.10.refs_5_ = bf16[512,128]{1,0:T(8,128)(2,1)S(1)} collective-permute-done((bf16[512,128]{1,0:T(8,128)(2,1)S(1)}, bf16[512,128]{1,0:T(8,128)(2,1)S(1)}, u32[]{:S(2)}, u32[]{:S(2)}) %collective-permute-start.10) | collective-permute-done | bytes 131104 | tf_op jit(solution)/shard_map/ppermute | solution.py:342
  34.8 0.5 %inter_block.1 = (f32[128,2048]{1,0:T(8,128)S(1)}, f32[8,128]{1,0:T(8,128)S(1)}) custom-call(f32[128,2048]{1,0:T(8,128)S(1)} %get-tuple-element.39.refs_0_, bf16[128,2048]{1,0:T(8,128)(2,1)S(1)} %get-tuple-element.40.refs_1_, f32[128,2048]{1,0:T(8,128)S(1)} %get-tuple-element.33.refs_4_.refs_2_, bf16[512,128]{1,0:T(8,128)(2,1)S(1)} %get-tuple-element.41.refs_3_, ...), custom_call_target="tpu_custom_call" | custom-call | flops 67108864 | bytes 4198400 | tf_op jit(solution)/shard_map/inter_block/pallas_call | solution.py:316
  35.3 1.5 %collective-permute-start.13 = (f32[8,128]{1,0:T(8,128)S(1)}, f32[8,128]{1,0:T(8,128)S(1)}, u32[]{:S(2)}, u32[]{:S(2)}) collective-permute-start(f32[8,128]{1,0:T(8,128)S(1)} %get-tuple-element.47.refs_3_), channel_id=1, source_target_pairs={{0,2},{1,3},{2,0},{3,1},{4,6},{5,7},{6,4},{7,5},{8,10},{9,11},{10,... | collective-permute-start | bytes 12296 | tf_op jit(solution)/shard_map/ppermute | solution.py:482
  36.8 0.4 %collective-permute-start.14 = (f32[8,128]{1,0:T(8,128)S(1)}, f32[8,128]{1,0:T(8,128)S(1)}, u32[]{:S(2)}, u32[]{:S(2)}) collective-permute-start(f32[8,128]{1,0:T(8,128)S(1)} %get-tuple-element.47.refs_3_), channel_id=1, source_target_pairs={{0,1},{1,0},{2,3},{3,2},{4,5},{5,4},{6,7},{7,6},{8,9},{9,8},{10,11... | collective-permute-start | bytes 12296 | tf_op jit(solution)/shard_map/ppermute | solution.py:482
  37.2 1.2 %softmax_last.1.refs_0_ = bf16[128,2048]{1,0:T(8,128)(2,1)S(1)} custom-call(s32[1]{0:T(128)S(6)} %copy.12.refs_0_, bf16[128,2048]{1,0:T(8,128)(2,1)S(1)} %copy-done.2, bf16[256,512]{1,0:T(8,128)(2,1)S(1)} %pad_maximum_fusion.refs_2_, f32[128,4096]{1,0:T(8,128)S(1)} %get-tuple-element.36.refs_3_, f32[128,1024]{1,0:T(8,128)S(1)} %get-tuple-element.37.refs_4_.refs_7_, ...), custom_call_target="tpu_custom_call" | custom-call | flops 268435456 | bytes 4456452 | tf_op jit(solution)/shard_map/softmax_last/pallas_call | solution.py:316
  38.4 0.6 %collective-permute-done.13.refs_5_ = f32[8,128]{1,0:T(8,128)S(1)} collective-permute-done((f32[8,128]{1,0:T(8,128)S(1)}, f32[8,128]{1,0:T(8,128)S(1)}, u32[]{:S(2)}, u32[]{:S(2)}) %collective-permute-start.13) | collective-permute-done | bytes 4128 | tf_op jit(solution)/shard_map/ppermute | solution.py:482
  39.0 1.1 %results.1 = (bf16[128,2048]{1,0:T(8,128)(2,1)}, bf16[128,2048]{1,0:T(8,128)(2,1)}) custom-call(bf16[128,2048]{1,0:T(8,128)(2,1)S(1)} %softmax_last.1.refs_0_, f32[128,2048]{1,0:T(8,128)S(1)} %get-tuple-element.45.refs_1_, f32[128,2048]{1,0:T(8,128)S(1)} %get-tuple-element.46.refs_2_, f32[8,128]{1,0:T(8,128)S(1)} %get-tuple-element.47.refs_3_, ...), custom_call_target="tpu_custom_call" | custom-call | flops 1048576 | bytes 3686400 | tf_op jit(solution)/shard_map/results/pallas_call | solution.py:316
  (37 shorter events, 0.6 us)
Async XLA Ops:
  0.6 0.7 %copy-start.7 = (f32[16,128]{1,0:T(8,128)S(1)}, f32[16,128]{1,0:T(8,128)}, u32[]{:S(2)}) copy-start(f32[16,128]{1,0:T(8,128)} %refs_2_.3) | copy-start | bytes 24580
  0.6 1.0 %copy-start.3 = (bf16[128,2048]{1,0:T(8,128)(2,1)S(1)}, bf16[128,2048]{1,0:T(8,128)(2,1)}, u32[]{:S(2)}) copy-start(bf16[128,2048]{1,0:T(8,128)(2,1)} %refs_2_.2) | copy-start | bytes 1572868
  0.7 1.2 %copy-start.4 = (bf16[128,2048]{1,0:T(8,128)(2,1)S(1)}, bf16[128,2048]{1,0:T(8,128)(2,1)}, u32[]{:S(2)}) copy-start(bf16[128,2048]{1,0:T(8,128)(2,1)} %refs_3_.2) | copy-start | bytes 1572868
  0.7 7.1 %copy-start.5 = (bf16[128,256]{1,0:T(8,128)(2,1)S(1)}, bf16[128,256]{1,0:T(8,128)(2,1)}, u32[]{:S(2)}) copy-start(bf16[128,256]{1,0:T(8,128)(2,1)} %refs_0_.3) | copy-start | bytes 196612
  0.7 7.1 %copy-start.6 = (bf16[128,256]{1,0:T(8,128)(2,1)S(1)}, bf16[128,256]{1,0:T(8,128)(2,1)}, u32[]{:S(2)}) copy-start(bf16[128,256]{1,0:T(8,128)(2,1)} %refs_1_.4) | copy-start | bytes 196612
  0.7 10.1 %copy-start = (bf16[128,2048]{1,0:T(8,128)(2,1)S(1)}, bf16[128,2048]{1,0:T(8,128)(2,1)}, u32[]{:S(2)}) copy-start(bf16[128,2048]{1,0:T(8,128)(2,1)} %refs_3_.3) | copy-start | bytes 1572868
  0.7 10.1 %copy-start.1 = (bf16[128,2048]{1,0:T(8,128)(2,1)S(1)}, bf16[128,2048]{1,0:T(8,128)(2,1)}, u32[]{:S(2)}) copy-start(bf16[128,2048]{1,0:T(8,128)(2,1)} %refs_6_.1) | copy-start | bytes 1572868
  0.7 10.1 %copy-start.8 = (f32[2048]{0:T(1024)S(1)}, f32[2048]{0:T(1024)}, u32[]{:S(2)}) copy-start(f32[2048]{0:T(1024)} %param.15) | copy-start | bytes 24580
  3.1 10.5 %collective-permute-start.1 = (bf16[528,128]{1,0:T(8,128)(2,1)S(1)}, bf16[528,128]{1,0:T(8,128)(2,1)S(1)}, u32[]{:S(2)}, u32[]{:S(2)}) collective-permute-start(bf16[528,128]{1,0:T(8,128)(2,1)S(1)} %get-tuple-element.27), channel_id=1, source_target_pairs={{0,12},{4,8},{8,4},{12,0},{16,28},{20,24},{24,20},{28,16},{1,13},{... | collective-permute-start | bytes 405512 | tf_op jit(solution)/shard_map/ppermute | solution.py:342
  7.2 9.4 %collective-permute-start.2 = (bf16[528,128]{1,0:T(8,128)(2,1)S(1)}, bf16[528,128]{1,0:T(8,128)(2,1)S(1)}, u32[]{:S(2)}, u32[]{:S(2)}) collective-permute-start(bf16[528,128]{1,0:T(8,128)(2,1)S(1)} %get-tuple-element.28), channel_id=1, source_target_pairs={{0,8},{4,12},{8,0},{12,4},{16,24},{20,28},{24,16},{28,20},{1,9},{5... | collective-permute-start | bytes 405512 | tf_op jit(solution)/shard_map/ppermute | solution.py:342
  7.6 9.0 %collective-permute-start.3 = (bf16[528,128]{1,0:T(8,128)(2,1)S(1)}, bf16[528,128]{1,0:T(8,128)(2,1)S(1)}, u32[]{:S(2)}, u32[]{:S(2)}) collective-permute-start(bf16[528,128]{1,0:T(8,128)(2,1)S(1)} %get-tuple-element.29), channel_id=1, source_target_pairs={{0,4},{4,0},{8,12},{12,8},{16,20},{20,16},{24,28},{28,24},{1,5},{5... | collective-permute-start | bytes 405512 | tf_op jit(solution)/shard_map/ppermute | solution.py:342
  7.8 10.4 %collective-permute-start = (bf16[128,512]{1,0:T(8,128)(2,1)S(1)}, bf16[128,512]{1,0:T(8,128)(2,1)S(1)}, u32[]{:S(2)}, u32[]{:S(2)}) collective-permute-start(bf16[128,512]{1,0:T(8,128)(2,1)S(1)} %keys_beside_values.1.refs_0_), channel_id=1, source_target_pairs={{0,16},{4,20},{8,24},{12,28},{16,0},{20,4},{24,8},{28,12},{1,17},{... | collective-permute-start | bytes 393224 | tf_op jit(solution)/shard_map/ppermute | solution.py:348
  16.8 8.4 %collective-permute-start.8 = (bf16[528,128]{1,0:T(8,128)(2,1)S(1)}, bf16[528,128]{1,0:T(8,128)(2,1)S(1)}, u32[]{:S(2)}, u32[]{:S(2)}) collective-permute-start(bf16[528,128]{1,0:T(8,128)(2,1)S(1)} %group_state.1.refs_2_), channel_id=1, source_target_pairs={{0,16},{4,20},{8,24},{12,28},{16,0},{20,4},{24,8},{28,12},{1,17},{... | collective-permute-start | bytes 405512 | tf_op jit(solution)/shard_map/ppermute | solution.py:348
  18.3 12.5 %copy-start.2 = (bf16[128,2048]{1,0:T(8,128)(2,1)S(1)}, bf16[128,2048]{1,0:T(8,128)(2,1)}, u32[]{:S(2)}) copy-start(bf16[128,2048]{1,0:T(8,128)(2,1)} %refs_1_.7) | copy-start | bytes 1572868
  18.3 10.6 %collective-permute-start.4 = (bf16[256,512]{1,0:T(8,128)(2,1)S(1)}, bf16[256,512]{1,0:T(8,128)(2,1)S(1)}, u32[]{:S(2)}, u32[]{:S(2)}) collective-permute-start(bf16[256,512]{1,0:T(8,128)(2,1)S(1)} %stack_keys_values.1.refs_2_), channel_id=1, source_target_pairs={{0,8},{4,12},{8,0},{12,4},{16,24},{20,28},{24,16},{28,20},{1,9},{5... | collective-permute-start | bytes 786440 | tf_op jit(solution)/shard_map/ppermute | solution.py:342
  20.9 8.0 %collective-permute-start.5 = (bf16[256,512]{1,0:T(8,128)(2,1)S(1)}, bf16[256,512]{1,0:T(8,128)(2,1)S(1)}, u32[]{:S(2)}, u32[]{:S(2)}) collective-permute-start(bf16[256,512]{1,0:T(8,128)(2,1)S(1)} %stack_keys_values.1.refs_2_), channel_id=1, source_target_pairs={{0,4},{4,0},{8,12},{12,8},{16,20},{20,16},{24,28},{28,24},{1,5},{5... | collective-permute-start | bytes 786440 | tf_op jit(solution)/shard_map/ppermute | solution.py:342
  25.3 7.9 %collective-permute-start.9 = (bf16[512,128]{1,0:T(8,128)(2,1)S(1)}, bf16[512,128]{1,0:T(8,128)(2,1)S(1)}, u32[]{:S(2)}, u32[]{:S(2)}) collective-permute-start(bf16[512,128]{1,0:T(8,128)(2,1)S(1)} %get-tuple-element.42), channel_id=1, source_target_pairs={{0,12},{4,8},{8,4},{12,0},{16,28},{20,24},{24,20},{28,16},{1,13},{... | collective-permute-start | bytes 393224 | tf_op jit(solution)/shard_map/ppermute | solution.py:342
  25.4 9.3 %collective-permute-start.10 = (bf16[512,128]{1,0:T(8,128)(2,1)S(1)}, bf16[512,128]{1,0:T(8,128)(2,1)S(1)}, u32[]{:S(2)}, u32[]{:S(2)}) collective-permute-start(bf16[512,128]{1,0:T(8,128)(2,1)S(1)} %get-tuple-element.43), channel_id=1, source_target_pairs={{0,8},{4,12},{8,0},{12,4},{16,24},{20,28},{24,16},{28,20},{1,9},{5... | collective-permute-start | bytes 393224 | tf_op jit(solution)/shard_map/ppermute | solution.py:342
  27.5 7.3 %collective-permute-start.11 = (bf16[512,128]{1,0:T(8,128)(2,1)S(1)}, bf16[512,128]{1,0:T(8,128)(2,1)S(1)}, u32[]{:S(2)}, u32[]{:S(2)}) collective-permute-start(bf16[512,128]{1,0:T(8,128)(2,1)S(1)} %get-tuple-element.44), channel_id=1, source_target_pairs={{0,4},{4,0},{8,12},{12,8},{16,20},{20,16},{24,28},{28,24},{1,5},{5... | collective-permute-start | bytes 393224 | tf_op jit(solution)/shard_map/ppermute | solution.py:342
  28.9 8.3 %collective-permute-start.7 = (bf16[128,512]{1,0:T(8,128)(2,1)S(1)}, bf16[128,512]{1,0:T(8,128)(2,1)S(1)}, u32[]{:S(2)}, u32[]{:S(2)}) collective-permute-start(bf16[128,512]{1,0:T(8,128)(2,1)S(1)} %get-tuple-element.35), channel_id=1, source_target_pairs={{0,8},{4,12},{8,0},{12,4},{16,24},{20,28},{24,16},{28,20},{1,9},{5... | collective-permute-start | bytes 393224 | tf_op jit(solution)/shard_map/ppermute | solution.py:342
  30.1 7.0 %collective-permute-start.6 = (bf16[128,512]{1,0:T(8,128)(2,1)S(1)}, bf16[128,512]{1,0:T(8,128)(2,1)S(1)}, u32[]{:S(2)}, u32[]{:S(2)}) collective-permute-start(bf16[128,512]{1,0:T(8,128)(2,1)S(1)} %get-tuple-element.34), channel_id=1, source_target_pairs={{0,4},{4,0},{8,12},{12,8},{16,20},{20,16},{24,28},{28,24},{1,5},{5... | collective-permute-start | bytes 393224 | tf_op jit(solution)/shard_map/ppermute | solution.py:342
  35.3 3.1 %collective-permute-start.12 = (f32[8,128]{1,0:T(8,128)S(1)}, f32[8,128]{1,0:T(8,128)S(1)}, u32[]{:S(2)}, u32[]{:S(2)}) collective-permute-start(f32[8,128]{1,0:T(8,128)S(1)} %get-tuple-element.47.refs_3_), channel_id=1, source_target_pairs={{0,3},{1,2},{2,1},{3,0},{4,7},{5,6},{6,5},{7,4},{8,11},{9,10},{10,... | collective-permute-start | bytes 12296 | tf_op jit(solution)/shard_map/ppermute | solution.py:482
  35.3 3.7 %collective-permute-start.13 = (f32[8,128]{1,0:T(8,128)S(1)}, f32[8,128]{1,0:T(8,128)S(1)}, u32[]{:S(2)}, u32[]{:S(2)}) collective-permute-start(f32[8,128]{1,0:T(8,128)S(1)} %get-tuple-element.47.refs_3_), channel_id=1, source_target_pairs={{0,2},{1,3},{2,0},{3,1},{4,6},{5,7},{6,4},{7,5},{8,10},{9,11},{10,... | collective-permute-start | bytes 12296 | tf_op jit(solution)/shard_map/ppermute | solution.py:482
  36.8 2.2 %collective-permute-start.14 = (f32[8,128]{1,0:T(8,128)S(1)}, f32[8,128]{1,0:T(8,128)S(1)}, u32[]{:S(2)}, u32[]{:S(2)}) collective-permute-start(f32[8,128]{1,0:T(8,128)S(1)} %get-tuple-element.47.refs_3_), channel_id=1, source_target_pairs={{0,1},{1,0},{2,3},{3,2},{4,5},{5,4},{6,7},{7,6},{8,9},{9,8},{10,11... | collective-permute-start | bytes 12296 | tf_op jit(solution)/shard_map/ppermute | solution.py:482

commit v20 on v19

--- a/solution.py
+++ b/solution.py
@@ -108,18 +108,14 @@
     return tail[j : j + 1] + tail[8 + j : 9 + j]
 
 
-def sent(group):
-    return [0, *range(group - 1, 0, -1)]
-
-
-def fill_slots(group, rank, pays, slots):
-    for s, pay in zip(sent(group), pays):
+def fill_slots(order, rank, pays, slots):
+    for s, pay in zip(order, pays):
         slots[rank ^ s] = pay[...]
 
 
-def total_kernel(group, per, *refs):
+def total_kernel(group, per, order, *refs):
     pays, out, slots = refs[:group], refs[group], refs[group + 1]
-    fill_slots(group, my_rank(group), pays, slots)
+    fill_slots(order, my_rank(group), pays, slots)
     base = per * HD
     tails = []
     for j in range(per):
@@ -137,7 +133,7 @@
     out[base:, :] = jnp.concatenate([high, total - high], axis=0).astype(BF16)
 
 
-def prefix_kernel(group, per, carried, *refs):
+def prefix_kernel(group, per, order, carried, *refs):
     pays, refs = refs[:group], refs[group:]
     carry = None
     if carried:
@@ -145,7 +141,7 @@
     outs, slots, prefixes = refs[:group], refs[group], refs[group + 1]
     rank = my_rank(group)
     later = lax.axis_index("ctx") >= group
-    fill_slots(group, rank, pays, slots)
+    fill_slots(order, rank, pays, slots)
     base = per * HD
     for j in range(per):
         rows = slice(j * HD, (j + 1) * HD)
@@ -180,12 +176,12 @@
         gain_out[:, cols] = gate * gain_ref[:, cols]
 
 
-def inter_kernel(group, heads, decay_ref, qa_ref, intra_ref, *rest):
+def inter_kernel(group, heads, order, decay_ref, qa_ref, intra_ref, *rest):
     parts, (lin_ref, squares_ref, states) = rest[:group], rest[group:]
     tokens = qa_ref.shape[0]
     per = heads // group
     rank = my_rank(group)
-    for s, part in zip(sent(group), parts):
+    for s, part in zip(order, parts):
         states[dyn(rank ^ s, per * HD), :] = part[...]
     acc = jnp.zeros((tokens, HD), F32)
     for h in range(heads):
@@ -341,8 +337,10 @@
     def swap(x, s):
         return lax.ppermute(x, "ctx", [(c, c ^ s) for c in range(n)])
 
-    def swap_all(xs):
-        return [swap(xs[s], s) if s else xs[s] for s in sent(group)]
+    to, back = (0, 2, 3, 1), (0, 3, 2, 1)
+
+    def swap_all(xs, order):
+        return [swap(xs[s], s) if s else xs[s] for s in order]
 
     def ahead(x, d):
         return lax.ppermute(x, "ctx", [(c, (c + d * group) % n) for c in range(n)])
@@ -368,7 +366,7 @@
         flops=4 * cube,
         exps=2 * tokens * width,
     )
-    pays = swap_all(pays)
+    pays = swap_all(pays, to)
     intra, qa, gain, decay = call(
         functools.partial(intra_kernel, heads),
         "intra_block",
@@ -387,7 +385,7 @@
     carry = ()
     if groups > 1:
         (total,) = call(
-            functools.partial(total_kernel, group, per),
+            functools.partial(total_kernel, group, per, to),
             "group_state",
             [shape((rows, HD), BF16)],
             pays,
@@ -412,14 +410,14 @@
             shift *= 2
         carry = (before,)
     prefixes = call(
-        functools.partial(prefix_kernel, group, per, bool(carry)),
+        functools.partial(prefix_kernel, group, per, to, bool(carry)),
         "prefix_states",
         [shape((per * HD, HD), BF16)] * group,
         (*pays, *carry),
         [slots, pltpu.VMEM((group, per * HD, HD), BF16)],
         flops=1 << 33,
     )
-    prefixes = swap_all(prefixes)
+    prefixes = swap_all(prefixes, back)
 
     (own,) = call(
         stack_kernel,
@@ -467,7 +465,7 @@
     )
 
     lin, squares = call(
-        functools.partial(inter_kernel, group, heads),
+        functools.partial(inter_kernel, group, heads, back),
         "inter_block",
         [shape((tokens, width), F32), shape((8, tokens), F32)],
         (decay, qa, intra, *prefixes),

time: 40.3 us -> 40.2 us (level)
  starting transfers between devices: 18.4 us -> 17.9 us
  waiting for transfers between devices: 9.39 us -> 9.8 us
    ppermute x10, waiting for transfers between devices: 4.54 us -> 4.98 us  [swap(): return lax.ppermute(x, 'ctx', [(c, c ^ s) for c in range(n)])]
  transfers between devices with their start and end apart: 15 -> 15, of which waited for: 4 -> 5; matrix products, arithmetic and copies ran while one was open for 0% -> 0% of each run, Pallas kernels for 18% -> 18%
where the time goes in v20:
time: 40.2 us; the launch traced here: 39.9 us
  starting transfers between devices  17.9 us (45%)
  waiting for transfers between devices  9.8 us (24%)
  Pallas kernels  9.65 us (24%)
  between operations  1.46 us (4%)
  local copies, waits for them, and re-layouts  1.15 us (3%)
    ppermute x10, starting transfers between devices, swap(): return lax.ppermute(x, 'ctx', [(c, c ^ s) for c in range(n)])  11.6 us
    pallas_call x12, Pallas kernels, call(): pl.pallas_call(run, name=name, out_shape=list(outs), in_specs=specs, scra...  9.65 us
    ppermute x10, waiting for transfers between devices, swap(): return lax.ppermute(x, 'ctx', [(c, c ^ s) for c in range(n)])  4.98 us
    ppermute x2, starting transfers between devices, ahead(): return lax.ppermute(x, 'ctx', [(c, (c + d * group) % n) for c in range(n)])  4.33 us
    ppermute x2, waiting for transfers between devices, ahead(): return lax.ppermute(x, 'ctx', [(c, (c + d * group) % n) for c in range(n)])  4.25 us
    ppermute x3, starting transfers between devices, body(): parts = [squares] + [lax.ppermute(squares, 'head', turn) for turn in turns]  1.89 us
    unnamed x18, local copies, waits for them, and re-layouts  1.15 us
  transfers between devices with their start and end apart: 15, of which 5 were waited for; matrix products, arithmetic and copies ran while one was open for 0% of the time, Pallas kernels for 18%

profile of v20, /device:TPU:0, one launch (start us, length us, event | category | flops | bytes accessed | tf_op | source)
XLA Modules:
  0.0 39.9 jit_solution(16394190526340705582)
XLA Ops:
  0.7 0.6 %copy-done.7 = f32[16,128]{1,0:T(8,128)S(1)} copy-done((f32[16,128]{1,0:T(8,128)S(1)}, f32[16,128]{1,0:T(8,128)}, u32[]{:S(2)}) %copy-start.7) | copy-done | bytes 8216
  1.3 0.4 copy-done.3
  1.8 1.2 %block_states.1 = (bf16[528,128]{1,0:T(8,128)(2,1)S(1)}, bf16[528,128]{1,0:T(8,128)(2,1)S(1)}, bf16[528,128]{1,0:T(8,128)(2,1)S(1)}, bf16[528,128]{1,0:T(8,128)(...) custom-call(f32[128,128]{1,0:T(8,128)S(1)} %get-tuple-element.25.refs_2_.refs_0_, ...), custom_call_target="tpu_custom_call" | custom-call | flops 134217728 | bytes 2711552 | tf_op jit(solution)/shard_map/block_states/pallas_call | solution.py:312
  3.1 3.1 %collective-permute-start.1 = (bf16[528,128]{1,0:T(8,128)(2,1)S(1)}, bf16[528,128]{1,0:T(8,128)(2,1)S(1)}, u32[]{:S(2)}, u32[]{:S(2)}) collective-permute-start(bf16[528,128]{1,0:T(8,128)(2,1)S(1)} %get-tuple-element.27), channel_id=1, source_target_pairs={{0,8},{4,12},{8,0},{12,4},{16,24},{20,28},{24,16},{28,20},{1,9},{5... | collective-permute-start | bytes 405512 | tf_op jit(solution)/shard_map/ppermute | solution.py:338
  6.2 1.4 %collective-permute-start.2 = (bf16[528,128]{1,0:T(8,128)(2,1)S(1)}, bf16[528,128]{1,0:T(8,128)(2,1)S(1)}, u32[]{:S(2)}, u32[]{:S(2)}) collective-permute-start(bf16[528,128]{1,0:T(8,128)(2,1)S(1)} %get-tuple-element.28), channel_id=1, source_target_pairs={{0,12},{4,8},{8,4},{12,0},{16,28},{20,24},{24,20},{28,16},{1,13},{... | collective-permute-start | bytes 405512 | tf_op jit(solution)/shard_map/ppermute | solution.py:338
  7.8 3.0 %collective-permute-start = (bf16[128,512]{1,0:T(8,128)(2,1)S(1)}, bf16[128,512]{1,0:T(8,128)(2,1)S(1)}, u32[]{:S(2)}, u32[]{:S(2)}) collective-permute-start(bf16[128,512]{1,0:T(8,128)(2,1)S(1)} %keys_beside_values.1.refs_0_), channel_id=1, source_target_pairs={{0,16},{4,20},{8,24},{12,28},{16,0},{20,4},{24,8},{28,12},{1,17},{... | collective-permute-start | bytes 393224 | tf_op jit(solution)/shard_map/ppermute | solution.py:346
  10.8 2.8 %intra_block.1 = (f32[128,2048]{1,0:T(8,128)S(1)}, bf16[128,2048]{1,0:T(8,128)(2,1)S(1)}, f32[128,2048]{1,0:T(8,128)S(1)}, f32[128,2048]{1,0:T(8,128)S(1)}) custom-call(f32[128,128]{1,0:T(8,128)S(1)} %get-tuple-element.25.refs_2_.refs_0_, f32[128,128]{1,0:T(8,128)S(1)} %get-tuple-element.30.refs_1_, f32[16,128]{1,0:T(8,128)S(1)} %copy-done.7, ...), custom_call_target="tpu_custom_call" | custom-call | flops 134217728 | bytes 5914624 | tf_op jit(solution)/shard_map/intra_block/pallas_call | solution.py:312
  13.6 3.0 %collective-permute-done.2.refs_2_ = bf16[528,128]{1,0:T(8,128)(2,1)S(1)} collective-permute-done((bf16[528,128]{1,0:T(8,128)(2,1)S(1)}, bf16[528,128]{1,0:T(8,128)(2,1)S(1)}, u32[]{:S(2)}, u32[]{:S(2)}) %collective-permute-start.2) | collective-permute-done | bytes 135200 | tf_op jit(solution)/shard_map/ppermute | solution.py:338
  16.8 1.3 %collective-permute-start.8 = (bf16[528,128]{1,0:T(8,128)(2,1)S(1)}, bf16[528,128]{1,0:T(8,128)(2,1)S(1)}, u32[]{:S(2)}, u32[]{:S(2)}) collective-permute-start(bf16[528,128]{1,0:T(8,128)(2,1)S(1)} %group_state.1.refs_2_), channel_id=1, source_target_pairs={{0,16},{4,20},{8,24},{12,28},{16,0},{20,4},{24,8},{28,12},{1,17},{... | collective-permute-start | bytes 405512 | tf_op jit(solution)/shard_map/ppermute | solution.py:346
  18.1 2.2 %collective-permute-start.4 = (bf16[256,512]{1,0:T(8,128)(2,1)S(1)}, bf16[256,512]{1,0:T(8,128)(2,1)S(1)}, u32[]{:S(2)}, u32[]{:S(2)}) collective-permute-start(bf16[256,512]{1,0:T(8,128)(2,1)S(1)} %stack_keys_values.1.refs_2_), channel_id=1, source_target_pairs={{0,8},{4,12},{8,0},{12,4},{16,24},{20,28},{24,16},{28,20},{1,9},{5... | collective-permute-start | bytes 786440 | tf_op jit(solution)/shard_map/ppermute | solution.py:338
  20.3 0.5 %collective-permute-start.5 = (bf16[256,512]{1,0:T(8,128)(2,1)S(1)}, bf16[256,512]{1,0:T(8,128)(2,1)S(1)}, u32[]{:S(2)}, u32[]{:S(2)}) collective-permute-start(bf16[256,512]{1,0:T(8,128)(2,1)S(1)} %stack_keys_values.1.refs_2_), channel_id=1, source_target_pairs={{0,4},{4,0},{8,12},{12,8},{16,20},{20,16},{24,28},{28,24},{1,5},{5... | collective-permute-start | bytes 786440 | tf_op jit(solution)/shard_map/ppermute | solution.py:338
  20.8 4.2 %collective-permute-done.8.refs_4_ = bf16[528,128]{1,0:T(8,128)(2,1)S(1)} collective-permute-done((bf16[528,128]{1,0:T(8,128)(2,1)S(1)}, bf16[528,128]{1,0:T(8,128)(2,1)S(1)}, u32[]{:S(2)}, u32[]{:S(2)}) %collective-permute-start.8) | collective-permute-done | bytes 135200 | tf_op jit(solution)/shard_map/ppermute | solution.py:346
  25.4 1.9 %collective-permute-start.10 = (bf16[512,128]{1,0:T(8,128)(2,1)S(1)}, bf16[512,128]{1,0:T(8,128)(2,1)S(1)}, u32[]{:S(2)}, u32[]{:S(2)}) collective-permute-start(bf16[512,128]{1,0:T(8,128)(2,1)S(1)} %get-tuple-element.43), channel_id=1, source_target_pairs={{0,8},{4,12},{8,0},{12,4},{16,24},{20,28},{24,16},{28,20},{1,9},{5... | collective-permute-start | bytes 393224 | tf_op jit(solution)/shard_map/ppermute | solution.py:338
  27.3 1.5 %collective-permute-start.11 = (bf16[512,128]{1,0:T(8,128)(2,1)S(1)}, bf16[512,128]{1,0:T(8,128)(2,1)S(1)}, u32[]{:S(2)}, u32[]{:S(2)}) collective-permute-start(bf16[512,128]{1,0:T(8,128)(2,1)S(1)} %get-tuple-element.44), channel_id=1, source_target_pairs={{0,4},{4,0},{8,12},{12,8},{16,20},{20,16},{24,28},{28,24},{1,5},{5... | collective-permute-start | bytes 393224 | tf_op jit(solution)/shard_map/ppermute | solution.py:338
  28.9 0.4 collective-permute-start.7
  29.3 0.3 collective-permute-start.6
  30.3 2.4 %softmax_first.1 = (f32[128,4096]{1,0:T(8,128)S(1)}, f32[128,1024]{1,0:T(8,128)S(1)}, f32[128,1024]{1,0:T(8,128)S(1)}) custom-call(s32[1]{0:T(128)S(6)} %copy.12.refs_0_, bf16[128,2048]{1,0:T(8,128)(2,1)S(1)} %copy-done.2, bf16[256,512]{1,0:T(8,128)(2,1)S(1)} %stack_keys_values.1.refs_2_, bf16[256,512]{1,0:T(8,128)(2,1)S(1)} %collective-permute-done.4.refs_0_.refs_3_, ...), custom_call_target="tpu_custom_call" | custom-call | flops 805306368 | bytes 4456452 | tf_op jit(solution)/shard_map/softmax_first/pallas_call | solution.py:312
  32.7 1.8 %collective-permute-done.10.refs_5_ = bf16[512,128]{1,0:T(8,128)(2,1)S(1)} collective-permute-done((bf16[512,128]{1,0:T(8,128)(2,1)S(1)}, bf16[512,128]{1,0:T(8,128)(2,1)S(1)}, u32[]{:S(2)}, u32[]{:S(2)}) %collective-permute-start.10) | collective-permute-done | bytes 131104 | tf_op jit(solution)/shard_map/ppermute | solution.py:338
  34.7 0.5 %inter_block.1 = (f32[128,2048]{1,0:T(8,128)S(1)}, f32[8,128]{1,0:T(8,128)S(1)}) custom-call(f32[128,2048]{1,0:T(8,128)S(1)} %get-tuple-element.39.refs_0_, bf16[128,2048]{1,0:T(8,128)(2,1)S(1)} %get-tuple-element.40.refs_1_, f32[128,2048]{1,0:T(8,128)S(1)} %get-tuple-element.33.refs_4_.refs_2_, bf16[512,128]{1,0:T(8,128)(2,1)S(1)} %get-tuple-element.41.refs_3_, ...), custom_call_target="tpu_custom_call" | custom-call | flops 67108864 | bytes 4198400 | tf_op jit(solution)/shard_map/inter_block/pallas_call | solution.py:312
  35.2 1.6 %collective-permute-start.13 = (f32[8,128]{1,0:T(8,128)S(1)}, f32[8,128]{1,0:T(8,128)S(1)}, u32[]{:S(2)}, u32[]{:S(2)}) collective-permute-start(f32[8,128]{1,0:T(8,128)S(1)} %get-tuple-element.47.refs_3_), channel_id=1, source_target_pairs={{0,2},{1,3},{2,0},{3,1},{4,6},{5,7},{6,4},{7,5},{8,10},{9,11},{10,... | collective-permute-start | bytes 12296 | tf_op jit(solution)/shard_map/ppermute | solution.py:480
  36.7 0.3 collective-permute-start.14
  37.1 1.2 %softmax_last.1.refs_0_ = bf16[128,2048]{1,0:T(8,128)(2,1)S(1)} custom-call(s32[1]{0:T(128)S(6)} %copy.12.refs_0_, bf16[128,2048]{1,0:T(8,128)(2,1)S(1)} %copy-done.2, bf16[256,512]{1,0:T(8,128)(2,1)S(1)} %pad_maximum_fusion.refs_2_, f32[128,4096]{1,0:T(8,128)S(1)} %get-tuple-element.36.refs_3_, f32[128,1024]{1,0:T(8,128)S(1)} %get-tuple-element.37.refs_4_.refs_7_, ...), custom_call_target="tpu_custom_call" | custom-call | flops 268435456 | bytes 4456452 | tf_op jit(solution)/shard_map/softmax_last/pallas_call | solution.py:312
  38.3 0.6 %collective-permute-done.13.refs_5_ = f32[8,128]{1,0:T(8,128)S(1)} collective-permute-done((f32[8,128]{1,0:T(8,128)S(1)}, f32[8,128]{1,0:T(8,128)S(1)}, u32[]{:S(2)}, u32[]{:S(2)}) %collective-permute-start.13) | collective-permute-done | bytes 4128 | tf_op jit(solution)/shard_map/ppermute | solution.py:480
  38.9 1.1 %results.1 = (bf16[128,2048]{1,0:T(8,128)(2,1)}, bf16[128,2048]{1,0:T(8,128)(2,1)}) custom-call(bf16[128,2048]{1,0:T(8,128)(2,1)S(1)} %softmax_last.1.refs_0_, f32[128,2048]{1,0:T(8,128)S(1)} %get-tuple-element.45.refs_1_, f32[128,2048]{1,0:T(8,128)S(1)} %get-tuple-element.46.refs_2_, f32[8,128]{1,0:T(8,128)S(1)} %get-tuple-element.47.refs_3_, ...), custom_call_target="tpu_custom_call" | custom-call | flops 1048576 | bytes 3686400 | tf_op jit(solution)/shard_map/results/pallas_call | solution.py:312
  (37 shorter events, 1.0 us)
Async XLA Ops:
  0.6 0.7 %copy-start.7 = (f32[16,128]{1,0:T(8,128)S(1)}, f32[16,128]{1,0:T(8,128)}, u32[]{:S(2)}) copy-start(f32[16,128]{1,0:T(8,128)} %refs_2_.3) | copy-start | bytes 24580
  0.6 1.0 %copy-start.3 = (bf16[128,2048]{1,0:T(8,128)(2,1)S(1)}, bf16[128,2048]{1,0:T(8,128)(2,1)}, u32[]{:S(2)}) copy-start(bf16[128,2048]{1,0:T(8,128)(2,1)} %refs_2_.2) | copy-start | bytes 1572868
  0.7 1.2 %copy-start.4 = (bf16[128,2048]{1,0:T(8,128)(2,1)S(1)}, bf16[128,2048]{1,0:T(8,128)(2,1)}, u32[]{:S(2)}) copy-start(bf16[128,2048]{1,0:T(8,128)(2,1)} %refs_3_.2) | copy-start | bytes 1572868
  0.7 7.1 %copy-start.5 = (bf16[128,256]{1,0:T(8,128)(2,1)S(1)}, bf16[128,256]{1,0:T(8,128)(2,1)}, u32[]{:S(2)}) copy-start(bf16[128,256]{1,0:T(8,128)(2,1)} %refs_0_.3) | copy-start | bytes 196612
  0.7 7.1 %copy-start.6 = (bf16[128,256]{1,0:T(8,128)(2,1)S(1)}, bf16[128,256]{1,0:T(8,128)(2,1)}, u32[]{:S(2)}) copy-start(bf16[128,256]{1,0:T(8,128)(2,1)} %refs_1_.4) | copy-start | bytes 196612
  0.7 10.1 %copy-start = (bf16[128,2048]{1,0:T(8,128)(2,1)S(1)}, bf16[128,2048]{1,0:T(8,128)(2,1)}, u32[]{:S(2)}) copy-start(bf16[128,2048]{1,0:T(8,128)(2,1)} %refs_3_.3) | copy-start | bytes 1572868
  0.7 10.1 %copy-start.1 = (bf16[128,2048]{1,0:T(8,128)(2,1)S(1)}, bf16[128,2048]{1,0:T(8,128)(2,1)}, u32[]{:S(2)}) copy-start(bf16[128,2048]{1,0:T(8,128)(2,1)} %refs_6_.1) | copy-start | bytes 1572868
  0.7 10.1 %copy-start.8 = (f32[2048]{0:T(1024)S(1)}, f32[2048]{0:T(1024)}, u32[]{:S(2)}) copy-start(f32[2048]{0:T(1024)} %param.15) | copy-start | bytes 24580
  3.1 10.5 %collective-permute-start.1 = (bf16[528,128]{1,0:T(8,128)(2,1)S(1)}, bf16[528,128]{1,0:T(8,128)(2,1)S(1)}, u32[]{:S(2)}, u32[]{:S(2)}) collective-permute-start(bf16[528,128]{1,0:T(8,128)(2,1)S(1)} %get-tuple-element.27), channel_id=1, source_target_pairs={{0,8},{4,12},{8,0},{12,4},{16,24},{20,28},{24,16},{28,20},{1,9},{5... | collective-permute-start | bytes 405512 | tf_op jit(solution)/shard_map/ppermute | solution.py:338
  6.2 10.4 %collective-permute-start.2 = (bf16[528,128]{1,0:T(8,128)(2,1)S(1)}, bf16[528,128]{1,0:T(8,128)(2,1)S(1)}, u32[]{:S(2)}, u32[]{:S(2)}) collective-permute-start(bf16[528,128]{1,0:T(8,128)(2,1)S(1)} %get-tuple-element.28), channel_id=1, source_target_pairs={{0,12},{4,8},{8,4},{12,0},{16,28},{20,24},{24,20},{28,16},{1,13},{... | collective-permute-start | bytes 405512 | tf_op jit(solution)/shard_map/ppermute | solution.py:338
  7.6 9.0 %collective-permute-start.3 = (bf16[528,128]{1,0:T(8,128)(2,1)S(1)}, bf16[528,128]{1,0:T(8,128)(2,1)S(1)}, u32[]{:S(2)}, u32[]{:S(2)}) collective-permute-start(bf16[528,128]{1,0:T(8,128)(2,1)S(1)} %get-tuple-element.29), channel_id=1, source_target_pairs={{0,4},{4,0},{8,12},{12,8},{16,20},{20,16},{24,28},{28,24},{1,5},{5... | collective-permute-start | bytes 405512 | tf_op jit(solution)/shard_map/ppermute | solution.py:338
  7.8 10.3 %collective-permute-start = (bf16[128,512]{1,0:T(8,128)(2,1)S(1)}, bf16[128,512]{1,0:T(8,128)(2,1)S(1)}, u32[]{:S(2)}, u32[]{:S(2)}) collective-permute-start(bf16[128,512]{1,0:T(8,128)(2,1)S(1)} %keys_beside_values.1.refs_0_), channel_id=1, source_target_pairs={{0,16},{4,20},{8,24},{12,28},{16,0},{20,4},{24,8},{28,12},{1,17},{... | collective-permute-start | bytes 393224 | tf_op jit(solution)/shard_map/ppermute | solution.py:346
  16.8 8.3 %collective-permute-start.8 = (bf16[528,128]{1,0:T(8,128)(2,1)S(1)}, bf16[528,128]{1,0:T(8,128)(2,1)S(1)}, u32[]{:S(2)}, u32[]{:S(2)}) collective-permute-start(bf16[528,128]{1,0:T(8,128)(2,1)S(1)} %group_state.1.refs_2_), channel_id=1, source_target_pairs={{0,16},{4,20},{8,24},{12,28},{16,0},{20,4},{24,8},{28,12},{1,17},{... | collective-permute-start | bytes 405512 | tf_op jit(solution)/shard_map/ppermute | solution.py:346
  18.1 12.2 %copy-start.2 = (bf16[128,2048]{1,0:T(8,128)(2,1)S(1)}, bf16[128,2048]{1,0:T(8,128)(2,1)}, u32[]{:S(2)}) copy-start(bf16[128,2048]{1,0:T(8,128)(2,1)} %refs_1_.7) | copy-start | bytes 1572868
  18.1 10.7 %collective-permute-start.4 = (bf16[256,512]{1,0:T(8,128)(2,1)S(1)}, bf16[256,512]{1,0:T(8,128)(2,1)S(1)}, u32[]{:S(2)}, u32[]{:S(2)}) collective-permute-start(bf16[256,512]{1,0:T(8,128)(2,1)S(1)} %stack_keys_values.1.refs_2_), channel_id=1, source_target_pairs={{0,8},{4,12},{8,0},{12,4},{16,24},{20,28},{24,16},{28,20},{1,9},{5... | collective-permute-start | bytes 786440 | tf_op jit(solution)/shard_map/ppermute | solution.py:338
  20.3 8.5 %collective-permute-start.5 = (bf16[256,512]{1,0:T(8,128)(2,1)S(1)}, bf16[256,512]{1,0:T(8,128)(2,1)S(1)}, u32[]{:S(2)}, u32[]{:S(2)}) collective-permute-start(bf16[256,512]{1,0:T(8,128)(2,1)S(1)} %stack_keys_values.1.refs_2_), channel_id=1, source_target_pairs={{0,4},{4,0},{8,12},{12,8},{16,20},{20,16},{24,28},{28,24},{1,5},{5... | collective-permute-start | bytes 786440 | tf_op jit(solution)/shard_map/ppermute | solution.py:338
  25.3 7.4 %collective-permute-start.9 = (bf16[512,128]{1,0:T(8,128)(2,1)S(1)}, bf16[512,128]{1,0:T(8,128)(2,1)S(1)}, u32[]{:S(2)}, u32[]{:S(2)}) collective-permute-start(bf16[512,128]{1,0:T(8,128)(2,1)S(1)} %get-tuple-element.42), channel_id=1, source_target_pairs={{0,12},{4,8},{8,4},{12,0},{16,28},{20,24},{24,20},{28,16},{1,13},{... | collective-permute-start | bytes 393224 | tf_op jit(solution)/shard_map/ppermute | solution.py:338
  25.4 9.1 %collective-permute-start.10 = (bf16[512,128]{1,0:T(8,128)(2,1)S(1)}, bf16[512,128]{1,0:T(8,128)(2,1)S(1)}, u32[]{:S(2)}, u32[]{:S(2)}) collective-permute-start(bf16[512,128]{1,0:T(8,128)(2,1)S(1)} %get-tuple-element.43), channel_id=1, source_target_pairs={{0,8},{4,12},{8,0},{12,4},{16,24},{20,28},{24,16},{28,20},{1,9},{5... | collective-permute-start | bytes 393224 | tf_op jit(solution)/shard_map/ppermute | solution.py:338
  27.3 7.3 %collective-permute-start.11 = (bf16[512,128]{1,0:T(8,128)(2,1)S(1)}, bf16[512,128]{1,0:T(8,128)(2,1)S(1)}, u32[]{:S(2)}, u32[]{:S(2)}) collective-permute-start(bf16[512,128]{1,0:T(8,128)(2,1)S(1)} %get-tuple-element.44), channel_id=1, source_target_pairs={{0,4},{4,0},{8,12},{12,8},{16,20},{20,16},{24,28},{28,24},{1,5},{5... | collective-permute-start | bytes 393224 | tf_op jit(solution)/shard_map/ppermute | solution.py:338
  28.9 8.2 %collective-permute-start.7 = (bf16[128,512]{1,0:T(8,128)(2,1)S(1)}, bf16[128,512]{1,0:T(8,128)(2,1)S(1)}, u32[]{:S(2)}, u32[]{:S(2)}) collective-permute-start(bf16[128,512]{1,0:T(8,128)(2,1)S(1)} %get-tuple-element.35), channel_id=1, source_target_pairs={{0,8},{4,12},{8,0},{12,4},{16,24},{20,28},{24,16},{28,20},{1,9},{5... | collective-permute-start | bytes 393224 | tf_op jit(solution)/shard_map/ppermute | solution.py:338
  29.3 7.8 %collective-permute-start.6 = (bf16[128,512]{1,0:T(8,128)(2,1)S(1)}, bf16[128,512]{1,0:T(8,128)(2,1)S(1)}, u32[]{:S(2)}, u32[]{:S(2)}) collective-permute-start(bf16[128,512]{1,0:T(8,128)(2,1)S(1)} %get-tuple-element.34), channel_id=1, source_target_pairs={{0,4},{4,0},{8,12},{12,8},{16,20},{20,16},{24,28},{28,24},{1,5},{5... | collective-permute-start | bytes 393224 | tf_op jit(solution)/shard_map/ppermute | solution.py:338
  35.2 3.1 %collective-permute-start.12 = (f32[8,128]{1,0:T(8,128)S(1)}, f32[8,128]{1,0:T(8,128)S(1)}, u32[]{:S(2)}, u32[]{:S(2)}) collective-permute-start(f32[8,128]{1,0:T(8,128)S(1)} %get-tuple-element.47.refs_3_), channel_id=1, source_target_pairs={{0,3},{1,2},{2,1},{3,0},{4,7},{5,6},{6,5},{7,4},{8,11},{9,10},{10,... | collective-permute-start | bytes 12296 | tf_op jit(solution)/shard_map/ppermute | solution.py:480
  35.2 3.7 %collective-permute-start.13 = (f32[8,128]{1,0:T(8,128)S(1)}, f32[8,128]{1,0:T(8,128)S(1)}, u32[]{:S(2)}, u32[]{:S(2)}) collective-permute-start(f32[8,128]{1,0:T(8,128)S(1)} %get-tuple-element.47.refs_3_), channel_id=1, source_target_pairs={{0,2},{1,3},{2,0},{3,1},{4,6},{5,7},{6,4},{7,5},{8,10},{9,11},{10,... | collective-permute-start | bytes 12296 | tf_op jit(solution)/shard_map/ppermute | solution.py:480
  36.7 2.1 %collective-permute-start.14 = (f32[8,128]{1,0:T(8,128)S(1)}, f32[8,128]{1,0:T(8,128)S(1)}, u32[]{:S(2)}, u32[]{:S(2)}) collective-permute-start(f32[8,128]{1,0:T(8,128)S(1)} %get-tuple-element.47.refs_3_), channel_id=1, source_target_pairs={{0,1},{1,0},{2,3},{3,2},{4,5},{5,4},{6,7},{7,6},{8,9},{9,8},{10,11... | collective-permute-start | bytes 12296 | tf_op jit(solution)/shard_map/ppermute | solution.py:480

commit v21 on v20

--- a/solution.py
+++ b/solution.py
@@ -337,7 +337,7 @@
     def swap(x, s):
         return lax.ppermute(x, "ctx", [(c, c ^ s) for c in range(n)])
 
-    to, back = (0, 2, 3, 1), (0, 3, 2, 1)
+    to, back = (0, 2, 3, 1), (0, 2, 3, 1)
 
     def swap_all(xs, order):
         return [swap(xs[s], s) if s else xs[s] for s in order]

time: 40.2 us -> 41.4 us (1.030)
  waiting for transfers between devices: 9.8 us -> 11 us
    ppermute x10, waiting for transfers between devices: 4.98 us -> 6.19 us  [swap(): return lax.ppermute(x, 'ctx', [(c, c ^ s) for c in range(n)])]
where the time goes in v21:
time: 41.4 us; the launch traced here: 41.2 us
  starting transfers between devices  17.9 us (43%)
  waiting for transfers between devices  11 us (27%)
  Pallas kernels  9.65 us (23%)
  between operations  1.47 us (4%)
  local copies, waits for them, and re-layouts  1.15 us (3%)
    ppermute x10, starting transfers between devices, swap(): return lax.ppermute(x, 'ctx', [(c, c ^ s) for c in range(n)])  11.6 us
    pallas_call x12, Pallas kernels, call(): pl.pallas_call(run, name=name, out_shape=list(outs), in_specs=specs, scra...  9.65 us
    ppermute x10, waiting for transfers between devices, swap(): return lax.ppermute(x, 'ctx', [(c, c ^ s) for c in range(n)])  6.19 us
    ppermute x2, starting transfers between devices, ahead(): return lax.ppermute(x, 'ctx', [(c, (c + d * group) % n) for c in range(n)])  4.33 us
    ppermute x2, waiting for transfers between devices, ahead(): return lax.ppermute(x, 'ctx', [(c, (c + d * group) % n) for c in range(n)])  4.25 us
    ppermute x3, starting transfers between devices, body(): parts = [squares] + [lax.ppermute(squares, 'head', turn) for turn in turns]  1.89 us
    unnamed x18, local copies, waits for them, and re-layouts  1.15 us
  transfers between devices with their start and end apart: 15, of which 5 were waited for; matrix products, arithmetic and copies ran while one was open for 0% of the time, Pallas kernels for 18%

profile of v21, /device:TPU:0, one launch (start us, length us, event | category | flops | bytes accessed | tf_op | source)
XLA Modules:
  0.0 41.2 jit_solution(10665609951460263318)
XLA Ops:
  0.7 0.6 %copy-done.7 = f32[16,128]{1,0:T(8,128)S(1)} copy-done((f32[16,128]{1,0:T(8,128)S(1)}, f32[16,128]{1,0:T(8,128)}, u32[]{:S(2)}) %copy-start.7) | copy-done | bytes 8216
  1.3 0.4 copy-done.3
  1.8 1.2 %block_states.1 = (bf16[528,128]{1,0:T(8,128)(2,1)S(1)}, bf16[528,128]{1,0:T(8,128)(2,1)S(1)}, bf16[528,128]{1,0:T(8,128)(2,1)S(1)}, bf16[528,128]{1,0:T(8,128)(...) custom-call(f32[128,128]{1,0:T(8,128)S(1)} %get-tuple-element.25.refs_2_.refs_0_, ...), custom_call_target="tpu_custom_call" | custom-call | flops 134217728 | bytes 2711552 | tf_op jit(solution)/shard_map/block_states/pallas_call | solution.py:312
  3.1 3.1 %collective-permute-start.1 = (bf16[528,128]{1,0:T(8,128)(2,1)S(1)}, bf16[528,128]{1,0:T(8,128)(2,1)S(1)}, u32[]{:S(2)}, u32[]{:S(2)}) collective-permute-start(bf16[528,128]{1,0:T(8,128)(2,1)S(1)} %get-tuple-element.27), channel_id=1, source_target_pairs={{0,8},{4,12},{8,0},{12,4},{16,24},{20,28},{24,16},{28,20},{1,9},{5... | collective-permute-start | bytes 405512 | tf_op jit(solution)/shard_map/ppermute | solution.py:338
  6.2 1.4 %collective-permute-start.2 = (bf16[528,128]{1,0:T(8,128)(2,1)S(1)}, bf16[528,128]{1,0:T(8,128)(2,1)S(1)}, u32[]{:S(2)}, u32[]{:S(2)}) collective-permute-start(bf16[528,128]{1,0:T(8,128)(2,1)S(1)} %get-tuple-element.28), channel_id=1, source_target_pairs={{0,12},{4,8},{8,4},{12,0},{16,28},{20,24},{24,20},{28,16},{1,13},{... | collective-permute-start | bytes 405512 | tf_op jit(solution)/shard_map/ppermute | solution.py:338
  7.8 3.0 %collective-permute-start = (bf16[128,512]{1,0:T(8,128)(2,1)S(1)}, bf16[128,512]{1,0:T(8,128)(2,1)S(1)}, u32[]{:S(2)}, u32[]{:S(2)}) collective-permute-start(bf16[128,512]{1,0:T(8,128)(2,1)S(1)} %keys_beside_values.1.refs_0_), channel_id=1, source_target_pairs={{0,16},{4,20},{8,24},{12,28},{16,0},{20,4},{24,8},{28,12},{1,17},{... | collective-permute-start | bytes 393224 | tf_op jit(solution)/shard_map/ppermute | solution.py:346
  10.8 2.8 %intra_block.1 = (f32[128,2048]{1,0:T(8,128)S(1)}, bf16[128,2048]{1,0:T(8,128)(2,1)S(1)}, f32[128,2048]{1,0:T(8,128)S(1)}, f32[128,2048]{1,0:T(8,128)S(1)}) custom-call(f32[128,128]{1,0:T(8,128)S(1)} %get-tuple-element.25.refs_2_.refs_0_, f32[128,128]{1,0:T(8,128)S(1)} %get-tuple-element.30.refs_1_, f32[16,128]{1,0:T(8,128)S(1)} %copy-done.7, ...), custom_call_target="tpu_custom_call" | custom-call | flops 134217728 | bytes 5914624 | tf_op jit(solution)/shard_map/intra_block/pallas_call | solution.py:312
  13.6 3.0 %collective-permute-done.2.refs_2_ = bf16[528,128]{1,0:T(8,128)(2,1)S(1)} collective-permute-done((bf16[528,128]{1,0:T(8,128)(2,1)S(1)}, bf16[528,128]{1,0:T(8,128)(2,1)S(1)}, u32[]{:S(2)}, u32[]{:S(2)}) %collective-permute-start.2) | collective-permute-done | bytes 135200 | tf_op jit(solution)/shard_map/ppermute | solution.py:338
  16.8 1.3 %collective-permute-start.8 = (bf16[528,128]{1,0:T(8,128)(2,1)S(1)}, bf16[528,128]{1,0:T(8,128)(2,1)S(1)}, u32[]{:S(2)}, u32[]{:S(2)}) collective-permute-start(bf16[528,128]{1,0:T(8,128)(2,1)S(1)} %group_state.1.refs_2_), channel_id=1, source_target_pairs={{0,16},{4,20},{8,24},{12,28},{16,0},{20,4},{24,8},{28,12},{1,17},{... | collective-permute-start | bytes 405512 | tf_op jit(solution)/shard_map/ppermute | solution.py:346
  18.1 2.2 %collective-permute-start.4 = (bf16[256,512]{1,0:T(8,128)(2,1)S(1)}, bf16[256,512]{1,0:T(8,128)(2,1)S(1)}, u32[]{:S(2)}, u32[]{:S(2)}) collective-permute-start(bf16[256,512]{1,0:T(8,128)(2,1)S(1)} %stack_keys_values.1.refs_2_), channel_id=1, source_target_pairs={{0,8},{4,12},{8,0},{12,4},{16,24},{20,28},{24,16},{28,20},{1,9},{5... | collective-permute-start | bytes 786440 | tf_op jit(solution)/shard_map/ppermute | solution.py:338
  20.3 0.5 %collective-permute-start.5 = (bf16[256,512]{1,0:T(8,128)(2,1)S(1)}, bf16[256,512]{1,0:T(8,128)(2,1)S(1)}, u32[]{:S(2)}, u32[]{:S(2)}) collective-permute-start(bf16[256,512]{1,0:T(8,128)(2,1)S(1)} %stack_keys_values.1.refs_2_), channel_id=1, source_target_pairs={{0,4},{4,0},{8,12},{12,8},{16,20},{20,16},{24,28},{28,24},{1,5},{5... | collective-permute-start | bytes 786440 | tf_op jit(solution)/shard_map/ppermute | solution.py:338
  20.8 4.2 %collective-permute-done.8.refs_4_ = bf16[528,128]{1,0:T(8,128)(2,1)S(1)} collective-permute-done((bf16[528,128]{1,0:T(8,128)(2,1)S(1)}, bf16[528,128]{1,0:T(8,128)(2,1)S(1)}, u32[]{:S(2)}, u32[]{:S(2)}) %collective-permute-start.8) | collective-permute-done | bytes 135200 | tf_op jit(solution)/shard_map/ppermute | solution.py:346
  25.4 1.9 %collective-permute-start.10 = (bf16[512,128]{1,0:T(8,128)(2,1)S(1)}, bf16[512,128]{1,0:T(8,128)(2,1)S(1)}, u32[]{:S(2)}, u32[]{:S(2)}) collective-permute-start(bf16[512,128]{1,0:T(8,128)(2,1)S(1)} %get-tuple-element.43), channel_id=1, source_target_pairs={{0,12},{4,8},{8,4},{12,0},{16,28},{20,24},{24,20},{28,16},{1,13},{... | collective-permute-start | bytes 393224 | tf_op jit(solution)/shard_map/ppermute | solution.py:338
  27.3 1.5 %collective-permute-start.11 = (bf16[512,128]{1,0:T(8,128)(2,1)S(1)}, bf16[512,128]{1,0:T(8,128)(2,1)S(1)}, u32[]{:S(2)}, u32[]{:S(2)}) collective-permute-start(bf16[512,128]{1,0:T(8,128)(2,1)S(1)} %get-tuple-element.44), channel_id=1, source_target_pairs={{0,4},{4,0},{8,12},{12,8},{16,20},{20,16},{24,28},{28,24},{1,5},{5... | collective-permute-start | bytes 393224 | tf_op jit(solution)/shard_map/ppermute | solution.py:338
  28.9 0.4 collective-permute-start.7
  30.3 2.4 %softmax_first.1 = (f32[128,4096]{1,0:T(8,128)S(1)}, f32[128,1024]{1,0:T(8,128)S(1)}, f32[128,1024]{1,0:T(8,128)S(1)}) custom-call(s32[1]{0:T(128)S(6)} %copy.12.refs_0_, bf16[128,2048]{1,0:T(8,128)(2,1)S(1)} %copy-done.2, bf16[256,512]{1,0:T(8,128)(2,1)S(1)} %stack_keys_values.1.refs_2_, bf16[256,512]{1,0:T(8,128)(2,1)S(1)} %collective-permute-done.4.refs_0_.refs_3_, ...), custom_call_target="tpu_custom_call" | custom-call | flops 805306368 | bytes 4456452 | tf_op jit(solution)/shard_map/softmax_first/pallas_call | solution.py:312
  32.7 1.9 %collective-permute-done.10.refs_5_ = bf16[512,128]{1,0:T(8,128)(2,1)S(1)} collective-permute-done((bf16[512,128]{1,0:T(8,128)(2,1)S(1)}, bf16[512,128]{1,0:T(8,128)(2,1)S(1)}, u32[]{:S(2)}, u32[]{:S(2)}) %collective-permute-start.10) | collective-permute-done | bytes 131104 | tf_op jit(solution)/shard_map/ppermute | solution.py:338
  34.6 1.3 %collective-permute-done.11.refs_6_ = bf16[512,128]{1,0:T(8,128)(2,1)S(1)} collective-permute-done((bf16[512,128]{1,0:T(8,128)(2,1)S(1)}, bf16[512,128]{1,0:T(8,128)(2,1)S(1)}, u32[]{:S(2)}, u32[]{:S(2)}) %collective-permute-start.11) | collective-permute-done | bytes 131104 | tf_op jit(solution)/shard_map/ppermute | solution.py:338
  35.9 0.5 %inter_block.1 = (f32[128,2048]{1,0:T(8,128)S(1)}, f32[8,128]{1,0:T(8,128)S(1)}) custom-call(f32[128,2048]{1,0:T(8,128)S(1)} %get-tuple-element.39.refs_0_, bf16[128,2048]{1,0:T(8,128)(2,1)S(1)} %get-tuple-element.40.refs_1_, f32[128,2048]{1,0:T(8,128)S(1)} %get-tuple-element.33.refs_4_.refs_2_, bf16[512,128]{1,0:T(8,128)(2,1)S(1)} %get-tuple-element.41.refs_3_, ...), custom_call_target="tpu_custom_call" | custom-call | flops 67108864 | bytes 4198400 | tf_op jit(solution)/shard_map/inter_block/pallas_call | solution.py:312
  36.4 1.4 %collective-permute-start.13 = (f32[8,128]{1,0:T(8,128)S(1)}, f32[8,128]{1,0:T(8,128)S(1)}, u32[]{:S(2)}, u32[]{:S(2)}) collective-permute-start(f32[8,128]{1,0:T(8,128)S(1)} %get-tuple-element.47.refs_3_), channel_id=1, source_target_pairs={{0,2},{1,3},{2,0},{3,1},{4,6},{5,7},{6,4},{7,5},{8,10},{9,11},{10,... | collective-permute-start | bytes 12296 | tf_op jit(solution)/shard_map/ppermute | solution.py:480
  37.9 0.4 %collective-permute-start.14 = (f32[8,128]{1,0:T(8,128)S(1)}, f32[8,128]{1,0:T(8,128)S(1)}, u32[]{:S(2)}, u32[]{:S(2)}) collective-permute-start(f32[8,128]{1,0:T(8,128)S(1)} %get-tuple-element.47.refs_3_), channel_id=1, source_target_pairs={{0,1},{1,0},{2,3},{3,2},{4,5},{5,4},{6,7},{7,6},{8,9},{9,8},{10,11... | collective-permute-start | bytes 12296 | tf_op jit(solution)/shard_map/ppermute | solution.py:480
  38.3 1.2 %softmax_last.1.refs_0_ = bf16[128,2048]{1,0:T(8,128)(2,1)S(1)} custom-call(s32[1]{0:T(128)S(6)} %copy.12.refs_0_, bf16[128,2048]{1,0:T(8,128)(2,1)S(1)} %copy-done.2, bf16[256,512]{1,0:T(8,128)(2,1)S(1)} %pad_maximum_fusion.refs_2_, f32[128,4096]{1,0:T(8,128)S(1)} %get-tuple-element.36.refs_3_, f32[128,1024]{1,0:T(8,128)S(1)} %get-tuple-element.37.refs_4_.refs_7_, ...), custom_call_target="tpu_custom_call" | custom-call | flops 268435456 | bytes 4456452 | tf_op jit(solution)/shard_map/softmax_last/pallas_call | solution.py:312
  39.5 0.6 %collective-permute-done.13.refs_5_ = f32[8,128]{1,0:T(8,128)S(1)} collective-permute-done((f32[8,128]{1,0:T(8,128)S(1)}, f32[8,128]{1,0:T(8,128)S(1)}, u32[]{:S(2)}, u32[]{:S(2)}) %collective-permute-start.13) | collective-permute-done | bytes 4128 | tf_op jit(solution)/shard_map/ppermute | solution.py:480
  40.1 1.1 %results.1 = (bf16[128,2048]{1,0:T(8,128)(2,1)}, bf16[128,2048]{1,0:T(8,128)(2,1)}) custom-call(bf16[128,2048]{1,0:T(8,128)(2,1)S(1)} %softmax_last.1.refs_0_, f32[128,2048]{1,0:T(8,128)S(1)} %get-tuple-element.45.refs_1_, f32[128,2048]{1,0:T(8,128)S(1)} %get-tuple-element.46.refs_2_, f32[8,128]{1,0:T(8,128)S(1)} %get-tuple-element.47.refs_3_, ...), custom_call_target="tpu_custom_call" | custom-call | flops 1048576 | bytes 3686400 | tf_op jit(solution)/shard_map/results/pallas_call | solution.py:312
  (37 shorter events, 1.2 us)
Async XLA Ops:
  0.6 0.7 %copy-start.7 = (f32[16,128]{1,0:T(8,128)S(1)}, f32[16,128]{1,0:T(8,128)}, u32[]{:S(2)}) copy-start(f32[16,128]{1,0:T(8,128)} %refs_2_.3) | copy-start | bytes 24580
  0.6 1.0 %copy-start.3 = (bf16[128,2048]{1,0:T(8,128)(2,1)S(1)}, bf16[128,2048]{1,0:T(8,128)(2,1)}, u32[]{:S(2)}) copy-start(bf16[128,2048]{1,0:T(8,128)(2,1)} %refs_2_.2) | copy-start | bytes 1572868
  0.7 1.2 %copy-start.4 = (bf16[128,2048]{1,0:T(8,128)(2,1)S(1)}, bf16[128,2048]{1,0:T(8,128)(2,1)}, u32[]{:S(2)}) copy-start(bf16[128,2048]{1,0:T(8,128)(2,1)} %refs_3_.2) | copy-start | bytes 1572868
  0.7 7.1 %copy-start.5 = (bf16[128,256]{1,0:T(8,128)(2,1)S(1)}, bf16[128,256]{1,0:T(8,128)(2,1)}, u32[]{:S(2)}) copy-start(bf16[128,256]{1,0:T(8,128)(2,1)} %refs_0_.3) | copy-start | bytes 196612
  0.7 7.1 %copy-start.6 = (bf16[128,256]{1,0:T(8,128)(2,1)S(1)}, bf16[128,256]{1,0:T(8,128)(2,1)}, u32[]{:S(2)}) copy-start(bf16[128,256]{1,0:T(8,128)(2,1)} %refs_1_.4) | copy-start | bytes 196612
  0.7 10.1 %copy-start = (bf16[128,2048]{1,0:T(8,128)(2,1)S(1)}, bf16[128,2048]{1,0:T(8,128)(2,1)}, u32[]{:S(2)}) copy-start(bf16[128,2048]{1,0:T(8,128)(2,1)} %refs_3_.3) | copy-start | bytes 1572868
  0.7 10.1 %copy-start.1 = (bf16[128,2048]{1,0:T(8,128)(2,1)S(1)}, bf16[128,2048]{1,0:T(8,128)(2,1)}, u32[]{:S(2)}) copy-start(bf16[128,2048]{1,0:T(8,128)(2,1)} %refs_6_.1) | copy-start | bytes 1572868
  0.7 10.1 %copy-start.8 = (f32[2048]{0:T(1024)S(1)}, f32[2048]{0:T(1024)}, u32[]{:S(2)}) copy-start(f32[2048]{0:T(1024)} %param.15) | copy-start | bytes 24580
  3.1 10.5 %collective-permute-start.1 = (bf16[528,128]{1,0:T(8,128)(2,1)S(1)}, bf16[528,128]{1,0:T(8,128)(2,1)S(1)}, u32[]{:S(2)}, u32[]{:S(2)}) collective-permute-start(bf16[528,128]{1,0:T(8,128)(2,1)S(1)} %get-tuple-element.27), channel_id=1, source_target_pairs={{0,8},{4,12},{8,0},{12,4},{16,24},{20,28},{24,16},{28,20},{1,9},{5... | collective-permute-start | bytes 405512 | tf_op jit(solution)/shard_map/ppermute | solution.py:338
  6.2 10.4 %collective-permute-start.2 = (bf16[528,128]{1,0:T(8,128)(2,1)S(1)}, bf16[528,128]{1,0:T(8,128)(2,1)S(1)}, u32[]{:S(2)}, u32[]{:S(2)}) collective-permute-start(bf16[528,128]{1,0:T(8,128)(2,1)S(1)} %get-tuple-element.28), channel_id=1, source_target_pairs={{0,12},{4,8},{8,4},{12,0},{16,28},{20,24},{24,20},{28,16},{1,13},{... | collective-permute-start | bytes 405512 | tf_op jit(solution)/shard_map/ppermute | solution.py:338
  7.6 9.0 %collective-permute-start.3 = (bf16[528,128]{1,0:T(8,128)(2,1)S(1)}, bf16[528,128]{1,0:T(8,128)(2,1)S(1)}, u32[]{:S(2)}, u32[]{:S(2)}) collective-permute-start(bf16[528,128]{1,0:T(8,128)(2,1)S(1)} %get-tuple-element.29), channel_id=1, source_target_pairs={{0,4},{4,0},{8,12},{12,8},{16,20},{20,16},{24,28},{28,24},{1,5},{5... | collective-permute-start | bytes 405512 | tf_op jit(solution)/shard_map/ppermute | solution.py:338
  7.8 10.3 %collective-permute-start = (bf16[128,512]{1,0:T(8,128)(2,1)S(1)}, bf16[128,512]{1,0:T(8,128)(2,1)S(1)}, u32[]{:S(2)}, u32[]{:S(2)}) collective-permute-start(bf16[128,512]{1,0:T(8,128)(2,1)S(1)} %keys_beside_values.1.refs_0_), channel_id=1, source_target_pairs={{0,16},{4,20},{8,24},{12,28},{16,0},{20,4},{24,8},{28,12},{1,17},{... | collective-permute-start | bytes 393224 | tf_op jit(solution)/shard_map/ppermute | solution.py:346
  16.8 8.3 %collective-permute-start.8 = (bf16[528,128]{1,0:T(8,128)(2,1)S(1)}, bf16[528,128]{1,0:T(8,128)(2,1)S(1)}, u32[]{:S(2)}, u32[]{:S(2)}) collective-permute-start(bf16[528,128]{1,0:T(8,128)(2,1)S(1)} %group_state.1.refs_2_), channel_id=1, source_target_pairs={{0,16},{4,20},{8,24},{12,28},{16,0},{20,4},{24,8},{28,12},{1,17},{... | collective-permute-start | bytes 405512 | tf_op jit(solution)/shard_map/ppermute | solution.py:346
  18.1 12.2 %copy-start.2 = (bf16[128,2048]{1,0:T(8,128)(2,1)S(1)}, bf16[128,2048]{1,0:T(8,128)(2,1)}, u32[]{:S(2)}) copy-start(bf16[128,2048]{1,0:T(8,128)(2,1)} %refs_1_.7) | copy-start | bytes 1572868
  18.1 10.7 %collective-permute-start.4 = (bf16[256,512]{1,0:T(8,128)(2,1)S(1)}, bf16[256,512]{1,0:T(8,128)(2,1)S(1)}, u32[]{:S(2)}, u32[]{:S(2)}) collective-permute-start(bf16[256,512]{1,0:T(8,128)(2,1)S(1)} %stack_keys_values.1.refs_2_), channel_id=1, source_target_pairs={{0,8},{4,12},{8,0},{12,4},{16,24},{20,28},{24,16},{28,20},{1,9},{5... | collective-permute-start | bytes 786440 | tf_op jit(solution)/shard_map/ppermute | solution.py:338
  20.3 8.5 %collective-permute-start.5 = (bf16[256,512]{1,0:T(8,128)(2,1)S(1)}, bf16[256,512]{1,0:T(8,128)(2,1)S(1)}, u32[]{:S(2)}, u32[]{:S(2)}) collective-permute-start(bf16[256,512]{1,0:T(8,128)(2,1)S(1)} %stack_keys_values.1.refs_2_), channel_id=1, source_target_pairs={{0,4},{4,0},{8,12},{12,8},{16,20},{20,16},{24,28},{28,24},{1,5},{5... | collective-permute-start | bytes 786440 | tf_op jit(solution)/shard_map/ppermute | solution.py:338
  25.3 7.4 %collective-permute-start.9 = (bf16[512,128]{1,0:T(8,128)(2,1)S(1)}, bf16[512,128]{1,0:T(8,128)(2,1)S(1)}, u32[]{:S(2)}, u32[]{:S(2)}) collective-permute-start(bf16[512,128]{1,0:T(8,128)(2,1)S(1)} %get-tuple-element.42), channel_id=1, source_target_pairs={{0,8},{4,12},{8,0},{12,4},{16,24},{20,28},{24,16},{28,20},{1,9},{5... | collective-permute-start | bytes 393224 | tf_op jit(solution)/shard_map/ppermute | solution.py:338
  25.4 9.2 %collective-permute-start.10 = (bf16[512,128]{1,0:T(8,128)(2,1)S(1)}, bf16[512,128]{1,0:T(8,128)(2,1)S(1)}, u32[]{:S(2)}, u32[]{:S(2)}) collective-permute-start(bf16[512,128]{1,0:T(8,128)(2,1)S(1)} %get-tuple-element.43), channel_id=1, source_target_pairs={{0,12},{4,8},{8,4},{12,0},{16,28},{20,24},{24,20},{28,16},{1,13},{... | collective-permute-start | bytes 393224 | tf_op jit(solution)/shard_map/ppermute | solution.py:338
  27.3 8.6 %collective-permute-start.11 = (bf16[512,128]{1,0:T(8,128)(2,1)S(1)}, bf16[512,128]{1,0:T(8,128)(2,1)S(1)}, u32[]{:S(2)}, u32[]{:S(2)}) collective-permute-start(bf16[512,128]{1,0:T(8,128)(2,1)S(1)} %get-tuple-element.44), channel_id=1, source_target_pairs={{0,4},{4,0},{8,12},{12,8},{16,20},{20,16},{24,28},{28,24},{1,5},{5... | collective-permute-start | bytes 393224 | tf_op jit(solution)/shard_map/ppermute | solution.py:338
  28.9 9.4 %collective-permute-start.7 = (bf16[128,512]{1,0:T(8,128)(2,1)S(1)}, bf16[128,512]{1,0:T(8,128)(2,1)S(1)}, u32[]{:S(2)}, u32[]{:S(2)}) collective-permute-start(bf16[128,512]{1,0:T(8,128)(2,1)S(1)} %get-tuple-element.35), channel_id=1, source_target_pairs={{0,8},{4,12},{8,0},{12,4},{16,24},{20,28},{24,16},{28,20},{1,9},{5... | collective-permute-start | bytes 393224 | tf_op jit(solution)/shard_map/ppermute | solution.py:338
  29.3 9.0 %collective-permute-start.6 = (bf16[128,512]{1,0:T(8,128)(2,1)S(1)}, bf16[128,512]{1,0:T(8,128)(2,1)S(1)}, u32[]{:S(2)}, u32[]{:S(2)}) collective-permute-start(bf16[128,512]{1,0:T(8,128)(2,1)S(1)} %get-tuple-element.34), channel_id=1, source_target_pairs={{0,4},{4,0},{8,12},{12,8},{16,20},{20,16},{24,28},{28,24},{1,5},{5... | collective-permute-start | bytes 393224 | tf_op jit(solution)/shard_map/ppermute | solution.py:338
  36.4 3.1 %collective-permute-start.12 = (f32[8,128]{1,0:T(8,128)S(1)}, f32[8,128]{1,0:T(8,128)S(1)}, u32[]{:S(2)}, u32[]{:S(2)}) collective-permute-start(f32[8,128]{1,0:T(8,128)S(1)} %get-tuple-element.47.refs_3_), channel_id=1, source_target_pairs={{0,3},{1,2},{2,1},{3,0},{4,7},{5,6},{6,5},{7,4},{8,11},{9,10},{10,... | collective-permute-start | bytes 12296 | tf_op jit(solution)/shard_map/ppermute | solution.py:480
  36.4 3.7 %collective-permute-start.13 = (f32[8,128]{1,0:T(8,128)S(1)}, f32[8,128]{1,0:T(8,128)S(1)}, u32[]{:S(2)}, u32[]{:S(2)}) collective-permute-start(f32[8,128]{1,0:T(8,128)S(1)} %get-tuple-element.47.refs_3_), channel_id=1, source_target_pairs={{0,2},{1,3},{2,0},{3,1},{4,6},{5,7},{6,4},{7,5},{8,10},{9,11},{10,... | collective-permute-start | bytes 12296 | tf_op jit(solution)/shard_map/ppermute | solution.py:480
  37.9 2.2 %collective-permute-start.14 = (f32[8,128]{1,0:T(8,128)S(1)}, f32[8,128]{1,0:T(8,128)S(1)}, u32[]{:S(2)}, u32[]{:S(2)}) collective-permute-start(f32[8,128]{1,0:T(8,128)S(1)} %get-tuple-element.47.refs_3_), channel_id=1, source_target_pairs={{0,1},{1,0},{2,3},{3,2},{4,5},{5,4},{6,7},{7,6},{8,9},{9,8},{10,11... | collective-permute-start | bytes 12296 | tf_op jit(solution)/shard_map/ppermute | solution.py:480

commit v22 on v20

--- a/solution.py
+++ b/solution.py
@@ -442,26 +442,26 @@
         return [pltpu.VMEM((keys, 2 * HD), BF16), pltpu.VMEM((tokens, keys), F32)]
 
     acc, *tops = call(
-        functools.partial(softmax_first_kernel, group, (0, 2, 1), kv_heads, pack),
+        functools.partial(softmax_first_kernel, group, (0, 1), kv_heads, pack),
         "softmax_first",
         [shape((tokens, 2 * width), F32)] + [shape((tokens, share), F32)] * kv_heads,
-        (order, queries, own, side, near),
-        scratch(3),
+        (order, queries, own, near),
+        scratch(2),
         flops=12 * tokens * width * span,
         exps=3 * tokens * span * width // HD,
         limit=room,
-        specs=[smem] + [VMEM] * 4,
+        specs=[smem] + [VMEM] * 3,
     )
     (attended,) = call(
-        functools.partial(softmax_last_kernel, group, (3,), kv_heads, pack),
+        functools.partial(softmax_last_kernel, group, (2, 3), kv_heads, pack),
         "softmax_last",
         [shape((tokens, width), BF16)],
-        (order, queries, across, acc, *tops),
-        scratch(1),
+        (order, queries, side, across, acc, *tops),
+        scratch(2),
         flops=4 * tokens * width * span,
         exps=tokens * span * width // HD,
         limit=room,
-        specs=[smem] + [VMEM] * (3 + kv_heads),
+        specs=[smem] + [VMEM] * (4 + kv_heads),
     )
 
     lin, squares = call(

time: 40.2 us -> 40.3 us (level)
    ppermute x10, waiting for transfers between devices: 4.98 us -> 5.76 us  [swap(): return lax.ppermute(x, 'ctx', [(c, c ^ s) for c in range(n)])]
    ppermute x3, waiting for transfers between devices: 0.57 us -> 0.01 us  [body(): parts = [squares] + [lax.ppermute(squares, 'head', turn) for turn in turns]]
where the time goes in v22:
time: 40.3 us; the launch traced here: 40.1 us
  starting transfers between devices  17.9 us (44%)
  waiting for transfers between devices  10 us (25%)
  Pallas kernels  9.55 us (24%)
  between operations  1.47 us (4%)
  local copies, waits for them, and re-layouts  1.15 us (3%)
    ppermute x10, starting transfers between devices, swap(): return lax.ppermute(x, 'ctx', [(c, c ^ s) for c in range(n)])  11.6 us
    pallas_call x12, Pallas kernels, call(): pl.pallas_call(run, name=name, out_shape=list(outs), in_specs=specs, scra...  9.55 us
    ppermute x10, waiting for transfers between devices, swap(): return lax.ppermute(x, 'ctx', [(c, c ^ s) for c in range(n)])  5.76 us
    ppermute x2, starting transfers between devices, ahead(): return lax.ppermute(x, 'ctx', [(c, (c + d * group) % n) for c in range(n)])  4.33 us
    ppermute x2, waiting for transfers between devices, ahead(): return lax.ppermute(x, 'ctx', [(c, (c + d * group) % n) for c in range(n)])  4.25 us
    ppermute x3, starting transfers between devices, body(): parts = [squares] + [lax.ppermute(squares, 'head', turn) for turn in turns]  1.89 us
    unnamed x18, local copies, waits for them, and re-layouts  1.15 us
  transfers between devices with their start and end apart: 15, of which 5 were waited for; matrix products, arithmetic and copies ran while one was open for 0% of the time, Pallas kernels for 18%

profile of v22, /device:TPU:0, one launch (start us, length us, event | category | flops | bytes accessed | tf_op | source)
XLA Modules:
  0.0 40.1 jit_solution(13684184754388063531)
XLA Ops:
  0.7 0.6 %copy-done.7 = f32[16,128]{1,0:T(8,128)S(1)} copy-done((f32[16,128]{1,0:T(8,128)S(1)}, f32[16,128]{1,0:T(8,128)}, u32[]{:S(2)}) %copy-start.7) | copy-done | bytes 8216
  1.3 0.4 copy-done.3
  1.8 1.2 %block_states.1 = (bf16[528,128]{1,0:T(8,128)(2,1)S(1)}, bf16[528,128]{1,0:T(8,128)(2,1)S(1)}, bf16[528,128]{1,0:T(8,128)(2,1)S(1)}, bf16[528,128]{1,0:T(8,128)(...) custom-call(f32[128,128]{1,0:T(8,128)S(1)} %get-tuple-element.25.refs_2_.refs_0_, ...), custom_call_target="tpu_custom_call" | custom-call | flops 134217728 | bytes 2711552 | tf_op jit(solution)/shard_map/block_states/pallas_call | solution.py:312
  3.1 3.1 %collective-permute-start.1 = (bf16[528,128]{1,0:T(8,128)(2,1)S(1)}, bf16[528,128]{1,0:T(8,128)(2,1)S(1)}, u32[]{:S(2)}, u32[]{:S(2)}) collective-permute-start(bf16[528,128]{1,0:T(8,128)(2,1)S(1)} %get-tuple-element.27), channel_id=1, source_target_pairs={{0,8},{4,12},{8,0},{12,4},{16,24},{20,28},{24,16},{28,20},{1,9},{5... | collective-permute-start | bytes 405512 | tf_op jit(solution)/shard_map/ppermute | solution.py:338
  6.2 1.4 %collective-permute-start.2 = (bf16[528,128]{1,0:T(8,128)(2,1)S(1)}, bf16[528,128]{1,0:T(8,128)(2,1)S(1)}, u32[]{:S(2)}, u32[]{:S(2)}) collective-permute-start(bf16[528,128]{1,0:T(8,128)(2,1)S(1)} %get-tuple-element.28), channel_id=1, source_target_pairs={{0,12},{4,8},{8,4},{12,0},{16,28},{20,24},{24,20},{28,16},{1,13},{... | collective-permute-start | bytes 405512 | tf_op jit(solution)/shard_map/ppermute | solution.py:338
  7.8 3.0 %collective-permute-start = (bf16[128,512]{1,0:T(8,128)(2,1)S(1)}, bf16[128,512]{1,0:T(8,128)(2,1)S(1)}, u32[]{:S(2)}, u32[]{:S(2)}) collective-permute-start(bf16[128,512]{1,0:T(8,128)(2,1)S(1)} %keys_beside_values.1.refs_0_), channel_id=1, source_target_pairs={{0,16},{4,20},{8,24},{12,28},{16,0},{20,4},{24,8},{28,12},{1,17},{... | collective-permute-start | bytes 393224 | tf_op jit(solution)/shard_map/ppermute | solution.py:346
  10.8 2.8 %intra_block.1 = (f32[128,2048]{1,0:T(8,128)S(1)}, bf16[128,2048]{1,0:T(8,128)(2,1)S(1)}, f32[128,2048]{1,0:T(8,128)S(1)}, f32[128,2048]{1,0:T(8,128)S(1)}) custom-call(f32[128,128]{1,0:T(8,128)S(1)} %get-tuple-element.25.refs_2_.refs_0_, f32[128,128]{1,0:T(8,128)S(1)} %get-tuple-element.30.refs_1_, f32[16,128]{1,0:T(8,128)S(1)} %copy-done.7, ...), custom_call_target="tpu_custom_call" | custom-call | flops 134217728 | bytes 5914624 | tf_op jit(solution)/shard_map/intra_block/pallas_call | solution.py:312
  13.6 3.0 %collective-permute-done.2.refs_2_ = bf16[528,128]{1,0:T(8,128)(2,1)S(1)} collective-permute-done((bf16[528,128]{1,0:T(8,128)(2,1)S(1)}, bf16[528,128]{1,0:T(8,128)(2,1)S(1)}, u32[]{:S(2)}, u32[]{:S(2)}) %collective-permute-start.2) | collective-permute-done | bytes 135200 | tf_op jit(solution)/shard_map/ppermute | solution.py:338
  16.8 1.3 %collective-permute-start.8 = (bf16[528,128]{1,0:T(8,128)(2,1)S(1)}, bf16[528,128]{1,0:T(8,128)(2,1)S(1)}, u32[]{:S(2)}, u32[]{:S(2)}) collective-permute-start(bf16[528,128]{1,0:T(8,128)(2,1)S(1)} %group_state.1.refs_2_), channel_id=1, source_target_pairs={{0,16},{4,20},{8,24},{12,28},{16,0},{20,4},{24,8},{28,12},{1,17},{... | collective-permute-start | bytes 405512 | tf_op jit(solution)/shard_map/ppermute | solution.py:346
  18.1 2.2 %collective-permute-start.4 = (bf16[256,512]{1,0:T(8,128)(2,1)S(1)}, bf16[256,512]{1,0:T(8,128)(2,1)S(1)}, u32[]{:S(2)}, u32[]{:S(2)}) collective-permute-start(bf16[256,512]{1,0:T(8,128)(2,1)S(1)} %stack_keys_values.1.refs_2_), channel_id=1, source_target_pairs={{0,8},{4,12},{8,0},{12,4},{16,24},{20,28},{24,16},{28,20},{1,9},{5... | collective-permute-start | bytes 786440 | tf_op jit(solution)/shard_map/ppermute | solution.py:338
  20.3 0.5 %collective-permute-start.5 = (bf16[256,512]{1,0:T(8,128)(2,1)S(1)}, bf16[256,512]{1,0:T(8,128)(2,1)S(1)}, u32[]{:S(2)}, u32[]{:S(2)}) collective-permute-start(bf16[256,512]{1,0:T(8,128)(2,1)S(1)} %stack_keys_values.1.refs_2_), channel_id=1, source_target_pairs={{0,4},{4,0},{8,12},{12,8},{16,20},{20,16},{24,28},{28,24},{1,5},{5... | collective-permute-start | bytes 786440 | tf_op jit(solution)/shard_map/ppermute | solution.py:338
  20.8 4.2 %collective-permute-done.8.refs_4_ = bf16[528,128]{1,0:T(8,128)(2,1)S(1)} collective-permute-done((bf16[528,128]{1,0:T(8,128)(2,1)S(1)}, bf16[528,128]{1,0:T(8,128)(2,1)S(1)}, u32[]{:S(2)}, u32[]{:S(2)}) %collective-permute-start.8) | collective-permute-done | bytes 135200 | tf_op jit(solution)/shard_map/ppermute | solution.py:346
  25.4 1.9 %collective-permute-start.10 = (bf16[512,128]{1,0:T(8,128)(2,1)S(1)}, bf16[512,128]{1,0:T(8,128)(2,1)S(1)}, u32[]{:S(2)}, u32[]{:S(2)}) collective-permute-start(bf16[512,128]{1,0:T(8,128)(2,1)S(1)} %get-tuple-element.43), channel_id=1, source_target_pairs={{0,8},{4,12},{8,0},{12,4},{16,24},{20,28},{24,16},{28,20},{1,9},{5... | collective-permute-start | bytes 393224 | tf_op jit(solution)/shard_map/ppermute | solution.py:338
  27.3 1.5 %collective-permute-start.11 = (bf16[512,128]{1,0:T(8,128)(2,1)S(1)}, bf16[512,128]{1,0:T(8,128)(2,1)S(1)}, u32[]{:S(2)}, u32[]{:S(2)}) collective-permute-start(bf16[512,128]{1,0:T(8,128)(2,1)S(1)} %get-tuple-element.44), channel_id=1, source_target_pairs={{0,4},{4,0},{8,12},{12,8},{16,20},{20,16},{24,28},{28,24},{1,5},{5... | collective-permute-start | bytes 393224 | tf_op jit(solution)/shard_map/ppermute | solution.py:338
  28.9 0.4 collective-permute-start.7
  29.3 0.3 collective-permute-start.6
  30.3 1.6 %softmax_first.1 = (f32[128,4096]{1,0:T(8,128)S(1)}, f32[128,1024]{1,0:T(8,128)S(1)}, f32[128,1024]{1,0:T(8,128)S(1)}) custom-call(s32[1]{0:T(128)S(6)} %copy.12.refs_0_, bf16[128,2048]{1,0:T(8,128)(2,1)S(1)} %copy-done.2, bf16[256,512]{1,0:T(8,128)(2,1)S(1)} %stack_keys_values.1.refs_2_, bf16[256,512]{1,0:T(8,128)(2,1)S(1)} %collective-permute-done.5.refs_1_.refs_3_), custom_call_target="tpu_custom_call" | custom-call | flops 805306368 | bytes 4194308 | tf_op jit(solution)/shard_map/softmax_first/pallas_call | solution.py:312
  31.9 0.8 %collective-permute-done.9.refs_4_ = bf16[512,128]{1,0:T(8,128)(2,1)S(1)} collective-permute-done((bf16[512,128]{1,0:T(8,128)(2,1)S(1)}, bf16[512,128]{1,0:T(8,128)(2,1)S(1)}, u32[]{:S(2)}, u32[]{:S(2)}) %collective-permute-start.9) | collective-permute-done | bytes 131104 | tf_op jit(solution)/shard_map/ppermute | solution.py:338
  32.7 1.8 %collective-permute-done.10.refs_5_ = bf16[512,128]{1,0:T(8,128)(2,1)S(1)} collective-permute-done((bf16[512,128]{1,0:T(8,128)(2,1)S(1)}, bf16[512,128]{1,0:T(8,128)(2,1)S(1)}, u32[]{:S(2)}, u32[]{:S(2)}) %collective-permute-start.10) | collective-permute-done | bytes 131104 | tf_op jit(solution)/shard_map/ppermute | solution.py:338
  34.7 0.5 %inter_block.1 = (f32[128,2048]{1,0:T(8,128)S(1)}, f32[8,128]{1,0:T(8,128)S(1)}) custom-call(f32[128,2048]{1,0:T(8,128)S(1)} %get-tuple-element.39.refs_0_, bf16[128,2048]{1,0:T(8,128)(2,1)S(1)} %get-tuple-element.40.refs_1_, f32[128,2048]{1,0:T(8,128)S(1)} %get-tuple-element.33.refs_4_.refs_2_, bf16[512,128]{1,0:T(8,128)(2,1)S(1)} %get-tuple-element.41.refs_3_, ...), custom_call_target="tpu_custom_call" | custom-call | flops 67108864 | bytes 4198400 | tf_op jit(solution)/shard_map/inter_block/pallas_call | solution.py:312
  35.2 1.6 %collective-permute-start.13 = (f32[8,128]{1,0:T(8,128)S(1)}, f32[8,128]{1,0:T(8,128)S(1)}, u32[]{:S(2)}, u32[]{:S(2)}) collective-permute-start(f32[8,128]{1,0:T(8,128)S(1)} %get-tuple-element.47.refs_3_), channel_id=1, source_target_pairs={{0,2},{1,3},{2,0},{3,1},{4,6},{5,7},{6,4},{7,5},{8,10},{9,11},{10,... | collective-permute-start | bytes 12296 | tf_op jit(solution)/shard_map/ppermute | solution.py:480
  36.7 0.3 collective-permute-start.14
  37.1 1.9 %softmax_last.1.refs_0_ = bf16[128,2048]{1,0:T(8,128)(2,1)S(1)} custom-call(s32[1]{0:T(128)S(6)} %copy.12.refs_0_, bf16[128,2048]{1,0:T(8,128)(2,1)S(1)} %copy-done.2, bf16[256,512]{1,0:T(8,128)(2,1)S(1)} %collective-permute-done.4.refs_0_.refs_2_, bf16[256,512]{1,0:T(8,128)(2,1)S(1)} %pad_maximum_fusion.refs_3_, f32[128,4096]{1,0:T(8,128)S(1)} %get-tuple-element.36.refs_4_, ...), custom_call_target="tpu_custom_call" | custom-call | flops 268435456 | bytes 4718596 | tf_op jit(solution)/shard_map/softmax_last/pallas_call | solution.py:312
  39.0 1.1 %results.1 = (bf16[128,2048]{1,0:T(8,128)(2,1)}, bf16[128,2048]{1,0:T(8,128)(2,1)}) custom-call(bf16[128,2048]{1,0:T(8,128)(2,1)S(1)} %softmax_last.1.refs_0_, f32[128,2048]{1,0:T(8,128)S(1)} %get-tuple-element.45.refs_1_, f32[128,2048]{1,0:T(8,128)S(1)} %get-tuple-element.46.refs_2_, f32[8,128]{1,0:T(8,128)S(1)} %get-tuple-element.47.refs_3_, ...), custom_call_target="tpu_custom_call" | custom-call | flops 1048576 | bytes 3686400 | tf_op jit(solution)/shard_map/results/pallas_call | solution.py:312
  (37 shorter events, 1.0 us)
Async XLA Ops:
  0.6 0.7 %copy-start.7 = (f32[16,128]{1,0:T(8,128)S(1)}, f32[16,128]{1,0:T(8,128)}, u32[]{:S(2)}) copy-start(f32[16,128]{1,0:T(8,128)} %refs_2_.3) | copy-start | bytes 24580
  0.6 1.0 %copy-start.3 = (bf16[128,2048]{1,0:T(8,128)(2,1)S(1)}, bf16[128,2048]{1,0:T(8,128)(2,1)}, u32[]{:S(2)}) copy-start(bf16[128,2048]{1,0:T(8,128)(2,1)} %refs_2_.2) | copy-start | bytes 1572868
  0.7 1.2 %copy-start.4 = (bf16[128,2048]{1,0:T(8,128)(2,1)S(1)}, bf16[128,2048]{1,0:T(8,128)(2,1)}, u32[]{:S(2)}) copy-start(bf16[128,2048]{1,0:T(8,128)(2,1)} %refs_3_.2) | copy-start | bytes 1572868
  0.7 7.1 %copy-start.5 = (bf16[128,256]{1,0:T(8,128)(2,1)S(1)}, bf16[128,256]{1,0:T(8,128)(2,1)}, u32[]{:S(2)}) copy-start(bf16[128,256]{1,0:T(8,128)(2,1)} %refs_0_.3) | copy-start | bytes 196612
  0.7 7.1 %copy-start.6 = (bf16[128,256]{1,0:T(8,128)(2,1)S(1)}, bf16[128,256]{1,0:T(8,128)(2,1)}, u32[]{:S(2)}) copy-start(bf16[128,256]{1,0:T(8,128)(2,1)} %refs_1_.4) | copy-start | bytes 196612
  0.7 10.1 %copy-start = (bf16[128,2048]{1,0:T(8,128)(2,1)S(1)}, bf16[128,2048]{1,0:T(8,128)(2,1)}, u32[]{:S(2)}) copy-start(bf16[128,2048]{1,0:T(8,128)(2,1)} %refs_3_.3) | copy-start | bytes 1572868
  0.7 10.1 %copy-start.1 = (bf16[128,2048]{1,0:T(8,128)(2,1)S(1)}, bf16[128,2048]{1,0:T(8,128)(2,1)}, u32[]{:S(2)}) copy-start(bf16[128,2048]{1,0:T(8,128)(2,1)} %refs_6_.1) | copy-start | bytes 1572868
  0.7 10.1 %copy-start.8 = (f32[2048]{0:T(1024)S(1)}, f32[2048]{0:T(1024)}, u32[]{:S(2)}) copy-start(f32[2048]{0:T(1024)} %param.15) | copy-start | bytes 24580
  3.1 10.5 %collective-permute-start.1 = (bf16[528,128]{1,0:T(8,128)(2,1)S(1)}, bf16[528,128]{1,0:T(8,128)(2,1)S(1)}, u32[]{:S(2)}, u32[]{:S(2)}) collective-permute-start(bf16[528,128]{1,0:T(8,128)(2,1)S(1)} %get-tuple-element.27), channel_id=1, source_target_pairs={{0,8},{4,12},{8,0},{12,4},{16,24},{20,28},{24,16},{28,20},{1,9},{5... | collective-permute-start | bytes 405512 | tf_op jit(solution)/shard_map/ppermute | solution.py:338
  6.2 10.4 %collective-permute-start.2 = (bf16[528,128]{1,0:T(8,128)(2,1)S(1)}, bf16[528,128]{1,0:T(8,128)(2,1)S(1)}, u32[]{:S(2)}, u32[]{:S(2)}) collective-permute-start(bf16[528,128]{1,0:T(8,128)(2,1)S(1)} %get-tuple-element.28), channel_id=1, source_target_pairs={{0,12},{4,8},{8,4},{12,0},{16,28},{20,24},{24,20},{28,16},{1,13},{... | collective-permute-start | bytes 405512 | tf_op jit(solution)/shard_map/ppermute | solution.py:338
  7.6 9.0 %collective-permute-start.3 = (bf16[528,128]{1,0:T(8,128)(2,1)S(1)}, bf16[528,128]{1,0:T(8,128)(2,1)S(1)}, u32[]{:S(2)}, u32[]{:S(2)}) collective-permute-start(bf16[528,128]{1,0:T(8,128)(2,1)S(1)} %get-tuple-element.29), channel_id=1, source_target_pairs={{0,4},{4,0},{8,12},{12,8},{16,20},{20,16},{24,28},{28,24},{1,5},{5... | collective-permute-start | bytes 405512 | tf_op jit(solution)/shard_map/ppermute | solution.py:338
  7.8 10.3 %collective-permute-start = (bf16[128,512]{1,0:T(8,128)(2,1)S(1)}, bf16[128,512]{1,0:T(8,128)(2,1)S(1)}, u32[]{:S(2)}, u32[]{:S(2)}) collective-permute-start(bf16[128,512]{1,0:T(8,128)(2,1)S(1)} %keys_beside_values.1.refs_0_), channel_id=1, source_target_pairs={{0,16},{4,20},{8,24},{12,28},{16,0},{20,4},{24,8},{28,12},{1,17},{... | collective-permute-start | bytes 393224 | tf_op jit(solution)/shard_map/ppermute | solution.py:346
  16.8 8.3 %collective-permute-start.8 = (bf16[528,128]{1,0:T(8,128)(2,1)S(1)}, bf16[528,128]{1,0:T(8,128)(2,1)S(1)}, u32[]{:S(2)}, u32[]{:S(2)}) collective-permute-start(bf16[528,128]{1,0:T(8,128)(2,1)S(1)} %group_state.1.refs_2_), channel_id=1, source_target_pairs={{0,16},{4,20},{8,24},{12,28},{16,0},{20,4},{24,8},{28,12},{1,17},{... | collective-permute-start | bytes 405512 | tf_op jit(solution)/shard_map/ppermute | solution.py:346
  18.1 12.2 %copy-start.2 = (bf16[128,2048]{1,0:T(8,128)(2,1)S(1)}, bf16[128,2048]{1,0:T(8,128)(2,1)}, u32[]{:S(2)}) copy-start(bf16[128,2048]{1,0:T(8,128)(2,1)} %refs_1_.7) | copy-start | bytes 1572868
  18.1 10.7 %collective-permute-start.4 = (bf16[256,512]{1,0:T(8,128)(2,1)S(1)}, bf16[256,512]{1,0:T(8,128)(2,1)S(1)}, u32[]{:S(2)}, u32[]{:S(2)}) collective-permute-start(bf16[256,512]{1,0:T(8,128)(2,1)S(1)} %stack_keys_values.1.refs_2_), channel_id=1, source_target_pairs={{0,8},{4,12},{8,0},{12,4},{16,24},{20,28},{24,16},{28,20},{1,9},{5... | collective-permute-start | bytes 786440 | tf_op jit(solution)/shard_map/ppermute | solution.py:338
  20.3 8.5 %collective-permute-start.5 = (bf16[256,512]{1,0:T(8,128)(2,1)S(1)}, bf16[256,512]{1,0:T(8,128)(2,1)S(1)}, u32[]{:S(2)}, u32[]{:S(2)}) collective-permute-start(bf16[256,512]{1,0:T(8,128)(2,1)S(1)} %stack_keys_values.1.refs_2_), channel_id=1, source_target_pairs={{0,4},{4,0},{8,12},{12,8},{16,20},{20,16},{24,28},{28,24},{1,5},{5... | collective-permute-start | bytes 786440 | tf_op jit(solution)/shard_map/ppermute | solution.py:338
  25.3 7.4 %collective-permute-start.9 = (bf16[512,128]{1,0:T(8,128)(2,1)S(1)}, bf16[512,128]{1,0:T(8,128)(2,1)S(1)}, u32[]{:S(2)}, u32[]{:S(2)}) collective-permute-start(bf16[512,128]{1,0:T(8,128)(2,1)S(1)} %get-tuple-element.42), channel_id=1, source_target_pairs={{0,12},{4,8},{8,4},{12,0},{16,28},{20,24},{24,20},{28,16},{1,13},{... | collective-permute-start | bytes 393224 | tf_op jit(solution)/shard_map/ppermute | solution.py:338
  25.4 9.1 %collective-permute-start.10 = (bf16[512,128]{1,0:T(8,128)(2,1)S(1)}, bf16[512,128]{1,0:T(8,128)(2,1)S(1)}, u32[]{:S(2)}, u32[]{:S(2)}) collective-permute-start(bf16[512,128]{1,0:T(8,128)(2,1)S(1)} %get-tuple-element.43), channel_id=1, source_target_pairs={{0,8},{4,12},{8,0},{12,4},{16,24},{20,28},{24,16},{28,20},{1,9},{5... | collective-permute-start | bytes 393224 | tf_op jit(solution)/shard_map/ppermute | solution.py:338
  27.3 7.3 %collective-permute-start.11 = (bf16[512,128]{1,0:T(8,128)(2,1)S(1)}, bf16[512,128]{1,0:T(8,128)(2,1)S(1)}, u32[]{:S(2)}, u32[]{:S(2)}) collective-permute-start(bf16[512,128]{1,0:T(8,128)(2,1)S(1)} %get-tuple-element.44), channel_id=1, source_target_pairs={{0,4},{4,0},{8,12},{12,8},{16,20},{20,16},{24,28},{28,24},{1,5},{5... | collective-permute-start | bytes 393224 | tf_op jit(solution)/shard_map/ppermute | solution.py:338
  28.9 8.2 %collective-permute-start.7 = (bf16[128,512]{1,0:T(8,128)(2,1)S(1)}, bf16[128,512]{1,0:T(8,128)(2,1)S(1)}, u32[]{:S(2)}, u32[]{:S(2)}) collective-permute-start(bf16[128,512]{1,0:T(8,128)(2,1)S(1)} %get-tuple-element.35), channel_id=1, source_target_pairs={{0,8},{4,12},{8,0},{12,4},{16,24},{20,28},{24,16},{28,20},{1,9},{5... | collective-permute-start | bytes 393224 | tf_op jit(solution)/shard_map/ppermute | solution.py:338
  29.3 7.8 %collective-permute-start.6 = (bf16[128,512]{1,0:T(8,128)(2,1)S(1)}, bf16[128,512]{1,0:T(8,128)(2,1)S(1)}, u32[]{:S(2)}, u32[]{:S(2)}) collective-permute-start(bf16[128,512]{1,0:T(8,128)(2,1)S(1)} %get-tuple-element.34), channel_id=1, source_target_pairs={{0,4},{4,0},{8,12},{12,8},{16,20},{20,16},{24,28},{28,24},{1,5},{5... | collective-permute-start | bytes 393224 | tf_op jit(solution)/shard_map/ppermute | solution.py:338
  35.2 3.8 %collective-permute-start.12 = (f32[8,128]{1,0:T(8,128)S(1)}, f32[8,128]{1,0:T(8,128)S(1)}, u32[]{:S(2)}, u32[]{:S(2)}) collective-permute-start(f32[8,128]{1,0:T(8,128)S(1)} %get-tuple-element.47.refs_3_), channel_id=1, source_target_pairs={{0,3},{1,2},{2,1},{3,0},{4,7},{5,6},{6,5},{7,4},{8,11},{9,10},{10,... | collective-permute-start | bytes 12296 | tf_op jit(solution)/shard_map/ppermute | solution.py:480
  35.2 3.8 %collective-permute-start.13 = (f32[8,128]{1,0:T(8,128)S(1)}, f32[8,128]{1,0:T(8,128)S(1)}, u32[]{:S(2)}, u32[]{:S(2)}) collective-permute-start(f32[8,128]{1,0:T(8,128)S(1)} %get-tuple-element.47.refs_3_), channel_id=1, source_target_pairs={{0,2},{1,3},{2,0},{3,1},{4,6},{5,7},{6,4},{7,5},{8,10},{9,11},{10,... | collective-permute-start | bytes 12296 | tf_op jit(solution)/shard_map/ppermute | solution.py:480
  36.7 2.2 %collective-permute-start.14 = (f32[8,128]{1,0:T(8,128)S(1)}, f32[8,128]{1,0:T(8,128)S(1)}, u32[]{:S(2)}, u32[]{:S(2)}) collective-permute-start(f32[8,128]{1,0:T(8,128)S(1)} %get-tuple-element.47.refs_3_), channel_id=1, source_target_pairs={{0,1},{1,0},{2,3},{3,2},{4,5},{5,4},{6,7},{7,6},{8,9},{9,8},{10,11... | collective-permute-start | bytes 12296 | tf_op jit(solution)/shard_map/ppermute | solution.py:480
